TPU v7x, 32 devices: a whole 2x2x4 slice. The times are simulated.
32 devices in a mesh: groups: 2 (over y), tp: 8 (over z, x), sub: 2 (over core).
Axes of the slice: x: 2, y: 2, z: 4, core: 2. Of those that a mesh axis runs over, the one named last changes fastest.
Arguments:
- queries: bfloat16 [4, 32, 64, 576], P(('groups', 'sub'), 'tp'), parts along dimension 0, may hold values from -48 to 48
- kv_cache: bfloat16 [4, 32, 256, 576], P(('groups', 'sub'), 'tp'), parts along dimension 0, may hold values from -6 to 6
- cache_lengths: int32 [4, 32], P(('groups', 'sub'), 'tp'), parts along dimension 0, may hold values from 1 to 256, as said below
- live_counts: int32 [4, 8], P(('groups', 'sub')), parts along dimension 0, may hold values from 0 to 4, as said below
- stream: bfloat16 [4, 32, 7168], P(('groups', 'sub'), 'tp'), parts along dimension 0, may hold values from -6 to 6
- norm_gain: float32 [7168], replicated, may hold values from 0.1 to 1.9
- w_gate: bfloat16 [9216, 7168], P('tp'), may hold values from -0.0625 to 0.0625
- w_up: bfloat16 [9216, 7168], P('tp'), may hold values from -0.0625 to 0.0625
- w_down: bfloat16 [9216, 7168], P('tp'), may hold values from -0.0625 to 0.0625
Outputs:
- latent_ctx: bfloat16 [4, 32, 64, 512], P(('groups', 'sub'), 'tp'), parts along dimension 0
- layer_out: bfloat16 [4, 8, 7168], P(('groups', 'sub'), 'tp'), parts along dimension 0
There are 2 independent parts, one for each index of `groups`. A program takes and returns all parts, laid end to end along the dimension named above; an argument that names none is the same for every part. Nothing has to cross between parts.
Inputs may be any that keep to these rules, and one draw needn't show every extreme that they name: `live_counts`: in each sub-batch the counts add up to 8; some device holds 4 live slots. `cache_lengths`: every device has a slot of length 256.
All inputs are finite; a program needn't handle non-finite values.
Results may differ from a plain program's by a relative error of at most 0.0051.
Values may be sent and summed in bfloat16 or wider, within the bound.
No kernel may reach another device: no remote copies, remote signals or barrier semaphores. Data moves between devices by JAX's collectives and lax.ppermute only.
A program may use at most 128 MiB of HBM per device.

v0:
```python
import jax
import jax.numpy as jnp
from jax import lax
from jax.sharding import PartitionSpec as P

KVL = 512


score_scale = 192.0 ** (-0.5)
norm_eps = 1e-06


def token_owner(counts_row):
    run_ends = jnp.cumsum(counts_row)
    starts = run_ends - counts_row
    positions = jnp.arange(counts_row.shape[0], dtype=jnp.int32)
    owners = jnp.sum((run_ends[None, :] <= positions[:, None]).astype(jnp.int32), axis=1)
    places = positions - starts[owners]
    return (owners, places)


def attend(queries_s, cache_s, lengths, in_use):
    scores = (
        jnp.einsum("shd,spd->shp", queries_s, cache_s, preferred_element_type=jnp.float32)
        * score_scale
    )
    visible = jnp.arange(cache_s.shape[1], dtype=jnp.int32)[None, None, :] < lengths[:, None, None]
    scores = jnp.where(visible, scores, -jnp.inf)
    row_max = jnp.max(scores, axis=2, keepdims=True)
    weights = jnp.exp(scores - row_max)
    weights_bf = (weights / jnp.sum(weights, axis=2, keepdims=True)).astype(jnp.bfloat16)
    values = cache_s[:, :, :KVL]
    context = jnp.einsum("shp,spd->shd", weights_bf, values, preferred_element_type=jnp.float32)
    return jnp.where(in_use[:, None, None], context, 0.0).astype(jnp.bfloat16)


def expand(rows_in, norm_gain, w_gate, w_up):
    widened = rows_in.astype(jnp.float32)
    inv_rms = lax.rsqrt(jnp.mean(widened * widened, axis=1, keepdims=True) + norm_eps)
    normed = (widened * inv_rms * norm_gain).astype(jnp.bfloat16)
    contract = (((1,), (1,)), ((), ()))
    gate_out = lax.dot_general(normed, w_gate, contract, preferred_element_type=jnp.float32)
    up_out = lax.dot_general(normed, w_up, contract, preferred_element_type=jnp.float32)
    return (jax.nn.silu(gate_out) * up_out).astype(jnp.bfloat16)


def shards(queries, kv_cache, cache_lengths, live_counts, stream, norm_gain, w_gate, w_up, w_down):
    slot_count = queries.shape[1]
    device = lax.axis_index("tp")
    counts_row = live_counts[0]
    own_count = lax.dynamic_index_in_dim(counts_row, device, 0, keepdims=False)
    in_use = jnp.arange(slot_count, dtype=jnp.int32) < own_count
    latent_ctx = attend(queries[0], kv_cache[0], cache_lengths[0], in_use)[None]
    local_rows = stream[0]
    owners, places = token_owner(counts_row)
    gathered = lax.all_gather(local_rows, "tp", axis=0, tiled=True)
    compact = jnp.take(gathered, owners * slot_count + places, axis=0)
    own_row = lax.dynamic_slice_in_dim(compact, device, 1, 0).astype(jnp.float32)
    hidden = expand(compact, norm_gain, w_gate, w_up)
    down_sum = lax.psum_scatter(
        jnp.dot(hidden, w_down, preferred_element_type=jnp.float32),
        "tp",
        scatter_dimension=0,
        tiled=True,
    )
    layer_out = (down_sum + own_row).astype(jnp.bfloat16)[None]
    return (latent_ctx, layer_out)


def solution(mesh):
    in_specs = (
        P(("groups", "sub"), "tp", None, None),
        P(("groups", "sub"), "tp", None, None),
        P(("groups", "sub"), "tp"),
        P(("groups", "sub"), None),
        P(("groups", "sub"), "tp", None),
        P(),
        P("tp", None),
        P("tp", None),
        P("tp", None),
    )
    out_specs = (P(("groups", "sub"), "tp", None, None), P(("groups", "sub"), "tp", None))
    return jax.shard_map(shards, mesh=mesh, in_specs=in_specs, out_specs=out_specs, check_vma=False)
```

profile of v0, /device:TPU:0, one launch (start us, length us, event | category | flops | bytes accessed | tf_op | source)
XLA Modules:
  0.0 152.8 jit_solution(16390478457816924890)
XLA Ops:
  7.2 0.0 copy-start
  7.2 0.0 copy-start.2
  7.2 0.0 all-reduce.3.cloned.1.call-start
  7.2 0.9 reduce-window.8
  8.1 0.7 bitcast_subtract_fusion.1
  8.8 0.1 convert_reduce_fusion
  8.9 0.6 gather_fusion
  9.6 0.9 copy.23
  10.5 34.1 %all-gather = bf16[1,32,7168]{2,0,1:T(2,128)(2,1)S(1)} all-gather(bf16[1,4,7168]{2,0,1:T(2,128)(2,1)S(1)} %copy.23), channel_id=2, replica_groups=mesh['groups'=2,'tp'=8,'sub'=2] {'tp'}, dimensions={1}, use_global_device_ids=true | all-gather | bytes 516096 | tf_op jit(solution)/shard_map/all_gather | solution.py:56
  44.6 0.2 copy.29
  44.8 0.6 gather_fusion.1
  45.4 0.2 fusion.17
  45.7 10.1 %fusion.30 = f32[8,1152]{1,0:T(8,128)S(1)} fusion(bf16[1152,7168]{1,0:T(8,128)(2,1)} %param.15, bf16[8,7168]{1,0:T(8,128)(2,1)S(1)} %get-tuple-element.3, f32[7168]{0:T(1024)} %param.14, f32[8]{0:T(128)S(1)} %add_rsqrt_fusion), kind=kOutput, calls=%fused_computation.34 | convolution fusion | flops 132349952 | bytes 16695328 | tf_op jit(solution)/shard_map/dot_general | solution.py:42
  55.7 0.0 copy-done.2
  55.7 0.0 copy-start.3
  55.7 0.0 copy-start.4
  55.8 0.0 copy-start.1
  55.8 0.0 copy-start.5
  55.8 16.4 %fusion.15 = f32[8,7168]{1,0:T(8,128)} fusion(bf16[1152,7168]{1,0:T(8,128)(2,1)} %param.17, bf16[1152,7168]{1,0:T(8,128)(2,1)} %param.16, f32[8,1152]{1,0:T(8,128)S(1)} %fusion.30, bf16[8,7168]{1,0:T(8,128)(2,1)S(1)} %get-tuple-element.3, f32[7168]{0:T(1024)S(1)} %copy-done.2, f32[8]{0:T(128)S(1)} %add_rsqrt_fusion), kind=kOutput, calls=%fused_computation.15 | convolution fusion | flops 264525824 | bytes 33439776 | tf_op jit(solution)/shard_map/dot_general | solution.py:61
  72.1 0.0 all-reduce.3.cloned.1.call-update
  72.2 0.0 copy-done.3
  72.2 0.6 constant_dynamic-slice_fusion
  72.8 0.0 copy-done.4
  72.8 0.1 iota_compare_fusion.1
  72.8 0.0 copy-done
  72.8 0.0 copy-done.1
  72.8 0.3 fusion.9
  73.2 0.2 fusion.38
  73.4 0.7 iota_compare_fusion.2
  74.1 0.7 copy.21
  74.8 0.0 copy-done.5
  74.8 0.6 dynamic-slice.1
  75.5 1.3 fusion.13
  76.7 67.0 %all-reduce.3.cloned.1.call-done = f32[8,7168]{1,0:T(8,128)} async-done(((f32[8,7168]{1,0:T(8,128)}), f32[8,7168]{1,0:T(8,128)}) %all-reduce.3.cloned.1.call-update) | async-done | bytes 229392
  143.7 2.3 %fusion.27 = bf16[1,1,7168]{2,1,0:T(2,128)(2,1)} fusion(f32[8,7168]{1,0:T(8,128)} %all-reduce.3.cloned.1.call-done, u32[]{:T(128)} %bitcast.14, bf16[8,7168]{1,0:T(8,128)(2,1)S(1)} %get-tuple-element.3, s32[]{:T(128)S(6)} %select_n.43), kind=kLoop, calls=%fused_computation.33 | loop fusion | flops 21504 | bytes 57352 | tf_op jit(solution)/shard_map/broadcast_in_dim | solution.py:66
  (6 shorter events, 0.0 us)
Async XLA Ops:
  7.2 65.7 %copy-start = (bf16[1,4,64,576]{3,2,1,0:T(8,128)(2,1)S(1)}, bf16[1,4,64,576]{3,2,1,0:T(8,128)(2,1)}, u32[]{:S(2)}) copy-start(bf16[1,4,64,576]{3,2,1,0:T(8,128)(2,1)} %param.9) | copy-start | bytes 884740
  7.2 48.6 %copy-start.2 = (f32[7168]{0:T(1024)S(1)}, f32[7168]{0:T(1024)}, u32[]{:S(2)}) copy-start(f32[7168]{0:T(1024)} %param.14) | copy-start | bytes 86020
  7.2 136.5 %all-reduce.3.cloned.1.call-start = ((), (), s32[]{:S(2)}) async-start(), calls=%async_computation | async-start | bytes 458752
  55.7 16.4 %copy-start.3 = (s32[1,8]{1,0:T(1,128)S(1)}, s32[1,8]{1,0:T(1,128)}, u32[]{:S(2)}) copy-start(s32[1,8]{1,0:T(1,128)} %param.12) | copy-start | bytes 100
  55.7 17.0 %copy-start.4 = (s32[1,4]{1,0:T(1,128)S(1)}, s32[1,4]{1,0:T(1,128)}, u32[]{:S(2)}) copy-start(s32[1,4]{1,0:T(1,128)} %param.11) | copy-start | bytes 52
  55.8 17.1 %copy-start.1 = (bf16[1,4,256,576]{2,3,1,0:T(8,128)(2,1)S(1)}, bf16[1,4,256,576]{2,3,1,0:T(8,128)(2,1)}, u32[]{:S(2)}) copy-start(bf16[1,4,256,576]{2,3,1,0:T(8,128)(2,1)} %param.10) | copy-start | bytes 3538948
  55.8 19.0 %copy-start.5 = (u32[32]{0:T(128)S(1)}, u32[32]{0:T(128)}, u32[]{:S(2)}) copy-start(u32[32]{0:T(128)} %constant.58) | copy-start | bytes 388
Sparse Core Ops, SparseCore 0:
  72.3 71.3 all-reduce.2
where the time goes:
time: 153 us
  waiting for transfers between devices  67 us (44%)
  blocking collectives  34.1 us (22%)
  matrix products  28.1 us (18%)
  between operations  14.2 us (9%)
  other arithmetic  5.14 us (3%)
  local copies, waits for them, and re-layouts  4.31 us (3%)
    unnamed x2, waiting for transfers between devices  67 us
    all_gather x1, blocking collectives, shards(): gathered = lax.all_gather(local_rows, 'tp', axis=0, tiled=True)  34.1 us
    dot_general x1, matrix products, shards(): jnp.dot(hidden, w_down, preferred_element_type=jnp.float32)  16.4 us
    dot_general x1, matrix products, expand(): lax.dot_general(normed, w_gate, contract, preferred_element_type=jnp.floa...  10.1 us
  transfers between devices with their start and end apart: 1, of which 1 were waited for; matrix products, arithmetic and copies ran while one was open for 3% of the time, Pallas kernels for 0%

commit v1 on v0

v1 whole, which is shorter than its diff:
```python
import jax
import jax.numpy as jnp
from jax import lax
from jax.experimental import pallas as pl
from jax.experimental.pallas import tpu as pltpu
from jax.sharding import PartitionSpec as P

KVL = 512
MIB = 1024 * 1024

score_scale = 192.0 ** (-0.5)
norm_eps = 1e-06


def bit_reverse(value, bits):
    out = 0
    for bit in range(bits):
        out |= ((value >> bit) & 1) << (bits - 1 - bit)
    return out


def swap(x, bit, size):
    return lax.ppermute(x, "tp", [(i, i ^ (1 << bit)) for i in range(size)])


def attend(queries_s, cache_s, lengths, in_use):
    scores = (
        jnp.einsum("shd,spd->shp", queries_s, cache_s, preferred_element_type=jnp.float32)
        * score_scale
    )
    visible = jnp.arange(cache_s.shape[1], dtype=jnp.int32)[None, None, :] < lengths[:, None, None]
    scores = jnp.where(visible, scores, -jnp.inf)
    row_max = jnp.max(scores, axis=2, keepdims=True)
    weights = jnp.exp(scores - row_max)
    weights_bf = (weights / jnp.sum(weights, axis=2, keepdims=True)).astype(jnp.bfloat16)
    values = cache_s[:, :, :KVL]
    context = jnp.einsum("shp,spd->shd", weights_bf, values, preferred_element_type=jnp.float32)
    return jnp.where(in_use[:, None, None], context, 0.0).astype(jnp.bfloat16)


def pick_matrix(counts_row, device, size, slots, bits):
    order = jnp.array([bit_reverse(p, bits) for p in range(size)], jnp.int32)
    owner = (order ^ device)[:, None]
    every = jnp.arange(size, dtype=jnp.int32)[None, :]
    start = jnp.sum(jnp.where(every < owner, counts_row[None, :], 0), axis=1)
    count = jnp.sum(jnp.where(every == owner, counts_row[None, :], 0), axis=1)
    place = jnp.arange(slots, dtype=jnp.int32)[None, :]
    request = jnp.where(place < count[:, None], start[:, None] + place, -1)
    return (request[None] == (order ^ device)[:, None, None]).astype(jnp.bfloat16).reshape(size, size * slots)


def load_rows(weight, first, rows, after):
    pieces = 4 if rows % 64 == 0 else 1
    step = rows // pieces

    def body(weight_ref, after_ref, out_ref, sems):
        copies = [
            pltpu.make_async_copy(
                weight_ref.at[pl.ds(first + i * step, step)], out_ref.at[pl.ds(i * step, step)], sems.at[i]
            )
            for i in range(pieces)
        ]
        for copy in copies:
            copy.start()
        for copy in copies:
            copy.wait()

    return pl.pallas_call(
        body,
        out_shape=pltpu.VMEM((rows, weight.shape[1]), weight.dtype),
        in_specs=[pl.BlockSpec(memory_space=pl.ANY)] * 2,
        out_specs=pl.BlockSpec(memory_space=pltpu.VMEM),
        scratch_shapes=[pltpu.SemaphoreType.DMA((pieces,))],
        compiler_params=pltpu.CompilerParams(vmem_limit_bytes=2 * MIB),
        cost_estimate=pl.CostEstimate(
            flops=0, transcendentals=0, bytes_accessed=2 * rows * weight.shape[1] * 2
        ),
        name="load_rows",
    )(pltpu.with_memory_space_constraint(weight, pltpu.HBM), after)


def feed_forward(pick, gain, blocks, gate_parts, up_parts, w_up, w_down):
    requests = pick.shape[0]
    units, width = w_down.shape
    block_count, gate_count, up_count = len(blocks), len(gate_parts), len(up_parts)
    loaded = sum(part.shape[0] for part in up_parts)
    late = units - loaded
    half = requests // 2
    column = 1024
    pieces = 8 if units % 128 == 0 else 1

    def body(*refs):
        pick_ref, gain_ref = refs[:2]
        refs = refs[2:]
        block_refs, refs = refs[:block_count], refs[block_count:]
        gate_refs, refs = refs[:gate_count], refs[gate_count:]
        up_refs, refs = refs[:up_count], refs[up_count:]
        up_hbm, down_hbm, keep_ref, send_ref, rows_ref, normed_ref, up_late, down_ref, up_sems, down_sems = refs

        copies_up = []
        if late:
            up_pieces = 4 if late % 64 == 0 else 1
            step = late // up_pieces
            copies_up = [
                pltpu.make_async_copy(
                    up_hbm.at[pl.ds(loaded + i * step, step)], up_late.at[pl.ds(i * step, step)], up_sems.at[i]
                )
                for i in range(up_pieces)
            ]
        step = units // pieces
        copies_down = [
            pltpu.make_async_copy(
                down_hbm.at[pl.ds(i * step, step)], down_ref.at[pl.ds(i * step, step)], down_sems.at[i]
            )
            for i in range(pieces)
        ]
        for copy in copies_up + copies_down:
            copy.start()

        pick_now = pick_ref[...]
        total = jnp.zeros((requests, 1), jnp.float32)
        for c in range(0, width, column):
            gathered = jnp.concatenate([ref[:, c : c + column].astype(jnp.float32) for ref in block_refs], axis=0)
            rows = jnp.dot(pick_now, gathered.astype(jnp.bfloat16), preferred_element_type=jnp.float32)
            rows_ref[:, c : c + column] = rows
            total += jnp.sum(rows * rows, axis=1, keepdims=True)
        inv_rms = lax.rsqrt(total / width + norm_eps)
        normed_ref[...] = (rows_ref[...] * inv_rms * gain_ref[...]).astype(jnp.bfloat16)
        normed = normed_ref[...]

        def project(ref):
            rows = ref.shape[0]
            chunk = 192 if rows % 192 == 0 else rows
            return [
                lax.dot_general(
                    ref[j : j + chunk, :], normed, (((1,), (1,)), ((), ())), preferred_element_type=jnp.float32
                )
                for j in range(0, rows, chunk)
            ]

        gate_out = jnp.concatenate([g for ref in gate_refs for g in project(ref)], axis=0)
        up_list = [u for ref in up_refs for u in project(ref)]
        if late:
            for copy in copies_up:
                copy.wait()
            up_list += project(up_late)
        up_out = jnp.concatenate(up_list, axis=0)
        hidden = (jax.nn.silu(gate_out) * up_out).T.astype(jnp.bfloat16)
        for copy in copies_down:
            copy.wait()
        for c in range(0, width, column):
            out = jnp.dot(hidden, down_ref[:, c : c + column], preferred_element_type=jnp.float32)
            first = lax.broadcasted_iota(jnp.int32, out.shape, 0) == 0
            out += jnp.where(first, rows_ref[:, c : c + column], 0.0)
            keep_ref[:, c : c + column] = out[:half]
            send_ref[:, c : c + column] = out[half:]

    vmem = pl.BlockSpec(memory_space=pltpu.VMEM)
    anywhere = pl.BlockSpec(memory_space=pl.ANY)
    out = jax.ShapeDtypeStruct((half, width), jnp.float32)
    return pl.pallas_call(
        body,
        out_shape=(out, out),
        in_specs=[vmem] * (2 + block_count + gate_count + up_count) + [anywhere] * 2,
        out_specs=(vmem, vmem),
        scratch_shapes=[
            pltpu.VMEM((requests, width), jnp.float32),
            pltpu.VMEM((requests, width), jnp.bfloat16),
            pltpu.VMEM((max(late, 16), width), jnp.bfloat16),
            pltpu.VMEM((units, width), jnp.bfloat16),
            pltpu.SemaphoreType.DMA((4,)),
            pltpu.SemaphoreType.DMA((pieces,)),
        ],
        compiler_params=pltpu.CompilerParams(vmem_limit_bytes=27 * MIB),
        cost_estimate=pl.CostEstimate(
            flops=6 * requests * units * width, transcendentals=requests * units, bytes_accessed=4 * units * width
        ),
        name="feed_forward",
    )(
        pick,
        gain[None],
        *blocks,
        *gate_parts,
        *up_parts,
        pltpu.with_memory_space_constraint(w_up, pltpu.HBM),
        pltpu.with_memory_space_constraint(w_down, pltpu.HBM),
    )


def make_shards(size):
    bits = size.bit_length() - 1

    def shards(queries, kv_cache, cache_lengths, live_counts, stream, norm_gain, w_gate, w_up, w_down):
        slots = queries.shape[1]
        units = w_gate.shape[0]
        device = lax.axis_index("tp")
        counts_row = live_counts[0]
        pick = pick_matrix(counts_row, device, size, slots, bits)

        part = units // 2 if units % 32 == 0 else units
        jobs = [(w_gate, first) for first in range(0, units, part)] + [(w_up, 0)]
        loaded = []
        blocks = [stream[0]]
        for step in range(bits):
            for weight, first in jobs[:1]:
                loaded.append(load_rows(weight, first, part, blocks[-1]))
            jobs = jobs[1:]
            if len(blocks) > 4:
                blocks = [jnp.concatenate(blocks, axis=0)]
            blocks = blocks + [swap(block, bits - 1 - step, size) for block in blocks]
        keep, send = feed_forward(
            pick, norm_gain, blocks, loaded[: units // part], loaded[units // part :], w_up, w_down
        )

        queries, send = lax.optimization_barrier((queries, send))
        own_count = jnp.sum(jnp.where(jnp.arange(size, dtype=jnp.int32) == device, counts_row, 0))
        in_use = jnp.arange(slots, dtype=jnp.int32) < own_count
        latent_ctx = attend(queries[0], kv_cache[0], cache_lengths[0], in_use)[None]

        for bit in range(bits):
            arrived = swap(send, bit, size)
            if bit == bits - 1:
                return (latent_ctx, (keep + arrived).astype(jnp.bfloat16)[None])
            half = keep.shape[0] // 2
            send = keep[half:] + arrived[half:]
            keep = keep[:half] + arrived[:half]

    return shards


def solution(mesh):
    in_specs = (
        P(("groups", "sub"), "tp", None, None),
        P(("groups", "sub"), "tp", None, None),
        P(("groups", "sub"), "tp"),
        P(("groups", "sub"), None),
        P(("groups", "sub"), "tp", None),
        P(),
        P("tp", None),
        P("tp", None),
        P("tp", None),
    )
    out_specs = (P(("groups", "sub"), "tp", None, None), P(("groups", "sub"), "tp", None))
    return jax.shard_map(
        make_shards(mesh.shape["tp"]), mesh=mesh, in_specs=in_specs, out_specs=out_specs, check_vma=False
    )
```

time: 153 us -> 64.6 us (0.42)
  waiting for transfers between devices: 67 us -> 10.7 us
  blocking collectives: 34.1 us -> 0 us
  Pallas kernels: 0 us -> 27.3 us
  matrix products: 28.1 us -> 1.64 us
  between operations: 14.2 us -> 0.82 us
  starting transfers between devices: 0.04 us -> 13 us
  local copies, waits for them, and re-layouts: 4.31 us -> 6.35 us
    unnamed x2 -> x0, waiting for transfers between devices: 67 us -> none
    all_gather x1 -> x0, blocking collectives: 34.1 us -> none  [shards(): gathered = lax.all_gather(local_rows, 'tp', axis=0, tiled=True)]
    pallas_call x0 -> x4, Pallas kernels: none -> 27.3 us  [the longest x1 16.6 us: feed_forward(): pl.pallas_call(body, out_shape=(out, out), in_specs=[vmem] * (2 + block_c...]
    dot_general x2 -> x0, matrix products: 26.4 us -> none  [the longest x1 16.4 us: shards(): jnp.dot(hidden, w_down, preferred_element_type=jnp.float32)]
    ppermute x0 -> x10, starting transfers between devices: none -> 13 us  [swap(): return lax.ppermute(x, 'tp', [(i, i ^ 1 << bit) for i in range(size)])]
    ppermute x0 -> x10, waiting for transfers between devices: none -> 10.7 us  [swap(): return lax.ppermute(x, 'tp', [(i, i ^ 1 << bit) for i in range(size)])]
    unnamed x16 -> x19, local copies, waits for them, and re-layouts: 2.47 us -> 5.97 us
    broadcast_in_dim x1, other arithmetic: 2.28 us -> 0.65 us  [shards(): return (latent_ctx, (keep + arrived).astype(jnp.bfloat16)[None])]
  transfers between devices with their start and end apart: 1 -> 10, of which waited for: 1 -> 4; matrix products, arithmetic and copies ran while one was open for 3% -> 10% of each run, Pallas kernels for 0% -> 17%
where the time goes in v1:
time: 64.6 us; the launch traced here: 64.4 us
  Pallas kernels  27.3 us (42%)
  starting transfers between devices  13 us (20%)
  waiting for transfers between devices  10.7 us (17%)
  local copies, waits for them, and re-layouts  6.35 us (10%)
  other arithmetic  4.58 us (7%)
  matrix products  1.64 us (3%)
  between operations  0.82 us (1%)
    pallas_call x1, Pallas kernels, feed_forward(): pl.pallas_call(body, out_shape=(out, out), in_specs=[vmem] * (2 + block_c...  16.6 us
    ppermute x10, starting transfers between devices, swap(): return lax.ppermute(x, 'tp', [(i, i ^ 1 << bit) for i in range(size)])  13 us
    pallas_call x3, Pallas kernels, load_rows(): pl.pallas_call(body, out_shape=pltpu.VMEM((rows, weight.shape[1]), weight...  10.8 us
    ppermute x10, waiting for transfers between devices, swap(): return lax.ppermute(x, 'tp', [(i, i ^ 1 << bit) for i in range(size)])  10.7 us
    unnamed x19, local copies, waits for them, and re-layouts  5.97 us
  transfers between devices with their start and end apart: 10, of which 4 were waited for; matrix products, arithmetic and copies ran while one was open for 10% of the time, Pallas kernels for 17%

profile of v1, /device:TPU:0, one launch (start us, length us, event | category | flops | bytes accessed | tf_op | source)
XLA Modules:
  0.0 64.4 jit_solution(13812241623385411022)
XLA Ops:
  0.6 0.0 copy-start
  0.6 4.1 %collective-permute-start = (bf16[4,7168]{1,0:T(4,128)(2,1)}, bf16[4,7168]{1,0:T(4,128)(2,1)S(1)}, u32[]{:S(2)}, u32[]{:S(2)}) collective-permute-start(bf16[4,7168]{1,0:T(4,128)(2,1)} %bitcast.28), channel_id=1, source_target_pairs={{0,8},{2,10},{4,12},{6,14},{8,0},{10,2},{12,4},{14,6},{1,9},{3,11}... | collective-permute-start | bytes 172040 | tf_op jit(solution)/shard_map/ppermute | solution.py:23
  4.7 1.6 %collective-permute-start.1 = (bf16[4,7168]{1,0:T(4,128)(2,1)}, bf16[4,7168]{1,0:T(4,128)(2,1)S(1)}, u32[]{:S(2)}, u32[]{:S(2)}) collective-permute-start(bf16[4,7168]{1,0:T(4,128)(2,1)} %bitcast.29), channel_id=1, source_target_pairs={{0,4},{2,6},{4,0},{6,2},{8,12},{10,14},{12,8},{14,10},{1,5},{3,7},... | collective-permute-start | bytes 172040 | tf_op jit(solution)/shard_map/ppermute | solution.py:23
  6.3 1.5 %collective-permute-start.3 = (bf16[4,7168]{1,0:T(4,128)(2,1)}, bf16[4,7168]{1,0:T(4,128)(2,1)S(1)}, u32[]{:S(2)}, u32[]{:S(2)}) collective-permute-start(bf16[4,7168]{1,0:T(4,128)(2,1)} %bitcast.30), channel_id=1, source_target_pairs={{0,2},{2,0},{4,6},{6,4},{8,10},{10,8},{12,14},{14,12},{1,3},{3,1},... | collective-permute-start | bytes 172040 | tf_op jit(solution)/shard_map/ppermute | solution.py:23
  7.8 0.7 %broadcast_xor_fusion = s32[8]{0:T(128)S(1)} fusion(s32[8]{0:T(128)} %constant.18.clone, s32[]{:T(128)S(6)} %axis_index.15), kind=kLoop, calls=%fused_computation.31 | loop fusion | flops 8 | bytes 68 | tf_op jit(solution)/shard_map/xor | solution.py:43
  8.5 0.9 %select_reduce_fusion = (s32[8]{0:T(128)S(1)}, s32[8]{0:T(128)S(1)}) fusion(s32[8]{0:T(128)} %bitcast.35, s32[8]{0:T(128)S(1)} %broadcast_xor_fusion), kind=kLoop, calls=%fused_computation.20 | loop fusion | flops 368 | bytes 128 | tf_op jit(solution)/shard_map/reduce_sum | solution.py:45
  9.3 0.1 add.32
  9.4 0.1 add.33
  9.5 0.1 lt.72
  9.6 0.1 lt.73
  9.6 0.1 lt.71
  9.7 0.1 compare_convert_fusion.refs_0_
  9.8 0.7 %iota_compare_fusion.2 = pred[4,256]{1,0:T(4,128)(4,1)S(1)} fusion(s32[4]{0:T(128)} %bitcast.36), kind=kLoop, calls=%fused_computation.24 | loop fusion | flops 1024 | bytes 1040 | tf_op jit(solution)/shard_map/lt | solution.py:31
  10.6 0.0 copy-start.2
  10.6 0.8 %copy-done.2 = bf16[1,4,7168]{2,1,0:T(4,128)(2,1)S(1)} copy-done((bf16[1,4,7168]{2,1,0:T(4,128)(2,1)S(1)}, bf16[1,4,7168]{2,1,0:T(4,128)(2,1)}, u32[]{:S(2)}) %copy-start.2) | copy-done | bytes 57368
  11.4 0.0 copy-start.5
  11.4 3.5 %load_rows.3.refs_10_ = bf16[576,7168]{1,0:T(8,128)(2,1)S(1)} custom-call(bf16[1152,7168]{1,0:T(8,128)(2,1)} %weight_ref.4, bf16[4,7168]{1,0:T(4,128)(2,1)S(1)} %bitcast.31), custom_call_target="tpu_custom_call" | custom-call | bytes 16515072 | tf_op jit(solution)/shard_map/load_rows/pallas_call | solution.py:68
  14.9 0.0 copy-start.1
  14.9 3.2 %copy-done.1 = bf16[576,7168]{1,0:T(8,128)(2,1)} copy-done((bf16[576,7168]{1,0:T(8,128)(2,1)}, bf16[576,7168]{1,0:T(8,128)(2,1)S(1)}, u32[]{:S(2)}) %copy-start.1) | copy-done | bytes 8257560
  18.1 0.0 copy-done.5
  18.1 0.0 copy-start.6
  18.1 0.7 %copy.16 = bf16[1,4,256,576]{3,2,1,0:T(8,128)(2,1)S(1)} copy(bf16[1,4,256,576]{2,3,1,0:T(8,128)(2,1)S(1)} %copy-done.5) | data formatting | bytes 2359296 | tf_op args[1]
  18.8 0.0 collective-permute-done.after_ref.refs_3_
  18.9 0.5 collective-permute-start.2
  19.4 0.0 copy-done.6
  19.4 0.6 fusion.17
  20.0 0.5 collective-permute-start.4
  20.5 0.0 collective-permute-done.1.refs_4_
  20.5 1.5 %collective-permute-start.5 = (bf16[4,7168]{1,0:T(4,128)(2,1)S(1)}, bf16[4,7168]{1,0:T(4,128)(2,1)S(1)}, u32[]{:S(2)}, u32[]{:S(2)}) collective-permute-start(bf16[4,7168]{1,0:T(4,128)(2,1)S(1)} %collective-permute-done.1.refs_4_), channel_id=1, source_target_pairs={{0,2},{2,0},{4,6},{6,4},{8,10},{10,8},{12,14},{14,12},{1,3},{3,1},... | collective-permute-start | bytes 172040 | tf_op jit(solution)/shard_map/ppermute | solution.py:23
  22.0 1.1 %collective-permute-done.2.after_ref.refs_5_ = bf16[4,7168]{1,0:T(4,128)(2,1)S(1)} collective-permute-done((bf16[4,7168]{1,0:T(4,128)(2,1)S(1)}, bf16[4,7168]{1,0:T(4,128)(2,1)S(1)}, u32[]{:S(2)}, u32[]{:S(2)}) %collective-permute-start.2) | collective-permute-done | bytes 57376 | tf_op jit(solution)/shard_map/ppermute | solution.py:23
  23.1 0.5 collective-permute-start.6
  23.6 0.6 %iota_compare_fusion.3 = pred[4]{0:T(512)(128)(4,1)S(1)} fusion(s32[]{:T(128)} %fusion.17), kind=kLoop, calls=%fused_computation.29 | loop fusion | flops 4 | bytes 8 | tf_op jit(solution)/shard_map/lt | solution.py:217
  24.3 0.0 slice-start
  24.3 3.6 %load_rows.4.refs_11_ = bf16[576,7168]{1,0:T(8,128)(2,1)S(1)} custom-call(bf16[1152,7168]{1,0:T(8,128)(2,1)} %weight_ref.4, bf16[4,7168]{1,0:T(4,128)(2,1)S(1)} %collective-permute-done.after_ref.refs_3_), custom_call_target="tpu_custom_call" | custom-call | bytes 16515072 | tf_op jit(solution)/shard_map/load_rows/pallas_call | solution.py:68
  27.9 0.0 slice-start.1
  27.9 0.0 copy-start.3
  27.9 0.0 copy-start.4
  27.9 3.6 %load_rows.5.refs_12_ = bf16[576,7168]{1,0:T(8,128)(2,1)S(1)} custom-call(bf16[1152,7168]{1,0:T(8,128)(2,1)} %refs_13_.1, bf16[4,7168]{1,0:T(4,128)(2,1)S(1)} %collective-permute-done.2.after_ref.refs_5_), custom_call_target="tpu_custom_call" | custom-call | bytes 16515072 | tf_op jit(solution)/shard_map/load_rows/pallas_call | solution.py:68
  31.6 0.0 collective-permute-done.3.refs_6_
  31.6 0.0 collective-permute-done.4.refs_7_
  31.6 0.0 collective-permute-done.5.refs_8_
  31.6 0.0 collective-permute-done.6.refs_9_
  31.6 0.0 slice-done
  31.6 1.2 %slice-done.1 = s8[4063232]{0:T(1024)(128)(4,1)S(1)} async-done(((s8[8257536]{0:T(1024)(128)(4,1)}), s8[4063232]{0:T(1024)(128)(4,1)S(1)}, s32[]{:S(2)}) %slice-start.1) | async-done | bytes 4063256
  32.8 0.0 copy-done.3
  32.8 0.0 copy-done.4
  32.8 16.6 %feed_forward.1 = (f32[4,7168]{1,0:T(4,128)S(1)}, f32[4,7168]{1,0:T(4,128)S(1)}) custom-call(bf16[8,32]{1,0:T(8,128)(2,1)S(1)} %compare_convert_fusion.refs_0_, f32[1,7168]{1,0:T(1,128)S(1)} %bitcast.33, bf16[4,7168]{1,0:T(4,128)(2,1)S(1)} %bitcast.32, bf16[4,7168]{1,0:T(4,128)(2,1)S(1)} %collective-permute-done.after_ref.refs_3_, ...), custom_call_target="tpu_custom_call" | custom-call | flops 396361728 | bytes 33030144 | tf_op jit(solution)/shard_map/feed_forward/pallas_call | solution.py:161
  49.4 1.6 %collective-permute-start.7 = (f32[4,7168]{1,0:T(4,128)S(1)}, f32[4,7168]{1,0:T(4,128)S(1)}, u32[]{:S(2)}, u32[]{:S(2)}) collective-permute-start(f32[4,7168]{1,0:T(4,128)S(1)} %get-tuple-element.9), channel_id=1, source_target_pairs={{0,2},{2,0},{4,6},{6,4},{8,10},{10,8},{12,14},{14,12},{1,3},{3,1},... | collective-permute-start | bytes 344072 | tf_op jit(solution)/shard_map/ppermute | solution.py:23
  51.0 0.0 copy-done
  51.0 0.3 fusion.8
  51.3 2.9 %collective-permute-done.7 = f32[4,7168]{1,0:T(4,128)S(1)} collective-permute-done((f32[4,7168]{1,0:T(4,128)S(1)}, f32[4,7168]{1,0:T(4,128)S(1)}, u32[]{:S(2)}, u32[]{:S(2)}) %collective-permute-start.7) | collective-permute-done | bytes 114720 | tf_op jit(solution)/shard_map/ppermute | solution.py:23
  54.3 0.1 slice_add_fusion.1
  54.3 0.6 collective-permute-start.8
  54.9 0.2 fusion.19
  55.1 3.6 %collective-permute-done.8 = f32[2,7168]{1,0:T(2,128)S(1)} collective-permute-done((f32[2,7168]{1,0:T(2,128)S(1)}, f32[2,7168]{1,0:T(2,128)S(1)}, u32[]{:S(2)}, u32[]{:S(2)}) %collective-permute-start.8) | collective-permute-done | bytes 57376 | tf_op jit(solution)/shard_map/ppermute | solution.py:23
  58.7 0.1 slice_add_fusion.2
  58.7 0.6 collective-permute-start.9
  59.4 1.3 %fusion.12 = bf16[1,4,64,512]{3,2,1,0:T(8,128)(2,1)} fusion(bf16[4,256,576]{2,1,0:T(8,128)(2,1)S(1)} %bitcast.34, pred[4]{0:T(512)(128)(4,1)S(1)} %iota_compare_fusion.3, f32[4,64]{1,0:T(4,128)S(1)} %fusion.19, f32[4,64,256]{2,1,0:T(8,128)S(1)} %fusion.8), kind=kOutput, calls=%fused_computation.9 | convolution fusion | flops 67568128 | bytes 1704964 | tf_op jit(solution)/shard_map/shp,spd->shd/dot_general | solution.py:37
  60.6 3.1 %collective-permute-done.9 = f32[1,7168]{1,0:T(1,128)S(1)} collective-permute-done((f32[1,7168]{1,0:T(1,128)S(1)}, f32[1,7168]{1,0:T(1,128)S(1)}, u32[]{:S(2)}, u32[]{:S(2)}) %collective-permute-start.9) | collective-permute-done | bytes 28704 | tf_op jit(solution)/shard_map/ppermute | solution.py:23
  63.7 0.7 %convert_bitcast_fusion = bf16[1,1,7168]{2,1,0:T(2,128)(2,1)} fusion(f32[1,7168]{1,0:T(1,128)S(1)} %collective-permute-done.9, f32[2,7168]{1,0:T(2,128)S(1)} %collective-permute-done.8, f32[2,7168]{1,0:T(2,128)S(1)} %get-tuple-element.12), kind=kLoop, calls=%fused_computation.19 | loop fusion | flops 21504 | bytes 100352 | tf_op jit(solution)/shard_map/broadcast_in_dim | solution.py:223
  (3 shorter events, 0.0 us)
Async XLA Ops:
  0.6 50.4 %copy-start = (bf16[1,4,64,576]{3,2,1,0:T(8,128)(2,1)S(1)}, bf16[1,4,64,576]{3,2,1,0:T(8,128)(2,1)}, u32[]{:S(2)}) copy-start(bf16[1,4,64,576]{3,2,1,0:T(8,128)(2,1)} %param.10) | copy-start | bytes 884740
  0.6 18.2 %collective-permute-start = (bf16[4,7168]{1,0:T(4,128)(2,1)}, bf16[4,7168]{1,0:T(4,128)(2,1)S(1)}, u32[]{:S(2)}, u32[]{:S(2)}) collective-permute-start(bf16[4,7168]{1,0:T(4,128)(2,1)} %bitcast.28), channel_id=1, source_target_pairs={{0,8},{2,10},{4,12},{6,14},{8,0},{10,2},{12,4},{14,6},{1,9},{3,11}... | collective-permute-start | bytes 172040 | tf_op jit(solution)/shard_map/ppermute | solution.py:23
  4.7 15.8 %collective-permute-start.1 = (bf16[4,7168]{1,0:T(4,128)(2,1)}, bf16[4,7168]{1,0:T(4,128)(2,1)S(1)}, u32[]{:S(2)}, u32[]{:S(2)}) collective-permute-start(bf16[4,7168]{1,0:T(4,128)(2,1)} %bitcast.29), channel_id=1, source_target_pairs={{0,4},{2,6},{4,0},{6,2},{8,12},{10,14},{12,8},{14,10},{1,5},{3,7},... | collective-permute-start | bytes 172040 | tf_op jit(solution)/shard_map/ppermute | solution.py:23
  6.3 25.2 %collective-permute-start.3 = (bf16[4,7168]{1,0:T(4,128)(2,1)}, bf16[4,7168]{1,0:T(4,128)(2,1)S(1)}, u32[]{:S(2)}, u32[]{:S(2)}) collective-permute-start(bf16[4,7168]{1,0:T(4,128)(2,1)} %bitcast.30), channel_id=1, source_target_pairs={{0,2},{2,0},{4,6},{6,4},{8,10},{10,8},{12,14},{14,12},{1,3},{3,1},... | collective-permute-start | bytes 172040 | tf_op jit(solution)/shard_map/ppermute | solution.py:23
  10.6 0.8 %copy-start.2 = (bf16[1,4,7168]{2,1,0:T(4,128)(2,1)S(1)}, bf16[1,4,7168]{2,1,0:T(4,128)(2,1)}, u32[]{:S(2)}) copy-start(bf16[1,4,7168]{2,1,0:T(4,128)(2,1)} %param.14) | copy-start | bytes 172036
  11.4 6.7 %copy-start.5 = (bf16[1,4,256,576]{2,3,1,0:T(8,128)(2,1)S(1)}, bf16[1,4,256,576]{2,3,1,0:T(8,128)(2,1)}, u32[]{:S(2)}) copy-start(bf16[1,4,256,576]{2,3,1,0:T(8,128)(2,1)} %param.11) | copy-start | bytes 3538948
  14.9 3.2 %copy-start.1 = (bf16[576,7168]{1,0:T(8,128)(2,1)}, bf16[576,7168]{1,0:T(8,128)(2,1)S(1)}, u32[]{:S(2)}) copy-start(bf16[576,7168]{1,0:T(8,128)(2,1)S(1)} %load_rows.3.refs_10_) | copy-start | bytes 24772612
  18.1 1.2 %copy-start.6 = (s32[1,8]{1,0:T(1,128)S(1)}, s32[1,8]{1,0:T(1,128)}, u32[]{:S(2)}) copy-start(s32[1,8]{1,0:T(1,128)} %param.13) | copy-start | bytes 100
  18.9 4.2 %collective-permute-start.2 = (bf16[4,7168]{1,0:T(4,128)(2,1)S(1)}, bf16[4,7168]{1,0:T(4,128)(2,1)S(1)}, u32[]{:S(2)}, u32[]{:S(2)}) collective-permute-start(bf16[4,7168]{1,0:T(4,128)(2,1)S(1)} %collective-permute-done.after_ref.refs_3_), channel_id=1, source_target_pairs={{0,4},{2,6},{4,0},{6,2},{8,12},{10,14},{12,8},{14,10},{1,5},{3,7},... | collective-permute-start | bytes 172040 | tf_op jit(solution)/shard_map/ppermute | solution.py:23
  20.0 11.6 %collective-permute-start.4 = (bf16[4,7168]{1,0:T(4,128)(2,1)S(1)}, bf16[4,7168]{1,0:T(4,128)(2,1)S(1)}, u32[]{:S(2)}, u32[]{:S(2)}) collective-permute-start(bf16[4,7168]{1,0:T(4,128)(2,1)S(1)} %collective-permute-done.after_ref.refs_3_), channel_id=1, source_target_pairs={{0,2},{2,0},{4,6},{6,4},{8,10},{10,8},{12,14},{14,12},{1,3},{3,1},... | collective-permute-start | bytes 172040 | tf_op jit(solution)/shard_map/ppermute | solution.py:23
  20.5 11.0 %collective-permute-start.5 = (bf16[4,7168]{1,0:T(4,128)(2,1)S(1)}, bf16[4,7168]{1,0:T(4,128)(2,1)S(1)}, u32[]{:S(2)}, u32[]{:S(2)}) collective-permute-start(bf16[4,7168]{1,0:T(4,128)(2,1)S(1)} %collective-permute-done.1.refs_4_), channel_id=1, source_target_pairs={{0,2},{2,0},{4,6},{6,4},{8,10},{10,8},{12,14},{14,12},{1,3},{3,1},... | collective-permute-start | bytes 172040 | tf_op jit(solution)/shard_map/ppermute | solution.py:23
  23.1 8.5 %collective-permute-start.6 = (bf16[4,7168]{1,0:T(4,128)(2,1)S(1)}, bf16[4,7168]{1,0:T(4,128)(2,1)S(1)}, u32[]{:S(2)}, u32[]{:S(2)}) collective-permute-start(bf16[4,7168]{1,0:T(4,128)(2,1)S(1)} %collective-permute-done.2.after_ref.refs_5_), channel_id=1, source_target_pairs={{0,2},{2,0},{4,6},{6,4},{8,10},{10,8},{12,14},{14,12},{1,3},{3,1},... | collective-permute-start | bytes 172040 | tf_op jit(solution)/shard_map/ppermute | solution.py:23
  24.3 7.3 %slice-start = ((s8[8257536]{0:T(1024)(128)(4,1)}), s8[4194304]{0:T(1024)(128)(4,1)S(1)}, s32[]{:S(2)}) async-start(s8[8257536]{0:T(1024)(128)(4,1)} %bitcast.26), calls=%async_computation | async-start | bytes 8388608
  27.9 4.9 %slice-start.1 = ((s8[8257536]{0:T(1024)(128)(4,1)}), s8[4063232]{0:T(1024)(128)(4,1)S(1)}, s32[]{:S(2)}) async-start(s8[8257536]{0:T(1024)(128)(4,1)} %bitcast.26), calls=%async_computation.1 | async-start | bytes 8126464
  27.9 4.9 %copy-start.3 = (bf16[1,4,7168]{2,1,0:T(4,128)(2,1)S(1)}, bf16[1,4,7168]{2,1,0:T(4,128)(2,1)}, u32[]{:S(2)}) copy-start(bf16[1,4,7168]{2,1,0:T(4,128)(2,1)} %param.14) | copy-start | bytes 172036
  27.9 4.9 %copy-start.4 = (f32[7168]{0:T(1024)S(1)}, f32[7168]{0:T(1024)}, u32[]{:S(2)}) copy-start(f32[7168]{0:T(1024)} %param.15) | copy-start | bytes 86020
  49.4 4.9 %collective-permute-start.7 = (f32[4,7168]{1,0:T(4,128)S(1)}, f32[4,7168]{1,0:T(4,128)S(1)}, u32[]{:S(2)}, u32[]{:S(2)}) collective-permute-start(f32[4,7168]{1,0:T(4,128)S(1)} %get-tuple-element.9), channel_id=1, source_target_pairs={{0,2},{2,0},{4,6},{6,4},{8,10},{10,8},{12,14},{14,12},{1,3},{3,1},... | collective-permute-start | bytes 344072 | tf_op jit(solution)/shard_map/ppermute | solution.py:23
  54.3 4.3 %collective-permute-start.8 = (f32[2,7168]{1,0:T(2,128)S(1)}, f32[2,7168]{1,0:T(2,128)S(1)}, u32[]{:S(2)}, u32[]{:S(2)}) collective-permute-start(f32[2,7168]{1,0:T(2,128)S(1)} %get-tuple-element.13), channel_id=1, source_target_pairs={{0,4},{2,6},{4,0},{6,2},{8,12},{10,14},{12,8},{14,10},{1,5},{3,7},... | collective-permute-start | bytes 172040 | tf_op jit(solution)/shard_map/ppermute | solution.py:23
  58.7 5.0 %collective-permute-start.9 = (f32[1,7168]{1,0:T(1,128)S(1)}, f32[1,7168]{1,0:T(1,128)S(1)}, u32[]{:S(2)}, u32[]{:S(2)}) collective-permute-start(f32[1,7168]{1,0:T(1,128)S(1)} %slice_add_fusion.2), channel_id=1, source_target_pairs={{0,8},{2,10},{4,12},{6,14},{8,0},{10,2},{12,4},{14,6},{1,9},{3,11}... | collective-permute-start | bytes 86024 | tf_op jit(solution)/shard_map/ppermute | solution.py:23

commit v2 on v0

v2 whole, which is shorter than its diff:
```python
import jax
import jax.numpy as jnp
from jax import lax
from jax.experimental import pallas as pl
from jax.experimental.pallas import tpu as pltpu
from jax.sharding import PartitionSpec as P

KVL = 512
MIB = 1024 * 1024

score_scale = 192.0 ** (-0.5)
norm_eps = 1e-06

VMEM = pl.BlockSpec(memory_space=pltpu.VMEM)
SMEM = pl.BlockSpec(memory_space=pltpu.SMEM)
ANY = pl.BlockSpec(memory_space=pl.ANY)


def bit_reverse(value, bits):
    out = 0
    for bit in range(bits):
        out = out | (((value >> bit) & 1) << (bits - 1 - bit))
    return out


def swap(x, axis, bit, size):
    return lax.ppermute(x, axis, [(i, i ^ (1 << bit)) for i in range(size)])


def pinned(weight):
    return pltpu.with_memory_space_constraint(weight, pltpu.HBM)


def row_copies(source, first, target, sems):
    rows = target.shape[0]
    pieces = sems.shape[0]
    step = rows // pieces
    return [
        pltpu.make_async_copy(
            source.at[pl.ds(first + i * step, step)], target.at[pl.ds(i * step, step)], sems.at[i]
        )
        for i in range(pieces)
    ]


def pieces_of(rows, most):
    return most if rows % (16 * most) == 0 else 1


def share_start(units, share):
    if share == units:
        return 0
    return pl.multiple_of(lax.axis_index("sub") * share, 16)


def pick_matrix(counts, device, size, slots, bits):
    slot = lax.broadcasted_iota(jnp.int32, (size, size // 2 * slots), 1)
    every = lax.broadcasted_iota(jnp.int32, (size, size // 2 * slots), 0)
    owner = bit_reverse(slot // slots, bits) ^ device
    known = jnp.broadcast_to(counts, (8, size)).astype(jnp.bfloat16)
    start = jnp.dot(known, (every < owner).astype(jnp.bfloat16), preferred_element_type=jnp.float32)[:1]
    count = jnp.dot(known, (every == owner).astype(jnp.bfloat16), preferred_element_type=jnp.float32)[:1]
    place = (slot % slots)[:1].astype(jnp.float32)
    request = jnp.where(place < count, start + place, -1.0)
    row = lax.broadcasted_iota(jnp.int32, (2 * size, size // 2 * slots), 0)
    wanted = bit_reverse(row % size, bits) ^ device ^ (row // size)
    return (request == wanted.astype(jnp.float32)).astype(jnp.bfloat16)


def load_rows(jobs, share, after, counts=None, slots=0):
    pieces = [pieces_of(rows, 4) for _, _, rows in jobs]
    size = 0 if counts is None else counts.shape[1]
    bits = max(size.bit_length() - 1, 0)

    def body(*refs):
        sources = refs[: len(jobs)]
        refs = refs[len(jobs) + 1 :]
        if counts is not None:
            counts_ref, refs = refs[0], refs[1:]
        targets, refs = refs[: len(jobs)], refs[len(jobs) :]
        copies = []
        for (weight, first, _), source, target, sems in zip(jobs, sources, targets, refs[-len(jobs) :]):
            copies += row_copies(source, share_start(weight.shape[0], share) + first, target, sems)
        for copy in copies:
            copy.start()
        if counts is not None:
            refs[0][...] = pick_matrix(counts_ref[...], lax.axis_index("tp"), size, slots, bits)
        for copy in copies:
            copy.wait()

    out_shape = [pltpu.VMEM((rows, weight.shape[1]), weight.dtype) for weight, _, rows in jobs]
    if counts is not None:
        out_shape.append(jax.ShapeDtypeStruct((2 * size, size // 2 * slots), jnp.bfloat16))
    return pl.pallas_call(
        body,
        out_shape=out_shape,
        in_specs=[ANY] * (len(jobs) + 1) + [VMEM] * (counts is not None),
        out_specs=[VMEM] * len(out_shape),
        scratch_shapes=[pltpu.SemaphoreType.DMA((count,)) for count in pieces],
        compiler_params=pltpu.CompilerParams(vmem_limit_bytes=2 * MIB),
        cost_estimate=pl.CostEstimate(
            flops=0, transcendentals=0, bytes_accessed=sum(4 * rows * weight.shape[1] for weight, _, rows in jobs)
        ),
        name="load_rows",
    )(*[pinned(weight) for weight, _, _ in jobs], after, *([counts] if counts is not None else []))


def compact(pick, blocks, after):
    size = pick.shape[0] // 2
    width = blocks[0].shape[1]
    column = 1024
    count = len(blocks)

    def body(*refs):
        pick_ref, block_refs, (_, own_ref, send_ref) = refs[0], refs[1 : 1 + count], refs[1 + count :]
        pick_now = pick_ref[...]
        for c in range(0, width, column):
            rows = [ref[:, c : c + column].astype(jnp.float32) for ref in block_refs]
            rows = rows[0] if count == 1 else jnp.concatenate(rows, axis=0)
            out = jnp.dot(pick_now, rows.astype(jnp.bfloat16), preferred_element_type=jnp.float32)
            out = out.astype(jnp.bfloat16)
            own_ref[:, c : c + column] = out[:size]
            send_ref[:, c : c + column] = out[size:]

    out = jax.ShapeDtypeStruct((size, width), jnp.bfloat16)
    return pl.pallas_call(
        body,
        out_shape=(out, out),
        in_specs=[VMEM] * (1 + count) + [ANY],
        out_specs=(VMEM, VMEM),
        compiler_params=pltpu.CompilerParams(vmem_limit_bytes=16 * MIB),
        name="compact",
    )(pick, *blocks, after)


def feed_forward(gain, row_sets, gate_parts, up_parts, w_down, share):
    requests, width = row_sets[0].shape
    units = w_down.shape[0]
    set_count, gate_count, up_count = len(row_sets), len(gate_parts), len(up_parts)
    column = 1024
    pieces = pieces_of(share, 4)

    def body(*refs):
        gain_ref, refs = refs[0], refs[1:]
        set_refs, refs = refs[:set_count], refs[set_count:]
        gate_refs, refs = refs[:gate_count], refs[gate_count:]
        up_refs, refs = refs[:up_count], refs[up_count:]
        down_hbm, refs = refs[0], refs[1:]
        out_refs, refs = refs[:set_count], refs[set_count:]
        down_ref, down_sems = refs

        copies = row_copies(down_hbm, share_start(units, share), down_ref, down_sems)
        for copy in copies:
            copy.start()

        rows = [ref[...].astype(jnp.float32) for ref in set_refs]
        rows = rows[0] if set_count == 1 else jnp.concatenate(rows, axis=0)
        inv_rms = lax.rsqrt(jnp.mean(rows * rows, axis=1, keepdims=True) + norm_eps)
        normed = (rows * inv_rms * gain_ref[...]).astype(jnp.bfloat16)

        def project(part_refs):
            out = []
            for ref in part_refs:
                count = ref.shape[0]
                chunk = 192 if count % 192 == 0 else count
                for j in range(0, count, chunk):
                    out.append(
                        lax.dot_general(
                            ref[j : j + chunk, :], normed, (((1,), (1,)), ((), ())), preferred_element_type=jnp.float32
                        )
                    )
            return out[0] if len(out) == 1 else jnp.concatenate(out, axis=0)

        gate_out = project(gate_refs)
        up_out = project(up_refs)
        hidden = (jax.nn.silu(gate_out) * up_out).T.astype(jnp.bfloat16)
        for copy in copies:
            copy.wait()
        for c in range(0, width, column):
            out = jnp.dot(hidden, down_ref[:, c : c + column], preferred_element_type=jnp.float32)
            own = out[:requests]
            first = lax.broadcasted_iota(jnp.int32, own.shape, 0) == 0
            own += jnp.where(first, set_refs[0][:, c : c + column].astype(jnp.float32), 0.0)
            out_refs[0][:, c : c + column] = own
            if set_count == 2:
                out_refs[1][:, c : c + column] = out[requests:].astype(jnp.bfloat16)

    outs = [
        jax.ShapeDtypeStruct((requests, width), jnp.float32),
        jax.ShapeDtypeStruct((requests, width), jnp.bfloat16),
    ][:set_count]
    return pl.pallas_call(
        body,
        out_shape=outs,
        in_specs=[VMEM] * (1 + set_count + gate_count + up_count) + [ANY],
        out_specs=[VMEM] * set_count,
        scratch_shapes=[pltpu.VMEM((share, width), jnp.bfloat16), pltpu.SemaphoreType.DMA((pieces,))],
        compiler_params=pltpu.CompilerParams(vmem_limit_bytes=20 * MIB),
        cost_estimate=pl.CostEstimate(
            flops=6 * requests * set_count * share * width,
            transcendentals=requests * share,
            bytes_accessed=6 * share * width,
        ),
        name="feed_forward",
    )(gain[None], *row_sets, *gate_parts, *up_parts, pinned(w_down))


def attend(queries, cache, lengths, counts, after):
    slots, heads, _ = queries.shape
    positions = cache.shape[2]

    def body(lengths_ref, counts_ref, queries_ref, cache_ref, after_ref, out_ref):
        live = counts_ref[0, lax.axis_index("tp")]
        spot = lax.broadcasted_iota(jnp.int32, (heads, positions), 1)
        for s in range(slots):
            scores = (
                jnp.dot(queries_ref[s], cache_ref[s], preferred_element_type=jnp.float32)
                * score_scale
            )
            scores = jnp.where(spot < lengths_ref[0, s], scores, -jnp.inf)
            weights = jnp.exp(scores - jnp.max(scores, axis=1, keepdims=True))
            probs = (weights / jnp.sum(weights, axis=1, keepdims=True)).astype(jnp.bfloat16)
            context = lax.dot_general(
                probs, cache_ref[s, :KVL, :], (((1,), (1,)), ((), ())), preferred_element_type=jnp.float32
            )
            out_ref[s] = jnp.where(s < live, context, 0.0).astype(jnp.bfloat16)

    return pl.pallas_call(
        body,
        out_shape=jax.ShapeDtypeStruct((slots, heads, KVL), jnp.bfloat16),
        in_specs=[SMEM, SMEM, VMEM, VMEM, ANY],
        out_specs=VMEM,
        compiler_params=pltpu.CompilerParams(vmem_limit_bytes=8 * MIB),
        cost_estimate=pl.CostEstimate(
            flops=4 * slots * heads * positions * KVL,
            transcendentals=slots * heads * positions,
            bytes_accessed=2 * (queries.size + cache.size),
        ),
        name="attend",
    )(lengths, counts, queries, cache, after)


def load_plan(gate, up, share):
    if share % 48 == 0 and share // 3 % 16 == 0:
        third = share // 3
        return [
            [(gate, 0, 2 * third)],
            [(gate, 2 * third, third), (up, 0, third)],
            [(up, third, 2 * third)],
        ]
    return [[(gate, 0, share)], [(up, 0, share)], []]


def make_shards(size, cores):
    bits = size.bit_length() - 1

    def shards(queries, kv_cache, cache_lengths, live_counts, stream, norm_gain, w_gate, w_up, w_down):
        slots = queries.shape[1]
        units = w_gate.shape[0]
        split = cores == 2 and units % 32 == 0
        share = units // 2 if split else units
        plan = load_plan(w_gate, w_up, share)
        gate_parts, up_parts = [], []

        def load(jobs, after, counts=None):
            *parts, last = [*load_rows(jobs, share, after, counts, slots), *[None] * (counts is None)]
            for (weight, _, _), part in zip(jobs, parts):
                (gate_parts if weight is w_gate else up_parts).append(part)
            return last

        blocks = [stream[0]]
        for step in range(bits - 1):
            if len(blocks) > 4:
                blocks = [jnp.concatenate(blocks, axis=0)]
            arrived = [swap(block, "tp", bits - 1 - step, size) for block in blocks]
            if step == 0:
                pick = load(plan[0], blocks[0], live_counts)
                arrived[0], gate_parts[0] = lax.optimization_barrier((arrived[0], gate_parts[0]))
            elif step == 1:
                load(plan[1], blocks[1])
            blocks = blocks + arrived

        own, send = compact(pick, blocks, up_parts[0])
        arrived = swap(send, "tp", 0, size)
        if plan[2]:
            load(plan[2], send)
            arrived, up_parts[-1] = lax.optimization_barrier((arrived, up_parts[-1]))
        rows = own + arrived
        row_sets = [rows, swap(rows, "sub", 0, cores)] if split else [rows]
        total, *other = feed_forward(norm_gain, row_sets, gate_parts, up_parts, w_down, share)

        if split:
            total = total + swap(other[0], "sub", 0, cores).astype(jnp.float32)
        for bit in range(bits):
            half = total.shape[0] // 2
            send = total[half:].astype(jnp.bfloat16 if bit < 2 else jnp.float32)
            if bit == 0:
                latent_ctx = attend(queries[0], jnp.swapaxes(kv_cache[0], 1, 2), cache_lengths, live_counts, send)[None]
            total = total[:half] + swap(send, "tp", bit, size).astype(jnp.float32)
        return (latent_ctx, total.astype(jnp.bfloat16)[None])

    return shards


def solution(mesh):
    in_specs = (
        P(("groups", "sub"), "tp", None, None),
        P(("groups", "sub"), "tp", None, None),
        P(("groups", "sub"), "tp"),
        P(("groups", "sub"), None),
        P(("groups", "sub"), "tp", None),
        P(),
        P("tp", None),
        P("tp", None),
        P("tp", None),
    )
    out_specs = (P(("groups", "sub"), "tp", None, None), P(("groups", "sub"), "tp", None))
    return jax.shard_map(
        make_shards(mesh.shape["tp"], mesh.shape["sub"]),
        mesh=mesh,
        in_specs=in_specs,
        out_specs=out_specs,
        check_vma=False,
    )
```

time: 153 us -> 46.1 us (0.30)
  waiting for transfers between devices: 67 us -> 12.3 us
  blocking collectives: 34.1 us -> 0 us
  matrix products: 28.1 us -> 0 us
  Pallas kernels: 0 us -> 19.9 us
  between operations: 14.2 us -> 0.77 us
  starting transfers between devices: 0.04 us -> 10.5 us
  other arithmetic: 5.14 us -> 0.77 us
  local copies, waits for them, and re-layouts: 4.31 us -> 1.63 us
    unnamed x2 -> x0, waiting for transfers between devices: 67 us -> none
    all_gather x1 -> x0, blocking collectives: 34.1 us -> none  [shards(): gathered = lax.all_gather(local_rows, 'tp', axis=0, tiled=True)]
    dot_general x4 -> x0, matrix products: 28.1 us -> none  [the longest x1 16.4 us: shards(): jnp.dot(hidden, w_down, preferred_element_type=jnp.float32)]
    pallas_call x0 -> x6, Pallas kernels: none -> 19.9 us  [the longest x1 9.17 us: feed_forward(): pl.pallas_call(body, out_shape=outs, in_specs=[VMEM] * (1 + set_count + g...]
    ppermute x0 -> x9, waiting for transfers between devices: none -> 12.3 us  [swap(): return lax.ppermute(x, axis, [(i, i ^ 1 << bit) for i in range(size)])]
    ppermute x0 -> x9, starting transfers between devices: none -> 10.5 us  [swap(): return lax.ppermute(x, axis, [(i, i ^ 1 << bit) for i in range(size)])]
    broadcast_in_dim x1, other arithmetic: 2.28 us -> 0.64 us  [shards(): return (latent_ctx, total.astype(jnp.bfloat16)[None])]
  transfers between devices with their start and end apart: 1 -> 9, of which waited for: 1 -> 7; matrix products, arithmetic and copies ran while one was open for 3% -> 0% of each run, Pallas kernels for 0% -> 23%
where the time goes in v2:
time: 46.1 us; the launch traced here: 45.9 us
  Pallas kernels  19.9 us (43%)
  waiting for transfers between devices  12.3 us (27%)
  starting transfers between devices  10.5 us (23%)
  local copies, waits for them, and re-layouts  1.63 us (4%)
  other arithmetic  0.77 us (2%)
  between operations  0.77 us (2%)
    ppermute x9, waiting for transfers between devices, swap(): return lax.ppermute(x, axis, [(i, i ^ 1 << bit) for i in range(size)])  12.3 us
    ppermute x9, starting transfers between devices, swap(): return lax.ppermute(x, axis, [(i, i ^ 1 << bit) for i in range(size)])  10.5 us
    pallas_call x1, Pallas kernels, feed_forward(): pl.pallas_call(body, out_shape=outs, in_specs=[VMEM] * (1 + set_count + g...  9.17 us
    pallas_call x3, Pallas kernels, load_rows(): pl.pallas_call(body, out_shape=out_shape, in_specs=[ANY] * (len(jobs) + 1...  7.86 us
    pallas_call x1, Pallas kernels, attend(): pl.pallas_call(body, out_shape=jax.ShapeDtypeStruct((slots, heads, KVL),...  2.71 us
    unnamed x16, local copies, waits for them, and re-layouts  1.54 us
  transfers between devices with their start and end apart: 9, of which 7 were waited for; matrix products, arithmetic and copies ran while one was open for 0% of the time, Pallas kernels for 23%

profile of v2, /device:TPU:0, one launch (start us, length us, event | category | flops | bytes accessed | tf_op | source)
XLA Modules:
  0.0 45.9 jit_solution(5392856185110606077)
XLA Ops:
  0.6 4.1 %collective-permute-start = (bf16[4,7168]{1,0:T(4,128)(2,1)}, bf16[4,7168]{1,0:T(4,128)(2,1)S(1)}, u32[]{:S(2)}, u32[]{:S(2)}) collective-permute-start(bf16[4,7168]{1,0:T(4,128)(2,1)} %bitcast.11), channel_id=1, source_target_pairs={{0,8},{2,10},{4,12},{6,14},{8,0},{10,2},{12,4},{14,6},{1,9},{3,11}... | collective-permute-start | bytes 172040 | tf_op jit(solution)/shard_map/ppermute | solution.py:27
  4.7 1.6 %collective-permute-start.1 = (bf16[4,7168]{1,0:T(4,128)(2,1)}, bf16[4,7168]{1,0:T(4,128)(2,1)S(1)}, u32[]{:S(2)}, u32[]{:S(2)}) collective-permute-start(bf16[4,7168]{1,0:T(4,128)(2,1)} %bitcast.12), channel_id=1, source_target_pairs={{0,4},{2,6},{4,0},{6,2},{8,12},{10,14},{12,8},{14,10},{1,5},{3,7},... | collective-permute-start | bytes 172040 | tf_op jit(solution)/shard_map/ppermute | solution.py:27
  6.3 0.0 copy-start.2
  6.3 0.9 %copy-done.2 = bf16[1,4,7168]{2,1,0:T(4,128)(2,1)S(1)} copy-done((bf16[1,4,7168]{2,1,0:T(4,128)(2,1)S(1)}, bf16[1,4,7168]{2,1,0:T(4,128)(2,1)}, u32[]{:S(2)}) %copy-start.2) | copy-done | bytes 57368
  7.2 0.0 copy-start.5
  7.2 0.7 %copy-done.5 = s32[1,8]{1,0:T(1,128)S(1)} copy-done((s32[1,8]{1,0:T(1,128)S(1)}, s32[1,8]{1,0:T(1,128)}, u32[]{:S(2)}) %copy-start.5) | copy-done | bytes 56
  7.8 2.6 %load_rows.3 = (bf16[384,7168]{1,0:T(8,128)(2,1)S(1)}, bf16[16,16]{1,0:T(8,128)(2,1)S(1)}) custom-call(bf16[1152,7168]{1,0:T(8,128)(2,1)} %refs_0_.4, bf16[4,7168]{1,0:T(4,128)(2,1)S(1)} %bitcast.13, s32[1,8]{1,0:T(1,128)S(1)} %copy-done.5), custom_call_target="tpu_custom_call" | custom-call | bytes 11010048 | tf_op jit(solution)/shard_map/load_rows/pallas_call | solution.py:94
  10.5 0.0 collective-permute-done.refs_2_
  10.5 0.0 copy-start.3
  10.5 0.5 %collective-permute-start.2 = (bf16[4,7168]{1,0:T(4,128)(2,1)S(1)}, bf16[4,7168]{1,0:T(4,128)(2,1)S(1)}, u32[]{:S(2)}, u32[]{:S(2)}) collective-permute-start(bf16[4,7168]{1,0:T(4,128)(2,1)S(1)} %collective-permute-done.refs_2_), channel_id=1, source_target_pairs={{0,4},{2,6},{4,0},{6,2},{8,12},{10,14},{12,8},{14,10},{1,5},{3,7},... | collective-permute-start | bytes 172040 | tf_op jit(solution)/shard_map/ppermute | solution.py:27
  11.0 2.6 %load_rows.4 = (bf16[192,7168]{1,0:T(8,128)(2,1)S(1)}, bf16[192,7168]{1,0:T(8,128)(2,1)S(1)}) custom-call(bf16[1152,7168]{1,0:T(8,128)(2,1)} %refs_0_.4, bf16[1152,7168]{1,0:T(8,128)(2,1)} %refs_0_.5, bf16[4,7168]{1,0:T(4,128)(2,1)S(1)} %collective-permute-done.refs_2_), custom_call_target="tpu_custom_call" | custom-call | bytes 11010048 | tf_op jit(solution)/shard_map/load_rows/pallas_call | solution.py:94
  13.6 0.0 collective-permute-done.1.refs_3_
  13.6 1.1 %collective-permute-done.2.refs_4_ = bf16[4,7168]{1,0:T(4,128)(2,1)S(1)} collective-permute-done((bf16[4,7168]{1,0:T(4,128)(2,1)S(1)}, bf16[4,7168]{1,0:T(4,128)(2,1)S(1)}, u32[]{:S(2)}, u32[]{:S(2)}) %collective-permute-start.2) | collective-permute-done | bytes 57376 | tf_op jit(solution)/shard_map/ppermute | solution.py:27
  14.7 0.0 copy-done.3
  14.7 0.2 compact.1
  14.9 0.0 copy-start.4
  14.9 1.6 %collective-permute-start.3 = (bf16[8,7168]{1,0:T(8,128)(2,1)S(1)}, bf16[8,7168]{1,0:T(8,128)(2,1)S(1)}, u32[]{:S(2)}, u32[]{:S(2)}) collective-permute-start(bf16[8,7168]{1,0:T(8,128)(2,1)S(1)} %get-tuple-element.19.refs_1_), channel_id=1, source_target_pairs={{0,2},{2,0},{4,6},{6,4},{8,10},{10,8},{12,14},{14,12},{1,3},{3,1},... | collective-permute-start | bytes 344072 | tf_op jit(solution)/shard_map/ppermute | solution.py:27
  16.5 2.6 %load_rows.5.refs_6_ = bf16[384,7168]{1,0:T(8,128)(2,1)S(1)} custom-call(bf16[1152,7168]{1,0:T(8,128)(2,1)} %refs_0_.5, bf16[8,7168]{1,0:T(8,128)(2,1)S(1)} %get-tuple-element.19.refs_1_), custom_call_target="tpu_custom_call" | custom-call | bytes 11010048 | tf_op jit(solution)/shard_map/load_rows/pallas_call | solution.py:94
  19.1 0.7 %collective-permute-done.3 = bf16[8,7168]{1,0:T(8,128)(2,1)S(1)} collective-permute-done((bf16[8,7168]{1,0:T(8,128)(2,1)S(1)}, bf16[8,7168]{1,0:T(8,128)(2,1)S(1)}, u32[]{:S(2)}, u32[]{:S(2)}) %collective-permute-start.3) | collective-permute-done | bytes 114720 | tf_op jit(solution)/shard_map/ppermute | solution.py:27
  19.8 0.1 collective-permute-start.4
  19.9 1.3 %collective-permute-done.4.refs_2_ = bf16[8,7168]{1,0:T(8,128)(2,1)S(1)} collective-permute-done((bf16[8,7168]{1,0:T(8,128)(2,1)S(1)}, bf16[8,7168]{1,0:T(8,128)(2,1)S(1)}, u32[]{:S(2)}, u32[]{:S(2)}) %collective-permute-start.4) | collective-permute-done | bytes 114720 | tf_op jit(solution)/shard_map/ppermute | solution.py:27
  21.2 0.0 copy-done.4
  21.2 0.0 copy-start
  21.2 0.0 copy-start.1
  21.2 0.0 copy-start.6
  21.2 0.0 copy-start.7
  21.2 9.2 %feed_forward.1 = (f32[8,7168]{1,0:T(8,128)S(1)}, bf16[8,7168]{1,0:T(8,128)(2,1)S(1)}) custom-call(f32[1,7168]{1,0:T(1,128)S(1)} %bitcast.15, bf16[8,7168]{1,0:T(8,128)(2,1)S(1)} %add.15.refs_1_, bf16[8,7168]{1,0:T(8,128)(2,1)S(1)} %collective-permute-done.4.refs_2_, bf16[384,7168]{1,0:T(8,128)(2,1)S(1)} %get-tuple-element.21.refs_3_, ...), custom_call_target="tpu_custom_call" | custom-call | flops 396361728 | bytes 24772608 | tf_op jit(solution)/shard_map/feed_forward/pallas_call | solution.py:192
  30.4 0.2 collective-permute-start.5
  30.6 1.2 %collective-permute-done.5 = bf16[8,7168]{1,0:T(8,128)(2,1)S(1)} collective-permute-done((bf16[8,7168]{1,0:T(8,128)(2,1)S(1)}, bf16[8,7168]{1,0:T(8,128)(2,1)S(1)}, u32[]{:S(2)}, u32[]{:S(2)}) %collective-permute-start.5) | collective-permute-done | bytes 114720 | tf_op jit(solution)/shard_map/ppermute | solution.py:27
  31.9 1.6 %collective-permute-start.6 = (bf16[4,7168]{1,0:T(4,128)(2,1)S(1)}, bf16[4,7168]{1,0:T(4,128)(2,1)S(1)}, u32[]{:S(2)}, u32[]{:S(2)}) collective-permute-start(bf16[4,7168]{1,0:T(4,128)(2,1)S(1)} %slice.41.after_ref), channel_id=1, source_target_pairs={{0,2},{2,0},{4,6},{6,4},{8,10},{10,8},{12,14},{14,12},{1,3},{3,1},... | collective-permute-start | bytes 172040 | tf_op jit(solution)/shard_map/ppermute | solution.py:27
  33.4 2.7 %collective-permute-done.6 = bf16[4,7168]{1,0:T(4,128)(2,1)S(1)} collective-permute-done((bf16[4,7168]{1,0:T(4,128)(2,1)S(1)}, bf16[4,7168]{1,0:T(4,128)(2,1)S(1)}, u32[]{:S(2)}, u32[]{:S(2)}) %collective-permute-start.6) | collective-permute-done | bytes 57376 | tf_op jit(solution)/shard_map/ppermute | solution.py:27
  36.2 0.6 %collective-permute-start.7 = (bf16[2,7168]{1,0:T(2,128)(2,1)S(1)}, bf16[2,7168]{1,0:T(2,128)(2,1)S(1)}, u32[]{:S(2)}, u32[]{:S(2)}) collective-permute-start(bf16[2,7168]{1,0:T(2,128)(2,1)S(1)} %slice.42), channel_id=1, source_target_pairs={{0,4},{2,6},{4,0},{6,2},{8,12},{10,14},{12,8},{14,10},{1,5},{3,7},... | collective-permute-start | bytes 86024 | tf_op jit(solution)/shard_map/ppermute | solution.py:27
  36.8 3.4 %collective-permute-done.7 = bf16[2,7168]{1,0:T(2,128)(2,1)S(1)} collective-permute-done((bf16[2,7168]{1,0:T(2,128)(2,1)S(1)}, bf16[2,7168]{1,0:T(2,128)(2,1)S(1)}, u32[]{:S(2)}, u32[]{:S(2)}) %collective-permute-start.7) | collective-permute-done | bytes 28704 | tf_op jit(solution)/shard_map/ppermute | solution.py:27
  40.2 0.4 collective-permute-start.8
  40.6 0.0 copy-done
  40.6 0.0 copy-done.1
  40.6 0.0 copy-done.6
  40.6 0.0 copy-done.7
  40.6 2.7 %attend.1 = bf16[4,64,512]{2,1,0:T(8,128)(2,1)} custom-call(s32[1,4]{1,0:T(1,128)S(1)} %copy-done.7, s32[1,8]{1,0:T(1,128)S(1)} %copy-done.6, bf16[4,64,576]{2,1,0:T(8,128)(2,1)S(1)} %bitcast.10, bf16[4,576,256]{2,1,0:T(8,128)(2,1)S(1)} %bitcast.9, bf16[4,7168]{1,0:T(4,128)(2,1)S(1)} %slice.41.after_ref), custom_call_target="tpu_custom_call" | custom-call | flops 134217728 | bytes 1474560 | tf_op jit(solution)/shard_map/attend/pallas_call | solution.py:228
  43.3 2.0 %collective-permute-done.8 = f32[1,7168]{1,0:T(1,128)S(1)} collective-permute-done((f32[1,7168]{1,0:T(1,128)S(1)}, f32[1,7168]{1,0:T(1,128)S(1)}, u32[]{:S(2)}, u32[]{:S(2)}) %collective-permute-start.8) | collective-permute-done | bytes 28704 | tf_op jit(solution)/shard_map/ppermute | solution.py:27
  45.3 0.6 %fusion.1 = bf16[1,1,7168]{2,1,0:T(2,128)(2,1)} fusion(f32[1,7168]{1,0:T(1,128)S(1)} %collective-permute-done.8, f32[2,7168]{1,0:T(2,128)S(1)} %slice_add_fusion.1), kind=kLoop, calls=%fused_computation.7 | loop fusion | flops 14336 | bytes 71680 | tf_op jit(solution)/shard_map/broadcast_in_dim | solution.py:300
  (7 shorter events, 0.2 us)
Async XLA Ops:
  0.6 9.8 %collective-permute-start = (bf16[4,7168]{1,0:T(4,128)(2,1)}, bf16[4,7168]{1,0:T(4,128)(2,1)S(1)}, u32[]{:S(2)}, u32[]{:S(2)}) collective-permute-start(bf16[4,7168]{1,0:T(4,128)(2,1)} %bitcast.11), channel_id=1, source_target_pairs={{0,8},{2,10},{4,12},{6,14},{8,0},{10,2},{12,4},{14,6},{1,9},{3,11}... | collective-permute-start | bytes 172040 | tf_op jit(solution)/shard_map/ppermute | solution.py:27
  4.7 8.9 %collective-permute-start.1 = (bf16[4,7168]{1,0:T(4,128)(2,1)}, bf16[4,7168]{1,0:T(4,128)(2,1)S(1)}, u32[]{:S(2)}, u32[]{:S(2)}) collective-permute-start(bf16[4,7168]{1,0:T(4,128)(2,1)} %bitcast.12), channel_id=1, source_target_pairs={{0,4},{2,6},{4,0},{6,2},{8,12},{10,14},{12,8},{14,10},{1,5},{3,7},... | collective-permute-start | bytes 172040 | tf_op jit(solution)/shard_map/ppermute | solution.py:27
  6.3 0.9 %copy-start.2 = (bf16[1,4,7168]{2,1,0:T(4,128)(2,1)S(1)}, bf16[1,4,7168]{2,1,0:T(4,128)(2,1)}, u32[]{:S(2)}) copy-start(bf16[1,4,7168]{2,1,0:T(4,128)(2,1)} %param.13) | copy-start | bytes 172036
  7.2 0.7 %copy-start.5 = (s32[1,8]{1,0:T(1,128)S(1)}, s32[1,8]{1,0:T(1,128)}, u32[]{:S(2)}) copy-start(s32[1,8]{1,0:T(1,128)} %counts_ref.1) | copy-start | bytes 100
  10.5 4.3 %copy-start.3 = (bf16[1,4,7168]{2,1,0:T(4,128)(2,1)S(1)}, bf16[1,4,7168]{2,1,0:T(4,128)(2,1)}, u32[]{:S(2)}) copy-start(bf16[1,4,7168]{2,1,0:T(4,128)(2,1)} %param.13) | copy-start | bytes 172036
  10.5 4.2 %collective-permute-start.2 = (bf16[4,7168]{1,0:T(4,128)(2,1)S(1)}, bf16[4,7168]{1,0:T(4,128)(2,1)S(1)}, u32[]{:S(2)}, u32[]{:S(2)}) collective-permute-start(bf16[4,7168]{1,0:T(4,128)(2,1)S(1)} %collective-permute-done.refs_2_), channel_id=1, source_target_pairs={{0,4},{2,6},{4,0},{6,2},{8,12},{10,14},{12,8},{14,10},{1,5},{3,7},... | collective-permute-start | bytes 172040 | tf_op jit(solution)/shard_map/ppermute | solution.py:27
  14.9 6.3 %copy-start.4 = (f32[7168]{0:T(1024)S(1)}, f32[7168]{0:T(1024)}, u32[]{:S(2)}) copy-start(f32[7168]{0:T(1024)} %param.14) | copy-start | bytes 86020
  14.9 4.9 %collective-permute-start.3 = (bf16[8,7168]{1,0:T(8,128)(2,1)S(1)}, bf16[8,7168]{1,0:T(8,128)(2,1)S(1)}, u32[]{:S(2)}, u32[]{:S(2)}) collective-permute-start(bf16[8,7168]{1,0:T(8,128)(2,1)S(1)} %get-tuple-element.19.refs_1_), channel_id=1, source_target_pairs={{0,2},{2,0},{4,6},{6,4},{8,10},{10,8},{12,14},{14,12},{1,3},{3,1},... | collective-permute-start | bytes 344072 | tf_op jit(solution)/shard_map/ppermute | solution.py:27
  19.8 1.4 %collective-permute-start.4 = (bf16[8,7168]{1,0:T(8,128)(2,1)S(1)}, bf16[8,7168]{1,0:T(8,128)(2,1)S(1)}, u32[]{:S(2)}, u32[]{:S(2)}) collective-permute-start(bf16[8,7168]{1,0:T(8,128)(2,1)S(1)} %add.15.refs_1_), channel_id=1, source_target_pairs={{0,1},{1,0},{2,3},{3,2},{4,5},{5,4},{6,7},{7,6},{8,9},{9,8},{10,11... | collective-permute-start | bytes 344072 | tf_op jit(solution)/shard_map/ppermute | solution.py:27
  21.2 19.4 %copy-start = (bf16[1,4,256,576]{2,3,1,0:T(8,128)(2,1)S(1)}, bf16[1,4,256,576]{2,3,1,0:T(8,128)(2,1)}, u32[]{:S(2)}) copy-start(bf16[1,4,256,576]{2,3,1,0:T(8,128)(2,1)} %param.10) | copy-start | bytes 3538948
  21.2 19.4 %copy-start.1 = (bf16[1,4,64,576]{3,2,1,0:T(8,128)(2,1)S(1)}, bf16[1,4,64,576]{3,2,1,0:T(8,128)(2,1)}, u32[]{:S(2)}) copy-start(bf16[1,4,64,576]{3,2,1,0:T(8,128)(2,1)} %param.9) | copy-start | bytes 884740
  21.2 19.4 %copy-start.6 = (s32[1,8]{1,0:T(1,128)S(1)}, s32[1,8]{1,0:T(1,128)}, u32[]{:S(2)}) copy-start(s32[1,8]{1,0:T(1,128)} %counts_ref.1) | copy-start | bytes 100
  21.2 19.4 %copy-start.7 = (s32[1,4]{1,0:T(1,128)S(1)}, s32[1,4]{1,0:T(1,128)}, u32[]{:S(2)}) copy-start(s32[1,4]{1,0:T(1,128)} %lengths_ref.1) | copy-start | bytes 52
  30.4 1.4 %collective-permute-start.5 = (bf16[8,7168]{1,0:T(8,128)(2,1)S(1)}, bf16[8,7168]{1,0:T(8,128)(2,1)S(1)}, u32[]{:S(2)}, u32[]{:S(2)}) collective-permute-start(bf16[8,7168]{1,0:T(8,128)(2,1)S(1)} %get-tuple-element.25), channel_id=1, source_target_pairs={{0,1},{1,0},{2,3},{3,2},{4,5},{5,4},{6,7},{7,6},{8,9},{9,8},{10,11... | collective-permute-start | bytes 344072 | tf_op jit(solution)/shard_map/ppermute | solution.py:27
  31.9 4.2 %collective-permute-start.6 = (bf16[4,7168]{1,0:T(4,128)(2,1)S(1)}, bf16[4,7168]{1,0:T(4,128)(2,1)S(1)}, u32[]{:S(2)}, u32[]{:S(2)}) collective-permute-start(bf16[4,7168]{1,0:T(4,128)(2,1)S(1)} %slice.41.after_ref), channel_id=1, source_target_pairs={{0,2},{2,0},{4,6},{6,4},{8,10},{10,8},{12,14},{14,12},{1,3},{3,1},... | collective-permute-start | bytes 172040 | tf_op jit(solution)/shard_map/ppermute | solution.py:27
  36.2 3.9 %collective-permute-start.7 = (bf16[2,7168]{1,0:T(2,128)(2,1)S(1)}, bf16[2,7168]{1,0:T(2,128)(2,1)S(1)}, u32[]{:S(2)}, u32[]{:S(2)}) collective-permute-start(bf16[2,7168]{1,0:T(2,128)(2,1)S(1)} %slice.42), channel_id=1, source_target_pairs={{0,4},{2,6},{4,0},{6,2},{8,12},{10,14},{12,8},{14,10},{1,5},{3,7},... | collective-permute-start | bytes 86024 | tf_op jit(solution)/shard_map/ppermute | solution.py:27
  40.2 5.1 %collective-permute-start.8 = (f32[1,7168]{1,0:T(1,128)S(1)}, f32[1,7168]{1,0:T(1,128)S(1)}, u32[]{:S(2)}, u32[]{:S(2)}) collective-permute-start(f32[1,7168]{1,0:T(1,128)S(1)} %slice.31), channel_id=1, source_target_pairs={{0,8},{2,10},{4,12},{6,14},{8,0},{10,2},{12,4},{14,6},{1,9},{3,11}... | collective-permute-start | bytes 86024 | tf_op jit(solution)/shard_map/ppermute | solution.py:27

commit v3 on v2

v3 whole, which is shorter than its diff:
```python
import jax
import jax.numpy as jnp
from jax import lax
from jax.experimental import pallas as pl
from jax.experimental.pallas import tpu as pltpu
from jax.sharding import PartitionSpec as P

KVL = 512
MIB = 1024 * 1024

score_scale = 192.0 ** (-0.5)
norm_eps = 1e-06

VMEM = pl.BlockSpec(memory_space=pltpu.VMEM)
SMEM = pl.BlockSpec(memory_space=pltpu.SMEM)
ANY = pl.BlockSpec(memory_space=pl.ANY)


def gather_stages(bits):
    stages, top = [], bits
    while top > 1:
        width = 1 if top % 2 == 0 else 2
        top -= width
        stages.append((top, width))
    return stages


def sum_stages(bits):
    return [(low, min(2, bits - low)) for low in range(0, bits, 2)]


def block_offset(position, stages):
    out = position * 0
    for low, width in stages:
        out = out | ((position & ((1 << width) - 1)) << low)
        position = position >> width
    return out


def row_offset(position, stages):
    return block_offset(position, stages[::-1])


def swap(x, axis, distance, size):
    return lax.ppermute(x, axis, [(i, i ^ distance) for i in range(size)])


def pinned(weight):
    return pltpu.with_memory_space_constraint(weight, pltpu.HBM)


def row_copies(source, first, target, sems):
    rows = target.shape[0]
    pieces = sems.shape[0]
    step = rows // pieces
    return [
        pltpu.make_async_copy(
            source.at[pl.ds(first + i * step, step)], target.at[pl.ds(i * step, step)], sems.at[i]
        )
        for i in range(pieces)
    ]


def pieces_of(rows, most):
    return most if rows % (16 * most) == 0 else 1


def share_start(units, share):
    if share == units:
        return 0
    return pl.multiple_of(lax.axis_index("sub") * share, 16)


def pick_matrix(counts, device, size, slots):
    stages = gather_stages(size.bit_length() - 1)
    shape = (size, size // 2 * slots)
    slot = lax.broadcasted_iota(jnp.int32, shape, 1)
    every = lax.broadcasted_iota(jnp.int32, shape, 0)
    owner = block_offset(slot // slots, stages) ^ device
    known = jnp.broadcast_to(counts, (8, size)).astype(jnp.bfloat16)
    start = jnp.dot(known, (every < owner).astype(jnp.bfloat16), preferred_element_type=jnp.float32)[:1]
    count = jnp.dot(known, (every == owner).astype(jnp.bfloat16), preferred_element_type=jnp.float32)[:1]
    place = (slot % slots)[:1].astype(jnp.float32)
    request = jnp.where(place < count, start + place, -1.0)
    return (request == every.astype(jnp.float32)).astype(jnp.bfloat16)


def load_rows(jobs, share, after=None, counts=None, slots=0):
    pieces = [pieces_of(rows, 4) for _, _, rows in jobs]
    size = 0 if counts is None else counts.shape[1]
    operands = [pinned(weight) for weight, _, _ in jobs]
    out_shape = [pltpu.VMEM((rows, weight.shape[1]), weight.dtype) for weight, _, rows in jobs]
    scratch = [pltpu.SemaphoreType.DMA((count,)) for count in pieces]
    if counts is not None:
        operands.append(pinned(counts))
        out_shape.append(jax.ShapeDtypeStruct((size, size // 2 * slots), jnp.bfloat16))
        scratch += [pltpu.VMEM((1, size), jnp.int32), pltpu.SemaphoreType.DMA]
    if after is not None:
        operands.append(after)

    def body(*refs):
        sources, refs = refs[: len(operands)], refs[len(operands) :]
        targets, refs = refs[: len(out_shape)], refs[len(out_shape) :]
        if counts is not None:
            small = pltpu.make_async_copy(sources[len(jobs)], refs[-2], refs[-1])
            small.start()
        copies = []
        for (weight, first, _), source, target, sems in zip(jobs, sources, targets, refs):
            copies += row_copies(source, share_start(weight.shape[0], share) + first, target, sems)
        for copy in copies:
            copy.start()
        if counts is not None:
            small.wait()
            targets[-1][...] = pick_matrix(refs[-2][...], lax.axis_index("tp"), size, slots)
        for copy in copies:
            copy.wait()

    return pl.pallas_call(
        body,
        out_shape=out_shape,
        in_specs=[ANY] * len(operands),
        out_specs=[VMEM] * len(out_shape),
        scratch_shapes=scratch,
        compiler_params=pltpu.CompilerParams(vmem_limit_bytes=2 * MIB),
        cost_estimate=pl.CostEstimate(
            flops=0, transcendentals=0, bytes_accessed=sum(4 * rows * weight.shape[1] for weight, _, rows in jobs)
        ),
        name="load_rows",
    )(*operands)


def compact(pick, blocks):
    size = pick.shape[0]
    width = blocks[0].shape[1]
    column = 1024
    count = len(blocks)

    def body(*refs):
        pick_ref, block_refs, out_ref = refs[0], refs[1 : 1 + count], refs[1 + count]
        pick_now = pick_ref[...]
        for c in range(0, width, column):
            rows = [ref[:, c : c + column].astype(jnp.float32) for ref in block_refs]
            rows = rows[0] if count == 1 else jnp.concatenate(rows, axis=0)
            out = jnp.dot(pick_now, rows.astype(jnp.bfloat16), preferred_element_type=jnp.float32)
            out_ref[:, c : c + column] = out.astype(jnp.bfloat16)

    return pl.pallas_call(
        body,
        out_shape=jax.ShapeDtypeStruct((size, width), jnp.bfloat16),
        in_specs=[VMEM] * (1 + count),
        out_specs=VMEM,
        compiler_params=pltpu.CompilerParams(vmem_limit_bytes=16 * MIB),
        name="compact",
    )(pick, *blocks)


def feed_forward(gain, row_sets, loaded, late, w_down, share, split):
    requests, width = row_sets[0].shape
    units = w_down.shape[0]
    set_count = len(row_sets)
    every = requests * set_count
    stages = sum_stages(requests.bit_length() - 1)
    column = 1024
    late_pieces = [pieces_of(rows, 4) for _, _, _, rows in late]
    pieces = pieces_of(share, 4)
    parts = [part for _, part in loaded]

    def body(*refs):
        gain_ref, refs = refs[0], refs[1:]
        set_refs, refs = refs[:set_count], refs[set_count:]
        part_refs, refs = refs[: len(parts)], refs[len(parts) :]
        late_hbm, refs = refs[: len(late)], refs[len(late) :]
        down_hbm, refs = refs[0], refs[1:]
        out_refs, refs = refs[:set_count], refs[set_count:]
        rows_ref, down_ref, down_sems, refs = refs[0], refs[1], refs[2], refs[3:]
        late_refs, late_sems = refs[: len(late)], refs[len(late) :]
        device = lax.axis_index("tp")

        late_copies = [
            row_copies(source, share_start(units, share) + first, target, sems)
            for (_, _, first, _), source, target, sems in zip(late, late_hbm, late_refs, late_sems)
        ]
        down_copies = row_copies(down_hbm, share_start(units, share), down_ref, down_sems)

        @pl.when(device >= 0)
        def _():
            for copies in late_copies:
                for copy in copies:
                    copy.start()
            for copy in down_copies:
                copy.start()

        place = lax.broadcasted_iota(jnp.int32, (every, every), 0)
        source_row = lax.broadcasted_iota(jnp.int32, (every, every), 1)
        wanted = (row_offset(place % requests, stages) ^ device) + place // requests * requests
        order = (source_row == wanted).astype(jnp.bfloat16)
        for c in range(0, width, column):
            rows = [ref[:, c : c + column].astype(jnp.float32) for ref in set_refs]
            rows = rows[0] if set_count == 1 else jnp.concatenate(rows, axis=0)
            rows_ref[:, c : c + column] = jnp.dot(
                order, rows.astype(jnp.bfloat16), preferred_element_type=jnp.float32
            )
        rows = rows_ref[...]
        inv_rms = lax.rsqrt(jnp.mean(rows * rows, axis=1, keepdims=True) + norm_eps)
        normed = (rows * inv_rms * gain_ref[...]).astype(jnp.bfloat16)

        results = [[], []]

        def project(which, ref):
            rows = ref.shape[0]
            chunk = next((c for c in (192, 160, 128, 64) if rows % c == 0), rows)
            for j in range(0, rows, chunk):
                results[which].append(
                    lax.dot_general(
                        ref[j : j + chunk, :], normed, (((1,), (1,)), ((), ())), preferred_element_type=jnp.float32
                    )
                )

        for (which, _), ref in zip(loaded, part_refs):
            project(which, ref)
        for (which, _, _, _), ref, copies in zip(late, late_refs, late_copies):
            for copy in copies:
                copy.wait()
            project(which, ref)
        gate_out, up_out = [out[0] if len(out) == 1 else jnp.concatenate(out, axis=0) for out in results]
        hidden = (jax.nn.silu(gate_out) * up_out).T.astype(jnp.bfloat16)
        for copy in down_copies:
            copy.wait()
        for c in range(0, width, column):
            out = jnp.dot(hidden, down_ref[:, c : c + column], preferred_element_type=jnp.float32)
            own = out[:requests]
            first = lax.broadcasted_iota(jnp.int32, own.shape, 0) == 0
            own += jnp.where(first, rows_ref[:requests, c : c + column], 0.0)
            out_refs[0][:, c : c + column] = own
            if set_count == 2:
                out_refs[1][:, c : c + column] = out[requests:].astype(jnp.bfloat16)

    outs = [
        jax.ShapeDtypeStruct((requests, width), jnp.float32),
        jax.ShapeDtypeStruct((requests, width), jnp.bfloat16),
    ][:set_count]
    return pl.pallas_call(
        body,
        out_shape=outs,
        in_specs=[VMEM] * (1 + set_count + len(parts)) + [ANY] * (len(late) + 1),
        out_specs=[VMEM] * set_count,
        scratch_shapes=[
            pltpu.VMEM((every, width), jnp.float32),
            pltpu.VMEM((share, width), jnp.bfloat16),
            pltpu.SemaphoreType.DMA((pieces,)),
            *[pltpu.VMEM((rows, width), jnp.bfloat16) for _, _, _, rows in late],
            *[pltpu.SemaphoreType.DMA((count,)) for count in late_pieces],
        ],
        compiler_params=pltpu.CompilerParams(vmem_limit_bytes=28 * MIB),
        cost_estimate=pl.CostEstimate(
            flops=6 * every * share * width,
            transcendentals=every * share,
            bytes_accessed=6 * share * width,
        ),
        name="feed_forward",
    )(gain[None], *row_sets, *parts, *[pinned(weight) for _, weight, _, _ in late], pinned(w_down))


def attend(queries, cache, lengths, counts, after):
    slots, heads, _ = queries.shape
    positions = cache.shape[2]

    def body(lengths_ref, counts_ref, queries_ref, cache_ref, after_ref, out_ref):
        live = counts_ref[0, lax.axis_index("tp")]
        spot = lax.broadcasted_iota(jnp.int32, (heads, positions), 1)
        for s in range(slots):
            scores = (
                jnp.dot(queries_ref[s], cache_ref[s], preferred_element_type=jnp.float32)
                * score_scale
            )
            scores = jnp.where(spot < lengths_ref[0, s], scores, -jnp.inf)
            weights = jnp.exp(scores - jnp.max(scores, axis=1, keepdims=True))
            probs = (weights / jnp.sum(weights, axis=1, keepdims=True)).astype(jnp.bfloat16)
            context = lax.dot_general(
                probs, cache_ref[s, :KVL, :], (((1,), (1,)), ((), ())), preferred_element_type=jnp.float32
            )
            out_ref[s] = jnp.where(s < live, context, 0.0).astype(jnp.bfloat16)

    return pl.pallas_call(
        body,
        out_shape=jax.ShapeDtypeStruct((slots, heads, KVL), jnp.bfloat16),
        in_specs=[SMEM, SMEM, VMEM, VMEM, ANY],
        out_specs=VMEM,
        compiler_params=pltpu.CompilerParams(vmem_limit_bytes=8 * MIB),
        cost_estimate=pl.CostEstimate(
            flops=4 * slots * heads * positions * KVL,
            transcendentals=slots * heads * positions,
            bytes_accessed=2 * (queries.size + cache.size),
        ),
        name="attend",
    )(lengths, counts, queries, cache, after)


def load_plan(share):
    if share % 192:
        return [(0, 0, share)], [(1, 0, share)], []
    early = share // 9 * 5
    return (
        [(0, 0, early)],
        [(0, early, share - early), (1, 0, 2 * early - share)],
        [(1, 2 * early - share, 2 * share - 2 * early)],
    )


def make_shards(size, cores):
    bits = size.bit_length() - 1

    def shards(queries, kv_cache, cache_lengths, live_counts, stream, norm_gain, w_gate, w_up, w_down):
        slots = queries.shape[1]
        units = w_gate.shape[0]
        split = cores == 2 and units % 32 == 0
        share = units // 2 if split else units
        weights = (w_gate, w_up)
        plan = load_plan(share)
        loaded = []

        def load(jobs, **more):
            parts = load_rows([(weights[which], first, rows) for which, first, rows in jobs], share, **more)
            loaded.extend((which, part) for (which, _, _), part in zip(jobs, parts))
            return parts

        block = stream[0]
        for step, (low, width) in enumerate(gather_stages(bits)):
            blocks = [block] + [swap(block, "tp", digit << low, size) for digit in range(1, 1 << width)]
            if step == 0:
                pick = load(plan[0], counts=live_counts, slots=slots)[-1]
            if low > 1:
                block = jnp.concatenate(blocks, axis=0)

        own = compact(pick, blocks)
        arrived = swap(own, "tp", 1, size)
        load(plan[1], after=own)
        last = loaded[-1]
        arrived, part = lax.optimization_barrier((arrived, last[1]))
        loaded[-1] = (last[0], part)
        rows = own + arrived
        row_sets = [rows, swap(rows, "sub", 1, cores)] if split else [rows]
        late = [(which, weights[which], first, count) for which, first, count in plan[2]]
        total, *other = feed_forward(norm_gain, row_sets, loaded, late, w_down, share, split)

        if split:
            total = total + swap(other[0], "sub", 1, cores).astype(jnp.float32)
        for step, (low, width) in enumerate(sum_stages(bits)):
            part = total.shape[0] >> width
            sends = [total[digit * part : (digit + 1) * part] for digit in range(1, 1 << width)]
            total = total[:part]
            if step == 0:
                sends = [send.astype(jnp.bfloat16) for send in sends]
                latent_ctx = attend(
                    queries[0], jnp.swapaxes(kv_cache[0], 1, 2), cache_lengths, live_counts, sends[0]
                )[None]
            for digit, send in enumerate(sends, 1):
                total = total + swap(send, "tp", digit << low, size).astype(jnp.float32)
        return (latent_ctx, total.astype(jnp.bfloat16)[None])

    return shards


def solution(mesh):
    in_specs = (
        P(("groups", "sub"), "tp", None, None),
        P(("groups", "sub"), "tp", None, None),
        P(("groups", "sub"), "tp"),
        P(("groups", "sub"), None),
        P(("groups", "sub"), "tp", None),
        P(),
        P("tp", None),
        P("tp", None),
        P("tp", None),
    )
    out_specs = (P(("groups", "sub"), "tp", None, None), P(("groups", "sub"), "tp", None))
    return jax.shard_map(
        make_shards(mesh.shape["tp"], mesh.shape["sub"]),
        mesh=mesh,
        in_specs=in_specs,
        out_specs=out_specs,
        check_vma=False,
    )
```

time: 46.1 us -> 41.9 us (0.909)
  waiting for transfers between devices: 12.3 us -> 9.14 us
  starting transfers between devices: 10.5 us -> 13.2 us
  Pallas kernels: 19.9 us -> 17.8 us
  local copies, waits for them, and re-layouts: 1.63 us -> 0.14 us
    ppermute x9 -> x10, waiting for transfers between devices: 12.3 us -> 9.14 us  [swap(): return lax.ppermute(x, axis, [(i, i ^ distance) for i in range(size)])]
    ppermute x9 -> x10, starting transfers between devices: 10.5 us -> 13.2 us  [swap(): return lax.ppermute(x, axis, [(i, i ^ distance) for i in range(size)])]
    pallas_call x5 -> x4, Pallas kernels: 17.2 us -> 15.1 us  [the longest x1 10.2 us: feed_forward(): pl.pallas_call(body, out_shape=outs, in_specs=[VMEM] * (1 + set_count + l...]
    unnamed x16 -> x12, local copies, waits for them, and re-layouts: 1.54 us -> 0.03 us
  transfers between devices with their start and end apart: 9 -> 10, of which waited for: 7 -> 8; matrix products, arithmetic and copies ran while one was open for 0% -> 0% of each run, Pallas kernels for 23% -> 18%
where the time goes in v3:
time: 41.9 us; the launch traced here: 41.8 us
  Pallas kernels  17.8 us (42%)
  starting transfers between devices  13.2 us (32%)
  waiting for transfers between devices  9.14 us (22%)
  other arithmetic  0.75 us (2%)
  between operations  0.75 us (2%)
    ppermute x10, starting transfers between devices, swap(): return lax.ppermute(x, axis, [(i, i ^ distance) for i in range(size)])  13.2 us
    pallas_call x1, Pallas kernels, feed_forward(): pl.pallas_call(body, out_shape=outs, in_specs=[VMEM] * (1 + set_count + l...  10.2 us
    ppermute x10, waiting for transfers between devices, swap(): return lax.ppermute(x, axis, [(i, i ^ distance) for i in range(size)])  9.14 us
    pallas_call x2, Pallas kernels, load_rows(): pl.pallas_call(body, out_shape=out_shape, in_specs=[ANY] * len(operands),...  4.67 us
    pallas_call x1, Pallas kernels, attend(): pl.pallas_call(body, out_shape=jax.ShapeDtypeStruct((slots, heads, KVL),...  2.71 us
  transfers between devices with their start and end apart: 10, of which 8 were waited for; matrix products, arithmetic and copies ran while one was open for 0% of the time, Pallas kernels for 18%

profile of v3, /device:TPU:0, one launch (start us, length us, event | category | flops | bytes accessed | tf_op | source)
XLA Modules:
  0.0 41.8 jit_solution(10381463636021939008)
XLA Ops:
  0.6 0.0 copy-start.2
  0.6 5.1 %collective-permute-start.2 = (bf16[4,7168]{1,0:T(4,128)(2,1)}, bf16[4,7168]{1,0:T(4,128)(2,1)S(1)}, u32[]{:S(2)}, u32[]{:S(2)}) collective-permute-start(bf16[4,7168]{1,0:T(4,128)(2,1)} %bitcast.11), channel_id=1, source_target_pairs={{0,12},{2,14},{4,8},{6,10},{8,4},{10,6},{12,0},{14,2},{1,13},{3,15... | collective-permute-start | bytes 172040 | tf_op jit(solution)/shard_map/ppermute | solution.py:45
  5.8 0.0 collective-permute-start.1
  5.8 0.6 %collective-permute-start = (bf16[4,7168]{1,0:T(4,128)(2,1)}, bf16[4,7168]{1,0:T(4,128)(2,1)S(1)}, u32[]{:S(2)}, u32[]{:S(2)}) collective-permute-start(bf16[4,7168]{1,0:T(4,128)(2,1)} %bitcast.13), channel_id=1, source_target_pairs={{0,4},{2,6},{4,0},{6,2},{8,12},{10,14},{12,8},{14,10},{1,5},{3,7},... | collective-permute-start | bytes 172040 | tf_op jit(solution)/shard_map/ppermute | solution.py:45
  6.4 2.4 %load_rows.2 = (bf16[320,7168]{1,0:T(8,128)(2,1)S(1)}, bf16[8,16]{1,0:T(8,128)(2,1)S(1)}) custom-call(bf16[1152,7168]{1,0:T(8,128)(2,1)} %refs_0_.3, s32[1,8]{1,0:T(1,128)} %counts_ref.1), custom_call_target="tpu_custom_call" | custom-call | bytes 9175040 | tf_op jit(solution)/shard_map/load_rows/pallas_call | solution.py:118
  8.8 0.0 collective-permute-done.2.refs_4_
  8.8 2.3 %collective-permute-done.1.refs_3_ = bf16[4,7168]{1,0:T(4,128)(2,1)S(1)} collective-permute-done((bf16[4,7168]{1,0:T(4,128)(2,1)}, bf16[4,7168]{1,0:T(4,128)(2,1)S(1)}, u32[]{:S(2)}, u32[]{:S(2)}) %collective-permute-start.1) | collective-permute-done | bytes 57376 | tf_op jit(solution)/shard_map/ppermute | solution.py:45
  11.0 0.0 collective-permute-done.refs_2_
  11.0 0.0 copy-done.2
  11.0 0.2 compact.1.refs_2_
  11.2 0.0 copy-start.3
  11.3 1.6 %collective-permute-start.3 = (bf16[8,7168]{1,0:T(8,128)(2,1)S(1)}, bf16[8,7168]{1,0:T(8,128)(2,1)S(1)}, u32[]{:S(2)}, u32[]{:S(2)}) collective-permute-start(bf16[8,7168]{1,0:T(8,128)(2,1)S(1)} %compact.1.refs_2_), channel_id=1, source_target_pairs={{0,2},{2,0},{4,6},{6,4},{8,10},{10,8},{12,14},{14,12},{1,3},{3,1},... | collective-permute-start | bytes 344072 | tf_op jit(solution)/shard_map/ppermute | solution.py:45
  12.8 2.3 %load_rows.3 = (bf16[256,7168]{1,0:T(8,128)(2,1)S(1)}, bf16[64,7168]{1,0:T(8,128)(2,1)S(1)}) custom-call(bf16[1152,7168]{1,0:T(8,128)(2,1)} %refs_0_.3, bf16[1152,7168]{1,0:T(8,128)(2,1)} %refs_6_.1, bf16[8,7168]{1,0:T(8,128)(2,1)S(1)} %compact.1.refs_2_), custom_call_target="tpu_custom_call" | custom-call | bytes 9175040 | tf_op jit(solution)/shard_map/load_rows/pallas_call | solution.py:118
  15.2 0.9 %collective-permute-done.3 = bf16[8,7168]{1,0:T(8,128)(2,1)S(1)} collective-permute-done((bf16[8,7168]{1,0:T(8,128)(2,1)S(1)}, bf16[8,7168]{1,0:T(8,128)(2,1)S(1)}, u32[]{:S(2)}, u32[]{:S(2)}) %collective-permute-start.3) | collective-permute-done | bytes 114720 | tf_op jit(solution)/shard_map/ppermute | solution.py:45
  16.1 0.1 collective-permute-start.4
  16.2 1.3 %collective-permute-done.4.refs_2_ = bf16[8,7168]{1,0:T(8,128)(2,1)S(1)} collective-permute-done((bf16[8,7168]{1,0:T(8,128)(2,1)S(1)}, bf16[8,7168]{1,0:T(8,128)(2,1)S(1)}, u32[]{:S(2)}, u32[]{:S(2)}) %collective-permute-start.4) | collective-permute-done | bytes 114720 | tf_op jit(solution)/shard_map/ppermute | solution.py:45
  17.5 0.0 copy-done.3
  17.5 0.0 copy-start
  17.5 0.0 copy-start.1
  17.5 0.0 copy-start.4
  17.6 0.0 copy-start.5
  17.6 10.2 %feed_forward.1 = (f32[8,7168]{1,0:T(8,128)S(1)}, bf16[8,7168]{1,0:T(8,128)(2,1)S(1)}) custom-call(f32[1,7168]{1,0:T(1,128)S(1)} %bitcast.15, bf16[8,7168]{1,0:T(8,128)(2,1)S(1)} %add.18.refs_1_, bf16[8,7168]{1,0:T(8,128)(2,1)S(1)} %collective-permute-done.4.refs_2_, bf16[320,7168]{1,0:T(8,128)(2,1)S(1)} %get-tuple-element.13.refs_3_, ...), custom_call_target="tpu_custom_call" | custom-call | flops 396361728 | bytes 24772608 | tf_op jit(solution)/shard_map/feed_forward/pallas_call | solution.py:242
  27.8 0.2 collective-permute-start.5
  28.0 1.2 %collective-permute-done.5 = bf16[8,7168]{1,0:T(8,128)(2,1)S(1)} collective-permute-done((bf16[8,7168]{1,0:T(8,128)(2,1)S(1)}, bf16[8,7168]{1,0:T(8,128)(2,1)S(1)}, u32[]{:S(2)}, u32[]{:S(2)}) %collective-permute-start.5) | collective-permute-done | bytes 114720 | tf_op jit(solution)/shard_map/ppermute | solution.py:45
  29.2 0.1 fusion.5
  29.3 1.1 %collective-permute-start.7 = (bf16[2,7168]{1,0:T(2,128)(2,1)S(1)}, bf16[2,7168]{1,0:T(2,128)(2,1)S(1)}, u32[]{:S(2)}, u32[]{:S(2)}) collective-permute-start(bf16[2,7168]{1,0:T(2,128)(2,1)S(1)} %get-tuple-element.20), channel_id=1, source_target_pairs={{0,4},{2,6},{4,0},{6,2},{8,12},{10,14},{12,8},{14,10},{1,5},{3,7},... | collective-permute-start | bytes 86024 | tf_op jit(solution)/shard_map/ppermute | solution.py:45
  30.4 1.9 %collective-permute-start.8 = (bf16[2,7168]{1,0:T(2,128)(2,1)S(1)}, bf16[2,7168]{1,0:T(2,128)(2,1)S(1)}, u32[]{:S(2)}, u32[]{:S(2)}) collective-permute-start(bf16[2,7168]{1,0:T(2,128)(2,1)S(1)} %get-tuple-element.21), channel_id=1, source_target_pairs={{0,6},{2,4},{4,2},{6,0},{8,14},{10,12},{12,10},{14,8},{1,7},{3,5},... | collective-permute-start | bytes 86024 | tf_op jit(solution)/shard_map/ppermute | solution.py:45
  32.3 0.5 %collective-permute-start.6 = (bf16[2,7168]{1,0:T(2,128)(2,1)S(1)}, bf16[2,7168]{1,0:T(2,128)(2,1)S(1)}, u32[]{:S(2)}, u32[]{:S(2)}) collective-permute-start(bf16[2,7168]{1,0:T(2,128)(2,1)S(1)} %get-tuple-element.22.after_ref), channel_id=1, source_target_pairs={{0,2},{2,0},{4,6},{6,4},{8,10},{10,8},{12,14},{14,12},{1,3},{3,1},... | collective-permute-start | bytes 86024 | tf_op jit(solution)/shard_map/ppermute | solution.py:45
  32.9 0.4 collective-permute-done.7
  33.2 2.0 %collective-permute-done.8 = bf16[2,7168]{1,0:T(2,128)(2,1)S(1)} collective-permute-done((bf16[2,7168]{1,0:T(2,128)(2,1)S(1)}, bf16[2,7168]{1,0:T(2,128)(2,1)S(1)}, u32[]{:S(2)}, u32[]{:S(2)}) %collective-permute-start.8) | collective-permute-done | bytes 28704 | tf_op jit(solution)/shard_map/ppermute | solution.py:45
  35.2 1.0 %collective-permute-done.6 = bf16[2,7168]{1,0:T(2,128)(2,1)S(1)} collective-permute-done((bf16[2,7168]{1,0:T(2,128)(2,1)S(1)}, bf16[2,7168]{1,0:T(2,128)(2,1)S(1)}, u32[]{:S(2)}, u32[]{:S(2)}) %collective-permute-start.6) | collective-permute-done | bytes 28704 | tf_op jit(solution)/shard_map/ppermute | solution.py:45
  36.2 0.1 fusion.1
  36.3 2.1 %collective-permute-start.9 = (f32[1,7168]{1,0:T(1,128)S(1)}, f32[1,7168]{1,0:T(1,128)S(1)}, u32[]{:S(2)}, u32[]{:S(2)}) collective-permute-start(f32[1,7168]{1,0:T(1,128)S(1)} %slice.32), channel_id=1, source_target_pairs={{0,8},{2,10},{4,12},{6,14},{8,0},{10,2},{12,4},{14,6},{1,9},{3,11}... | collective-permute-start | bytes 86024 | tf_op jit(solution)/shard_map/ppermute | solution.py:45
  38.4 0.0 copy-done
  38.4 0.0 copy-done.1
  38.4 0.0 copy-done.4
  38.4 0.0 copy-done.5
  38.4 2.7 %attend.1 = bf16[4,64,512]{2,1,0:T(8,128)(2,1)} custom-call(s32[1,4]{1,0:T(1,128)S(1)} %copy-done.5, s32[1,8]{1,0:T(1,128)S(1)} %copy-done.4, bf16[4,64,576]{2,1,0:T(8,128)(2,1)S(1)} %bitcast.10, bf16[4,576,256]{2,1,0:T(8,128)(2,1)S(1)} %bitcast.9, bf16[2,7168]{1,0:T(2,128)(2,1)S(1)} %get-tuple-element.22.after_ref), custom_call_target="tpu_custom_call" | custom-call | flops 134217728 | bytes 1474560 | tf_op jit(solution)/shard_map/attend/pallas_call | solution.py:284
  41.1 0.1 collective-permute-done.9
  41.1 0.6 %fusion.3 = bf16[1,1,7168]{2,1,0:T(2,128)(2,1)} fusion(f32[1,7168]{1,0:T(1,128)S(1)} %collective-permute-done.9, f32[2,7168]{1,0:T(2,128)S(1)} %fusion.1), kind=kLoop, calls=%fused_computation.6 | loop fusion | flops 14336 | bytes 71680 | tf_op jit(solution)/shard_map/broadcast_in_dim | solution.py:359
  (3 shorter events, 0.1 us)
Async XLA Ops:
  0.6 10.4 %copy-start.2 = (bf16[1,4,7168]{2,1,0:T(4,128)(2,1)S(1)}, bf16[1,4,7168]{2,1,0:T(4,128)(2,1)}, u32[]{:S(2)}) copy-start(bf16[1,4,7168]{2,1,0:T(4,128)(2,1)} %param.13) | copy-start | bytes 172036
  0.6 8.1 %collective-permute-start.2 = (bf16[4,7168]{1,0:T(4,128)(2,1)}, bf16[4,7168]{1,0:T(4,128)(2,1)S(1)}, u32[]{:S(2)}, u32[]{:S(2)}) collective-permute-start(bf16[4,7168]{1,0:T(4,128)(2,1)} %bitcast.11), channel_id=1, source_target_pairs={{0,12},{2,14},{4,8},{6,10},{8,4},{10,6},{12,0},{14,2},{1,13},{3,15... | collective-permute-start | bytes 172040 | tf_op jit(solution)/shard_map/ppermute | solution.py:45
  5.8 5.3 %collective-permute-start.1 = (bf16[4,7168]{1,0:T(4,128)(2,1)}, bf16[4,7168]{1,0:T(4,128)(2,1)S(1)}, u32[]{:S(2)}, u32[]{:S(2)}) collective-permute-start(bf16[4,7168]{1,0:T(4,128)(2,1)} %bitcast.12), channel_id=1, source_target_pairs={{0,8},{2,10},{4,12},{6,14},{8,0},{10,2},{12,4},{14,6},{1,9},{3,11}... | collective-permute-start | bytes 172040 | tf_op jit(solution)/shard_map/ppermute | solution.py:45
  5.8 5.3 %collective-permute-start = (bf16[4,7168]{1,0:T(4,128)(2,1)}, bf16[4,7168]{1,0:T(4,128)(2,1)S(1)}, u32[]{:S(2)}, u32[]{:S(2)}) collective-permute-start(bf16[4,7168]{1,0:T(4,128)(2,1)} %bitcast.13), channel_id=1, source_target_pairs={{0,4},{2,6},{4,0},{6,2},{8,12},{10,14},{12,8},{14,10},{1,5},{3,7},... | collective-permute-start | bytes 172040 | tf_op jit(solution)/shard_map/ppermute | solution.py:45
  11.2 6.3 %copy-start.3 = (f32[7168]{0:T(1024)S(1)}, f32[7168]{0:T(1024)}, u32[]{:S(2)}) copy-start(f32[7168]{0:T(1024)} %param.14) | copy-start | bytes 86020
  11.3 4.9 %collective-permute-start.3 = (bf16[8,7168]{1,0:T(8,128)(2,1)S(1)}, bf16[8,7168]{1,0:T(8,128)(2,1)S(1)}, u32[]{:S(2)}, u32[]{:S(2)}) collective-permute-start(bf16[8,7168]{1,0:T(8,128)(2,1)S(1)} %compact.1.refs_2_), channel_id=1, source_target_pairs={{0,2},{2,0},{4,6},{6,4},{8,10},{10,8},{12,14},{14,12},{1,3},{3,1},... | collective-permute-start | bytes 344072 | tf_op jit(solution)/shard_map/ppermute | solution.py:45
  16.1 1.4 %collective-permute-start.4 = (bf16[8,7168]{1,0:T(8,128)(2,1)S(1)}, bf16[8,7168]{1,0:T(8,128)(2,1)S(1)}, u32[]{:S(2)}, u32[]{:S(2)}) collective-permute-start(bf16[8,7168]{1,0:T(8,128)(2,1)S(1)} %add.18.refs_1_), channel_id=1, source_target_pairs={{0,1},{1,0},{2,3},{3,2},{4,5},{5,4},{6,7},{7,6},{8,9},{9,8},{10,11... | collective-permute-start | bytes 344072 | tf_op jit(solution)/shard_map/ppermute | solution.py:45
  17.5 20.8 %copy-start = (bf16[1,4,256,576]{2,3,1,0:T(8,128)(2,1)S(1)}, bf16[1,4,256,576]{2,3,1,0:T(8,128)(2,1)}, u32[]{:S(2)}) copy-start(bf16[1,4,256,576]{2,3,1,0:T(8,128)(2,1)} %param.10) | copy-start | bytes 3538948
  17.5 20.8 %copy-start.1 = (bf16[1,4,64,576]{3,2,1,0:T(8,128)(2,1)S(1)}, bf16[1,4,64,576]{3,2,1,0:T(8,128)(2,1)}, u32[]{:S(2)}) copy-start(bf16[1,4,64,576]{3,2,1,0:T(8,128)(2,1)} %param.9) | copy-start | bytes 884740
  17.5 20.8 %copy-start.4 = (s32[1,8]{1,0:T(1,128)S(1)}, s32[1,8]{1,0:T(1,128)}, u32[]{:S(2)}) copy-start(s32[1,8]{1,0:T(1,128)} %counts_ref.1) | copy-start | bytes 100
  17.6 20.8 %copy-start.5 = (s32[1,4]{1,0:T(1,128)S(1)}, s32[1,4]{1,0:T(1,128)}, u32[]{:S(2)}) copy-start(s32[1,4]{1,0:T(1,128)} %lengths_ref.1) | copy-start | bytes 52
  27.8 1.4 %collective-permute-start.5 = (bf16[8,7168]{1,0:T(8,128)(2,1)S(1)}, bf16[8,7168]{1,0:T(8,128)(2,1)S(1)}, u32[]{:S(2)}, u32[]{:S(2)}) collective-permute-start(bf16[8,7168]{1,0:T(8,128)(2,1)S(1)} %get-tuple-element.17), channel_id=1, source_target_pairs={{0,1},{1,0},{2,3},{3,2},{4,5},{5,4},{6,7},{7,6},{8,9},{9,8},{10,11... | collective-permute-start | bytes 344072 | tf_op jit(solution)/shard_map/ppermute | solution.py:45
  29.3 3.9 %collective-permute-start.7 = (bf16[2,7168]{1,0:T(2,128)(2,1)S(1)}, bf16[2,7168]{1,0:T(2,128)(2,1)S(1)}, u32[]{:S(2)}, u32[]{:S(2)}) collective-permute-start(bf16[2,7168]{1,0:T(2,128)(2,1)S(1)} %get-tuple-element.20), channel_id=1, source_target_pairs={{0,4},{2,6},{4,0},{6,2},{8,12},{10,14},{12,8},{14,10},{1,5},{3,7},... | collective-permute-start | bytes 86024 | tf_op jit(solution)/shard_map/ppermute | solution.py:45
  30.4 4.8 %collective-permute-start.8 = (bf16[2,7168]{1,0:T(2,128)(2,1)S(1)}, bf16[2,7168]{1,0:T(2,128)(2,1)S(1)}, u32[]{:S(2)}, u32[]{:S(2)}) collective-permute-start(bf16[2,7168]{1,0:T(2,128)(2,1)S(1)} %get-tuple-element.21), channel_id=1, source_target_pairs={{0,6},{2,4},{4,2},{6,0},{8,14},{10,12},{12,10},{14,8},{1,7},{3,5},... | collective-permute-start | bytes 86024 | tf_op jit(solution)/shard_map/ppermute | solution.py:45
  32.3 3.9 %collective-permute-start.6 = (bf16[2,7168]{1,0:T(2,128)(2,1)S(1)}, bf16[2,7168]{1,0:T(2,128)(2,1)S(1)}, u32[]{:S(2)}, u32[]{:S(2)}) collective-permute-start(bf16[2,7168]{1,0:T(2,128)(2,1)S(1)} %get-tuple-element.22.after_ref), channel_id=1, source_target_pairs={{0,2},{2,0},{4,6},{6,4},{8,10},{10,8},{12,14},{14,12},{1,3},{3,1},... | collective-permute-start | bytes 86024 | tf_op jit(solution)/shard_map/ppermute | solution.py:45
  36.3 4.8 %collective-permute-start.9 = (f32[1,7168]{1,0:T(1,128)S(1)}, f32[1,7168]{1,0:T(1,128)S(1)}, u32[]{:S(2)}, u32[]{:S(2)}) collective-permute-start(f32[1,7168]{1,0:T(1,128)S(1)} %slice.32), channel_id=1, source_target_pairs={{0,8},{2,10},{4,12},{6,14},{8,0},{10,2},{12,4},{14,6},{1,9},{3,11}... | collective-permute-start | bytes 86024 | tf_op jit(solution)/shard_map/ppermute | solution.py:45

commit v4 on v3

--- a/solution.py
+++ b/solution.py
@@ -49,16 +49,24 @@
     return pltpu.with_memory_space_constraint(weight, pltpu.HBM)
 
 
-def row_copies(source, first, target, sems):
-    rows = target.shape[0]
-    pieces = sems.shape[0]
-    step = rows // pieces
-    return [
-        pltpu.make_async_copy(
-            source.at[pl.ds(first + i * step, step)], target.at[pl.ds(i * step, step)], sems.at[i]
-        )
-        for i in range(pieces)
-    ]
+def row_copy(source, first, target, sems, i):
+    step = target.shape[0] // sems.shape[0]
+    here = pl.multiple_of(i * step, step)
+    return pltpu.make_async_copy(
+        source.at[pl.ds(first + here, step)], target.at[pl.ds(here, step)], sems.at[i]
+    )
+
+
+def start_rows(source, first, target, sems, pieces=None):
+    @pl.loop(*(pieces or (0, sems.shape[0])))
+    def _(i):
+        row_copy(source, first, target, sems, i).start()
+
+
+def wait_rows(source, first, target, sems):
+    @pl.loop(0, sems.shape[0])
+    def _(i):
+        row_copy(source, first, target, sems, i).wait()
 
 
 def pieces_of(rows, most):
@@ -104,16 +112,17 @@
         if counts is not None:
             small = pltpu.make_async_copy(sources[len(jobs)], refs[-2], refs[-1])
             small.start()
-        copies = []
-        for (weight, first, _), source, target, sems in zip(jobs, sources, targets, refs):
-            copies += row_copies(source, share_start(weight.shape[0], share) + first, target, sems)
+        copies = [
+            (source, share_start(weight.shape[0], share) + first, target, sems)
+            for (weight, first, _), source, target, sems in zip(jobs, sources, targets, refs)
+        ]
         for copy in copies:
-            copy.start()
+            start_rows(*copy)
         if counts is not None:
             small.wait()
             targets[-1][...] = pick_matrix(refs[-2][...], lax.axis_index("tp"), size, slots)
         for copy in copies:
-            copy.wait()
+            wait_rows(*copy)
 
     return pl.pallas_call(
         body,
@@ -163,7 +172,7 @@
     column = 1024
     late_pieces = [pieces_of(rows, 4) for _, _, _, rows in late]
     pieces = pieces_of(share, 4)
-    parts = [part for _, part in loaded]
+    parts = [part for _, _, part in loaded]
 
     def body(*refs):
         gain_ref, refs = refs[0], refs[1:]
@@ -172,23 +181,27 @@
         late_hbm, refs = refs[: len(late)], refs[len(late) :]
         down_hbm, refs = refs[0], refs[1:]
         out_refs, refs = refs[:set_count], refs[set_count:]
-        rows_ref, down_ref, down_sems, refs = refs[0], refs[1], refs[2], refs[3:]
+        rows_ref, normed_ref, down_ref, down_sems = refs[:4]
+        projected_refs, refs = refs[4:6], refs[6:]
         late_refs, late_sems = refs[: len(late)], refs[len(late) :]
         device = lax.axis_index("tp")
 
+        start = share_start(units, share)
         late_copies = [
-            row_copies(source, share_start(units, share) + first, target, sems)
+            (source, start + first, target, sems)
             for (_, _, first, _), source, target, sems in zip(late, late_hbm, late_refs, late_sems)
         ]
-        down_copies = row_copies(down_hbm, share_start(units, share), down_ref, down_sems)
-
-        @pl.when(device >= 0)
-        def _():
-            for copies in late_copies:
-                for copy in copies:
-                    copy.start()
-            for copy in down_copies:
-                copy.start()
+        down_copy = (down_hbm, start, down_ref, down_sems)
+        for copy in late_copies:
+            start_rows(*copy)
+
+        def project(which, ref, at):
+            rows = ref.shape[0]
+            chunk = next((c for c in (192, 160, 128, 64) if rows % c == 0), rows)
+            for j in range(0, rows, chunk):
+                projected_refs[which][at + j : at + j + chunk, :] = lax.dot_general(
+                    ref[j : j + chunk, :], normed_ref[...], (((1,), (1,)), ((), ())), preferred_element_type=jnp.float32
+                )
 
         place = lax.broadcasted_iota(jnp.int32, (every, every), 0)
         source_row = lax.broadcasted_iota(jnp.int32, (every, every), 1)
@@ -202,30 +215,19 @@
             )
         rows = rows_ref[...]
         inv_rms = lax.rsqrt(jnp.mean(rows * rows, axis=1, keepdims=True) + norm_eps)
-        normed = (rows * inv_rms * gain_ref[...]).astype(jnp.bfloat16)
-
-        results = [[], []]
-
-        def project(which, ref):
-            rows = ref.shape[0]
-            chunk = next((c for c in (192, 160, 128, 64) if rows % c == 0), rows)
-            for j in range(0, rows, chunk):
-                results[which].append(
-                    lax.dot_general(
-                        ref[j : j + chunk, :], normed, (((1,), (1,)), ((), ())), preferred_element_type=jnp.float32
-                    )
-                )
-
-        for (which, _), ref in zip(loaded, part_refs):
-            project(which, ref)
-        for (which, _, _, _), ref, copies in zip(late, late_refs, late_copies):
-            for copy in copies:
-                copy.wait()
-            project(which, ref)
-        gate_out, up_out = [out[0] if len(out) == 1 else jnp.concatenate(out, axis=0) for out in results]
-        hidden = (jax.nn.silu(gate_out) * up_out).T.astype(jnp.bfloat16)
-        for copy in down_copies:
-            copy.wait()
+        normed_ref[...] = (rows * inv_rms * gain_ref[...]).astype(jnp.bfloat16)
+
+        for part, ((which, first, _), ref) in enumerate(zip(loaded, part_refs)):
+            project(which, ref, first)
+            if part == 0:
+                start_rows(*down_copy, pieces=(0, pieces // 2))
+        for copy in late_copies:
+            wait_rows(*copy)
+        start_rows(*down_copy, pieces=(pieces // 2, pieces))
+        for (which, _, first, _), ref in zip(late, late_refs):
+            project(which, ref, first)
+        hidden = (jax.nn.silu(projected_refs[0][...]) * projected_refs[1][...]).T.astype(jnp.bfloat16)
+        wait_rows(*down_copy)
         for c in range(0, width, column):
             out = jnp.dot(hidden, down_ref[:, c : c + column], preferred_element_type=jnp.float32)
             own = out[:requests]
@@ -246,8 +248,10 @@
         out_specs=[VMEM] * set_count,
         scratch_shapes=[
             pltpu.VMEM((every, width), jnp.float32),
+            pltpu.VMEM((every, width), jnp.bfloat16),
             pltpu.VMEM((share, width), jnp.bfloat16),
             pltpu.SemaphoreType.DMA((pieces,)),
+            *[pltpu.VMEM((share, every), jnp.float32)] * 2,
             *[pltpu.VMEM((rows, width), jnp.bfloat16) for _, _, _, rows in late],
             *[pltpu.SemaphoreType.DMA((count,)) for count in late_pieces],
         ],
@@ -321,7 +325,7 @@
 
         def load(jobs, **more):
             parts = load_rows([(weights[which], first, rows) for which, first, rows in jobs], share, **more)
-            loaded.extend((which, part) for (which, _, _), part in zip(jobs, parts))
+            loaded.extend((which, first, part) for (which, first, _), part in zip(jobs, parts))
             return parts
 
         block = stream[0]
@@ -335,9 +339,9 @@
         own = compact(pick, blocks)
         arrived = swap(own, "tp", 1, size)
         load(plan[1], after=own)
-        last = loaded[-1]
-        arrived, part = lax.optimization_barrier((arrived, last[1]))
-        loaded[-1] = (last[0], part)
+        *last, part = loaded[-1]
+        arrived, part = lax.optimization_barrier((arrived, part))
+        loaded[-1] = (*last, part)
         rows = own + arrived
         row_sets = [rows, swap(rows, "sub", 1, cores)] if split else [rows]
         late = [(which, weights[which], first, count) for which, first, count in plan[2]]

time: 41.9 us -> 39.3 us (0.938)
  Pallas kernels: 17.8 us -> 15.2 us
    pallas_call x1, Pallas kernels: 10.2 us -> 7.61 us  [feed_forward(): pl.pallas_call(body, out_shape=outs, in_specs=[VMEM] * (1 + set_count + l...]
  transfers between devices with their start and end apart: 10 -> 10, of which waited for: 8 -> 8; matrix products, arithmetic and copies ran while one was open for 0% -> 0% of each run, Pallas kernels for 18% -> 19%
where the time goes in v4:
time: 39.3 us; the launch traced here: 39.2 us
  Pallas kernels  15.2 us (39%)
  starting transfers between devices  13.2 us (34%)
  waiting for transfers between devices  9.13 us (23%)
  other arithmetic  0.75 us (2%)
  between operations  0.75 us (2%)
    ppermute x10, starting transfers between devices, swap(): return lax.ppermute(x, axis, [(i, i ^ distance) for i in range(size)])  13.2 us
    ppermute x10, waiting for transfers between devices, swap(): return lax.ppermute(x, axis, [(i, i ^ distance) for i in range(size)])  9.13 us
    pallas_call x1, Pallas kernels, feed_forward(): pl.pallas_call(body, out_shape=outs, in_specs=[VMEM] * (1 + set_count + l...  7.61 us
    pallas_call x2, Pallas kernels, load_rows(): pl.pallas_call(body, out_shape=out_shape, in_specs=[ANY] * len(operands),...  4.67 us
    pallas_call x1, Pallas kernels, attend(): pl.pallas_call(body, out_shape=jax.ShapeDtypeStruct((slots, heads, KVL),...  2.71 us
  transfers between devices with their start and end apart: 10, of which 8 were waited for; matrix products, arithmetic and copies ran while one was open for 0% of the time, Pallas kernels for 19%

profile of v4, /device:TPU:0, one launch (start us, length us, event | category | flops | bytes accessed | tf_op | source)
XLA Modules:
  0.0 39.2 jit_solution(505351754666742305)
XLA Ops:
  0.6 0.0 copy-start.2
  0.6 5.1 %collective-permute-start.2 = (bf16[4,7168]{1,0:T(4,128)(2,1)}, bf16[4,7168]{1,0:T(4,128)(2,1)S(1)}, u32[]{:S(2)}, u32[]{:S(2)}) collective-permute-start(bf16[4,7168]{1,0:T(4,128)(2,1)} %bitcast.11), channel_id=1, source_target_pairs={{0,12},{2,14},{4,8},{6,10},{8,4},{10,6},{12,0},{14,2},{1,13},{3,15... | collective-permute-start | bytes 172040 | tf_op jit(solution)/shard_map/ppermute | solution.py:45
  5.8 0.0 collective-permute-start.1
  5.8 0.6 %collective-permute-start = (bf16[4,7168]{1,0:T(4,128)(2,1)}, bf16[4,7168]{1,0:T(4,128)(2,1)S(1)}, u32[]{:S(2)}, u32[]{:S(2)}) collective-permute-start(bf16[4,7168]{1,0:T(4,128)(2,1)} %bitcast.13), channel_id=1, source_target_pairs={{0,4},{2,6},{4,0},{6,2},{8,12},{10,14},{12,8},{14,10},{1,5},{3,7},... | collective-permute-start | bytes 172040 | tf_op jit(solution)/shard_map/ppermute | solution.py:45
  6.4 2.4 %load_rows.2 = (bf16[320,7168]{1,0:T(8,128)(2,1)S(1)}, bf16[8,16]{1,0:T(8,128)(2,1)S(1)}) custom-call(bf16[1152,7168]{1,0:T(8,128)(2,1)} %refs_0_.3, s32[1,8]{1,0:T(1,128)} %counts_ref.1), custom_call_target="tpu_custom_call" | custom-call | bytes 9175040 | tf_op jit(solution)/shard_map/load_rows/pallas_call | solution.py:127
  8.8 0.0 collective-permute-done.2.refs_4_
  8.8 2.3 %collective-permute-done.1.refs_3_ = bf16[4,7168]{1,0:T(4,128)(2,1)S(1)} collective-permute-done((bf16[4,7168]{1,0:T(4,128)(2,1)}, bf16[4,7168]{1,0:T(4,128)(2,1)S(1)}, u32[]{:S(2)}, u32[]{:S(2)}) %collective-permute-start.1) | collective-permute-done | bytes 57376 | tf_op jit(solution)/shard_map/ppermute | solution.py:45
  11.0 0.0 collective-permute-done.refs_2_
  11.0 0.0 copy-done.2
  11.0 0.2 compact.1.refs_2_
  11.2 0.0 copy-start.3
  11.3 1.6 %collective-permute-start.3 = (bf16[8,7168]{1,0:T(8,128)(2,1)S(1)}, bf16[8,7168]{1,0:T(8,128)(2,1)S(1)}, u32[]{:S(2)}, u32[]{:S(2)}) collective-permute-start(bf16[8,7168]{1,0:T(8,128)(2,1)S(1)} %compact.1.refs_2_), channel_id=1, source_target_pairs={{0,2},{2,0},{4,6},{6,4},{8,10},{10,8},{12,14},{14,12},{1,3},{3,1},... | collective-permute-start | bytes 344072 | tf_op jit(solution)/shard_map/ppermute | solution.py:45
  12.8 2.3 %load_rows.3 = (bf16[256,7168]{1,0:T(8,128)(2,1)S(1)}, bf16[64,7168]{1,0:T(8,128)(2,1)S(1)}) custom-call(bf16[1152,7168]{1,0:T(8,128)(2,1)} %refs_0_.3, bf16[1152,7168]{1,0:T(8,128)(2,1)} %refs_6_.1, bf16[8,7168]{1,0:T(8,128)(2,1)S(1)} %compact.1.refs_2_), custom_call_target="tpu_custom_call" | custom-call | bytes 9175040 | tf_op jit(solution)/shard_map/load_rows/pallas_call | solution.py:127
  15.2 0.9 %collective-permute-done.3 = bf16[8,7168]{1,0:T(8,128)(2,1)S(1)} collective-permute-done((bf16[8,7168]{1,0:T(8,128)(2,1)S(1)}, bf16[8,7168]{1,0:T(8,128)(2,1)S(1)}, u32[]{:S(2)}, u32[]{:S(2)}) %collective-permute-start.3) | collective-permute-done | bytes 114720 | tf_op jit(solution)/shard_map/ppermute | solution.py:45
  16.1 0.1 collective-permute-start.4
  16.2 1.3 %collective-permute-done.4.refs_2_ = bf16[8,7168]{1,0:T(8,128)(2,1)S(1)} collective-permute-done((bf16[8,7168]{1,0:T(8,128)(2,1)S(1)}, bf16[8,7168]{1,0:T(8,128)(2,1)S(1)}, u32[]{:S(2)}, u32[]{:S(2)}) %collective-permute-start.4) | collective-permute-done | bytes 114720 | tf_op jit(solution)/shard_map/ppermute | solution.py:45
  17.5 0.0 copy-done.3
  17.5 0.0 copy-start
  17.5 0.0 copy-start.1
  17.5 0.0 copy-start.4
  17.6 0.0 copy-start.5
  17.6 7.6 %feed_forward.1 = (f32[8,7168]{1,0:T(8,128)S(1)}, bf16[8,7168]{1,0:T(8,128)(2,1)S(1)}) custom-call(f32[1,7168]{1,0:T(1,128)S(1)} %bitcast.15, bf16[8,7168]{1,0:T(8,128)(2,1)S(1)} %add.18.refs_1_, bf16[8,7168]{1,0:T(8,128)(2,1)S(1)} %collective-permute-done.4.refs_2_, bf16[320,7168]{1,0:T(8,128)(2,1)S(1)} %get-tuple-element.13.refs_3_, ...), custom_call_target="tpu_custom_call" | custom-call | flops 396361728 | bytes 24772608 | tf_op jit(solution)/shard_map/feed_forward/pallas_call | solution.py:244
  25.2 0.2 collective-permute-start.5
  25.4 1.2 %collective-permute-done.5 = bf16[8,7168]{1,0:T(8,128)(2,1)S(1)} collective-permute-done((bf16[8,7168]{1,0:T(8,128)(2,1)S(1)}, bf16[8,7168]{1,0:T(8,128)(2,1)S(1)}, u32[]{:S(2)}, u32[]{:S(2)}) %collective-permute-start.5) | collective-permute-done | bytes 114720 | tf_op jit(solution)/shard_map/ppermute | solution.py:45
  26.6 0.1 fusion.5
  26.7 1.1 %collective-permute-start.7 = (bf16[2,7168]{1,0:T(2,128)(2,1)S(1)}, bf16[2,7168]{1,0:T(2,128)(2,1)S(1)}, u32[]{:S(2)}, u32[]{:S(2)}) collective-permute-start(bf16[2,7168]{1,0:T(2,128)(2,1)S(1)} %get-tuple-element.20), channel_id=1, source_target_pairs={{0,4},{2,6},{4,0},{6,2},{8,12},{10,14},{12,8},{14,10},{1,5},{3,7},... | collective-permute-start | bytes 86024 | tf_op jit(solution)/shard_map/ppermute | solution.py:45
  27.8 1.9 %collective-permute-start.8 = (bf16[2,7168]{1,0:T(2,128)(2,1)S(1)}, bf16[2,7168]{1,0:T(2,128)(2,1)S(1)}, u32[]{:S(2)}, u32[]{:S(2)}) collective-permute-start(bf16[2,7168]{1,0:T(2,128)(2,1)S(1)} %get-tuple-element.21), channel_id=1, source_target_pairs={{0,6},{2,4},{4,2},{6,0},{8,14},{10,12},{12,10},{14,8},{1,7},{3,5},... | collective-permute-start | bytes 86024 | tf_op jit(solution)/shard_map/ppermute | solution.py:45
  29.7 0.5 %collective-permute-start.6 = (bf16[2,7168]{1,0:T(2,128)(2,1)S(1)}, bf16[2,7168]{1,0:T(2,128)(2,1)S(1)}, u32[]{:S(2)}, u32[]{:S(2)}) collective-permute-start(bf16[2,7168]{1,0:T(2,128)(2,1)S(1)} %get-tuple-element.22.after_ref), channel_id=1, source_target_pairs={{0,2},{2,0},{4,6},{6,4},{8,10},{10,8},{12,14},{14,12},{1,3},{3,1},... | collective-permute-start | bytes 86024 | tf_op jit(solution)/shard_map/ppermute | solution.py:45
  30.2 0.4 collective-permute-done.7
  30.6 2.0 %collective-permute-done.8 = bf16[2,7168]{1,0:T(2,128)(2,1)S(1)} collective-permute-done((bf16[2,7168]{1,0:T(2,128)(2,1)S(1)}, bf16[2,7168]{1,0:T(2,128)(2,1)S(1)}, u32[]{:S(2)}, u32[]{:S(2)}) %collective-permute-start.8) | collective-permute-done | bytes 28704 | tf_op jit(solution)/shard_map/ppermute | solution.py:45
  32.6 1.0 %collective-permute-done.6 = bf16[2,7168]{1,0:T(2,128)(2,1)S(1)} collective-permute-done((bf16[2,7168]{1,0:T(2,128)(2,1)S(1)}, bf16[2,7168]{1,0:T(2,128)(2,1)S(1)}, u32[]{:S(2)}, u32[]{:S(2)}) %collective-permute-start.6) | collective-permute-done | bytes 28704 | tf_op jit(solution)/shard_map/ppermute | solution.py:45
  33.6 0.1 fusion.1
  33.7 2.1 %collective-permute-start.9 = (f32[1,7168]{1,0:T(1,128)S(1)}, f32[1,7168]{1,0:T(1,128)S(1)}, u32[]{:S(2)}, u32[]{:S(2)}) collective-permute-start(f32[1,7168]{1,0:T(1,128)S(1)} %slice.32), channel_id=1, source_target_pairs={{0,8},{2,10},{4,12},{6,14},{8,0},{10,2},{12,4},{14,6},{1,9},{3,11}... | collective-permute-start | bytes 86024 | tf_op jit(solution)/shard_map/ppermute | solution.py:45
  35.8 0.0 copy-done
  35.8 0.0 copy-done.1
  35.8 0.0 copy-done.4
  35.8 0.0 copy-done.5
  35.8 2.7 %attend.1 = bf16[4,64,512]{2,1,0:T(8,128)(2,1)} custom-call(s32[1,4]{1,0:T(1,128)S(1)} %copy-done.5, s32[1,8]{1,0:T(1,128)S(1)} %copy-done.4, bf16[4,64,576]{2,1,0:T(8,128)(2,1)S(1)} %bitcast.10, bf16[4,576,256]{2,1,0:T(8,128)(2,1)S(1)} %bitcast.9, bf16[2,7168]{1,0:T(2,128)(2,1)S(1)} %get-tuple-element.22.after_ref), custom_call_target="tpu_custom_call" | custom-call | flops 134217728 | bytes 1474560 | tf_op jit(solution)/shard_map/attend/pallas_call | solution.py:288
  38.5 0.1 collective-permute-done.9
  38.5 0.6 %fusion.3 = bf16[1,1,7168]{2,1,0:T(2,128)(2,1)} fusion(f32[1,7168]{1,0:T(1,128)S(1)} %collective-permute-done.9, f32[2,7168]{1,0:T(2,128)S(1)} %fusion.1), kind=kLoop, calls=%fused_computation.6 | loop fusion | flops 14336 | bytes 71680 | tf_op jit(solution)/shard_map/broadcast_in_dim | solution.py:363
  (3 shorter events, 0.1 us)
Async XLA Ops:
  0.6 10.4 %copy-start.2 = (bf16[1,4,7168]{2,1,0:T(4,128)(2,1)S(1)}, bf16[1,4,7168]{2,1,0:T(4,128)(2,1)}, u32[]{:S(2)}) copy-start(bf16[1,4,7168]{2,1,0:T(4,128)(2,1)} %param.13) | copy-start | bytes 172036
  0.6 8.1 %collective-permute-start.2 = (bf16[4,7168]{1,0:T(4,128)(2,1)}, bf16[4,7168]{1,0:T(4,128)(2,1)S(1)}, u32[]{:S(2)}, u32[]{:S(2)}) collective-permute-start(bf16[4,7168]{1,0:T(4,128)(2,1)} %bitcast.11), channel_id=1, source_target_pairs={{0,12},{2,14},{4,8},{6,10},{8,4},{10,6},{12,0},{14,2},{1,13},{3,15... | collective-permute-start | bytes 172040 | tf_op jit(solution)/shard_map/ppermute | solution.py:45
  5.8 5.3 %collective-permute-start.1 = (bf16[4,7168]{1,0:T(4,128)(2,1)}, bf16[4,7168]{1,0:T(4,128)(2,1)S(1)}, u32[]{:S(2)}, u32[]{:S(2)}) collective-permute-start(bf16[4,7168]{1,0:T(4,128)(2,1)} %bitcast.12), channel_id=1, source_target_pairs={{0,8},{2,10},{4,12},{6,14},{8,0},{10,2},{12,4},{14,6},{1,9},{3,11}... | collective-permute-start | bytes 172040 | tf_op jit(solution)/shard_map/ppermute | solution.py:45
  5.8 5.3 %collective-permute-start = (bf16[4,7168]{1,0:T(4,128)(2,1)}, bf16[4,7168]{1,0:T(4,128)(2,1)S(1)}, u32[]{:S(2)}, u32[]{:S(2)}) collective-permute-start(bf16[4,7168]{1,0:T(4,128)(2,1)} %bitcast.13), channel_id=1, source_target_pairs={{0,4},{2,6},{4,0},{6,2},{8,12},{10,14},{12,8},{14,10},{1,5},{3,7},... | collective-permute-start | bytes 172040 | tf_op jit(solution)/shard_map/ppermute | solution.py:45
  11.2 6.3 %copy-start.3 = (f32[7168]{0:T(1024)S(1)}, f32[7168]{0:T(1024)}, u32[]{:S(2)}) copy-start(f32[7168]{0:T(1024)} %param.14) | copy-start | bytes 86020
  11.3 4.9 %collective-permute-start.3 = (bf16[8,7168]{1,0:T(8,128)(2,1)S(1)}, bf16[8,7168]{1,0:T(8,128)(2,1)S(1)}, u32[]{:S(2)}, u32[]{:S(2)}) collective-permute-start(bf16[8,7168]{1,0:T(8,128)(2,1)S(1)} %compact.1.refs_2_), channel_id=1, source_target_pairs={{0,2},{2,0},{4,6},{6,4},{8,10},{10,8},{12,14},{14,12},{1,3},{3,1},... | collective-permute-start | bytes 344072 | tf_op jit(solution)/shard_map/ppermute | solution.py:45
  16.1 1.4 %collective-permute-start.4 = (bf16[8,7168]{1,0:T(8,128)(2,1)S(1)}, bf16[8,7168]{1,0:T(8,128)(2,1)S(1)}, u32[]{:S(2)}, u32[]{:S(2)}) collective-permute-start(bf16[8,7168]{1,0:T(8,128)(2,1)S(1)} %add.18.refs_1_), channel_id=1, source_target_pairs={{0,1},{1,0},{2,3},{3,2},{4,5},{5,4},{6,7},{7,6},{8,9},{9,8},{10,11... | collective-permute-start | bytes 344072 | tf_op jit(solution)/shard_map/ppermute | solution.py:45
  17.5 18.2 %copy-start = (bf16[1,4,256,576]{2,3,1,0:T(8,128)(2,1)S(1)}, bf16[1,4,256,576]{2,3,1,0:T(8,128)(2,1)}, u32[]{:S(2)}) copy-start(bf16[1,4,256,576]{2,3,1,0:T(8,128)(2,1)} %param.10) | copy-start | bytes 3538948
  17.5 18.2 %copy-start.1 = (bf16[1,4,64,576]{3,2,1,0:T(8,128)(2,1)S(1)}, bf16[1,4,64,576]{3,2,1,0:T(8,128)(2,1)}, u32[]{:S(2)}) copy-start(bf16[1,4,64,576]{3,2,1,0:T(8,128)(2,1)} %param.9) | copy-start | bytes 884740
  17.5 18.2 %copy-start.4 = (s32[1,8]{1,0:T(1,128)S(1)}, s32[1,8]{1,0:T(1,128)}, u32[]{:S(2)}) copy-start(s32[1,8]{1,0:T(1,128)} %counts_ref.1) | copy-start | bytes 100
  17.6 18.2 %copy-start.5 = (s32[1,4]{1,0:T(1,128)S(1)}, s32[1,4]{1,0:T(1,128)}, u32[]{:S(2)}) copy-start(s32[1,4]{1,0:T(1,128)} %lengths_ref.1) | copy-start | bytes 52
  25.2 1.4 %collective-permute-start.5 = (bf16[8,7168]{1,0:T(8,128)(2,1)S(1)}, bf16[8,7168]{1,0:T(8,128)(2,1)S(1)}, u32[]{:S(2)}, u32[]{:S(2)}) collective-permute-start(bf16[8,7168]{1,0:T(8,128)(2,1)S(1)} %get-tuple-element.17), channel_id=1, source_target_pairs={{0,1},{1,0},{2,3},{3,2},{4,5},{5,4},{6,7},{7,6},{8,9},{9,8},{10,11... | collective-permute-start | bytes 344072 | tf_op jit(solution)/shard_map/ppermute | solution.py:45
  26.7 3.9 %collective-permute-start.7 = (bf16[2,7168]{1,0:T(2,128)(2,1)S(1)}, bf16[2,7168]{1,0:T(2,128)(2,1)S(1)}, u32[]{:S(2)}, u32[]{:S(2)}) collective-permute-start(bf16[2,7168]{1,0:T(2,128)(2,1)S(1)} %get-tuple-element.20), channel_id=1, source_target_pairs={{0,4},{2,6},{4,0},{6,2},{8,12},{10,14},{12,8},{14,10},{1,5},{3,7},... | collective-permute-start | bytes 86024 | tf_op jit(solution)/shard_map/ppermute | solution.py:45
  27.8 4.8 %collective-permute-start.8 = (bf16[2,7168]{1,0:T(2,128)(2,1)S(1)}, bf16[2,7168]{1,0:T(2,128)(2,1)S(1)}, u32[]{:S(2)}, u32[]{:S(2)}) collective-permute-start(bf16[2,7168]{1,0:T(2,128)(2,1)S(1)} %get-tuple-element.21), channel_id=1, source_target_pairs={{0,6},{2,4},{4,2},{6,0},{8,14},{10,12},{12,10},{14,8},{1,7},{3,5},... | collective-permute-start | bytes 86024 | tf_op jit(solution)/shard_map/ppermute | solution.py:45
  29.7 3.9 %collective-permute-start.6 = (bf16[2,7168]{1,0:T(2,128)(2,1)S(1)}, bf16[2,7168]{1,0:T(2,128)(2,1)S(1)}, u32[]{:S(2)}, u32[]{:S(2)}) collective-permute-start(bf16[2,7168]{1,0:T(2,128)(2,1)S(1)} %get-tuple-element.22.after_ref), channel_id=1, source_target_pairs={{0,2},{2,0},{4,6},{6,4},{8,10},{10,8},{12,14},{14,12},{1,3},{3,1},... | collective-permute-start | bytes 86024 | tf_op jit(solution)/shard_map/ppermute | solution.py:45
  33.7 4.8 %collective-permute-start.9 = (f32[1,7168]{1,0:T(1,128)S(1)}, f32[1,7168]{1,0:T(1,128)S(1)}, u32[]{:S(2)}, u32[]{:S(2)}) collective-permute-start(f32[1,7168]{1,0:T(1,128)S(1)} %slice.32), channel_id=1, source_target_pairs={{0,8},{2,10},{4,12},{6,14},{8,0},{10,2},{12,4},{14,6},{1,9},{3,11}... | collective-permute-start | bytes 86024 | tf_op jit(solution)/shard_map/ppermute | solution.py:45

commit v5 on v4

--- a/solution.py
+++ b/solution.py
@@ -52,21 +52,26 @@
 def row_copy(source, first, target, sems, i):
     step = target.shape[0] // sems.shape[0]
     here = pl.multiple_of(i * step, step)
-    return pltpu.make_async_copy(
-        source.at[pl.ds(first + here, step)], target.at[pl.ds(here, step)], sems.at[i]
-    )
-
-
-def start_rows(source, first, target, sems, pieces=None):
-    @pl.loop(*(pieces or (0, sems.shape[0])))
+    return pltpu.make_async_copy(source.at[pl.ds(first + here, step)], target.at[pl.ds(here, step)], sems.at[i])
+
+
+def column_copy(source, first, target, sems, i):
+    rows, width = target.shape
+    step = width // sems.shape[0]
+    here = pl.ds(pl.multiple_of(i * step, step), step)
+    return pltpu.make_async_copy(source.at[pl.ds(first, rows), here], target.at[:, here], sems.at[i])
+
+
+def start_pieces(piece, copy, first=0, count=None):
+    @pl.loop(first, first + (count or copy[-1].shape[0]))
     def _(i):
-        row_copy(source, first, target, sems, i).start()
-
-
-def wait_rows(source, first, target, sems):
-    @pl.loop(0, sems.shape[0])
+        piece(*copy, i).start()
+
+
+def wait_pieces(piece, copy):
+    @pl.loop(0, copy[-1].shape[0])
     def _(i):
-        row_copy(source, first, target, sems, i).wait()
+        piece(*copy, i).wait()
 
 
 def pieces_of(rows, most):
@@ -80,17 +85,19 @@
 
 
 def pick_matrix(counts, device, size, slots):
-    stages = gather_stages(size.bit_length() - 1)
+    bits = size.bit_length() - 1
     shape = (size, size // 2 * slots)
     slot = lax.broadcasted_iota(jnp.int32, shape, 1)
     every = lax.broadcasted_iota(jnp.int32, shape, 0)
-    owner = block_offset(slot // slots, stages) ^ device
+    owner = block_offset(slot // slots, gather_stages(bits)) ^ device
     known = jnp.broadcast_to(counts, (8, size)).astype(jnp.bfloat16)
     start = jnp.dot(known, (every < owner).astype(jnp.bfloat16), preferred_element_type=jnp.float32)[:1]
     count = jnp.dot(known, (every == owner).astype(jnp.bfloat16), preferred_element_type=jnp.float32)[:1]
     place = (slot % slots)[:1].astype(jnp.float32)
     request = jnp.where(place < count, start + place, -1.0)
-    return (request == every.astype(jnp.float32)).astype(jnp.bfloat16)
+    row = lax.broadcasted_iota(jnp.int32, (2 * size, shape[1]), 0)
+    wanted = row_offset(row % size, sum_stages(bits)) ^ device ^ (row // size)
+    return (request == wanted.astype(jnp.float32)).astype(jnp.bfloat16)
 
 
 def load_rows(jobs, share, after=None, counts=None, slots=0):
@@ -101,7 +108,7 @@
     scratch = [pltpu.SemaphoreType.DMA((count,)) for count in pieces]
     if counts is not None:
         operands.append(pinned(counts))
-        out_shape.append(jax.ShapeDtypeStruct((size, size // 2 * slots), jnp.bfloat16))
+        out_shape.append(jax.ShapeDtypeStruct((2 * size, size // 2 * slots), jnp.bfloat16))
         scratch += [pltpu.VMEM((1, size), jnp.int32), pltpu.SemaphoreType.DMA]
     if after is not None:
         operands.append(after)
@@ -117,12 +124,12 @@
             for (weight, first, _), source, target, sems in zip(jobs, sources, targets, refs)
         ]
         for copy in copies:
-            start_rows(*copy)
+            start_pieces(row_copy, copy)
         if counts is not None:
             small.wait()
             targets[-1][...] = pick_matrix(refs[-2][...], lax.axis_index("tp"), size, slots)
         for copy in copies:
-            wait_rows(*copy)
+            wait_pieces(row_copy, copy)
 
     return pl.pallas_call(
         body,
@@ -139,39 +146,40 @@
 
 
 def compact(pick, blocks):
-    size = pick.shape[0]
+    size = pick.shape[0] // 2
     width = blocks[0].shape[1]
     column = 1024
     count = len(blocks)
 
     def body(*refs):
-        pick_ref, block_refs, out_ref = refs[0], refs[1 : 1 + count], refs[1 + count]
+        pick_ref, block_refs, (own_ref, send_ref) = refs[0], refs[1 : 1 + count], refs[1 + count :]
         pick_now = pick_ref[...]
         for c in range(0, width, column):
             rows = [ref[:, c : c + column].astype(jnp.float32) for ref in block_refs]
             rows = rows[0] if count == 1 else jnp.concatenate(rows, axis=0)
             out = jnp.dot(pick_now, rows.astype(jnp.bfloat16), preferred_element_type=jnp.float32)
-            out_ref[:, c : c + column] = out.astype(jnp.bfloat16)
-
+            own_ref[:, c : c + column] = out[:size].astype(jnp.bfloat16)
+            send_ref[:, c : c + column] = out[size:].astype(jnp.bfloat16)
+
+    out = jax.ShapeDtypeStruct((size, width), jnp.bfloat16)
     return pl.pallas_call(
         body,
-        out_shape=jax.ShapeDtypeStruct((size, width), jnp.bfloat16),
+        out_shape=(out, out),
         in_specs=[VMEM] * (1 + count),
-        out_specs=VMEM,
+        out_specs=(VMEM, VMEM),
         compiler_params=pltpu.CompilerParams(vmem_limit_bytes=16 * MIB),
         name="compact",
     )(pick, *blocks)
 
 
-def feed_forward(gain, row_sets, loaded, late, w_down, share, split):
+def feed_forward(gain, row_sets, loaded, late, w_down, share):
     requests, width = row_sets[0].shape
     units = w_down.shape[0]
     set_count = len(row_sets)
     every = requests * set_count
-    stages = sum_stages(requests.bit_length() - 1)
-    column = 1024
     late_pieces = [pieces_of(rows, 4) for _, _, _, rows in late]
-    pieces = pieces_of(share, 4)
+    pieces = 4
+    column = width // pieces
     parts = [part for _, _, part in loaded]
 
     def body(*refs):
@@ -181,10 +189,9 @@
         late_hbm, refs = refs[: len(late)], refs[len(late) :]
         down_hbm, refs = refs[0], refs[1:]
         out_refs, refs = refs[:set_count], refs[set_count:]
-        rows_ref, normed_ref, down_ref, down_sems = refs[:4]
+        normed_ref, hidden_ref, down_ref, down_sems = refs[:4]
         projected_refs, refs = refs[4:6], refs[6:]
         late_refs, late_sems = refs[: len(late)], refs[len(late) :]
-        device = lax.axis_index("tp")
 
         start = share_start(units, share)
         late_copies = [
@@ -193,7 +200,7 @@
         ]
         down_copy = (down_hbm, start, down_ref, down_sems)
         for copy in late_copies:
-            start_rows(*copy)
+            start_pieces(row_copy, copy)
 
         def project(which, ref, at):
             rows = ref.shape[0]
@@ -203,39 +210,33 @@
                     ref[j : j + chunk, :], normed_ref[...], (((1,), (1,)), ((), ())), preferred_element_type=jnp.float32
                 )
 
-        place = lax.broadcasted_iota(jnp.int32, (every, every), 0)
-        source_row = lax.broadcasted_iota(jnp.int32, (every, every), 1)
-        wanted = (row_offset(place % requests, stages) ^ device) + place // requests * requests
-        order = (source_row == wanted).astype(jnp.bfloat16)
-        for c in range(0, width, column):
-            rows = [ref[:, c : c + column].astype(jnp.float32) for ref in set_refs]
-            rows = rows[0] if set_count == 1 else jnp.concatenate(rows, axis=0)
-            rows_ref[:, c : c + column] = jnp.dot(
-                order, rows.astype(jnp.bfloat16), preferred_element_type=jnp.float32
-            )
-        rows = rows_ref[...]
+        rows = [ref[...].astype(jnp.float32) for ref in set_refs]
+        rows = rows[0] if set_count == 1 else jnp.concatenate(rows, axis=0)
         inv_rms = lax.rsqrt(jnp.mean(rows * rows, axis=1, keepdims=True) + norm_eps)
         normed_ref[...] = (rows * inv_rms * gain_ref[...]).astype(jnp.bfloat16)
 
         for part, ((which, first, _), ref) in enumerate(zip(loaded, part_refs)):
             project(which, ref, first)
             if part == 0:
-                start_rows(*down_copy, pieces=(0, pieces // 2))
+                start_pieces(column_copy, down_copy, 0, pieces - 1)
         for copy in late_copies:
-            wait_rows(*copy)
-        start_rows(*down_copy, pieces=(pieces // 2, pieces))
+            wait_pieces(row_copy, copy)
+        start_pieces(column_copy, down_copy, pieces - 1, 1)
         for (which, _, first, _), ref in zip(late, late_refs):
             project(which, ref, first)
-        hidden = (jax.nn.silu(projected_refs[0][...]) * projected_refs[1][...]).T.astype(jnp.bfloat16)
-        wait_rows(*down_copy)
-        for c in range(0, width, column):
-            out = jnp.dot(hidden, down_ref[:, c : c + column], preferred_element_type=jnp.float32)
+        hidden_ref[...] = (jax.nn.silu(projected_refs[0][...]) * projected_refs[1][...]).T.astype(jnp.bfloat16)
+
+        @pl.loop(0, pieces)
+        def _(i):
+            column_copy(*down_copy, i).wait()
+            here = pl.ds(pl.multiple_of(i * column, column), column)
+            out = jnp.dot(hidden_ref[...], down_ref[:, here], preferred_element_type=jnp.float32)
             own = out[:requests]
             first = lax.broadcasted_iota(jnp.int32, own.shape, 0) == 0
-            own += jnp.where(first, rows_ref[:requests, c : c + column], 0.0)
-            out_refs[0][:, c : c + column] = own
+            own += jnp.where(first, set_refs[0][:, here].astype(jnp.float32), 0.0)
+            out_refs[0][:, here] = own
             if set_count == 2:
-                out_refs[1][:, c : c + column] = out[requests:].astype(jnp.bfloat16)
+                out_refs[1][:, here] = out[requests:].astype(jnp.bfloat16)
 
     outs = [
         jax.ShapeDtypeStruct((requests, width), jnp.float32),
@@ -247,8 +248,8 @@
         in_specs=[VMEM] * (1 + set_count + len(parts)) + [ANY] * (len(late) + 1),
         out_specs=[VMEM] * set_count,
         scratch_shapes=[
-            pltpu.VMEM((every, width), jnp.float32),
             pltpu.VMEM((every, width), jnp.bfloat16),
+            pltpu.VMEM((every, share), jnp.bfloat16),
             pltpu.VMEM((share, width), jnp.bfloat16),
             pltpu.SemaphoreType.DMA((pieces,)),
             *[pltpu.VMEM((share, every), jnp.float32)] * 2,
@@ -272,16 +273,22 @@
     def body(lengths_ref, counts_ref, queries_ref, cache_ref, after_ref, out_ref):
         live = counts_ref[0, lax.axis_index("tp")]
         spot = lax.broadcasted_iota(jnp.int32, (heads, positions), 1)
+        every = []
         for s in range(slots):
             scores = (
                 jnp.dot(queries_ref[s], cache_ref[s], preferred_element_type=jnp.float32)
                 * score_scale
             )
-            scores = jnp.where(spot < lengths_ref[0, s], scores, -jnp.inf)
-            weights = jnp.exp(scores - jnp.max(scores, axis=1, keepdims=True))
-            probs = (weights / jnp.sum(weights, axis=1, keepdims=True)).astype(jnp.bfloat16)
+            every.append(jnp.where(spot < lengths_ref[0, s], scores, -jnp.inf))
+        scores = jnp.concatenate(every, axis=0)
+        weights = jnp.exp(scores - jnp.max(scores, axis=1, keepdims=True))
+        probs = (weights / jnp.sum(weights, axis=1, keepdims=True)).astype(jnp.bfloat16)
+        for s in range(slots):
             context = lax.dot_general(
-                probs, cache_ref[s, :KVL, :], (((1,), (1,)), ((), ())), preferred_element_type=jnp.float32
+                probs[s * heads : (s + 1) * heads],
+                cache_ref[s, :KVL, :],
+                (((1,), (1,)), ((), ())),
+                preferred_element_type=jnp.float32,
             )
             out_ref[s] = jnp.where(s < live, context, 0.0).astype(jnp.bfloat16)
 
@@ -303,7 +310,7 @@
 def load_plan(share):
     if share % 192:
         return [(0, 0, share)], [(1, 0, share)], []
-    early = share // 9 * 5
+    early = share // 3 * 2
     return (
         [(0, 0, early)],
         [(0, early, share - early), (1, 0, 2 * early - share)],
@@ -336,16 +343,16 @@
             if low > 1:
                 block = jnp.concatenate(blocks, axis=0)
 
-        own = compact(pick, blocks)
-        arrived = swap(own, "tp", 1, size)
-        load(plan[1], after=own)
+        own, send = compact(pick, blocks)
+        arrived = swap(send, "tp", 1, size)
+        load(plan[1], after=send)
         *last, part = loaded[-1]
         arrived, part = lax.optimization_barrier((arrived, part))
         loaded[-1] = (*last, part)
         rows = own + arrived
         row_sets = [rows, swap(rows, "sub", 1, cores)] if split else [rows]
         late = [(which, weights[which], first, count) for which, first, count in plan[2]]
-        total, *other = feed_forward(norm_gain, row_sets, loaded, late, w_down, share, split)
+        total, *other = feed_forward(norm_gain, row_sets, loaded, late, w_down, share)
 
         if split:
             total = total + swap(other[0], "sub", 1, cores).astype(jnp.float32)

time: 39.3 us -> 38.3 us (0.975)
  Pallas kernels: 15.2 us -> 14.2 us
    pallas_call x1, Pallas kernels: 7.61 us -> 6.62 us  [feed_forward(): pl.pallas_call(body, out_shape=outs, in_specs=[VMEM] * (1 + set_count + l...]
    pallas_call x1, Pallas kernels: 2.71 us -> 2.1 us  [attend(): pl.pallas_call(body, out_shape=jax.ShapeDtypeStruct((slots, heads, KVL),...]
    pallas_call x2, Pallas kernels: 4.67 us -> 5.26 us  [load_rows(): pl.pallas_call(body, out_shape=out_shape, in_specs=[ANY] * len(operands),...]
where the time goes in v5:
time: 38.3 us; the launch traced here: 38.2 us
  Pallas kernels  14.2 us (37%)
  starting transfers between devices  13.2 us (34%)
  waiting for transfers between devices  9.13 us (24%)
  other arithmetic  0.75 us (2%)
  between operations  0.75 us (2%)
    ppermute x10, starting transfers between devices, swap(): return lax.ppermute(x, axis, [(i, i ^ distance) for i in range(size)])  13.2 us
    ppermute x10, waiting for transfers between devices, swap(): return lax.ppermute(x, axis, [(i, i ^ distance) for i in range(size)])  9.13 us
    pallas_call x1, Pallas kernels, feed_forward(): pl.pallas_call(body, out_shape=outs, in_specs=[VMEM] * (1 + set_count + l...  6.62 us
    pallas_call x2, Pallas kernels, load_rows(): pl.pallas_call(body, out_shape=out_shape, in_specs=[ANY] * len(operands),...  5.26 us
    pallas_call x1, Pallas kernels, attend(): pl.pallas_call(body, out_shape=jax.ShapeDtypeStruct((slots, heads, KVL),...  2.1 us
  transfers between devices with their start and end apart: 10, of which 8 were waited for; matrix products, arithmetic and copies ran while one was open for 0% of the time, Pallas kernels for 19%

profile of v5, /device:TPU:0, one launch (start us, length us, event | category | flops | bytes accessed | tf_op | source)
XLA Modules:
  0.0 38.2 jit_solution(13367242144035901772)
XLA Ops:
  0.6 0.0 copy-start.2
  0.6 5.1 %collective-permute-start.2 = (bf16[4,7168]{1,0:T(4,128)(2,1)}, bf16[4,7168]{1,0:T(4,128)(2,1)S(1)}, u32[]{:S(2)}, u32[]{:S(2)}) collective-permute-start(bf16[4,7168]{1,0:T(4,128)(2,1)} %bitcast.11), channel_id=1, source_target_pairs={{0,12},{2,14},{4,8},{6,10},{8,4},{10,6},{12,0},{14,2},{1,13},{3,15... | collective-permute-start | bytes 172040 | tf_op jit(solution)/shard_map/ppermute | solution.py:45
  5.8 0.0 collective-permute-start.1
  5.8 0.6 %collective-permute-start = (bf16[4,7168]{1,0:T(4,128)(2,1)}, bf16[4,7168]{1,0:T(4,128)(2,1)S(1)}, u32[]{:S(2)}, u32[]{:S(2)}) collective-permute-start(bf16[4,7168]{1,0:T(4,128)(2,1)} %bitcast.13), channel_id=1, source_target_pairs={{0,4},{2,6},{4,0},{6,2},{8,12},{10,14},{12,8},{14,10},{1,5},{3,7},... | collective-permute-start | bytes 172040 | tf_op jit(solution)/shard_map/ppermute | solution.py:45
  6.4 2.6 %load_rows.2 = (bf16[384,7168]{1,0:T(8,128)(2,1)S(1)}, bf16[16,16]{1,0:T(8,128)(2,1)S(1)}) custom-call(bf16[1152,7168]{1,0:T(8,128)(2,1)} %refs_0_.3, s32[1,8]{1,0:T(1,128)} %counts_ref.1), custom_call_target="tpu_custom_call" | custom-call | bytes 11010048 | tf_op jit(solution)/shard_map/load_rows/pallas_call | solution.py:134
  9.0 0.0 collective-permute-done.2.refs_4_
  9.1 2.0 %collective-permute-done.1.refs_3_ = bf16[4,7168]{1,0:T(4,128)(2,1)S(1)} collective-permute-done((bf16[4,7168]{1,0:T(4,128)(2,1)}, bf16[4,7168]{1,0:T(4,128)(2,1)S(1)}, u32[]{:S(2)}, u32[]{:S(2)}) %collective-permute-start.1) | collective-permute-done | bytes 57376 | tf_op jit(solution)/shard_map/ppermute | solution.py:45
  11.0 0.0 collective-permute-done.refs_2_
  11.0 0.0 copy-done.2
  11.0 0.2 compact.1
  11.2 0.0 copy-start.3
  11.3 1.6 %collective-permute-start.3 = (bf16[8,7168]{1,0:T(8,128)(2,1)S(1)}, bf16[8,7168]{1,0:T(8,128)(2,1)S(1)}, u32[]{:S(2)}, u32[]{:S(2)}) collective-permute-start(bf16[8,7168]{1,0:T(8,128)(2,1)S(1)} %get-tuple-element.14.refs_2_), channel_id=1, source_target_pairs={{0,2},{2,0},{4,6},{6,4},{8,10},{10,8},{12,14},{14,12},{1,3},{3,1},... | collective-permute-start | bytes 344072 | tf_op jit(solution)/shard_map/ppermute | solution.py:45
  12.8 2.6 %load_rows.3 = (bf16[192,7168]{1,0:T(8,128)(2,1)S(1)}, bf16[192,7168]{1,0:T(8,128)(2,1)S(1)}) custom-call(bf16[1152,7168]{1,0:T(8,128)(2,1)} %refs_0_.3, bf16[1152,7168]{1,0:T(8,128)(2,1)} %refs_6_.1, bf16[8,7168]{1,0:T(8,128)(2,1)S(1)} %get-tuple-element.14.refs_2_), custom_call_target="tpu_custom_call" | custom-call | bytes 11010048 | tf_op jit(solution)/shard_map/load_rows/pallas_call | solution.py:134
  15.5 0.6 %collective-permute-done.3 = bf16[8,7168]{1,0:T(8,128)(2,1)S(1)} collective-permute-done((bf16[8,7168]{1,0:T(8,128)(2,1)S(1)}, bf16[8,7168]{1,0:T(8,128)(2,1)S(1)}, u32[]{:S(2)}, u32[]{:S(2)}) %collective-permute-start.3) | collective-permute-done | bytes 114720 | tf_op jit(solution)/shard_map/ppermute | solution.py:45
  16.2 0.1 collective-permute-start.4
  16.2 1.3 %collective-permute-done.4.refs_2_ = bf16[8,7168]{1,0:T(8,128)(2,1)S(1)} collective-permute-done((bf16[8,7168]{1,0:T(8,128)(2,1)S(1)}, bf16[8,7168]{1,0:T(8,128)(2,1)S(1)}, u32[]{:S(2)}, u32[]{:S(2)}) %collective-permute-start.4) | collective-permute-done | bytes 114720 | tf_op jit(solution)/shard_map/ppermute | solution.py:45
  17.5 0.0 copy-done.3
  17.5 0.0 copy-start
  17.5 0.0 copy-start.1
  17.5 0.0 copy-start.4
  17.6 0.0 copy-start.5
  17.6 6.6 %feed_forward.1 = (f32[8,7168]{1,0:T(8,128)S(1)}, bf16[8,7168]{1,0:T(8,128)(2,1)S(1)}) custom-call(f32[1,7168]{1,0:T(1,128)S(1)} %bitcast.15, bf16[8,7168]{1,0:T(8,128)(2,1)S(1)} %add.18.refs_1_, bf16[8,7168]{1,0:T(8,128)(2,1)S(1)} %collective-permute-done.4.refs_2_, bf16[384,7168]{1,0:T(8,128)(2,1)S(1)} %get-tuple-element.17.refs_3_, ...), custom_call_target="tpu_custom_call" | custom-call | flops 396361728 | bytes 24772608 | tf_op jit(solution)/shard_map/feed_forward/pallas_call | solution.py:245
  24.2 0.2 collective-permute-start.5
  24.4 1.2 %collective-permute-done.5 = bf16[8,7168]{1,0:T(8,128)(2,1)S(1)} collective-permute-done((bf16[8,7168]{1,0:T(8,128)(2,1)S(1)}, bf16[8,7168]{1,0:T(8,128)(2,1)S(1)}, u32[]{:S(2)}, u32[]{:S(2)}) %collective-permute-start.5) | collective-permute-done | bytes 114720 | tf_op jit(solution)/shard_map/ppermute | solution.py:45
  25.6 0.1 fusion.5
  25.7 1.1 %collective-permute-start.7 = (bf16[2,7168]{1,0:T(2,128)(2,1)S(1)}, bf16[2,7168]{1,0:T(2,128)(2,1)S(1)}, u32[]{:S(2)}, u32[]{:S(2)}) collective-permute-start(bf16[2,7168]{1,0:T(2,128)(2,1)S(1)} %get-tuple-element.24), channel_id=1, source_target_pairs={{0,4},{2,6},{4,0},{6,2},{8,12},{10,14},{12,8},{14,10},{1,5},{3,7},... | collective-permute-start | bytes 86024 | tf_op jit(solution)/shard_map/ppermute | solution.py:45
  26.8 1.9 %collective-permute-start.8 = (bf16[2,7168]{1,0:T(2,128)(2,1)S(1)}, bf16[2,7168]{1,0:T(2,128)(2,1)S(1)}, u32[]{:S(2)}, u32[]{:S(2)}) collective-permute-start(bf16[2,7168]{1,0:T(2,128)(2,1)S(1)} %get-tuple-element.25), channel_id=1, source_target_pairs={{0,6},{2,4},{4,2},{6,0},{8,14},{10,12},{12,10},{14,8},{1,7},{3,5},... | collective-permute-start | bytes 86024 | tf_op jit(solution)/shard_map/ppermute | solution.py:45
  28.7 0.5 %collective-permute-start.6 = (bf16[2,7168]{1,0:T(2,128)(2,1)S(1)}, bf16[2,7168]{1,0:T(2,128)(2,1)S(1)}, u32[]{:S(2)}, u32[]{:S(2)}) collective-permute-start(bf16[2,7168]{1,0:T(2,128)(2,1)S(1)} %get-tuple-element.26.after_ref), channel_id=1, source_target_pairs={{0,2},{2,0},{4,6},{6,4},{8,10},{10,8},{12,14},{14,12},{1,3},{3,1},... | collective-permute-start | bytes 86024 | tf_op jit(solution)/shard_map/ppermute | solution.py:45
  29.3 0.4 collective-permute-done.7
  29.6 2.0 %collective-permute-done.8 = bf16[2,7168]{1,0:T(2,128)(2,1)S(1)} collective-permute-done((bf16[2,7168]{1,0:T(2,128)(2,1)S(1)}, bf16[2,7168]{1,0:T(2,128)(2,1)S(1)}, u32[]{:S(2)}, u32[]{:S(2)}) %collective-permute-start.8) | collective-permute-done | bytes 28704 | tf_op jit(solution)/shard_map/ppermute | solution.py:45
  31.6 1.0 %collective-permute-done.6 = bf16[2,7168]{1,0:T(2,128)(2,1)S(1)} collective-permute-done((bf16[2,7168]{1,0:T(2,128)(2,1)S(1)}, bf16[2,7168]{1,0:T(2,128)(2,1)S(1)}, u32[]{:S(2)}, u32[]{:S(2)}) %collective-permute-start.6) | collective-permute-done | bytes 28704 | tf_op jit(solution)/shard_map/ppermute | solution.py:45
  32.6 0.1 fusion.1
  32.7 2.1 %collective-permute-start.9 = (f32[1,7168]{1,0:T(1,128)S(1)}, f32[1,7168]{1,0:T(1,128)S(1)}, u32[]{:S(2)}, u32[]{:S(2)}) collective-permute-start(f32[1,7168]{1,0:T(1,128)S(1)} %slice.32), channel_id=1, source_target_pairs={{0,8},{2,10},{4,12},{6,14},{8,0},{10,2},{12,4},{14,6},{1,9},{3,11}... | collective-permute-start | bytes 86024 | tf_op jit(solution)/shard_map/ppermute | solution.py:45
  34.8 0.0 copy-done
  34.8 0.0 copy-done.1
  34.8 0.0 copy-done.4
  34.8 0.0 copy-done.5
  34.8 2.1 %attend.1 = bf16[4,64,512]{2,1,0:T(8,128)(2,1)} custom-call(s32[1,4]{1,0:T(1,128)S(1)} %copy-done.5, s32[1,8]{1,0:T(1,128)S(1)} %copy-done.4, bf16[4,64,576]{2,1,0:T(8,128)(2,1)S(1)} %bitcast.10, bf16[4,576,256]{2,1,0:T(8,128)(2,1)S(1)} %bitcast.9, bf16[2,7168]{1,0:T(2,128)(2,1)S(1)} %get-tuple-element.26.after_ref), custom_call_target="tpu_custom_call" | custom-call | flops 134217728 | bytes 1474560 | tf_op jit(solution)/shard_map/attend/pallas_call | solution.py:295
  36.9 0.7 %collective-permute-done.9 = f32[1,7168]{1,0:T(1,128)S(1)} collective-permute-done((f32[1,7168]{1,0:T(1,128)S(1)}, f32[1,7168]{1,0:T(1,128)S(1)}, u32[]{:S(2)}, u32[]{:S(2)}) %collective-permute-start.9) | collective-permute-done | bytes 28704 | tf_op jit(solution)/shard_map/ppermute | solution.py:45
  37.5 0.6 %fusion.3 = bf16[1,1,7168]{2,1,0:T(2,128)(2,1)} fusion(f32[1,7168]{1,0:T(1,128)S(1)} %collective-permute-done.9, f32[2,7168]{1,0:T(2,128)S(1)} %fusion.1), kind=kLoop, calls=%fused_computation.6 | loop fusion | flops 14336 | bytes 71680 | tf_op jit(solution)/shard_map/broadcast_in_dim | solution.py:370
  (3 shorter events, 0.1 us)
Async XLA Ops:
  0.6 10.4 %copy-start.2 = (bf16[1,4,7168]{2,1,0:T(4,128)(2,1)S(1)}, bf16[1,4,7168]{2,1,0:T(4,128)(2,1)}, u32[]{:S(2)}) copy-start(bf16[1,4,7168]{2,1,0:T(4,128)(2,1)} %param.13) | copy-start | bytes 172036
  0.6 8.4 %collective-permute-start.2 = (bf16[4,7168]{1,0:T(4,128)(2,1)}, bf16[4,7168]{1,0:T(4,128)(2,1)S(1)}, u32[]{:S(2)}, u32[]{:S(2)}) collective-permute-start(bf16[4,7168]{1,0:T(4,128)(2,1)} %bitcast.11), channel_id=1, source_target_pairs={{0,12},{2,14},{4,8},{6,10},{8,4},{10,6},{12,0},{14,2},{1,13},{3,15... | collective-permute-start | bytes 172040 | tf_op jit(solution)/shard_map/ppermute | solution.py:45
  5.8 5.3 %collective-permute-start.1 = (bf16[4,7168]{1,0:T(4,128)(2,1)}, bf16[4,7168]{1,0:T(4,128)(2,1)S(1)}, u32[]{:S(2)}, u32[]{:S(2)}) collective-permute-start(bf16[4,7168]{1,0:T(4,128)(2,1)} %bitcast.12), channel_id=1, source_target_pairs={{0,8},{2,10},{4,12},{6,14},{8,0},{10,2},{12,4},{14,6},{1,9},{3,11}... | collective-permute-start | bytes 172040 | tf_op jit(solution)/shard_map/ppermute | solution.py:45
  5.8 5.3 %collective-permute-start = (bf16[4,7168]{1,0:T(4,128)(2,1)}, bf16[4,7168]{1,0:T(4,128)(2,1)S(1)}, u32[]{:S(2)}, u32[]{:S(2)}) collective-permute-start(bf16[4,7168]{1,0:T(4,128)(2,1)} %bitcast.13), channel_id=1, source_target_pairs={{0,4},{2,6},{4,0},{6,2},{8,12},{10,14},{12,8},{14,10},{1,5},{3,7},... | collective-permute-start | bytes 172040 | tf_op jit(solution)/shard_map/ppermute | solution.py:45
  11.2 6.3 %copy-start.3 = (f32[7168]{0:T(1024)S(1)}, f32[7168]{0:T(1024)}, u32[]{:S(2)}) copy-start(f32[7168]{0:T(1024)} %param.14) | copy-start | bytes 86020
  11.3 4.9 %collective-permute-start.3 = (bf16[8,7168]{1,0:T(8,128)(2,1)S(1)}, bf16[8,7168]{1,0:T(8,128)(2,1)S(1)}, u32[]{:S(2)}, u32[]{:S(2)}) collective-permute-start(bf16[8,7168]{1,0:T(8,128)(2,1)S(1)} %get-tuple-element.14.refs_2_), channel_id=1, source_target_pairs={{0,2},{2,0},{4,6},{6,4},{8,10},{10,8},{12,14},{14,12},{1,3},{3,1},... | collective-permute-start | bytes 344072 | tf_op jit(solution)/shard_map/ppermute | solution.py:45
  16.2 1.4 %collective-permute-start.4 = (bf16[8,7168]{1,0:T(8,128)(2,1)S(1)}, bf16[8,7168]{1,0:T(8,128)(2,1)S(1)}, u32[]{:S(2)}, u32[]{:S(2)}) collective-permute-start(bf16[8,7168]{1,0:T(8,128)(2,1)S(1)} %add.18.refs_1_), channel_id=1, source_target_pairs={{0,1},{1,0},{2,3},{3,2},{4,5},{5,4},{6,7},{7,6},{8,9},{9,8},{10,11... | collective-permute-start | bytes 344072 | tf_op jit(solution)/shard_map/ppermute | solution.py:45
  17.5 17.2 %copy-start = (bf16[1,4,256,576]{2,3,1,0:T(8,128)(2,1)S(1)}, bf16[1,4,256,576]{2,3,1,0:T(8,128)(2,1)}, u32[]{:S(2)}) copy-start(bf16[1,4,256,576]{2,3,1,0:T(8,128)(2,1)} %param.10) | copy-start | bytes 3538948
  17.5 17.2 %copy-start.1 = (bf16[1,4,64,576]{3,2,1,0:T(8,128)(2,1)S(1)}, bf16[1,4,64,576]{3,2,1,0:T(8,128)(2,1)}, u32[]{:S(2)}) copy-start(bf16[1,4,64,576]{3,2,1,0:T(8,128)(2,1)} %param.9) | copy-start | bytes 884740
  17.5 17.2 %copy-start.4 = (s32[1,8]{1,0:T(1,128)S(1)}, s32[1,8]{1,0:T(1,128)}, u32[]{:S(2)}) copy-start(s32[1,8]{1,0:T(1,128)} %counts_ref.1) | copy-start | bytes 100
  17.6 17.2 %copy-start.5 = (s32[1,4]{1,0:T(1,128)S(1)}, s32[1,4]{1,0:T(1,128)}, u32[]{:S(2)}) copy-start(s32[1,4]{1,0:T(1,128)} %lengths_ref.1) | copy-start | bytes 52
  24.2 1.4 %collective-permute-start.5 = (bf16[8,7168]{1,0:T(8,128)(2,1)S(1)}, bf16[8,7168]{1,0:T(8,128)(2,1)S(1)}, u32[]{:S(2)}, u32[]{:S(2)}) collective-permute-start(bf16[8,7168]{1,0:T(8,128)(2,1)S(1)} %get-tuple-element.21), channel_id=1, source_target_pairs={{0,1},{1,0},{2,3},{3,2},{4,5},{5,4},{6,7},{7,6},{8,9},{9,8},{10,11... | collective-permute-start | bytes 344072 | tf_op jit(solution)/shard_map/ppermute | solution.py:45
  25.7 3.9 %collective-permute-start.7 = (bf16[2,7168]{1,0:T(2,128)(2,1)S(1)}, bf16[2,7168]{1,0:T(2,128)(2,1)S(1)}, u32[]{:S(2)}, u32[]{:S(2)}) collective-permute-start(bf16[2,7168]{1,0:T(2,128)(2,1)S(1)} %get-tuple-element.24), channel_id=1, source_target_pairs={{0,4},{2,6},{4,0},{6,2},{8,12},{10,14},{12,8},{14,10},{1,5},{3,7},... | collective-permute-start | bytes 86024 | tf_op jit(solution)/shard_map/ppermute | solution.py:45
  26.8 4.8 %collective-permute-start.8 = (bf16[2,7168]{1,0:T(2,128)(2,1)S(1)}, bf16[2,7168]{1,0:T(2,128)(2,1)S(1)}, u32[]{:S(2)}, u32[]{:S(2)}) collective-permute-start(bf16[2,7168]{1,0:T(2,128)(2,1)S(1)} %get-tuple-element.25), channel_id=1, source_target_pairs={{0,6},{2,4},{4,2},{6,0},{8,14},{10,12},{12,10},{14,8},{1,7},{3,5},... | collective-permute-start | bytes 86024 | tf_op jit(solution)/shard_map/ppermute | solution.py:45
  28.7 3.9 %collective-permute-start.6 = (bf16[2,7168]{1,0:T(2,128)(2,1)S(1)}, bf16[2,7168]{1,0:T(2,128)(2,1)S(1)}, u32[]{:S(2)}, u32[]{:S(2)}) collective-permute-start(bf16[2,7168]{1,0:T(2,128)(2,1)S(1)} %get-tuple-element.26.after_ref), channel_id=1, source_target_pairs={{0,2},{2,0},{4,6},{6,4},{8,10},{10,8},{12,14},{14,12},{1,3},{3,1},... | collective-permute-start | bytes 86024 | tf_op jit(solution)/shard_map/ppermute | solution.py:45
  32.7 4.8 %collective-permute-start.9 = (f32[1,7168]{1,0:T(1,128)S(1)}, f32[1,7168]{1,0:T(1,128)S(1)}, u32[]{:S(2)}, u32[]{:S(2)}) collective-permute-start(f32[1,7168]{1,0:T(1,128)S(1)} %slice.32), channel_id=1, source_target_pairs={{0,8},{2,10},{4,12},{6,14},{8,0},{10,2},{12,4},{14,6},{1,9},{3,11}... | collective-permute-start | bytes 86024 | tf_op jit(solution)/shard_map/ppermute | solution.py:45

commit v6 on v5

--- a/solution.py
+++ b/solution.py
@@ -29,20 +29,36 @@
     return [(low, min(2, bits - low)) for low in range(0, bits, 2)]
 
 
+def direct_offset(place, core):
+    return ((-place) & 3) | (core * 4)
+
+
 def block_offset(position, stages):
     out = position * 0
     for low, width in stages:
+        out = out | ((-position & ((1 << width) - 1)) << low)
+        position = position >> width
+    return out
+
+
+def row_offset(position, stages):
+    out = position * 0
+    for low, width in stages[::-1]:
         out = out | ((position & ((1 << width) - 1)) << low)
         position = position >> width
     return out
 
 
-def row_offset(position, stages):
-    return block_offset(position, stages[::-1])
-
-
 def swap(x, axis, distance, size):
     return lax.ppermute(x, axis, [(i, i ^ distance) for i in range(size)])
+
+
+def direct_swap(x, place, size):
+    pairs = []
+    for core in range(2):
+        distance = direct_offset(place, core) or 2
+        pairs += [(2 * i + core, 2 * (i ^ distance) + core) for i in range(size)]
+    return lax.ppermute(x, ("tp", "sub"), pairs)
 
 
 def pinned(weight):
@@ -84,7 +100,7 @@
     return pl.multiple_of(lax.axis_index("sub") * share, 16)
 
 
-def pick_matrix(counts, device, size, slots):
+def pick_matrix(counts, device, size, slots, stages):
     bits = size.bit_length() - 1
     shape = (size, size // 2 * slots)
     slot = lax.broadcasted_iota(jnp.int32, shape, 1)
@@ -96,11 +112,11 @@
     place = (slot % slots)[:1].astype(jnp.float32)
     request = jnp.where(place < count, start + place, -1.0)
     row = lax.broadcasted_iota(jnp.int32, (2 * size, shape[1]), 0)
-    wanted = row_offset(row % size, sum_stages(bits)) ^ device ^ (row // size)
+    wanted = row_offset(row % size, stages) ^ device ^ (row // size)
     return (request == wanted.astype(jnp.float32)).astype(jnp.bfloat16)
 
 
-def load_rows(jobs, share, after=None, counts=None, slots=0):
+def load_rows(jobs, share, after=None, counts=None, slots=0, stages=()):
     pieces = [pieces_of(rows, 4) for _, _, rows in jobs]
     size = 0 if counts is None else counts.shape[1]
     operands = [pinned(weight) for weight, _, _ in jobs]
@@ -127,7 +143,7 @@
             start_pieces(row_copy, copy)
         if counts is not None:
             small.wait()
-            targets[-1][...] = pick_matrix(refs[-2][...], lax.axis_index("tp"), size, slots)
+            targets[-1][...] = pick_matrix(refs[-2][...], lax.axis_index("tp"), size, slots, stages)
         for copy in copies:
             wait_pieces(row_copy, copy)
 
@@ -224,17 +240,24 @@
         start_pieces(column_copy, down_copy, pieces - 1, 1)
         for (which, _, first, _), ref in zip(late, late_refs):
             project(which, ref, first)
-        hidden_ref[...] = (jax.nn.silu(projected_refs[0][...]) * projected_refs[1][...]).T.astype(jnp.bfloat16)
+        hidden = (jax.nn.silu(projected_refs[0][...]) * projected_refs[1][...]).astype(jnp.bfloat16)
+        place = lax.broadcasted_iota(jnp.int32, (every, every), 0)
+        if set_count == 2:
+            core = lax.axis_index("sub")
+            other = place // requests
+            distance = direct_offset(place % requests // 2, core ^ other)
+            place = distance + ((place % 2) ^ other) * requests
+        order = (lax.broadcasted_iota(jnp.int32, (every, every), 1) == place).astype(jnp.bfloat16)
+        hidden_ref[...] = lax.dot_general(
+            order, hidden, (((1,), (1,)), ((), ())), preferred_element_type=jnp.float32
+        ).astype(jnp.bfloat16)
 
         @pl.loop(0, pieces)
         def _(i):
             column_copy(*down_copy, i).wait()
             here = pl.ds(pl.multiple_of(i * column, column), column)
             out = jnp.dot(hidden_ref[...], down_ref[:, here], preferred_element_type=jnp.float32)
-            own = out[:requests]
-            first = lax.broadcasted_iota(jnp.int32, own.shape, 0) == 0
-            own += jnp.where(first, set_refs[0][:, here].astype(jnp.float32), 0.0)
-            out_refs[0][:, here] = own
+            out_refs[0][:, here] = out[:requests]
             if set_count == 2:
                 out_refs[1][:, here] = out[requests:].astype(jnp.bfloat16)
 
@@ -324,9 +347,10 @@
     def shards(queries, kv_cache, cache_lengths, live_counts, stream, norm_gain, w_gate, w_up, w_down):
         slots = queries.shape[1]
         units = w_gate.shape[0]
-        split = cores == 2 and units % 32 == 0
+        split = cores == 2 and size == 8 and units % 32 == 0
         share = units // 2 if split else units
         weights = (w_gate, w_up)
+        stages = [(0, bits)] if split else sum_stages(bits)
         plan = load_plan(share)
         loaded = []
 
@@ -337,9 +361,9 @@
 
         block = stream[0]
         for step, (low, width) in enumerate(gather_stages(bits)):
-            blocks = [block] + [swap(block, "tp", digit << low, size) for digit in range(1, 1 << width)]
+            blocks = [block] + [swap(block, "tp", digit << low, size) for digit in range((1 << width) - 1, 0, -1)]
             if step == 0:
-                pick = load(plan[0], counts=live_counts, slots=slots)[-1]
+                pick = load(plan[0], counts=live_counts, slots=slots, stages=stages)[-1]
             if low > 1:
                 block = jnp.concatenate(blocks, axis=0)
 
@@ -354,20 +378,27 @@
         late = [(which, weights[which], first, count) for which, first, count in plan[2]]
         total, *other = feed_forward(norm_gain, row_sets, loaded, late, w_down, share)
 
+        after = other[0] if split else total
+        latent_ctx = attend(queries[0], jnp.swapaxes(kv_cache[0], 1, 2), cache_lengths, live_counts, after)[None]
+        own_row = rows[:1].astype(jnp.float32)
         if split:
             total = total + swap(other[0], "sub", 1, cores).astype(jnp.float32)
-        for step, (low, width) in enumerate(sum_stages(bits)):
-            part = total.shape[0] >> width
-            sends = [total[digit * part : (digit + 1) * part] for digit in range(1, 1 << width)]
-            total = total[:part]
-            if step == 0:
-                sends = [send.astype(jnp.bfloat16) for send in sends]
-                latent_ctx = attend(
-                    queries[0], jnp.swapaxes(kv_cache[0], 1, 2), cache_lengths, live_counts, sends[0]
-                )[None]
-            for digit, send in enumerate(sends, 1):
-                total = total + swap(send, "tp", digit << low, size).astype(jnp.float32)
-        return (latent_ctx, total.astype(jnp.bfloat16)[None])
+            places = [total[2 * place : 2 * place + 2] for place in range(4)]
+            sums = [
+                direct_swap(places[place].astype(jnp.bfloat16), place, size).astype(jnp.float32)
+                for place in (1, 2, 3, 0)
+            ]
+            total = jnp.where(lax.axis_index("sub") == 0, places[0], sums[3]) + sums[0] + sums[2] + sums[1]
+            total, latent_ctx = lax.optimization_barrier((total, latent_ctx))
+            total = total[:1] + swap(total[1:], "sub", 1, cores)
+        else:
+            for step, (low, width) in enumerate(stages):
+                part = total.shape[0] >> width
+                sends = [total[digit * part : (digit + 1) * part] for digit in range(1, 1 << width)]
+                total = total[:part]
+                for digit, send in enumerate(sends, 1):
+                    total = total + swap(send, "tp", digit << low, size)
+        return (latent_ctx, (total + own_row).astype(jnp.bfloat16)[None])
 
     return shards
 

time: 38.3 us -> 36.7 us (0.958)
  waiting for transfers between devices: 9.13 us -> 6.73 us
  starting transfers between devices: 13.2 us -> 13.7 us
    ppermute x0 -> x4, starting transfers between devices: none -> 4.69 us  [direct_swap(): return lax.ppermute(x, ('tp', 'sub'), pairs)]
    ppermute x10 -> x7, starting transfers between devices: 13.2 us -> 9.05 us  [swap(): return lax.ppermute(x, axis, [(i, i ^ distance) for i in range(size)])]
    ppermute x10 -> x7, waiting for transfers between devices: 9.13 us -> 5.99 us  [swap(): return lax.ppermute(x, axis, [(i, i ^ distance) for i in range(size)])]
    ppermute x0 -> x4, waiting for transfers between devices: none -> 0.74 us  [direct_swap(): return lax.ppermute(x, ('tp', 'sub'), pairs)]
  transfers between devices with their start and end apart: 10 -> 11, of which waited for: 8 -> 6; matrix products, arithmetic and copies ran while one was open for 0% -> 0% of each run, Pallas kernels for 19% -> 20%
where the time goes in v6:
time: 36.7 us; the launch traced here: 36.6 us
  Pallas kernels  14.4 us (39%)
  starting transfers between devices  13.7 us (37%)
  waiting for transfers between devices  6.73 us (18%)
  other arithmetic  0.77 us (2%)
  between operations  0.75 us (2%)
    ppermute x7, starting transfers between devices, swap(): return lax.ppermute(x, axis, [(i, i ^ distance) for i in range(size)])  9.05 us
    pallas_call x1, Pallas kernels, feed_forward(): pl.pallas_call(body, out_shape=outs, in_specs=[VMEM] * (1 + set_count + l...  6.89 us
    ppermute x7, waiting for transfers between devices, swap(): return lax.ppermute(x, axis, [(i, i ^ distance) for i in range(size)])  5.99 us
    pallas_call x2, Pallas kernels, load_rows(): pl.pallas_call(body, out_shape=out_shape, in_specs=[ANY] * len(operands),...  5.26 us
    ppermute x4, starting transfers between devices, direct_swap(): return lax.ppermute(x, ('tp', 'sub'), pairs)  4.69 us
    pallas_call x1, Pallas kernels, attend(): pl.pallas_call(body, out_shape=jax.ShapeDtypeStruct((slots, heads, KVL),...  2.1 us
    ppermute x4, waiting for transfers between devices, direct_swap(): return lax.ppermute(x, ('tp', 'sub'), pairs)  0.74 us
  transfers between devices with their start and end apart: 11, of which 6 were waited for; matrix products, arithmetic and copies ran while one was open for 0% of the time, Pallas kernels for 20%

profile of v6, /device:TPU:0, one launch (start us, length us, event | category | flops | bytes accessed | tf_op | source)
XLA Modules:
  0.0 36.6 jit_solution(8249749171792747535)
XLA Ops:
  0.6 0.0 copy-start.2
  0.6 5.1 %collective-permute-start = (bf16[4,7168]{1,0:T(4,128)(2,1)}, bf16[4,7168]{1,0:T(4,128)(2,1)S(1)}, u32[]{:S(2)}, u32[]{:S(2)}) collective-permute-start(bf16[4,7168]{1,0:T(4,128)(2,1)} %bitcast.11), channel_id=1, source_target_pairs={{0,12},{2,14},{4,8},{6,10},{8,4},{10,6},{12,0},{14,2},{1,13},{3,15... | collective-permute-start | bytes 172040 | tf_op jit(solution)/shard_map/ppermute | solution.py:53
  5.8 0.0 collective-permute-start.1
  5.8 0.6 %collective-permute-start.2 = (bf16[4,7168]{1,0:T(4,128)(2,1)}, bf16[4,7168]{1,0:T(4,128)(2,1)S(1)}, u32[]{:S(2)}, u32[]{:S(2)}) collective-permute-start(bf16[4,7168]{1,0:T(4,128)(2,1)} %bitcast.13), channel_id=1, source_target_pairs={{0,4},{2,6},{4,0},{6,2},{8,12},{10,14},{12,8},{14,10},{1,5},{3,7},... | collective-permute-start | bytes 172040 | tf_op jit(solution)/shard_map/ppermute | solution.py:53
  6.4 2.6 %load_rows.2 = (bf16[384,7168]{1,0:T(8,128)(2,1)S(1)}, bf16[16,16]{1,0:T(8,128)(2,1)S(1)}) custom-call(bf16[1152,7168]{1,0:T(8,128)(2,1)} %refs_0_.3, s32[1,8]{1,0:T(1,128)} %counts_ref.1), custom_call_target="tpu_custom_call" | custom-call | bytes 11010048 | tf_op jit(solution)/shard_map/load_rows/pallas_call | solution.py:150
  9.0 0.0 collective-permute-done.refs_2_
  9.1 2.0 %collective-permute-done.1.refs_3_ = bf16[4,7168]{1,0:T(4,128)(2,1)S(1)} collective-permute-done((bf16[4,7168]{1,0:T(4,128)(2,1)}, bf16[4,7168]{1,0:T(4,128)(2,1)S(1)}, u32[]{:S(2)}, u32[]{:S(2)}) %collective-permute-start.1) | collective-permute-done | bytes 57376 | tf_op jit(solution)/shard_map/ppermute | solution.py:53
  11.0 0.0 collective-permute-done.2.refs_4_
  11.0 0.0 copy-done.2
  11.0 0.2 compact.1
  11.2 0.0 copy-start.3
  11.3 1.6 %collective-permute-start.3 = (bf16[8,7168]{1,0:T(8,128)(2,1)S(1)}, bf16[8,7168]{1,0:T(8,128)(2,1)S(1)}, u32[]{:S(2)}, u32[]{:S(2)}) collective-permute-start(bf16[8,7168]{1,0:T(8,128)(2,1)S(1)} %get-tuple-element.16.refs_2_), channel_id=1, source_target_pairs={{0,2},{2,0},{4,6},{6,4},{8,10},{10,8},{12,14},{14,12},{1,3},{3,1},... | collective-permute-start | bytes 344072 | tf_op jit(solution)/shard_map/ppermute | solution.py:53
  12.8 2.6 %load_rows.3 = (bf16[192,7168]{1,0:T(8,128)(2,1)S(1)}, bf16[192,7168]{1,0:T(8,128)(2,1)S(1)}) custom-call(bf16[1152,7168]{1,0:T(8,128)(2,1)} %refs_0_.3, bf16[1152,7168]{1,0:T(8,128)(2,1)} %refs_6_.1, bf16[8,7168]{1,0:T(8,128)(2,1)S(1)} %get-tuple-element.16.refs_2_), custom_call_target="tpu_custom_call" | custom-call | bytes 11010048 | tf_op jit(solution)/shard_map/load_rows/pallas_call | solution.py:150
  15.5 0.6 %collective-permute-done.3 = bf16[8,7168]{1,0:T(8,128)(2,1)S(1)} collective-permute-done((bf16[8,7168]{1,0:T(8,128)(2,1)S(1)}, bf16[8,7168]{1,0:T(8,128)(2,1)S(1)}, u32[]{:S(2)}, u32[]{:S(2)}) %collective-permute-start.3) | collective-permute-done | bytes 114720 | tf_op jit(solution)/shard_map/ppermute | solution.py:53
  16.2 0.1 collective-permute-start.4
  16.2 1.3 %collective-permute-done.4.refs_2_ = bf16[8,7168]{1,0:T(8,128)(2,1)S(1)} collective-permute-done((bf16[8,7168]{1,0:T(8,128)(2,1)S(1)}, bf16[8,7168]{1,0:T(8,128)(2,1)S(1)}, u32[]{:S(2)}, u32[]{:S(2)}) %collective-permute-start.4) | collective-permute-done | bytes 114720 | tf_op jit(solution)/shard_map/ppermute | solution.py:53
  17.5 0.0 copy-done.3
  17.5 0.0 copy-start
  17.5 0.0 copy-start.1
  17.5 0.0 copy-start.4
  17.6 0.0 copy-start.5
  17.6 6.9 %feed_forward.1 = (f32[8,7168]{1,0:T(8,128)S(1)}, bf16[8,7168]{1,0:T(8,128)(2,1)S(1)}) custom-call(f32[1,7168]{1,0:T(1,128)S(1)} %bitcast.15, bf16[8,7168]{1,0:T(8,128)(2,1)S(1)} %add.21.refs_1_, bf16[8,7168]{1,0:T(8,128)(2,1)S(1)} %collective-permute-done.4.refs_2_, bf16[384,7168]{1,0:T(8,128)(2,1)S(1)} %get-tuple-element.19.refs_3_, ...), custom_call_target="tpu_custom_call" | custom-call | flops 396361728 | bytes 24772608 | tf_op jit(solution)/shard_map/feed_forward/pallas_call | solution.py:268
  24.5 0.2 collective-permute-start.5
  24.7 1.2 %collective-permute-done.5 = bf16[8,7168]{1,0:T(8,128)(2,1)S(1)} collective-permute-done((bf16[8,7168]{1,0:T(8,128)(2,1)S(1)}, bf16[8,7168]{1,0:T(8,128)(2,1)S(1)}, u32[]{:S(2)}, u32[]{:S(2)}) %collective-permute-start.5) | collective-permute-done | bytes 114720 | tf_op jit(solution)/shard_map/ppermute | solution.py:53
  25.9 0.1 fusion.4
  26.0 2.1 %collective-permute-start.7 = (bf16[2,7168]{1,0:T(2,128)(2,1)S(1)}, bf16[2,7168]{1,0:T(2,128)(2,1)S(1)}, u32[]{:S(2)}, u32[]{:S(2)}) collective-permute-start(bf16[2,7168]{1,0:T(2,128)(2,1)S(1)} %get-tuple-element.28), channel_id=1, source_target_pairs={{0,6},{2,4},{4,2},{6,0},{8,14},{10,12},{12,10},{14,8},{1,15},{3,13... | collective-permute-start | bytes 86024 | tf_op jit(solution)/shard_map/ppermute | solution.py:61
  28.0 0.5 %collective-permute-start.8 = (bf16[2,7168]{1,0:T(2,128)(2,1)S(1)}, bf16[2,7168]{1,0:T(2,128)(2,1)S(1)}, u32[]{:S(2)}, u32[]{:S(2)}) collective-permute-start(bf16[2,7168]{1,0:T(2,128)(2,1)S(1)} %get-tuple-element.30), channel_id=1, source_target_pairs={{0,2},{2,0},{4,6},{6,4},{8,10},{10,8},{12,14},{14,12},{1,11},{3,9}... | collective-permute-start | bytes 86024 | tf_op jit(solution)/shard_map/ppermute | solution.py:61
  28.6 1.0 %collective-permute-start.9 = (bf16[2,7168]{1,0:T(2,128)(2,1)S(1)}, bf16[2,7168]{1,0:T(2,128)(2,1)S(1)}, u32[]{:S(2)}, u32[]{:S(2)}) collective-permute-start(bf16[2,7168]{1,0:T(2,128)(2,1)S(1)} %get-tuple-element.29), channel_id=1, source_target_pairs={{0,4},{2,6},{4,0},{6,2},{8,12},{10,14},{12,8},{14,10},{1,13},{3,15... | collective-permute-start | bytes 86024 | tf_op jit(solution)/shard_map/ppermute | solution.py:61
  29.5 1.1 %collective-permute-start.6 = (bf16[2,7168]{1,0:T(2,128)(2,1)S(1)}, bf16[2,7168]{1,0:T(2,128)(2,1)S(1)}, u32[]{:S(2)}, u32[]{:S(2)}) collective-permute-start(bf16[2,7168]{1,0:T(2,128)(2,1)S(1)} %slice.46), channel_id=1, source_target_pairs={{0,4},{2,6},{4,0},{6,2},{8,12},{10,14},{12,8},{14,10},{1,9},{3,11}... | collective-permute-start | bytes 86024 | tf_op jit(solution)/shard_map/ppermute | solution.py:61
  30.7 0.0 copy-done
  30.7 0.0 copy-done.1
  30.7 0.0 copy-done.4
  30.7 0.0 copy-done.5
  30.7 2.1 %attend.1 = bf16[4,64,512]{2,1,0:T(8,128)(2,1)} custom-call(s32[1,4]{1,0:T(1,128)S(1)} %copy-done.5, s32[1,8]{1,0:T(1,128)S(1)} %copy-done.4, bf16[4,64,576]{2,1,0:T(8,128)(2,1)S(1)} %bitcast.10, bf16[4,576,256]{2,1,0:T(8,128)(2,1)S(1)} %bitcast.9, bf16[8,7168]{1,0:T(8,128)(2,1)S(1)} %get-tuple-element.23.after_ref), custom_call_target="tpu_custom_call" | custom-call | flops 134217728 | bytes 1474560 | tf_op jit(solution)/shard_map/attend/pallas_call | solution.py:318
  32.8 0.0 collective-permute-done.7
  32.8 0.0 collective-permute-done.8
  32.8 0.0 collective-permute-done.9
  32.8 0.7 %collective-permute-done.6 = bf16[2,7168]{1,0:T(2,128)(2,1)S(1)} collective-permute-done((bf16[2,7168]{1,0:T(2,128)(2,1)S(1)}, bf16[2,7168]{1,0:T(2,128)(2,1)S(1)}, u32[]{:S(2)}, u32[]{:S(2)}) %collective-permute-start.6) | collective-permute-done | bytes 28704 | tf_op jit(solution)/shard_map/ppermute | solution.py:61
  33.5 0.1 convert_add_fusion.1
  33.6 1.4 %collective-permute-start.10 = (f32[1,7168]{1,0:T(1,128)S(1)}, f32[1,7168]{1,0:T(1,128)S(1)}, u32[]{:S(2)}, u32[]{:S(2)}) collective-permute-start(f32[1,7168]{1,0:T(1,128)S(1)} %slice.29), channel_id=1, source_target_pairs={{0,1},{1,0},{2,3},{3,2},{4,5},{5,4},{6,7},{7,6},{8,9},{9,8},{10,11... | collective-permute-start | bytes 86024 | tf_op jit(solution)/shard_map/ppermute | solution.py:53
  35.1 0.9 %collective-permute-done.10 = f32[1,7168]{1,0:T(1,128)S(1)} collective-permute-done((f32[1,7168]{1,0:T(1,128)S(1)}, f32[1,7168]{1,0:T(1,128)S(1)}, u32[]{:S(2)}, u32[]{:S(2)}) %collective-permute-start.10) | collective-permute-done | bytes 28704 | tf_op jit(solution)/shard_map/ppermute | solution.py:53
  35.9 0.6 %fusion.2 = bf16[1,1,7168]{2,1,0:T(2,128)(2,1)} fusion(bf16[8,7168]{1,0:T(8,128)(2,1)S(1)} %add.21.refs_1_, f32[1,7168]{1,0:T(1,128)S(1)} %collective-permute-done.10, f32[2,7168]{1,0:T(2,128)S(1)} %convert_add_fusion.1), kind=kLoop, calls=%fused_computation.6 | loop fusion | flops 28672 | bytes 86016 | tf_op jit(solution)/shard_map/broadcast_in_dim | solution.py:401
  (4 shorter events, 0.1 us)
Async XLA Ops:
  0.6 10.4 %copy-start.2 = (bf16[1,4,7168]{2,1,0:T(4,128)(2,1)S(1)}, bf16[1,4,7168]{2,1,0:T(4,128)(2,1)}, u32[]{:S(2)}) copy-start(bf16[1,4,7168]{2,1,0:T(4,128)(2,1)} %param.13) | copy-start | bytes 172036
  0.6 8.4 %collective-permute-start = (bf16[4,7168]{1,0:T(4,128)(2,1)}, bf16[4,7168]{1,0:T(4,128)(2,1)S(1)}, u32[]{:S(2)}, u32[]{:S(2)}) collective-permute-start(bf16[4,7168]{1,0:T(4,128)(2,1)} %bitcast.11), channel_id=1, source_target_pairs={{0,12},{2,14},{4,8},{6,10},{8,4},{10,6},{12,0},{14,2},{1,13},{3,15... | collective-permute-start | bytes 172040 | tf_op jit(solution)/shard_map/ppermute | solution.py:53
  5.8 5.3 %collective-permute-start.1 = (bf16[4,7168]{1,0:T(4,128)(2,1)}, bf16[4,7168]{1,0:T(4,128)(2,1)S(1)}, u32[]{:S(2)}, u32[]{:S(2)}) collective-permute-start(bf16[4,7168]{1,0:T(4,128)(2,1)} %bitcast.12), channel_id=1, source_target_pairs={{0,8},{2,10},{4,12},{6,14},{8,0},{10,2},{12,4},{14,6},{1,9},{3,11}... | collective-permute-start | bytes 172040 | tf_op jit(solution)/shard_map/ppermute | solution.py:53
  5.8 5.3 %collective-permute-start.2 = (bf16[4,7168]{1,0:T(4,128)(2,1)}, bf16[4,7168]{1,0:T(4,128)(2,1)S(1)}, u32[]{:S(2)}, u32[]{:S(2)}) collective-permute-start(bf16[4,7168]{1,0:T(4,128)(2,1)} %bitcast.13), channel_id=1, source_target_pairs={{0,4},{2,6},{4,0},{6,2},{8,12},{10,14},{12,8},{14,10},{1,5},{3,7},... | collective-permute-start | bytes 172040 | tf_op jit(solution)/shard_map/ppermute | solution.py:53
  11.2 6.3 %copy-start.3 = (f32[7168]{0:T(1024)S(1)}, f32[7168]{0:T(1024)}, u32[]{:S(2)}) copy-start(f32[7168]{0:T(1024)} %param.14) | copy-start | bytes 86020
  11.3 4.9 %collective-permute-start.3 = (bf16[8,7168]{1,0:T(8,128)(2,1)S(1)}, bf16[8,7168]{1,0:T(8,128)(2,1)S(1)}, u32[]{:S(2)}, u32[]{:S(2)}) collective-permute-start(bf16[8,7168]{1,0:T(8,128)(2,1)S(1)} %get-tuple-element.16.refs_2_), channel_id=1, source_target_pairs={{0,2},{2,0},{4,6},{6,4},{8,10},{10,8},{12,14},{14,12},{1,3},{3,1},... | collective-permute-start | bytes 344072 | tf_op jit(solution)/shard_map/ppermute | solution.py:53
  16.2 1.4 %collective-permute-start.4 = (bf16[8,7168]{1,0:T(8,128)(2,1)S(1)}, bf16[8,7168]{1,0:T(8,128)(2,1)S(1)}, u32[]{:S(2)}, u32[]{:S(2)}) collective-permute-start(bf16[8,7168]{1,0:T(8,128)(2,1)S(1)} %add.21.refs_1_), channel_id=1, source_target_pairs={{0,1},{1,0},{2,3},{3,2},{4,5},{5,4},{6,7},{7,6},{8,9},{9,8},{10,11... | collective-permute-start | bytes 344072 | tf_op jit(solution)/shard_map/ppermute | solution.py:53
  17.5 13.1 %copy-start = (bf16[1,4,256,576]{2,3,1,0:T(8,128)(2,1)S(1)}, bf16[1,4,256,576]{2,3,1,0:T(8,128)(2,1)}, u32[]{:S(2)}) copy-start(bf16[1,4,256,576]{2,3,1,0:T(8,128)(2,1)} %param.10) | copy-start | bytes 3538948
  17.5 13.1 %copy-start.1 = (bf16[1,4,64,576]{3,2,1,0:T(8,128)(2,1)S(1)}, bf16[1,4,64,576]{3,2,1,0:T(8,128)(2,1)}, u32[]{:S(2)}) copy-start(bf16[1,4,64,576]{3,2,1,0:T(8,128)(2,1)} %param.9) | copy-start | bytes 884740
  17.5 13.1 %copy-start.4 = (s32[1,8]{1,0:T(1,128)S(1)}, s32[1,8]{1,0:T(1,128)}, u32[]{:S(2)}) copy-start(s32[1,8]{1,0:T(1,128)} %counts_ref.1) | copy-start | bytes 100
  17.6 13.1 %copy-start.5 = (s32[1,4]{1,0:T(1,128)S(1)}, s32[1,4]{1,0:T(1,128)}, u32[]{:S(2)}) copy-start(s32[1,4]{1,0:T(1,128)} %lengths_ref.1) | copy-start | bytes 52
  24.5 1.4 %collective-permute-start.5 = (bf16[8,7168]{1,0:T(8,128)(2,1)S(1)}, bf16[8,7168]{1,0:T(8,128)(2,1)S(1)}, u32[]{:S(2)}, u32[]{:S(2)}) collective-permute-start(bf16[8,7168]{1,0:T(8,128)(2,1)S(1)} %get-tuple-element.23.after_ref), channel_id=1, source_target_pairs={{0,1},{1,0},{2,3},{3,2},{4,5},{5,4},{6,7},{7,6},{8,9},{9,8},{10,11... | collective-permute-start | bytes 344072 | tf_op jit(solution)/shard_map/ppermute | solution.py:53
  26.0 6.8 %collective-permute-start.7 = (bf16[2,7168]{1,0:T(2,128)(2,1)S(1)}, bf16[2,7168]{1,0:T(2,128)(2,1)S(1)}, u32[]{:S(2)}, u32[]{:S(2)}) collective-permute-start(bf16[2,7168]{1,0:T(2,128)(2,1)S(1)} %get-tuple-element.28), channel_id=1, source_target_pairs={{0,6},{2,4},{4,2},{6,0},{8,14},{10,12},{12,10},{14,8},{1,15},{3,13... | collective-permute-start | bytes 86024 | tf_op jit(solution)/shard_map/ppermute | solution.py:61
  28.0 4.8 %collective-permute-start.8 = (bf16[2,7168]{1,0:T(2,128)(2,1)S(1)}, bf16[2,7168]{1,0:T(2,128)(2,1)S(1)}, u32[]{:S(2)}, u32[]{:S(2)}) collective-permute-start(bf16[2,7168]{1,0:T(2,128)(2,1)S(1)} %get-tuple-element.30), channel_id=1, source_target_pairs={{0,2},{2,0},{4,6},{6,4},{8,10},{10,8},{12,14},{14,12},{1,11},{3,9}... | collective-permute-start | bytes 86024 | tf_op jit(solution)/shard_map/ppermute | solution.py:61
  28.6 4.2 %collective-permute-start.9 = (bf16[2,7168]{1,0:T(2,128)(2,1)S(1)}, bf16[2,7168]{1,0:T(2,128)(2,1)S(1)}, u32[]{:S(2)}, u32[]{:S(2)}) collective-permute-start(bf16[2,7168]{1,0:T(2,128)(2,1)S(1)} %get-tuple-element.29), channel_id=1, source_target_pairs={{0,4},{2,6},{4,0},{6,2},{8,12},{10,14},{12,8},{14,10},{1,13},{3,15... | collective-permute-start | bytes 86024 | tf_op jit(solution)/shard_map/ppermute | solution.py:61
  29.5 4.0 %collective-permute-start.6 = (bf16[2,7168]{1,0:T(2,128)(2,1)S(1)}, bf16[2,7168]{1,0:T(2,128)(2,1)S(1)}, u32[]{:S(2)}, u32[]{:S(2)}) collective-permute-start(bf16[2,7168]{1,0:T(2,128)(2,1)S(1)} %slice.46), channel_id=1, source_target_pairs={{0,4},{2,6},{4,0},{6,2},{8,12},{10,14},{12,8},{14,10},{1,9},{3,11}... | collective-permute-start | bytes 86024 | tf_op jit(solution)/shard_map/ppermute | solution.py:61
  33.6 2.3 %collective-permute-start.10 = (f32[1,7168]{1,0:T(1,128)S(1)}, f32[1,7168]{1,0:T(1,128)S(1)}, u32[]{:S(2)}, u32[]{:S(2)}) collective-permute-start(f32[1,7168]{1,0:T(1,128)S(1)} %slice.29), channel_id=1, source_target_pairs={{0,1},{1,0},{2,3},{3,2},{4,5},{5,4},{6,7},{7,6},{8,9},{9,8},{10,11... | collective-permute-start | bytes 86024 | tf_op jit(solution)/shard_map/ppermute | solution.py:53

commit v7 on v6

v7 whole, which is shorter than its diff:
```python
import jax
import jax.numpy as jnp
from jax import lax
from jax.experimental import pallas as pl
from jax.experimental.pallas import tpu as pltpu
from jax.sharding import PartitionSpec as P

KVL = 512
MIB = 1024 * 1024

score_scale = 192.0 ** (-0.5)
norm_eps = 1e-06

VMEM = pl.BlockSpec(memory_space=pltpu.VMEM)
SMEM = pl.BlockSpec(memory_space=pltpu.SMEM)
ANY = pl.BlockSpec(memory_space=pl.ANY)


def gather_stages(bits):
    stages, top = [], bits
    while top > 1:
        width = 1 if top % 2 == 0 else 2
        top -= width
        stages.append((top, width))
    return stages


def sum_stages(bits):
    return [(low, min(2, bits - low)) for low in range(0, bits, 2)]


def direct_offset(place, core):
    return ((-place) & 3) | (core * 4)


def block_offset(position, stages):
    out = position * 0
    for low, width in stages:
        out = out | ((-position & ((1 << width) - 1)) << low)
        position = position >> width
    return out


def row_offset(position, stages):
    out = position * 0
    for low, width in stages[::-1]:
        out = out | ((position & ((1 << width) - 1)) << low)
        position = position >> width
    return out


def swap(x, axis, distance, size):
    return lax.ppermute(x, axis, [(i, i ^ distance) for i in range(size)])


def direct_swap(x, place, size):
    pairs = []
    for core in range(2):
        distance = direct_offset(place, core) or 2
        pairs += [(2 * i + core, 2 * (i ^ distance) + core) for i in range(size)]
    return lax.ppermute(x, ("tp", "sub"), pairs)


def pinned(weight):
    return pltpu.with_memory_space_constraint(weight, pltpu.HBM)


def row_copy(source, first, target, sems, i):
    step = target.shape[0] // sems.shape[0]
    here = pl.multiple_of(i * step, step)
    return pltpu.make_async_copy(source.at[pl.ds(first + here, step)], target.at[pl.ds(here, step)], sems.at[i])


def start_pieces(copy):
    @pl.loop(0, copy[-1].shape[0])
    def _(i):
        row_copy(*copy, i).start()


def wait_pieces(copy):
    @pl.loop(0, copy[-1].shape[0])
    def _(i):
        row_copy(*copy, i).wait()


def pieces_of(rows, most):
    return most if rows % (16 * most) == 0 else 1


def share_start(units, share):
    if share == units:
        return 0
    return pl.multiple_of(lax.axis_index("sub") * share, 16)


def pick_matrix(counts, device, size, slots, stages):
    bits = size.bit_length() - 1
    shape = (size, size // 2 * slots)
    slot = lax.broadcasted_iota(jnp.int32, shape, 1)
    every = lax.broadcasted_iota(jnp.int32, shape, 0)
    owner = block_offset(slot // slots, gather_stages(bits)) ^ device
    known = jnp.broadcast_to(counts, (8, size)).astype(jnp.bfloat16)
    start = jnp.dot(known, (every < owner).astype(jnp.bfloat16), preferred_element_type=jnp.float32)[:1]
    count = jnp.dot(known, (every == owner).astype(jnp.bfloat16), preferred_element_type=jnp.float32)[:1]
    place = (slot % slots)[:1].astype(jnp.float32)
    request = jnp.where(place < count, start + place, -1.0)
    row = lax.broadcasted_iota(jnp.int32, (2 * size, shape[1]), 0)
    wanted = row_offset(row % size, stages) ^ device ^ (row // size)
    return (request == wanted.astype(jnp.float32)).astype(jnp.bfloat16)


def attend(lengths_ref, counts_ref, queries_ref, cache_ref, out_ref):
    slots, heads, _ = queries_ref.shape
    positions = cache_ref.shape[2]
    live = counts_ref[0, lax.axis_index("tp")]
    spot = lax.broadcasted_iota(jnp.int32, (heads, positions), 1)
    every = []
    for s in range(slots):
        scores = jnp.dot(queries_ref[s], cache_ref[s], preferred_element_type=jnp.float32) * score_scale
        every.append(jnp.where(spot < lengths_ref[0, s], scores, -jnp.inf))
    scores = jnp.concatenate(every, axis=0)
    weights = jnp.exp(scores - jnp.max(scores, axis=1, keepdims=True))
    probs = (weights / jnp.sum(weights, axis=1, keepdims=True)).astype(jnp.bfloat16)
    for s in range(slots):
        context = lax.dot_general(
            probs[s * heads : (s + 1) * heads],
            cache_ref[s, :KVL, :],
            (((1,), (1,)), ((), ())),
            preferred_element_type=jnp.float32,
        )
        out_ref[s] = jnp.where(s < live, context, 0.0).astype(jnp.bfloat16)


def load_kernel(body, jobs, share, operands, specs, out_shape, out_specs, scratch, name):
    pieces = [pieces_of(rows, 4) for _, _, rows in jobs]
    count = len(jobs)

    def kernel(*refs):
        sources, refs = refs[:count], refs[count:]
        inputs, refs = refs[: len(operands)], refs[len(operands) :]
        targets, refs = refs[:count], refs[count:]
        copies = [
            (source, share_start(weight.shape[0], share) + first, target, sems)
            for (weight, first, _), source, target, sems in zip(jobs, sources, targets, refs[-count:])
        ]
        body([lambda copy=copy: start_pieces(copy) for copy in copies], *inputs, *refs[:-count])
        for copy in copies:
            wait_pieces(copy)

    return pl.pallas_call(
        kernel,
        out_shape=[pltpu.VMEM((rows, weight.shape[1]), weight.dtype) for weight, _, rows in jobs] + out_shape,
        in_specs=[ANY] * count + specs,
        out_specs=[VMEM] * count + out_specs,
        scratch_shapes=scratch + [pltpu.SemaphoreType.DMA((piece_count,)) for piece_count in pieces],
        compiler_params=pltpu.CompilerParams(vmem_limit_bytes=8 * MIB),
        cost_estimate=pl.CostEstimate(
            flops=0, transcendentals=0, bytes_accessed=sum(4 * rows * weight.shape[1] for weight, _, rows in jobs)
        ),
        name=name,
    )(*[pinned(weight) for weight, _, _ in jobs], *operands)


def load_and_pick(jobs, share, counts, slots, stages):
    size = counts.shape[1]

    def body(starts, counts_hbm, pick_ref, counts_ref, counts_sem):
        small = pltpu.make_async_copy(counts_hbm, counts_ref, counts_sem)
        small.start()
        for start in starts:
            start()
        small.wait()
        pick_ref[...] = pick_matrix(counts_ref[...], lax.axis_index("tp"), size, slots, stages)

    pick = jax.ShapeDtypeStruct((2 * size, size // 2 * slots), jnp.bfloat16)
    scratch = [pltpu.VMEM((1, size), jnp.int32), pltpu.SemaphoreType.DMA]
    return load_kernel(body, jobs, share, [pinned(counts)], [ANY], [pick], [VMEM], scratch, "load_and_pick")


def load_and_attend(jobs, share, queries, cache, lengths, counts, after):
    slots, heads, _ = queries.shape

    def body(starts, lengths_ref, counts_ref, queries_hbm, cache_hbm, _, out_hbm, queries_ref, cache_ref, out_ref, sems):
        copies = [
            pltpu.make_async_copy(queries_hbm, queries_ref, sems.at[0]),
            pltpu.make_async_copy(cache_hbm, cache_ref, sems.at[1]),
        ]
        for copy in copies:
            copy.start()
        starts[0]()
        for copy in copies:
            copy.wait()
        for start in starts[1:]:
            start()
        attend(lengths_ref, counts_ref, queries_ref, cache_ref, out_ref)
        out = pltpu.make_async_copy(out_ref, out_hbm, sems.at[2])
        out.start()
        out.wait()

    context = jax.ShapeDtypeStruct((slots, heads, KVL), jnp.bfloat16)
    scratch = [
        pltpu.VMEM(queries.shape, queries.dtype),
        pltpu.VMEM(cache.shape, cache.dtype),
        pltpu.VMEM(context.shape, context.dtype),
        pltpu.SemaphoreType.DMA((3,)),
    ]
    operands = [lengths, counts, pinned(queries), pinned(cache), after]
    specs = [SMEM, SMEM, ANY, ANY, ANY]
    return load_kernel(body, jobs, share, operands, specs, [context], [ANY], scratch, "load_and_attend")


def compact(pick, blocks):
    size = pick.shape[0] // 2
    width = blocks[0].shape[1]
    column = 1024
    count = len(blocks)

    def body(*refs):
        pick_ref, block_refs, (own_ref, send_ref) = refs[0], refs[1 : 1 + count], refs[1 + count :]
        pick_now = pick_ref[...]
        for c in range(0, width, column):
            rows = [ref[:, c : c + column].astype(jnp.float32) for ref in block_refs]
            rows = rows[0] if count == 1 else jnp.concatenate(rows, axis=0)
            out = jnp.dot(pick_now, rows.astype(jnp.bfloat16), preferred_element_type=jnp.float32)
            own_ref[:, c : c + column] = out[:size].astype(jnp.bfloat16)
            send_ref[:, c : c + column] = out[size:].astype(jnp.bfloat16)

    out = jax.ShapeDtypeStruct((size, width), jnp.bfloat16)
    return pl.pallas_call(
        body,
        out_shape=(out, out),
        in_specs=[VMEM] * (1 + count),
        out_specs=(VMEM, VMEM),
        compiler_params=pltpu.CompilerParams(vmem_limit_bytes=16 * MIB),
        name="compact",
    )(pick, *blocks)


def feed_forward(gain, row_sets, loaded, w_down, share):
    requests, width = row_sets[0].shape
    units = w_down.shape[0]
    set_count = len(row_sets)
    every = requests * set_count
    column = 512
    pieces = pieces_of(share, 4)
    parts = [part for _, _, part in loaded]

    def body(*refs):
        gain_ref, refs = refs[0], refs[1:]
        set_refs, refs = refs[:set_count], refs[set_count:]
        part_refs, refs = refs[: len(parts)], refs[len(parts) :]
        down_hbm, refs = refs[0], refs[1:]
        out_refs, refs = refs[:set_count], refs[set_count:]
        normed_ref, gate_ref, up_ref, hidden_ref, down_ref, down_sems = refs

        down_copy = (down_hbm, share_start(units, share), down_ref, down_sems)
        start_pieces(down_copy)

        rows = [ref[...].astype(jnp.float32) for ref in set_refs]
        rows = rows[0] if set_count == 1 else jnp.concatenate(rows, axis=0)
        inv_rms = lax.rsqrt(jnp.mean(rows * rows, axis=1, keepdims=True) + norm_eps)
        normed_ref[...] = (rows * inv_rms * gain_ref[...]).astype(jnp.bfloat16)

        for (which, first, _), ref in zip(loaded, part_refs):
            count = ref.shape[0]
            chunk = next((c for c in (192, 160, 128, 64) if count % c == 0), count)
            for j in range(0, count, chunk):
                (gate_ref, up_ref)[which][first + j : first + j + chunk, :] = lax.dot_general(
                    ref[j : j + chunk, :], normed_ref[...], (((1,), (1,)), ((), ())), preferred_element_type=jnp.float32
                )
        hidden = (jax.nn.silu(gate_ref[...]) * up_ref[...]).astype(jnp.bfloat16)
        place = lax.broadcasted_iota(jnp.int32, (every, every), 0)
        if set_count == 2:
            core = lax.axis_index("sub")
            other = place // requests
            distance = direct_offset(place % requests // 2, core ^ other)
            place = distance + ((place % 2) ^ other) * requests
        order = (lax.broadcasted_iota(jnp.int32, (every, every), 1) == place).astype(jnp.bfloat16)
        hidden_ref[...] = lax.dot_general(
            order, hidden, (((1,), (1,)), ((), ())), preferred_element_type=jnp.float32
        ).astype(jnp.bfloat16)

        wait_pieces(down_copy)
        for c in range(0, width, column):
            out = jnp.dot(hidden_ref[...], down_ref[:, c : c + column], preferred_element_type=jnp.float32)
            out_refs[0][:, c : c + column] = out[:requests]
            if set_count == 2:
                out_refs[1][:, c : c + column] = out[requests:].astype(jnp.bfloat16)

    outs = [
        jax.ShapeDtypeStruct((requests, width), jnp.float32),
        jax.ShapeDtypeStruct((requests, width), jnp.bfloat16),
    ][:set_count]
    return pl.pallas_call(
        body,
        out_shape=outs,
        in_specs=[VMEM] * (1 + set_count + len(parts)) + [ANY],
        out_specs=[VMEM] * set_count,
        scratch_shapes=[
            pltpu.VMEM((every, width), jnp.bfloat16),
            pltpu.VMEM((share, every), jnp.float32),
            pltpu.VMEM((share, every), jnp.float32),
            pltpu.VMEM((every, share), jnp.bfloat16),
            pltpu.VMEM((share, width), jnp.bfloat16),
            pltpu.SemaphoreType.DMA((pieces,)),
        ],
        compiler_params=pltpu.CompilerParams(vmem_limit_bytes=24 * MIB),
        cost_estimate=pl.CostEstimate(
            flops=6 * every * share * width,
            transcendentals=every * share,
            bytes_accessed=6 * share * width,
        ),
        name="feed_forward",
    )(gain[None], *row_sets, *parts, pinned(w_down))


def load_plan(share):
    if share % 192:
        return [(0, 0, share)], [(1, 0, share)]
    early = share // 3 * 2
    return [(0, 0, early)], [(0, early, share - early), (1, 0, share)]


def make_shards(size, cores):
    bits = size.bit_length() - 1

    def shards(queries, kv_cache, cache_lengths, live_counts, stream, norm_gain, w_gate, w_up, w_down):
        slots = queries.shape[1]
        units = w_gate.shape[0]
        split = cores == 2 and size == 8 and units % 32 == 0
        share = units // 2 if split else units
        weights = (w_gate, w_up)
        stages = [(0, bits)] if split else sum_stages(bits)
        plan = load_plan(share)
        loaded = []

        def load(kernel, jobs, *more):
            *parts, extra = kernel([(weights[which], first, rows) for which, first, rows in jobs], share, *more)
            loaded.extend((which, first, part) for (which, first, _), part in zip(jobs, parts))
            return extra

        block = stream[0]
        for step, (low, width) in enumerate(gather_stages(bits)):
            blocks = [block] + [swap(block, "tp", digit << low, size) for digit in range((1 << width) - 1, 0, -1)]
            if step == 0:
                pick = load(load_and_pick, plan[0], live_counts, slots, stages)
            if low > 1:
                block = jnp.concatenate(blocks, axis=0)

        own, send = compact(pick, blocks)
        arrived = swap(send, "tp", 1, size)
        cache = jnp.swapaxes(kv_cache[0], 1, 2)
        latent_ctx = load(load_and_attend, plan[1], queries[0], cache, cache_lengths, live_counts, send)[None]
        *last, part = loaded[-1]
        arrived, part = lax.optimization_barrier((arrived, part))
        loaded[-1] = (*last, part)
        rows = own + arrived
        row_sets = [rows, swap(rows, "sub", 1, cores)] if split else [rows]
        total, *other = feed_forward(norm_gain, row_sets, loaded, w_down, share)

        own_row = rows[:1].astype(jnp.float32)
        if split:
            total = total + swap(other[0], "sub", 1, cores).astype(jnp.float32)
            places = [total[2 * place : 2 * place + 2] for place in range(4)]
            sums = [
                direct_swap(places[place].astype(jnp.bfloat16), place, size).astype(jnp.float32)
                for place in (1, 2, 3, 0)
            ]
            total = jnp.where(lax.axis_index("sub") == 0, places[0], sums[3]) + sums[1] + sums[2] + sums[0]
            total = total[:1] + swap(total[1:], "sub", 1, cores)
        else:
            for step, (low, width) in enumerate(stages):
                part = total.shape[0] >> width
                sends = [total[digit * part : (digit + 1) * part] for digit in range(1, 1 << width)]
                total = total[:part]
                for digit, send in enumerate(sends, 1):
                    total = total + swap(send, "tp", digit << low, size)
        return (latent_ctx, (total + own_row).astype(jnp.bfloat16)[None])

    return shards


def solution(mesh):
    in_specs = (
        P(("groups", "sub"), "tp", None, None),
        P(("groups", "sub"), "tp", None, None),
        P(("groups", "sub"), "tp"),
        P(("groups", "sub"), None),
        P(("groups", "sub"), "tp", None),
        P(),
        P("tp", None),
        P("tp", None),
        P("tp", None),
    )
    out_specs = (P(("groups", "sub"), "tp", None, None), P(("groups", "sub"), "tp", None))
    return jax.shard_map(
        make_shards(mesh.shape["tp"], mesh.shape["sub"]),
        mesh=mesh,
        in_specs=in_specs,
        out_specs=out_specs,
        check_vma=False,
    )
```

time: 36.7 us -> 38.3 us (1.044)
  waiting for transfers between devices: 6.73 us -> 8.19 us
    ppermute x4, waiting for transfers between devices: 0.74 us -> 2.86 us  [direct_swap(): return lax.ppermute(x, ('tp', 'sub'), pairs)]
    pallas_call x3 -> x2, Pallas kernels: 7.36 us -> 8.32 us  [load_kernel(): pl.pallas_call(kernel, out_shape=[pltpu.VMEM((rows, weight.shape[1]), wei...]
    pallas_call x1, Pallas kernels: 6.89 us -> 6.04 us  [feed_forward(): pl.pallas_call(body, out_shape=outs, in_specs=[VMEM] * (1 + set_count + l...]
    ppermute x7, waiting for transfers between devices: 5.99 us -> 5.33 us  [swap(): return lax.ppermute(x, axis, [(i, i ^ distance) for i in range(size)])]
  transfers between devices with their start and end apart: 11 -> 11, of which waited for: 6 -> 8; matrix products, arithmetic and copies ran while one was open for 0% -> 0% of each run, Pallas kernels for 20% -> 22%
where the time goes in v7:
time: 38.3 us; the launch traced here: 38.1 us
  Pallas kernels  14.6 us (38%)
  starting transfers between devices  13.7 us (36%)
  waiting for transfers between devices  8.19 us (21%)
  other arithmetic  0.78 us (2%)
  between operations  0.75 us (2%)
    ppermute x7, starting transfers between devices, swap(): return lax.ppermute(x, axis, [(i, i ^ distance) for i in range(size)])  9.04 us
    pallas_call x2, Pallas kernels, load_kernel(): pl.pallas_call(kernel, out_shape=[pltpu.VMEM((rows, weight.shape[1]), wei...  8.32 us
    pallas_call x1, Pallas kernels, feed_forward(): pl.pallas_call(body, out_shape=outs, in_specs=[VMEM] * (1 + set_count + l...  6.04 us
    ppermute x7, waiting for transfers between devices, swap(): return lax.ppermute(x, axis, [(i, i ^ distance) for i in range(size)])  5.33 us
    ppermute x4, starting transfers between devices, direct_swap(): return lax.ppermute(x, ('tp', 'sub'), pairs)  4.68 us
    ppermute x4, waiting for transfers between devices, direct_swap(): return lax.ppermute(x, ('tp', 'sub'), pairs)  2.86 us
  transfers between devices with their start and end apart: 11, of which 8 were waited for; matrix products, arithmetic and copies ran while one was open for 0% of the time, Pallas kernels for 22%

profile of v7, /device:TPU:0, one launch (start us, length us, event | category | flops | bytes accessed | tf_op | source)
XLA Modules:
  0.0 38.1 jit_solution(16021155489043144968)
XLA Ops:
  0.6 0.0 copy-start
  0.6 0.0 copy-start.2
  0.7 0.0 copy-start.3
  0.7 5.1 %collective-permute-start = (bf16[4,7168]{1,0:T(4,128)(2,1)}, bf16[4,7168]{1,0:T(4,128)(2,1)S(1)}, u32[]{:S(2)}, u32[]{:S(2)}) collective-permute-start(bf16[4,7168]{1,0:T(4,128)(2,1)} %bitcast.9), channel_id=1, source_target_pairs={{0,12},{2,14},{4,8},{6,10},{8,4},{10,6},{12,0},{14,2},{1,13},{3,15... | collective-permute-start | bytes 172040 | tf_op jit(solution)/shard_map/ppermute | solution.py:53
  5.8 0.0 collective-permute-start.1
  5.8 0.6 %collective-permute-start.2 = (bf16[4,7168]{1,0:T(4,128)(2,1)}, bf16[4,7168]{1,0:T(4,128)(2,1)S(1)}, u32[]{:S(2)}, u32[]{:S(2)}) collective-permute-start(bf16[4,7168]{1,0:T(4,128)(2,1)} %bitcast.11), channel_id=1, source_target_pairs={{0,4},{2,6},{4,0},{6,2},{8,12},{10,14},{12,8},{14,10},{1,5},{3,7},... | collective-permute-start | bytes 172040 | tf_op jit(solution)/shard_map/ppermute | solution.py:53
  6.4 2.6 %load_and_pick.1 = (bf16[384,7168]{1,0:T(8,128)(2,1)S(1)}, bf16[16,16]{1,0:T(8,128)(2,1)S(1)}) custom-call(bf16[1152,7168]{1,0:T(8,128)(2,1)} %refs_0_.3, s32[1,8]{1,0:T(1,128)} %refs_3_.1), custom_call_target="tpu_custom_call" | custom-call | bytes 11010048 | tf_op jit(solution)/shard_map/load_and_pick/pallas_call | solution.py:150
  9.1 0.0 collective-permute-done.refs_2_
  9.1 2.0 %collective-permute-done.1.refs_3_ = bf16[4,7168]{1,0:T(4,128)(2,1)S(1)} collective-permute-done((bf16[4,7168]{1,0:T(4,128)(2,1)}, bf16[4,7168]{1,0:T(4,128)(2,1)S(1)}, u32[]{:S(2)}, u32[]{:S(2)}) %collective-permute-start.1) | collective-permute-done | bytes 57376 | tf_op jit(solution)/shard_map/ppermute | solution.py:53
  11.1 0.0 collective-permute-done.2.refs_4_
  11.1 0.0 copy-done
  11.1 0.2 compact.1
  11.3 1.6 %collective-permute-start.3 = (bf16[8,7168]{1,0:T(8,128)(2,1)S(1)}, bf16[8,7168]{1,0:T(8,128)(2,1)S(1)}, u32[]{:S(2)}, u32[]{:S(2)}) collective-permute-start(bf16[8,7168]{1,0:T(8,128)(2,1)S(1)} %get-tuple-element.14.refs_6_), channel_id=1, source_target_pairs={{0,2},{2,0},{4,6},{6,4},{8,10},{10,8},{12,14},{14,12},{1,3},{3,1},... | collective-permute-start | bytes 344072 | tf_op jit(solution)/shard_map/ppermute | solution.py:53
  12.9 0.0 copy-done.2
  12.9 0.0 copy-done.3
  12.9 0.0 copy-start.1
  12.9 5.7 %load_and_attend.1 = (bf16[192,7168]{1,0:T(8,128)(2,1)S(1)}, bf16[576,7168]{1,0:T(8,128)(2,1)S(1)}, bf16[4,64,512]{2,1,0:T(8,128)(2,1)}) custom-call(bf16[1152,7168]{1,0:T(8,128)(2,1)} %refs_0_.3, bf16[1152,7168]{1,0:T(8,128)(2,1)} %refs_1_.3, s32[1,4]{1,0:T(1,128)S(1)} %copy-done.3, s32[1,8]{1,0:T(1,128)S(1)} %copy-done.2, bf16[4,64,576]{2,1,0:T(8,128)(2,1)} %bitcast.15, ...), custom_call_target="tpu_custom_call" | custom-call | bytes 22020096 | tf_op jit(solution)/shard_map/load_and_attend/pallas_call | solution.py:150
  18.6 0.0 collective-permute-done.3
  18.6 0.1 collective-permute-start.4
  18.7 1.3 %collective-permute-done.4.refs_2_ = bf16[8,7168]{1,0:T(8,128)(2,1)S(1)} collective-permute-done((bf16[8,7168]{1,0:T(8,128)(2,1)S(1)}, bf16[8,7168]{1,0:T(8,128)(2,1)S(1)}, u32[]{:S(2)}, u32[]{:S(2)}) %collective-permute-start.4) | collective-permute-done | bytes 114720 | tf_op jit(solution)/shard_map/ppermute | solution.py:53
  20.0 0.0 copy-done.1
  20.0 6.0 %feed_forward.1 = (f32[8,7168]{1,0:T(8,128)S(1)}, bf16[8,7168]{1,0:T(8,128)(2,1)S(1)}) custom-call(f32[1,7168]{1,0:T(1,128)S(1)} %bitcast.13, bf16[8,7168]{1,0:T(8,128)(2,1)S(1)} %add.21.refs_1_, bf16[8,7168]{1,0:T(8,128)(2,1)S(1)} %collective-permute-done.4.refs_2_, bf16[384,7168]{1,0:T(8,128)(2,1)S(1)} %get-tuple-element.19.refs_3_, ...), custom_call_target="tpu_custom_call" | custom-call | flops 396361728 | bytes 24772608 | tf_op jit(solution)/shard_map/feed_forward/pallas_call | solution.py:294
  26.0 0.2 collective-permute-start.5
  26.3 1.2 %collective-permute-done.5 = bf16[8,7168]{1,0:T(8,128)(2,1)S(1)} collective-permute-done((bf16[8,7168]{1,0:T(8,128)(2,1)S(1)}, bf16[8,7168]{1,0:T(8,128)(2,1)S(1)}, u32[]{:S(2)}, u32[]{:S(2)}) %collective-permute-start.5) | collective-permute-done | bytes 114720 | tf_op jit(solution)/shard_map/ppermute | solution.py:53
  27.5 0.1 fusion.4
  27.5 1.1 %collective-permute-start.9 = (bf16[2,7168]{1,0:T(2,128)(2,1)S(1)}, bf16[2,7168]{1,0:T(2,128)(2,1)S(1)}, u32[]{:S(2)}, u32[]{:S(2)}) collective-permute-start(bf16[2,7168]{1,0:T(2,128)(2,1)S(1)} %get-tuple-element.27), channel_id=1, source_target_pairs={{0,6},{2,4},{4,2},{6,0},{8,14},{10,12},{12,10},{14,8},{1,15},{3,13... | collective-permute-start | bytes 86024 | tf_op jit(solution)/shard_map/ppermute | solution.py:61
  28.6 1.5 %collective-permute-start.8 = (bf16[2,7168]{1,0:T(2,128)(2,1)S(1)}, bf16[2,7168]{1,0:T(2,128)(2,1)S(1)}, u32[]{:S(2)}, u32[]{:S(2)}) collective-permute-start(bf16[2,7168]{1,0:T(2,128)(2,1)S(1)} %get-tuple-element.28), channel_id=1, source_target_pairs={{0,2},{2,0},{4,6},{6,4},{8,10},{10,8},{12,14},{14,12},{1,11},{3,9}... | collective-permute-start | bytes 86024 | tf_op jit(solution)/shard_map/ppermute | solution.py:61
  30.1 1.0 %collective-permute-start.7 = (bf16[2,7168]{1,0:T(2,128)(2,1)S(1)}, bf16[2,7168]{1,0:T(2,128)(2,1)S(1)}, u32[]{:S(2)}, u32[]{:S(2)}) collective-permute-start(bf16[2,7168]{1,0:T(2,128)(2,1)S(1)} %get-tuple-element.26), channel_id=1, source_target_pairs={{0,4},{2,6},{4,0},{6,2},{8,12},{10,14},{12,8},{14,10},{1,13},{3,15... | collective-permute-start | bytes 86024 | tf_op jit(solution)/shard_map/ppermute | solution.py:61
  31.1 1.1 %collective-permute-start.6 = (bf16[2,7168]{1,0:T(2,128)(2,1)S(1)}, bf16[2,7168]{1,0:T(2,128)(2,1)S(1)}, u32[]{:S(2)}, u32[]{:S(2)}) collective-permute-start(bf16[2,7168]{1,0:T(2,128)(2,1)S(1)} %slice.50), channel_id=1, source_target_pairs={{0,4},{2,6},{4,0},{6,2},{8,12},{10,14},{12,8},{14,10},{1,9},{3,11}... | collective-permute-start | bytes 86024 | tf_op jit(solution)/shard_map/ppermute | solution.py:61
  32.2 0.2 collective-permute-done.9
  32.4 0.3 collective-permute-done.8
  32.7 1.3 %collective-permute-done.7 = bf16[2,7168]{1,0:T(2,128)(2,1)S(1)} collective-permute-done((bf16[2,7168]{1,0:T(2,128)(2,1)S(1)}, bf16[2,7168]{1,0:T(2,128)(2,1)S(1)}, u32[]{:S(2)}, u32[]{:S(2)}) %collective-permute-start.7) | collective-permute-done | bytes 28704 | tf_op jit(solution)/shard_map/ppermute | solution.py:61
  34.0 1.1 %collective-permute-done.6 = bf16[2,7168]{1,0:T(2,128)(2,1)S(1)} collective-permute-done((bf16[2,7168]{1,0:T(2,128)(2,1)S(1)}, bf16[2,7168]{1,0:T(2,128)(2,1)S(1)}, u32[]{:S(2)}, u32[]{:S(2)}) %collective-permute-start.6) | collective-permute-done | bytes 28704 | tf_op jit(solution)/shard_map/ppermute | solution.py:61
  35.1 0.1 convert_add_fusion.1
  35.2 1.4 %collective-permute-start.10 = (f32[1,7168]{1,0:T(1,128)S(1)}, f32[1,7168]{1,0:T(1,128)S(1)}, u32[]{:S(2)}, u32[]{:S(2)}) collective-permute-start(f32[1,7168]{1,0:T(1,128)S(1)} %slice.36), channel_id=1, source_target_pairs={{0,1},{1,0},{2,3},{3,2},{4,5},{5,4},{6,7},{7,6},{8,9},{9,8},{10,11... | collective-permute-start | bytes 86024 | tf_op jit(solution)/shard_map/ppermute | solution.py:53
  36.6 0.9 %collective-permute-done.10 = f32[1,7168]{1,0:T(1,128)S(1)} collective-permute-done((f32[1,7168]{1,0:T(1,128)S(1)}, f32[1,7168]{1,0:T(1,128)S(1)}, u32[]{:S(2)}, u32[]{:S(2)}) %collective-permute-start.10) | collective-permute-done | bytes 28704 | tf_op jit(solution)/shard_map/ppermute | solution.py:53
  37.5 0.7 %fusion.2 = bf16[1,1,7168]{2,1,0:T(2,128)(2,1)} fusion(bf16[8,7168]{1,0:T(8,128)(2,1)S(1)} %add.21.refs_1_, f32[1,7168]{1,0:T(1,128)S(1)} %collective-permute-done.10, f32[2,7168]{1,0:T(2,128)S(1)} %convert_add_fusion.1), kind=kLoop, calls=%fused_computation.6 | loop fusion | flops 28672 | bytes 86016 | tf_op jit(solution)/shard_map/broadcast_in_dim | solution.py:378
  (4 shorter events, 0.1 us)
Async XLA Ops:
  0.6 10.4 %copy-start = (bf16[1,4,7168]{2,1,0:T(4,128)(2,1)S(1)}, bf16[1,4,7168]{2,1,0:T(4,128)(2,1)}, u32[]{:S(2)}) copy-start(bf16[1,4,7168]{2,1,0:T(4,128)(2,1)} %param.13) | copy-start | bytes 172036
  0.6 12.2 %copy-start.2 = (s32[1,8]{1,0:T(1,128)S(1)}, s32[1,8]{1,0:T(1,128)}, u32[]{:S(2)}) copy-start(s32[1,8]{1,0:T(1,128)} %refs_3_.1) | copy-start | bytes 100
  0.7 12.2 %copy-start.3 = (s32[1,4]{1,0:T(1,128)S(1)}, s32[1,4]{1,0:T(1,128)}, u32[]{:S(2)}) copy-start(s32[1,4]{1,0:T(1,128)} %refs_2_.1) | copy-start | bytes 52
  0.7 8.4 %collective-permute-start = (bf16[4,7168]{1,0:T(4,128)(2,1)}, bf16[4,7168]{1,0:T(4,128)(2,1)S(1)}, u32[]{:S(2)}, u32[]{:S(2)}) collective-permute-start(bf16[4,7168]{1,0:T(4,128)(2,1)} %bitcast.9), channel_id=1, source_target_pairs={{0,12},{2,14},{4,8},{6,10},{8,4},{10,6},{12,0},{14,2},{1,13},{3,15... | collective-permute-start | bytes 172040 | tf_op jit(solution)/shard_map/ppermute | solution.py:53
  5.8 5.3 %collective-permute-start.1 = (bf16[4,7168]{1,0:T(4,128)(2,1)}, bf16[4,7168]{1,0:T(4,128)(2,1)S(1)}, u32[]{:S(2)}, u32[]{:S(2)}) collective-permute-start(bf16[4,7168]{1,0:T(4,128)(2,1)} %bitcast.10), channel_id=1, source_target_pairs={{0,8},{2,10},{4,12},{6,14},{8,0},{10,2},{12,4},{14,6},{1,9},{3,11}... | collective-permute-start | bytes 172040 | tf_op jit(solution)/shard_map/ppermute | solution.py:53
  5.8 5.3 %collective-permute-start.2 = (bf16[4,7168]{1,0:T(4,128)(2,1)}, bf16[4,7168]{1,0:T(4,128)(2,1)S(1)}, u32[]{:S(2)}, u32[]{:S(2)}) collective-permute-start(bf16[4,7168]{1,0:T(4,128)(2,1)} %bitcast.11), channel_id=1, source_target_pairs={{0,4},{2,6},{4,0},{6,2},{8,12},{10,14},{12,8},{14,10},{1,5},{3,7},... | collective-permute-start | bytes 172040 | tf_op jit(solution)/shard_map/ppermute | solution.py:53
  11.3 7.3 %collective-permute-start.3 = (bf16[8,7168]{1,0:T(8,128)(2,1)S(1)}, bf16[8,7168]{1,0:T(8,128)(2,1)S(1)}, u32[]{:S(2)}, u32[]{:S(2)}) collective-permute-start(bf16[8,7168]{1,0:T(8,128)(2,1)S(1)} %get-tuple-element.14.refs_6_), channel_id=1, source_target_pairs={{0,2},{2,0},{4,6},{6,4},{8,10},{10,8},{12,14},{14,12},{1,3},{3,1},... | collective-permute-start | bytes 344072 | tf_op jit(solution)/shard_map/ppermute | solution.py:53
  12.9 7.1 %copy-start.1 = (f32[7168]{0:T(1024)S(1)}, f32[7168]{0:T(1024)}, u32[]{:S(2)}) copy-start(f32[7168]{0:T(1024)} %param.14) | copy-start | bytes 86020
  18.6 1.4 %collective-permute-start.4 = (bf16[8,7168]{1,0:T(8,128)(2,1)S(1)}, bf16[8,7168]{1,0:T(8,128)(2,1)S(1)}, u32[]{:S(2)}, u32[]{:S(2)}) collective-permute-start(bf16[8,7168]{1,0:T(8,128)(2,1)S(1)} %add.21.refs_1_), channel_id=1, source_target_pairs={{0,1},{1,0},{2,3},{3,2},{4,5},{5,4},{6,7},{7,6},{8,9},{9,8},{10,11... | collective-permute-start | bytes 344072 | tf_op jit(solution)/shard_map/ppermute | solution.py:53
  26.0 1.4 %collective-permute-start.5 = (bf16[8,7168]{1,0:T(8,128)(2,1)S(1)}, bf16[8,7168]{1,0:T(8,128)(2,1)S(1)}, u32[]{:S(2)}, u32[]{:S(2)}) collective-permute-start(bf16[8,7168]{1,0:T(8,128)(2,1)S(1)} %get-tuple-element.23), channel_id=1, source_target_pairs={{0,1},{1,0},{2,3},{3,2},{4,5},{5,4},{6,7},{7,6},{8,9},{9,8},{10,11... | collective-permute-start | bytes 344072 | tf_op jit(solution)/shard_map/ppermute | solution.py:53
  27.5 4.9 %collective-permute-start.9 = (bf16[2,7168]{1,0:T(2,128)(2,1)S(1)}, bf16[2,7168]{1,0:T(2,128)(2,1)S(1)}, u32[]{:S(2)}, u32[]{:S(2)}) collective-permute-start(bf16[2,7168]{1,0:T(2,128)(2,1)S(1)} %get-tuple-element.27), channel_id=1, source_target_pairs={{0,6},{2,4},{4,2},{6,0},{8,14},{10,12},{12,10},{14,8},{1,15},{3,13... | collective-permute-start | bytes 86024 | tf_op jit(solution)/shard_map/ppermute | solution.py:61
  28.6 4.0 %collective-permute-start.8 = (bf16[2,7168]{1,0:T(2,128)(2,1)S(1)}, bf16[2,7168]{1,0:T(2,128)(2,1)S(1)}, u32[]{:S(2)}, u32[]{:S(2)}) collective-permute-start(bf16[2,7168]{1,0:T(2,128)(2,1)S(1)} %get-tuple-element.28), channel_id=1, source_target_pairs={{0,2},{2,0},{4,6},{6,4},{8,10},{10,8},{12,14},{14,12},{1,11},{3,9}... | collective-permute-start | bytes 86024 | tf_op jit(solution)/shard_map/ppermute | solution.py:61
  30.1 3.9 %collective-permute-start.7 = (bf16[2,7168]{1,0:T(2,128)(2,1)S(1)}, bf16[2,7168]{1,0:T(2,128)(2,1)S(1)}, u32[]{:S(2)}, u32[]{:S(2)}) collective-permute-start(bf16[2,7168]{1,0:T(2,128)(2,1)S(1)} %get-tuple-element.26), channel_id=1, source_target_pairs={{0,4},{2,6},{4,0},{6,2},{8,12},{10,14},{12,8},{14,10},{1,13},{3,15... | collective-permute-start | bytes 86024 | tf_op jit(solution)/shard_map/ppermute | solution.py:61
  31.1 4.0 %collective-permute-start.6 = (bf16[2,7168]{1,0:T(2,128)(2,1)S(1)}, bf16[2,7168]{1,0:T(2,128)(2,1)S(1)}, u32[]{:S(2)}, u32[]{:S(2)}) collective-permute-start(bf16[2,7168]{1,0:T(2,128)(2,1)S(1)} %slice.50), channel_id=1, source_target_pairs={{0,4},{2,6},{4,0},{6,2},{8,12},{10,14},{12,8},{14,10},{1,9},{3,11}... | collective-permute-start | bytes 86024 | tf_op jit(solution)/shard_map/ppermute | solution.py:61
  35.2 2.3 %collective-permute-start.10 = (f32[1,7168]{1,0:T(1,128)S(1)}, f32[1,7168]{1,0:T(1,128)S(1)}, u32[]{:S(2)}, u32[]{:S(2)}) collective-permute-start(f32[1,7168]{1,0:T(1,128)S(1)} %slice.36), channel_id=1, source_target_pairs={{0,1},{1,0},{2,3},{3,2},{4,5},{5,4},{6,7},{7,6},{8,9},{9,8},{10,11... | collective-permute-start | bytes 86024 | tf_op jit(solution)/shard_map/ppermute | solution.py:53

commit v8 on v7

--- a/solution.py
+++ b/solution.py
@@ -12,7 +12,6 @@
 norm_eps = 1e-06
 
 VMEM = pl.BlockSpec(memory_space=pltpu.VMEM)
-SMEM = pl.BlockSpec(memory_space=pltpu.SMEM)
 ANY = pl.BlockSpec(memory_space=pl.ANY)
 
 
@@ -109,104 +108,90 @@
     return (request == wanted.astype(jnp.float32)).astype(jnp.bfloat16)
 
 
-def attend(lengths_ref, counts_ref, queries_ref, cache_ref, out_ref):
-    slots, heads, _ = queries_ref.shape
-    positions = cache_ref.shape[2]
-    live = counts_ref[0, lax.axis_index("tp")]
-    spot = lax.broadcasted_iota(jnp.int32, (heads, positions), 1)
-    every = []
-    for s in range(slots):
-        scores = jnp.dot(queries_ref[s], cache_ref[s], preferred_element_type=jnp.float32) * score_scale
-        every.append(jnp.where(spot < lengths_ref[0, s], scores, -jnp.inf))
-    scores = jnp.concatenate(every, axis=0)
-    weights = jnp.exp(scores - jnp.max(scores, axis=1, keepdims=True))
-    probs = (weights / jnp.sum(weights, axis=1, keepdims=True)).astype(jnp.bfloat16)
-    for s in range(slots):
-        context = lax.dot_general(
-            probs[s * heads : (s + 1) * heads],
-            cache_ref[s, :KVL, :],
-            (((1,), (1,)), ((), ())),
-            preferred_element_type=jnp.float32,
-        )
-        out_ref[s] = jnp.where(s < live, context, 0.0).astype(jnp.bfloat16)
-
-
-def load_kernel(body, jobs, share, operands, specs, out_shape, out_specs, scratch, name):
-    pieces = [pieces_of(rows, 4) for _, _, rows in jobs]
-    count = len(jobs)
-
-    def kernel(*refs):
-        sources, refs = refs[:count], refs[count:]
-        inputs, refs = refs[: len(operands)], refs[len(operands) :]
-        targets, refs = refs[:count], refs[count:]
+def attend(queries, cache, lengths, counts, after):
+    slots, heads, _ = queries.shape
+    positions = cache.shape[2]
+
+    def body(lengths_ref, counts_ref, queries_ref, cache_ref, _, out_ref):
+        lengths = lengths_ref[...]
+        counts = counts_ref[...]
+        here = lax.broadcasted_iota(jnp.int32, counts.shape, 1) == lax.axis_index("tp")
+        live = jnp.sum(jnp.where(here, counts, 0), axis=1, keepdims=True)
+        spot = lax.broadcasted_iota(jnp.int32, (heads, positions), 1)
+        every = []
+        for s in range(slots):
+            scores = jnp.dot(queries_ref[s], cache_ref[s], preferred_element_type=jnp.float32) * score_scale
+            every.append(jnp.where(spot < lengths[:, s : s + 1], scores, -jnp.inf))
+        scores = jnp.concatenate(every, axis=0)
+        weights = jnp.exp(scores - jnp.max(scores, axis=1, keepdims=True))
+        probs = (weights / jnp.sum(weights, axis=1, keepdims=True)).astype(jnp.bfloat16)
+        for s in range(slots):
+            context = lax.dot_general(
+                probs[s * heads : (s + 1) * heads],
+                cache_ref[s, :KVL, :],
+                (((1,), (1,)), ((), ())),
+                preferred_element_type=jnp.float32,
+            )
+            out_ref[s] = jnp.where(s < live, context, 0.0).astype(jnp.bfloat16)
+
+    return pl.pallas_call(
+        body,
+        out_shape=jax.ShapeDtypeStruct((slots, heads, KVL), jnp.bfloat16),
+        in_specs=[VMEM] * 4 + [ANY],
+        out_specs=VMEM,
+        compiler_params=pltpu.CompilerParams(vmem_limit_bytes=8 * MIB),
+        cost_estimate=pl.CostEstimate(
+            flops=4 * slots * heads * positions * KVL,
+            transcendentals=slots * heads * positions,
+            bytes_accessed=2 * (queries.size + cache.size),
+        ),
+        name="attend",
+    )(lengths, counts, queries, cache, after)
+
+
+def load_rows(jobs, share, after=None, counts=None, slots=0, stages=()):
+    size = 0 if counts is None else counts.shape[1]
+    pieces = [pieces_of(rows, 2) for _, _, rows in jobs]
+    operands = [pinned(weight) for weight, _, _ in jobs]
+    out_shape = [pltpu.VMEM((rows, weight.shape[1]), weight.dtype) for weight, _, rows in jobs]
+    scratch = [pltpu.SemaphoreType.DMA((count,)) for count in pieces]
+    if counts is not None:
+        operands.append(pinned(counts))
+        out_shape.append(jax.ShapeDtypeStruct((2 * size, size // 2 * slots), jnp.bfloat16))
+        scratch += [pltpu.VMEM((1, size), jnp.int32), pltpu.SemaphoreType.DMA]
+    if after is not None:
+        operands.append(after)
+
+    def body(*refs):
+        sources, refs = refs[: len(operands)], refs[len(operands) :]
+        targets, refs = refs[: len(out_shape)], refs[len(out_shape) :]
+        if counts is not None:
+            small = pltpu.make_async_copy(sources[len(jobs)], refs[-2], refs[-1])
+            small.start()
         copies = [
             (source, share_start(weight.shape[0], share) + first, target, sems)
-            for (weight, first, _), source, target, sems in zip(jobs, sources, targets, refs[-count:])
+            for (weight, first, _), source, target, sems in zip(jobs, sources, targets, refs)
         ]
-        body([lambda copy=copy: start_pieces(copy) for copy in copies], *inputs, *refs[:-count])
+        for copy in copies:
+            start_pieces(copy)
+        if counts is not None:
+            small.wait()
+            targets[-1][...] = pick_matrix(refs[-2][...], lax.axis_index("tp"), size, slots, stages)
         for copy in copies:
             wait_pieces(copy)
 
     return pl.pallas_call(
-        kernel,
-        out_shape=[pltpu.VMEM((rows, weight.shape[1]), weight.dtype) for weight, _, rows in jobs] + out_shape,
-        in_specs=[ANY] * count + specs,
-        out_specs=[VMEM] * count + out_specs,
-        scratch_shapes=scratch + [pltpu.SemaphoreType.DMA((piece_count,)) for piece_count in pieces],
-        compiler_params=pltpu.CompilerParams(vmem_limit_bytes=8 * MIB),
+        body,
+        out_shape=out_shape,
+        in_specs=[ANY] * len(operands),
+        out_specs=[VMEM] * len(out_shape),
+        scratch_shapes=scratch,
+        compiler_params=pltpu.CompilerParams(vmem_limit_bytes=2 * MIB),
         cost_estimate=pl.CostEstimate(
             flops=0, transcendentals=0, bytes_accessed=sum(4 * rows * weight.shape[1] for weight, _, rows in jobs)
         ),
-        name=name,
-    )(*[pinned(weight) for weight, _, _ in jobs], *operands)
-
-
-def load_and_pick(jobs, share, counts, slots, stages):
-    size = counts.shape[1]
-
-    def body(starts, counts_hbm, pick_ref, counts_ref, counts_sem):
-        small = pltpu.make_async_copy(counts_hbm, counts_ref, counts_sem)
-        small.start()
-        for start in starts:
-            start()
-        small.wait()
-        pick_ref[...] = pick_matrix(counts_ref[...], lax.axis_index("tp"), size, slots, stages)
-
-    pick = jax.ShapeDtypeStruct((2 * size, size // 2 * slots), jnp.bfloat16)
-    scratch = [pltpu.VMEM((1, size), jnp.int32), pltpu.SemaphoreType.DMA]
-    return load_kernel(body, jobs, share, [pinned(counts)], [ANY], [pick], [VMEM], scratch, "load_and_pick")
-
-
-def load_and_attend(jobs, share, queries, cache, lengths, counts, after):
-    slots, heads, _ = queries.shape
-
-    def body(starts, lengths_ref, counts_ref, queries_hbm, cache_hbm, _, out_hbm, queries_ref, cache_ref, out_ref, sems):
-        copies = [
-            pltpu.make_async_copy(queries_hbm, queries_ref, sems.at[0]),
-            pltpu.make_async_copy(cache_hbm, cache_ref, sems.at[1]),
-        ]
-        for copy in copies:
-            copy.start()
-        starts[0]()
-        for copy in copies:
-            copy.wait()
-        for start in starts[1:]:
-            start()
-        attend(lengths_ref, counts_ref, queries_ref, cache_ref, out_ref)
-        out = pltpu.make_async_copy(out_ref, out_hbm, sems.at[2])
-        out.start()
-        out.wait()
-
-    context = jax.ShapeDtypeStruct((slots, heads, KVL), jnp.bfloat16)
-    scratch = [
-        pltpu.VMEM(queries.shape, queries.dtype),
-        pltpu.VMEM(cache.shape, cache.dtype),
-        pltpu.VMEM(context.shape, context.dtype),
-        pltpu.SemaphoreType.DMA((3,)),
-    ]
-    operands = [lengths, counts, pinned(queries), pinned(cache), after]
-    specs = [SMEM, SMEM, ANY, ANY, ANY]
-    return load_kernel(body, jobs, share, operands, specs, [context], [ANY], scratch, "load_and_attend")
+        name="load_rows",
+    )(*operands)
 
 
 def compact(pick, blocks):
@@ -334,23 +319,22 @@
         plan = load_plan(share)
         loaded = []
 
-        def load(kernel, jobs, *more):
-            *parts, extra = kernel([(weights[which], first, rows) for which, first, rows in jobs], share, *more)
+        def load(jobs, **more):
+            parts = load_rows([(weights[which], first, rows) for which, first, rows in jobs], share, **more)
             loaded.extend((which, first, part) for (which, first, _), part in zip(jobs, parts))
-            return extra
+            return parts[-1]
 
         block = stream[0]
         for step, (low, width) in enumerate(gather_stages(bits)):
             blocks = [block] + [swap(block, "tp", digit << low, size) for digit in range((1 << width) - 1, 0, -1)]
             if step == 0:
-                pick = load(load_and_pick, plan[0], live_counts, slots, stages)
+                pick = load(plan[0], counts=live_counts, slots=slots, stages=stages)
             if low > 1:
                 block = jnp.concatenate(blocks, axis=0)
 
         own, send = compact(pick, blocks)
         arrived = swap(send, "tp", 1, size)
-        cache = jnp.swapaxes(kv_cache[0], 1, 2)
-        latent_ctx = load(load_and_attend, plan[1], queries[0], cache, cache_lengths, live_counts, send)[None]
+        load(plan[1], after=send)
         *last, part = loaded[-1]
         arrived, part = lax.optimization_barrier((arrived, part))
         loaded[-1] = (*last, part)
@@ -358,6 +342,9 @@
         row_sets = [rows, swap(rows, "sub", 1, cores)] if split else [rows]
         total, *other = feed_forward(norm_gain, row_sets, loaded, w_down, share)
 
+        cache = jnp.swapaxes(kv_cache[0], 1, 2)
+        after = other[0] if split else total
+        latent_ctx = attend(queries[0], cache, cache_lengths, live_counts, after)
         own_row = rows[:1].astype(jnp.float32)
         if split:
             total = total + swap(other[0], "sub", 1, cores).astype(jnp.float32)
@@ -366,7 +353,8 @@
                 direct_swap(places[place].astype(jnp.bfloat16), place, size).astype(jnp.float32)
                 for place in (1, 2, 3, 0)
             ]
-            total = jnp.where(lax.axis_index("sub") == 0, places[0], sums[3]) + sums[1] + sums[2] + sums[0]
+            total = jnp.where(lax.axis_index("sub") == 0, places[0], sums[3]) + sums[0] + sums[2] + sums[1]
+            total, latent_ctx = lax.optimization_barrier((total, latent_ctx))
             total = total[:1] + swap(total[1:], "sub", 1, cores)
         else:
             for step, (low, width) in enumerate(stages):
@@ -375,7 +363,7 @@
                 total = total[:part]
                 for digit, send in enumerate(sends, 1):
                     total = total + swap(send, "tp", digit << low, size)
-        return (latent_ctx, (total + own_row).astype(jnp.bfloat16)[None])
+        return (latent_ctx[None], (total + own_row).astype(jnp.bfloat16)[None])
 
     return shards
 

time: 38.3 us -> 36.9 us (0.963)
  waiting for transfers between devices: 8.19 us -> 6.58 us
    ppermute x4, waiting for transfers between devices: 2.86 us -> 1.25 us  [direct_swap(): return lax.ppermute(x, ('tp', 'sub'), pairs)]
    pallas_call x2 -> x3, Pallas kernels: 8.32 us -> 8.47 us  [the longest x2 6.87 us: load_rows(): pl.pallas_call(body, out_shape=out_shape, in_specs=[ANY] * len(operands),...]
  transfers between devices with their start and end apart: 11 -> 11, of which waited for: 8 -> 6; matrix products, arithmetic and copies ran while one was open for 0% -> 0% of each run, Pallas kernels for 22% -> 23%
where the time goes in v8:
time: 36.9 us; the launch traced here: 36.7 us
  Pallas kernels  14.7 us (40%)
  starting transfers between devices  13.7 us (37%)
  waiting for transfers between devices  6.58 us (18%)
  other arithmetic  0.77 us (2%)
  between operations  0.76 us (2%)
    ppermute x7, starting transfers between devices, swap(): return lax.ppermute(x, axis, [(i, i ^ distance) for i in range(size)])  9.03 us
    pallas_call x2, Pallas kernels, load_rows(): pl.pallas_call(body, out_shape=out_shape, in_specs=[ANY] * len(operands),...  6.87 us
    pallas_call x1, Pallas kernels, feed_forward(): pl.pallas_call(body, out_shape=outs, in_specs=[VMEM] * (1 + set_count + l...  6.08 us
    ppermute x7, waiting for transfers between devices, swap(): return lax.ppermute(x, axis, [(i, i ^ distance) for i in range(size)])  5.33 us
    ppermute x4, starting transfers between devices, direct_swap(): return lax.ppermute(x, ('tp', 'sub'), pairs)  4.67 us
    pallas_call x1, Pallas kernels, attend(): pl.pallas_call(body, out_shape=jax.ShapeDtypeStruct((slots, heads, KVL),...  1.6 us
    ppermute x4, waiting for transfers between devices, direct_swap(): return lax.ppermute(x, ('tp', 'sub'), pairs)  1.25 us
  transfers between devices with their start and end apart: 11, of which 6 were waited for; matrix products, arithmetic and copies ran while one was open for 0% of the time, Pallas kernels for 23%

profile of v8, /device:TPU:0, one launch (start us, length us, event | category | flops | bytes accessed | tf_op | source)
XLA Modules:
  0.0 36.7 jit_solution(13172607540965688912)
XLA Ops:
  0.6 0.0 copy-start.2
  0.6 5.1 %collective-permute-start = (bf16[4,7168]{1,0:T(4,128)(2,1)}, bf16[4,7168]{1,0:T(4,128)(2,1)S(1)}, u32[]{:S(2)}, u32[]{:S(2)}) collective-permute-start(bf16[4,7168]{1,0:T(4,128)(2,1)} %bitcast.11), channel_id=1, source_target_pairs={{0,12},{2,14},{4,8},{6,10},{8,4},{10,6},{12,0},{14,2},{1,13},{3,15... | collective-permute-start | bytes 172040 | tf_op jit(solution)/shard_map/ppermute | solution.py:52
  5.8 0.0 collective-permute-start.1
  5.8 0.6 %collective-permute-start.2 = (bf16[4,7168]{1,0:T(4,128)(2,1)}, bf16[4,7168]{1,0:T(4,128)(2,1)S(1)}, u32[]{:S(2)}, u32[]{:S(2)}) collective-permute-start(bf16[4,7168]{1,0:T(4,128)(2,1)} %bitcast.13), channel_id=1, source_target_pairs={{0,4},{2,6},{4,0},{6,2},{8,12},{10,14},{12,8},{14,10},{1,5},{3,7},... | collective-permute-start | bytes 172040 | tf_op jit(solution)/shard_map/ppermute | solution.py:52
  6.4 2.6 %load_rows.2 = (bf16[384,7168]{1,0:T(8,128)(2,1)S(1)}, bf16[16,16]{1,0:T(8,128)(2,1)S(1)}) custom-call(bf16[1152,7168]{1,0:T(8,128)(2,1)} %refs_0_.3, s32[1,8]{1,0:T(1,128)} %counts_ref.1), custom_call_target="tpu_custom_call" | custom-call | bytes 11010048 | tf_op jit(solution)/shard_map/load_rows/pallas_call | solution.py:183
  9.1 0.0 collective-permute-done.refs_2_
  9.1 2.0 %collective-permute-done.1.refs_3_ = bf16[4,7168]{1,0:T(4,128)(2,1)S(1)} collective-permute-done((bf16[4,7168]{1,0:T(4,128)(2,1)}, bf16[4,7168]{1,0:T(4,128)(2,1)S(1)}, u32[]{:S(2)}, u32[]{:S(2)}) %collective-permute-start.1) | collective-permute-done | bytes 57376 | tf_op jit(solution)/shard_map/ppermute | solution.py:52
  11.0 0.0 collective-permute-done.2.refs_4_
  11.0 0.0 copy-done.2
  11.0 0.2 compact.1
  11.2 0.0 copy-start.3
  11.3 1.6 %collective-permute-start.3 = (bf16[8,7168]{1,0:T(8,128)(2,1)S(1)}, bf16[8,7168]{1,0:T(8,128)(2,1)S(1)}, u32[]{:S(2)}, u32[]{:S(2)}) collective-permute-start(bf16[8,7168]{1,0:T(8,128)(2,1)S(1)} %get-tuple-element.16.refs_2_), channel_id=1, source_target_pairs={{0,2},{2,0},{4,6},{6,4},{8,10},{10,8},{12,14},{14,12},{1,3},{3,1},... | collective-permute-start | bytes 344072 | tf_op jit(solution)/shard_map/ppermute | solution.py:52
  12.8 4.2 %load_rows.3 = (bf16[192,7168]{1,0:T(8,128)(2,1)S(1)}, bf16[576,7168]{1,0:T(8,128)(2,1)S(1)}) custom-call(bf16[1152,7168]{1,0:T(8,128)(2,1)} %refs_0_.3, bf16[1152,7168]{1,0:T(8,128)(2,1)} %refs_1_.3, bf16[8,7168]{1,0:T(8,128)(2,1)S(1)} %get-tuple-element.16.refs_2_), custom_call_target="tpu_custom_call" | custom-call | bytes 22020096 | tf_op jit(solution)/shard_map/load_rows/pallas_call | solution.py:183
  17.1 0.0 collective-permute-done.3
  17.1 0.1 collective-permute-start.4
  17.2 1.3 %collective-permute-done.4.refs_2_ = bf16[8,7168]{1,0:T(8,128)(2,1)S(1)} collective-permute-done((bf16[8,7168]{1,0:T(8,128)(2,1)S(1)}, bf16[8,7168]{1,0:T(8,128)(2,1)S(1)}, u32[]{:S(2)}, u32[]{:S(2)}) %collective-permute-start.4) | collective-permute-done | bytes 114720 | tf_op jit(solution)/shard_map/ppermute | solution.py:52
  18.5 0.0 copy-done.3
  18.5 0.0 copy-start
  18.5 0.0 copy-start.1
  18.5 0.0 copy-start.4
  18.5 0.0 copy-start.5
  18.5 6.1 %feed_forward.1 = (f32[8,7168]{1,0:T(8,128)S(1)}, bf16[8,7168]{1,0:T(8,128)(2,1)S(1)}) custom-call(f32[1,7168]{1,0:T(1,128)S(1)} %bitcast.15, bf16[8,7168]{1,0:T(8,128)(2,1)S(1)} %add.21.refs_1_, bf16[8,7168]{1,0:T(8,128)(2,1)S(1)} %collective-permute-done.4.refs_2_, bf16[384,7168]{1,0:T(8,128)(2,1)S(1)} %get-tuple-element.19.refs_3_, ...), custom_call_target="tpu_custom_call" | custom-call | flops 396361728 | bytes 24772608 | tf_op jit(solution)/shard_map/feed_forward/pallas_call | solution.py:279
  24.6 0.2 collective-permute-start.5
  24.8 1.2 %collective-permute-done.5 = bf16[8,7168]{1,0:T(8,128)(2,1)S(1)} collective-permute-done((bf16[8,7168]{1,0:T(8,128)(2,1)S(1)}, bf16[8,7168]{1,0:T(8,128)(2,1)S(1)}, u32[]{:S(2)}, u32[]{:S(2)}) %collective-permute-start.5) | collective-permute-done | bytes 114720 | tf_op jit(solution)/shard_map/ppermute | solution.py:52
  26.0 0.1 fusion.4
  26.1 1.1 %collective-permute-start.7 = (bf16[2,7168]{1,0:T(2,128)(2,1)S(1)}, bf16[2,7168]{1,0:T(2,128)(2,1)S(1)}, u32[]{:S(2)}, u32[]{:S(2)}) collective-permute-start(bf16[2,7168]{1,0:T(2,128)(2,1)S(1)} %get-tuple-element.28), channel_id=1, source_target_pairs={{0,6},{2,4},{4,2},{6,0},{8,14},{10,12},{12,10},{14,8},{1,15},{3,13... | collective-permute-start | bytes 86024 | tf_op jit(solution)/shard_map/ppermute | solution.py:60
  27.2 1.5 %collective-permute-start.8 = (bf16[2,7168]{1,0:T(2,128)(2,1)S(1)}, bf16[2,7168]{1,0:T(2,128)(2,1)S(1)}, u32[]{:S(2)}, u32[]{:S(2)}) collective-permute-start(bf16[2,7168]{1,0:T(2,128)(2,1)S(1)} %get-tuple-element.30), channel_id=1, source_target_pairs={{0,2},{2,0},{4,6},{6,4},{8,10},{10,8},{12,14},{14,12},{1,11},{3,9}... | collective-permute-start | bytes 86024 | tf_op jit(solution)/shard_map/ppermute | solution.py:60
  28.7 1.0 %collective-permute-start.9 = (bf16[2,7168]{1,0:T(2,128)(2,1)S(1)}, bf16[2,7168]{1,0:T(2,128)(2,1)S(1)}, u32[]{:S(2)}, u32[]{:S(2)}) collective-permute-start(bf16[2,7168]{1,0:T(2,128)(2,1)S(1)} %get-tuple-element.29), channel_id=1, source_target_pairs={{0,4},{2,6},{4,0},{6,2},{8,12},{10,14},{12,8},{14,10},{1,13},{3,15... | collective-permute-start | bytes 86024 | tf_op jit(solution)/shard_map/ppermute | solution.py:60
  29.7 1.1 %collective-permute-start.6 = (bf16[2,7168]{1,0:T(2,128)(2,1)S(1)}, bf16[2,7168]{1,0:T(2,128)(2,1)S(1)}, u32[]{:S(2)}, u32[]{:S(2)}) collective-permute-start(bf16[2,7168]{1,0:T(2,128)(2,1)S(1)} %slice.46), channel_id=1, source_target_pairs={{0,4},{2,6},{4,0},{6,2},{8,12},{10,14},{12,8},{14,10},{1,9},{3,11}... | collective-permute-start | bytes 86024 | tf_op jit(solution)/shard_map/ppermute | solution.py:60
  30.8 0.0 copy-done
  30.8 0.0 copy-done.1
  30.8 0.0 copy-done.4
  30.8 0.0 copy-done.5
  30.8 1.6 %attend.1 = bf16[4,64,512]{2,1,0:T(8,128)(2,1)} custom-call(s32[1,4]{1,0:T(1,128)S(1)} %copy-done.5, s32[1,8]{1,0:T(1,128)S(1)} %copy-done.4, bf16[4,64,576]{2,1,0:T(8,128)(2,1)S(1)} %bitcast.10, bf16[4,576,256]{2,1,0:T(8,128)(2,1)S(1)} %bitcast.9, bf16[8,7168]{1,0:T(8,128)(2,1)S(1)} %get-tuple-element.23._), custom_call_target="tpu_custom_call" | custom-call | flops 134217728 | bytes 1474560 | tf_op jit(solution)/shard_map/attend/pallas_call | solution.py:137
  32.4 0.0 collective-permute-done.7
  32.4 0.0 collective-permute-done.8
  32.4 0.1 collective-permute-done.9
  32.6 1.1 %collective-permute-done.6 = bf16[2,7168]{1,0:T(2,128)(2,1)S(1)} collective-permute-done((bf16[2,7168]{1,0:T(2,128)(2,1)S(1)}, bf16[2,7168]{1,0:T(2,128)(2,1)S(1)}, u32[]{:S(2)}, u32[]{:S(2)}) %collective-permute-start.6) | collective-permute-done | bytes 28704 | tf_op jit(solution)/shard_map/ppermute | solution.py:60
  33.7 0.1 convert_add_fusion.1
  33.8 1.4 %collective-permute-start.10 = (f32[1,7168]{1,0:T(1,128)S(1)}, f32[1,7168]{1,0:T(1,128)S(1)}, u32[]{:S(2)}, u32[]{:S(2)}) collective-permute-start(f32[1,7168]{1,0:T(1,128)S(1)} %slice.29), channel_id=1, source_target_pairs={{0,1},{1,0},{2,3},{3,2},{4,5},{5,4},{6,7},{7,6},{8,9},{9,8},{10,11... | collective-permute-start | bytes 86024 | tf_op jit(solution)/shard_map/ppermute | solution.py:52
  35.2 0.9 %collective-permute-done.10 = f32[1,7168]{1,0:T(1,128)S(1)} collective-permute-done((f32[1,7168]{1,0:T(1,128)S(1)}, f32[1,7168]{1,0:T(1,128)S(1)}, u32[]{:S(2)}, u32[]{:S(2)}) %collective-permute-start.10) | collective-permute-done | bytes 28704 | tf_op jit(solution)/shard_map/ppermute | solution.py:52
  36.1 0.6 %fusion.2 = bf16[1,1,7168]{2,1,0:T(2,128)(2,1)} fusion(bf16[8,7168]{1,0:T(8,128)(2,1)S(1)} %add.21.refs_1_, f32[1,7168]{1,0:T(1,128)S(1)} %collective-permute-done.10, f32[2,7168]{1,0:T(2,128)S(1)} %convert_add_fusion.1), kind=kLoop, calls=%fused_computation.6 | loop fusion | flops 28672 | bytes 86016 | tf_op jit(solution)/shard_map/broadcast_in_dim | solution.py:366
  (4 shorter events, 0.1 us)
Async XLA Ops:
  0.6 10.4 %copy-start.2 = (bf16[1,4,7168]{2,1,0:T(4,128)(2,1)S(1)}, bf16[1,4,7168]{2,1,0:T(4,128)(2,1)}, u32[]{:S(2)}) copy-start(bf16[1,4,7168]{2,1,0:T(4,128)(2,1)} %param.13) | copy-start | bytes 172036
  0.6 8.4 %collective-permute-start = (bf16[4,7168]{1,0:T(4,128)(2,1)}, bf16[4,7168]{1,0:T(4,128)(2,1)S(1)}, u32[]{:S(2)}, u32[]{:S(2)}) collective-permute-start(bf16[4,7168]{1,0:T(4,128)(2,1)} %bitcast.11), channel_id=1, source_target_pairs={{0,12},{2,14},{4,8},{6,10},{8,4},{10,6},{12,0},{14,2},{1,13},{3,15... | collective-permute-start | bytes 172040 | tf_op jit(solution)/shard_map/ppermute | solution.py:52
  5.8 5.3 %collective-permute-start.1 = (bf16[4,7168]{1,0:T(4,128)(2,1)}, bf16[4,7168]{1,0:T(4,128)(2,1)S(1)}, u32[]{:S(2)}, u32[]{:S(2)}) collective-permute-start(bf16[4,7168]{1,0:T(4,128)(2,1)} %bitcast.12), channel_id=1, source_target_pairs={{0,8},{2,10},{4,12},{6,14},{8,0},{10,2},{12,4},{14,6},{1,9},{3,11}... | collective-permute-start | bytes 172040 | tf_op jit(solution)/shard_map/ppermute | solution.py:52
  5.8 5.3 %collective-permute-start.2 = (bf16[4,7168]{1,0:T(4,128)(2,1)}, bf16[4,7168]{1,0:T(4,128)(2,1)S(1)}, u32[]{:S(2)}, u32[]{:S(2)}) collective-permute-start(bf16[4,7168]{1,0:T(4,128)(2,1)} %bitcast.13), channel_id=1, source_target_pairs={{0,4},{2,6},{4,0},{6,2},{8,12},{10,14},{12,8},{14,10},{1,5},{3,7},... | collective-permute-start | bytes 172040 | tf_op jit(solution)/shard_map/ppermute | solution.py:52
  11.2 7.3 %copy-start.3 = (f32[7168]{0:T(1024)S(1)}, f32[7168]{0:T(1024)}, u32[]{:S(2)}) copy-start(f32[7168]{0:T(1024)} %param.14) | copy-start | bytes 86020
  11.3 5.8 %collective-permute-start.3 = (bf16[8,7168]{1,0:T(8,128)(2,1)S(1)}, bf16[8,7168]{1,0:T(8,128)(2,1)S(1)}, u32[]{:S(2)}, u32[]{:S(2)}) collective-permute-start(bf16[8,7168]{1,0:T(8,128)(2,1)S(1)} %get-tuple-element.16.refs_2_), channel_id=1, source_target_pairs={{0,2},{2,0},{4,6},{6,4},{8,10},{10,8},{12,14},{14,12},{1,3},{3,1},... | collective-permute-start | bytes 344072 | tf_op jit(solution)/shard_map/ppermute | solution.py:52
  17.1 1.4 %collective-permute-start.4 = (bf16[8,7168]{1,0:T(8,128)(2,1)S(1)}, bf16[8,7168]{1,0:T(8,128)(2,1)S(1)}, u32[]{:S(2)}, u32[]{:S(2)}) collective-permute-start(bf16[8,7168]{1,0:T(8,128)(2,1)S(1)} %add.21.refs_1_), channel_id=1, source_target_pairs={{0,1},{1,0},{2,3},{3,2},{4,5},{5,4},{6,7},{7,6},{8,9},{9,8},{10,11... | collective-permute-start | bytes 344072 | tf_op jit(solution)/shard_map/ppermute | solution.py:52
  18.5 12.3 %copy-start = (bf16[1,4,256,576]{2,3,1,0:T(8,128)(2,1)S(1)}, bf16[1,4,256,576]{2,3,1,0:T(8,128)(2,1)}, u32[]{:S(2)}) copy-start(bf16[1,4,256,576]{2,3,1,0:T(8,128)(2,1)} %param.10) | copy-start | bytes 3538948
  18.5 12.3 %copy-start.1 = (bf16[1,4,64,576]{3,2,1,0:T(8,128)(2,1)S(1)}, bf16[1,4,64,576]{3,2,1,0:T(8,128)(2,1)}, u32[]{:S(2)}) copy-start(bf16[1,4,64,576]{3,2,1,0:T(8,128)(2,1)} %param.9) | copy-start | bytes 884740
  18.5 12.3 %copy-start.4 = (s32[1,8]{1,0:T(1,128)S(1)}, s32[1,8]{1,0:T(1,128)}, u32[]{:S(2)}) copy-start(s32[1,8]{1,0:T(1,128)} %counts_ref.1) | copy-start | bytes 100
  18.5 12.3 %copy-start.5 = (s32[1,4]{1,0:T(1,128)S(1)}, s32[1,4]{1,0:T(1,128)}, u32[]{:S(2)}) copy-start(s32[1,4]{1,0:T(1,128)} %lengths_ref.1) | copy-start | bytes 52
  24.6 1.4 %collective-permute-start.5 = (bf16[8,7168]{1,0:T(8,128)(2,1)S(1)}, bf16[8,7168]{1,0:T(8,128)(2,1)S(1)}, u32[]{:S(2)}, u32[]{:S(2)}) collective-permute-start(bf16[8,7168]{1,0:T(8,128)(2,1)S(1)} %get-tuple-element.23._), channel_id=1, source_target_pairs={{0,1},{1,0},{2,3},{3,2},{4,5},{5,4},{6,7},{7,6},{8,9},{9,8},{10,11... | collective-permute-start | bytes 344072 | tf_op jit(solution)/shard_map/ppermute | solution.py:52
  26.1 6.3 %collective-permute-start.7 = (bf16[2,7168]{1,0:T(2,128)(2,1)S(1)}, bf16[2,7168]{1,0:T(2,128)(2,1)S(1)}, u32[]{:S(2)}, u32[]{:S(2)}) collective-permute-start(bf16[2,7168]{1,0:T(2,128)(2,1)S(1)} %get-tuple-element.28), channel_id=1, source_target_pairs={{0,6},{2,4},{4,2},{6,0},{8,14},{10,12},{12,10},{14,8},{1,15},{3,13... | collective-permute-start | bytes 86024 | tf_op jit(solution)/shard_map/ppermute | solution.py:60
  27.2 5.2 %collective-permute-start.8 = (bf16[2,7168]{1,0:T(2,128)(2,1)S(1)}, bf16[2,7168]{1,0:T(2,128)(2,1)S(1)}, u32[]{:S(2)}, u32[]{:S(2)}) collective-permute-start(bf16[2,7168]{1,0:T(2,128)(2,1)S(1)} %get-tuple-element.30), channel_id=1, source_target_pairs={{0,2},{2,0},{4,6},{6,4},{8,10},{10,8},{12,14},{14,12},{1,11},{3,9}... | collective-permute-start | bytes 86024 | tf_op jit(solution)/shard_map/ppermute | solution.py:60
  28.7 3.9 %collective-permute-start.9 = (bf16[2,7168]{1,0:T(2,128)(2,1)S(1)}, bf16[2,7168]{1,0:T(2,128)(2,1)S(1)}, u32[]{:S(2)}, u32[]{:S(2)}) collective-permute-start(bf16[2,7168]{1,0:T(2,128)(2,1)S(1)} %get-tuple-element.29), channel_id=1, source_target_pairs={{0,4},{2,6},{4,0},{6,2},{8,12},{10,14},{12,8},{14,10},{1,13},{3,15... | collective-permute-start | bytes 86024 | tf_op jit(solution)/shard_map/ppermute | solution.py:60
  29.7 4.0 %collective-permute-start.6 = (bf16[2,7168]{1,0:T(2,128)(2,1)S(1)}, bf16[2,7168]{1,0:T(2,128)(2,1)S(1)}, u32[]{:S(2)}, u32[]{:S(2)}) collective-permute-start(bf16[2,7168]{1,0:T(2,128)(2,1)S(1)} %slice.46), channel_id=1, source_target_pairs={{0,4},{2,6},{4,0},{6,2},{8,12},{10,14},{12,8},{14,10},{1,9},{3,11}... | collective-permute-start | bytes 86024 | tf_op jit(solution)/shard_map/ppermute | solution.py:60
  33.8 2.3 %collective-permute-start.10 = (f32[1,7168]{1,0:T(1,128)S(1)}, f32[1,7168]{1,0:T(1,128)S(1)}, u32[]{:S(2)}, u32[]{:S(2)}) collective-permute-start(f32[1,7168]{1,0:T(1,128)S(1)} %slice.29), channel_id=1, source_target_pairs={{0,1},{1,0},{2,3},{3,2},{4,5},{5,4},{6,7},{7,6},{8,9},{9,8},{10,11... | collective-permute-start | bytes 86024 | tf_op jit(solution)/shard_map/ppermute | solution.py:52

commit v9 on v8

--- a/solution.py
+++ b/solution.py
@@ -82,8 +82,8 @@
         row_copy(*copy, i).wait()
 
 
-def pieces_of(rows, most):
-    return most if rows % (16 * most) == 0 else 1
+def pieces_of(rows):
+    return 2 if rows % 32 == 0 else 1
 
 
 def share_start(units, share):
@@ -149,12 +149,12 @@
     )(lengths, counts, queries, cache, after)
 
 
-def load_rows(jobs, share, after=None, counts=None, slots=0, stages=()):
+def load_rows(weight, share, after=None, counts=None, slots=0, stages=()):
     size = 0 if counts is None else counts.shape[1]
-    pieces = [pieces_of(rows, 2) for _, _, rows in jobs]
-    operands = [pinned(weight) for weight, _, _ in jobs]
-    out_shape = [pltpu.VMEM((rows, weight.shape[1]), weight.dtype) for weight, _, rows in jobs]
-    scratch = [pltpu.SemaphoreType.DMA((count,)) for count in pieces]
+    units, width = weight.shape
+    operands = [pinned(weight)]
+    out_shape = [pltpu.VMEM((share, width), weight.dtype)]
+    scratch = [pltpu.SemaphoreType.DMA((pieces_of(share),))]
     if counts is not None:
         operands.append(pinned(counts))
         out_shape.append(jax.ShapeDtypeStruct((2 * size, size // 2 * slots), jnp.bfloat16))
@@ -164,21 +164,16 @@
 
     def body(*refs):
         sources, refs = refs[: len(operands)], refs[len(operands) :]
-        targets, refs = refs[: len(out_shape)], refs[len(out_shape) :]
+        targets, (sems, *small_refs) = refs[: len(out_shape)], refs[len(out_shape) :]
         if counts is not None:
-            small = pltpu.make_async_copy(sources[len(jobs)], refs[-2], refs[-1])
+            small = pltpu.make_async_copy(sources[1], *small_refs)
             small.start()
-        copies = [
-            (source, share_start(weight.shape[0], share) + first, target, sems)
-            for (weight, first, _), source, target, sems in zip(jobs, sources, targets, refs)
-        ]
-        for copy in copies:
-            start_pieces(copy)
+        copy = (sources[0], share_start(units, share), targets[0], sems)
+        start_pieces(copy)
         if counts is not None:
             small.wait()
-            targets[-1][...] = pick_matrix(refs[-2][...], lax.axis_index("tp"), size, slots, stages)
-        for copy in copies:
-            wait_pieces(copy)
+            targets[1][...] = pick_matrix(small_refs[0][...], lax.axis_index("tp"), size, slots, stages)
+        wait_pieces(copy)
 
     return pl.pallas_call(
         body,
@@ -187,9 +182,7 @@
         out_specs=[VMEM] * len(out_shape),
         scratch_shapes=scratch,
         compiler_params=pltpu.CompilerParams(vmem_limit_bytes=2 * MIB),
-        cost_estimate=pl.CostEstimate(
-            flops=0, transcendentals=0, bytes_accessed=sum(4 * rows * weight.shape[1] for weight, _, rows in jobs)
-        ),
+        cost_estimate=pl.CostEstimate(flops=0, transcendentals=0, bytes_accessed=4 * share * width),
         name="load_rows",
     )(*operands)
 
@@ -221,20 +214,19 @@
     )(pick, *blocks)
 
 
-def feed_forward(gain, row_sets, loaded, w_down, share):
+def feed_forward(gain, row_sets, gate, up, w_down):
     requests, width = row_sets[0].shape
     units = w_down.shape[0]
+    share = gate.shape[0]
     set_count = len(row_sets)
     every = requests * set_count
     column = 512
-    pieces = pieces_of(share, 4)
-    parts = [part for _, _, part in loaded]
+    chunk = 192 if share % 192 == 0 else share
 
     def body(*refs):
         gain_ref, refs = refs[0], refs[1:]
         set_refs, refs = refs[:set_count], refs[set_count:]
-        part_refs, refs = refs[: len(parts)], refs[len(parts) :]
-        down_hbm, refs = refs[0], refs[1:]
+        gate_weight, up_weight, down_hbm, *refs = refs
         out_refs, refs = refs[:set_count], refs[set_count:]
         normed_ref, gate_ref, up_ref, hidden_ref, down_ref, down_sems = refs
 
@@ -246,12 +238,10 @@
         inv_rms = lax.rsqrt(jnp.mean(rows * rows, axis=1, keepdims=True) + norm_eps)
         normed_ref[...] = (rows * inv_rms * gain_ref[...]).astype(jnp.bfloat16)
 
-        for (which, first, _), ref in zip(loaded, part_refs):
-            count = ref.shape[0]
-            chunk = next((c for c in (192, 160, 128, 64) if count % c == 0), count)
-            for j in range(0, count, chunk):
-                (gate_ref, up_ref)[which][first + j : first + j + chunk, :] = lax.dot_general(
-                    ref[j : j + chunk, :], normed_ref[...], (((1,), (1,)), ((), ())), preferred_element_type=jnp.float32
+        for weight_ref, out_ref in ((gate_weight, gate_ref), (up_weight, up_ref)):
+            for j in range(0, share, chunk):
+                out_ref[j : j + chunk, :] = lax.dot_general(
+                    weight_ref[j : j + chunk, :], normed_ref[...], (((1,), (1,)), ((), ())), preferred_element_type=jnp.float32
                 )
         hidden = (jax.nn.silu(gate_ref[...]) * up_ref[...]).astype(jnp.bfloat16)
         place = lax.broadcasted_iota(jnp.int32, (every, every), 0)
@@ -279,7 +269,7 @@
     return pl.pallas_call(
         body,
         out_shape=outs,
-        in_specs=[VMEM] * (1 + set_count + len(parts)) + [ANY],
+        in_specs=[VMEM] * (3 + set_count) + [ANY],
         out_specs=[VMEM] * set_count,
         scratch_shapes=[
             pltpu.VMEM((every, width), jnp.bfloat16),
@@ -287,7 +277,7 @@
             pltpu.VMEM((share, every), jnp.float32),
             pltpu.VMEM((every, share), jnp.bfloat16),
             pltpu.VMEM((share, width), jnp.bfloat16),
-            pltpu.SemaphoreType.DMA((pieces,)),
+            pltpu.SemaphoreType.DMA((pieces_of(share),)),
         ],
         compiler_params=pltpu.CompilerParams(vmem_limit_bytes=24 * MIB),
         cost_estimate=pl.CostEstimate(
@@ -296,14 +286,7 @@
             bytes_accessed=6 * share * width,
         ),
         name="feed_forward",
-    )(gain[None], *row_sets, *parts, pinned(w_down))
-
-
-def load_plan(share):
-    if share % 192:
-        return [(0, 0, share)], [(1, 0, share)]
-    early = share // 3 * 2
-    return [(0, 0, early)], [(0, early, share - early), (1, 0, share)]
+    )(gain[None], *row_sets, gate, up, pinned(w_down))
 
 
 def make_shards(size, cores):
@@ -314,33 +297,22 @@
         units = w_gate.shape[0]
         split = cores == 2 and size == 8 and units % 32 == 0
         share = units // 2 if split else units
-        weights = (w_gate, w_up)
         stages = [(0, bits)] if split else sum_stages(bits)
-        plan = load_plan(share)
-        loaded = []
-
-        def load(jobs, **more):
-            parts = load_rows([(weights[which], first, rows) for which, first, rows in jobs], share, **more)
-            loaded.extend((which, first, part) for (which, first, _), part in zip(jobs, parts))
-            return parts[-1]
-
         block = stream[0]
         for step, (low, width) in enumerate(gather_stages(bits)):
             blocks = [block] + [swap(block, "tp", digit << low, size) for digit in range((1 << width) - 1, 0, -1)]
             if step == 0:
-                pick = load(plan[0], counts=live_counts, slots=slots, stages=stages)
+                gate, pick = load_rows(w_gate, share, counts=live_counts, slots=slots, stages=stages)
             if low > 1:
                 block = jnp.concatenate(blocks, axis=0)
 
         own, send = compact(pick, blocks)
         arrived = swap(send, "tp", 1, size)
-        load(plan[1], after=send)
-        *last, part = loaded[-1]
-        arrived, part = lax.optimization_barrier((arrived, part))
-        loaded[-1] = (*last, part)
+        (up,) = load_rows(w_up, share, after=send)
+        arrived, up = lax.optimization_barrier((arrived, up))
         rows = own + arrived
         row_sets = [rows, swap(rows, "sub", 1, cores)] if split else [rows]
-        total, *other = feed_forward(norm_gain, row_sets, loaded, w_down, share)
+        total, *other = feed_forward(norm_gain, row_sets, gate, up, w_down)
 
         cache = jnp.swapaxes(kv_cache[0], 1, 2)
         after = other[0] if split else total

time: 36.9 us -> 36 us (0.976)
  waiting for transfers between devices: 6.58 us -> 5.73 us
    ppermute x7, waiting for transfers between devices: 5.33 us -> 4.5 us  [swap(): return lax.ppermute(x, axis, [(i, i ^ distance) for i in range(size)])]
  transfers between devices with their start and end apart: 11 -> 11, of which waited for: 6 -> 6; matrix products, arithmetic and copies ran while one was open for 0% -> 0% of each run, Pallas kernels for 23% -> 24%
where the time goes in v9:
time: 36 us; the launch traced here: 35.9 us
  Pallas kernels  14.7 us (41%)
  starting transfers between devices  13.7 us (38%)
  waiting for transfers between devices  5.73 us (16%)
  other arithmetic  0.77 us (2%)
  between operations  0.76 us (2%)
    ppermute x7, starting transfers between devices, swap(): return lax.ppermute(x, axis, [(i, i ^ distance) for i in range(size)])  9.04 us
    pallas_call x2, Pallas kernels, load_rows(): pl.pallas_call(body, out_shape=out_shape, in_specs=[ANY] * len(operands),...  6.91 us
    pallas_call x1, Pallas kernels, feed_forward(): pl.pallas_call(body, out_shape=outs, in_specs=[VMEM] * (3 + set_count) +...  6.04 us
    ppermute x4, starting transfers between devices, direct_swap(): return lax.ppermute(x, ('tp', 'sub'), pairs)  4.67 us
    ppermute x7, waiting for transfers between devices, swap(): return lax.ppermute(x, axis, [(i, i ^ distance) for i in range(size)])  4.5 us
    pallas_call x1, Pallas kernels, attend(): pl.pallas_call(body, out_shape=jax.ShapeDtypeStruct((slots, heads, KVL),...  1.6 us
    ppermute x4, waiting for transfers between devices, direct_swap(): return lax.ppermute(x, ('tp', 'sub'), pairs)  1.23 us
  transfers between devices with their start and end apart: 11, of which 6 were waited for; matrix products, arithmetic and copies ran while one was open for 0% of the time, Pallas kernels for 24%

profile of v9, /device:TPU:0, one launch (start us, length us, event | category | flops | bytes accessed | tf_op | source)
XLA Modules:
  0.0 35.9 jit_solution(16179126038172057238)
XLA Ops:
  0.6 0.0 copy-start.2
  0.6 5.1 %collective-permute-start = (bf16[4,7168]{1,0:T(4,128)(2,1)}, bf16[4,7168]{1,0:T(4,128)(2,1)S(1)}, u32[]{:S(2)}, u32[]{:S(2)}) collective-permute-start(bf16[4,7168]{1,0:T(4,128)(2,1)} %bitcast.11), channel_id=1, source_target_pairs={{0,12},{2,14},{4,8},{6,10},{8,4},{10,6},{12,0},{14,2},{1,13},{3,15... | collective-permute-start | bytes 172040 | tf_op jit(solution)/shard_map/ppermute | solution.py:52
  5.8 0.0 collective-permute-start.1
  5.8 0.6 %collective-permute-start.2 = (bf16[4,7168]{1,0:T(4,128)(2,1)}, bf16[4,7168]{1,0:T(4,128)(2,1)S(1)}, u32[]{:S(2)}, u32[]{:S(2)}) collective-permute-start(bf16[4,7168]{1,0:T(4,128)(2,1)} %bitcast.13), channel_id=1, source_target_pairs={{0,4},{2,6},{4,0},{6,2},{8,12},{10,14},{12,8},{14,10},{1,5},{3,7},... | collective-permute-start | bytes 172040 | tf_op jit(solution)/shard_map/ppermute | solution.py:52
  6.4 3.5 %load_rows.2 = (bf16[576,7168]{1,0:T(8,128)(2,1)S(1)}, bf16[16,16]{1,0:T(8,128)(2,1)S(1)}) custom-call(bf16[1152,7168]{1,0:T(8,128)(2,1)} %refs_0_.2, s32[1,8]{1,0:T(1,128)} %counts_ref.1), custom_call_target="tpu_custom_call" | custom-call | bytes 16515072 | tf_op jit(solution)/shard_map/load_rows/pallas_call | solution.py:178
  9.9 0.0 copy-start.3
  9.9 0.0 collective-permute-done.refs_2_
  9.9 1.1 %collective-permute-done.1.refs_3_ = bf16[4,7168]{1,0:T(4,128)(2,1)S(1)} collective-permute-done((bf16[4,7168]{1,0:T(4,128)(2,1)}, bf16[4,7168]{1,0:T(4,128)(2,1)S(1)}, u32[]{:S(2)}, u32[]{:S(2)}) %collective-permute-start.1) | collective-permute-done | bytes 57376 | tf_op jit(solution)/shard_map/ppermute | solution.py:52
  11.0 0.0 collective-permute-done.2.refs_4_
  11.0 0.0 copy-done.2
  11.0 0.2 compact.1
  11.2 1.6 %collective-permute-start.3 = (bf16[8,7168]{1,0:T(8,128)(2,1)S(1)}, bf16[8,7168]{1,0:T(8,128)(2,1)S(1)}, u32[]{:S(2)}, u32[]{:S(2)}) collective-permute-start(bf16[8,7168]{1,0:T(8,128)(2,1)S(1)} %get-tuple-element.14.refs_1_), channel_id=1, source_target_pairs={{0,2},{2,0},{4,6},{6,4},{8,10},{10,8},{12,14},{14,12},{1,3},{3,1},... | collective-permute-start | bytes 344072 | tf_op jit(solution)/shard_map/ppermute | solution.py:52
  12.8 3.4 %load_rows.3.refs_4_ = bf16[576,7168]{1,0:T(8,128)(2,1)S(1)} custom-call(bf16[1152,7168]{1,0:T(8,128)(2,1)} %refs_0_.3, bf16[8,7168]{1,0:T(8,128)(2,1)S(1)} %get-tuple-element.14.refs_1_), custom_call_target="tpu_custom_call" | custom-call | bytes 16515072 | tf_op jit(solution)/shard_map/load_rows/pallas_call | solution.py:178
  16.3 0.0 collective-permute-done.3
  16.3 0.1 collective-permute-start.4
  16.4 1.3 %collective-permute-done.4.refs_2_ = bf16[8,7168]{1,0:T(8,128)(2,1)S(1)} collective-permute-done((bf16[8,7168]{1,0:T(8,128)(2,1)S(1)}, bf16[8,7168]{1,0:T(8,128)(2,1)S(1)}, u32[]{:S(2)}, u32[]{:S(2)}) %collective-permute-start.4) | collective-permute-done | bytes 114720 | tf_op jit(solution)/shard_map/ppermute | solution.py:52
  17.7 0.0 copy-done.3
  17.7 0.0 copy-start
  17.7 0.0 copy-start.1
  17.7 0.0 copy-start.4
  17.7 0.0 copy-start.5
  17.7 6.0 %feed_forward.1 = (f32[8,7168]{1,0:T(8,128)S(1)}, bf16[8,7168]{1,0:T(8,128)(2,1)S(1)}) custom-call(f32[1,7168]{1,0:T(1,128)S(1)} %bitcast.15, bf16[8,7168]{1,0:T(8,128)(2,1)S(1)} %add.21.refs_1_, bf16[8,7168]{1,0:T(8,128)(2,1)S(1)} %collective-permute-done.4.refs_2_, bf16[576,7168]{1,0:T(8,128)(2,1)S(1)} %get-tuple-element.16.refs_3_, ...), custom_call_target="tpu_custom_call" | custom-call | flops 396361728 | bytes 24772608 | tf_op jit(solution)/shard_map/feed_forward/pallas_call | solution.py:269
  23.8 0.2 collective-permute-start.5
  24.0 1.2 %collective-permute-done.5 = bf16[8,7168]{1,0:T(8,128)(2,1)S(1)} collective-permute-done((bf16[8,7168]{1,0:T(8,128)(2,1)S(1)}, bf16[8,7168]{1,0:T(8,128)(2,1)S(1)}, u32[]{:S(2)}, u32[]{:S(2)}) %collective-permute-start.5) | collective-permute-done | bytes 114720 | tf_op jit(solution)/shard_map/ppermute | solution.py:52
  25.2 0.1 fusion.4
  25.3 1.9 %collective-permute-start.7 = (bf16[2,7168]{1,0:T(2,128)(2,1)S(1)}, bf16[2,7168]{1,0:T(2,128)(2,1)S(1)}, u32[]{:S(2)}, u32[]{:S(2)}) collective-permute-start(bf16[2,7168]{1,0:T(2,128)(2,1)S(1)} %get-tuple-element.24), channel_id=1, source_target_pairs={{0,6},{2,4},{4,2},{6,0},{8,14},{10,12},{12,10},{14,8},{1,15},{3,13... | collective-permute-start | bytes 86024 | tf_op jit(solution)/shard_map/ppermute | solution.py:60
  27.2 0.7 %collective-permute-start.8 = (bf16[2,7168]{1,0:T(2,128)(2,1)S(1)}, bf16[2,7168]{1,0:T(2,128)(2,1)S(1)}, u32[]{:S(2)}, u32[]{:S(2)}) collective-permute-start(bf16[2,7168]{1,0:T(2,128)(2,1)S(1)} %get-tuple-element.26), channel_id=1, source_target_pairs={{0,2},{2,0},{4,6},{6,4},{8,10},{10,8},{12,14},{14,12},{1,11},{3,9}... | collective-permute-start | bytes 86024 | tf_op jit(solution)/shard_map/ppermute | solution.py:60
  27.9 1.0 %collective-permute-start.9 = (bf16[2,7168]{1,0:T(2,128)(2,1)S(1)}, bf16[2,7168]{1,0:T(2,128)(2,1)S(1)}, u32[]{:S(2)}, u32[]{:S(2)}) collective-permute-start(bf16[2,7168]{1,0:T(2,128)(2,1)S(1)} %get-tuple-element.25), channel_id=1, source_target_pairs={{0,4},{2,6},{4,0},{6,2},{8,12},{10,14},{12,8},{14,10},{1,13},{3,15... | collective-permute-start | bytes 86024 | tf_op jit(solution)/shard_map/ppermute | solution.py:60
  28.9 1.1 %collective-permute-start.6 = (bf16[2,7168]{1,0:T(2,128)(2,1)S(1)}, bf16[2,7168]{1,0:T(2,128)(2,1)S(1)}, u32[]{:S(2)}, u32[]{:S(2)}) collective-permute-start(bf16[2,7168]{1,0:T(2,128)(2,1)S(1)} %slice.46), channel_id=1, source_target_pairs={{0,4},{2,6},{4,0},{6,2},{8,12},{10,14},{12,8},{14,10},{1,9},{3,11}... | collective-permute-start | bytes 86024 | tf_op jit(solution)/shard_map/ppermute | solution.py:60
  30.0 0.0 copy-done
  30.0 0.0 copy-done.1
  30.0 0.0 copy-done.4
  30.0 0.0 copy-done.5
  30.0 1.6 %attend.1 = bf16[4,64,512]{2,1,0:T(8,128)(2,1)} custom-call(s32[1,4]{1,0:T(1,128)S(1)} %copy-done.5, s32[1,8]{1,0:T(1,128)S(1)} %copy-done.4, bf16[4,64,576]{2,1,0:T(8,128)(2,1)S(1)} %bitcast.10, bf16[4,576,256]{2,1,0:T(8,128)(2,1)S(1)} %bitcast.9, bf16[8,7168]{1,0:T(8,128)(2,1)S(1)} %get-tuple-element.19._), custom_call_target="tpu_custom_call" | custom-call | flops 134217728 | bytes 1474560 | tf_op jit(solution)/shard_map/attend/pallas_call | solution.py:137
  31.6 0.0 collective-permute-done.7
  31.6 0.0 collective-permute-done.8
  31.6 0.1 collective-permute-done.9
  31.8 1.1 %collective-permute-done.6 = bf16[2,7168]{1,0:T(2,128)(2,1)S(1)} collective-permute-done((bf16[2,7168]{1,0:T(2,128)(2,1)S(1)}, bf16[2,7168]{1,0:T(2,128)(2,1)S(1)}, u32[]{:S(2)}, u32[]{:S(2)}) %collective-permute-start.6) | collective-permute-done | bytes 28704 | tf_op jit(solution)/shard_map/ppermute | solution.py:60
  32.9 0.1 convert_add_fusion.1
  33.0 1.4 %collective-permute-start.10 = (f32[1,7168]{1,0:T(1,128)S(1)}, f32[1,7168]{1,0:T(1,128)S(1)}, u32[]{:S(2)}, u32[]{:S(2)}) collective-permute-start(f32[1,7168]{1,0:T(1,128)S(1)} %slice.29), channel_id=1, source_target_pairs={{0,1},{1,0},{2,3},{3,2},{4,5},{5,4},{6,7},{7,6},{8,9},{9,8},{10,11... | collective-permute-start | bytes 86024 | tf_op jit(solution)/shard_map/ppermute | solution.py:52
  34.4 0.9 %collective-permute-done.10 = f32[1,7168]{1,0:T(1,128)S(1)} collective-permute-done((f32[1,7168]{1,0:T(1,128)S(1)}, f32[1,7168]{1,0:T(1,128)S(1)}, u32[]{:S(2)}, u32[]{:S(2)}) %collective-permute-start.10) | collective-permute-done | bytes 28704 | tf_op jit(solution)/shard_map/ppermute | solution.py:52
  35.2 0.6 %fusion.2 = bf16[1,1,7168]{2,1,0:T(2,128)(2,1)} fusion(bf16[8,7168]{1,0:T(8,128)(2,1)S(1)} %add.21.refs_1_, f32[1,7168]{1,0:T(1,128)S(1)} %collective-permute-done.10, f32[2,7168]{1,0:T(2,128)S(1)} %convert_add_fusion.1), kind=kLoop, calls=%fused_computation.6 | loop fusion | flops 28672 | bytes 86016 | tf_op jit(solution)/shard_map/broadcast_in_dim | solution.py:338
  (4 shorter events, 0.1 us)
Async XLA Ops:
  0.6 10.4 %copy-start.2 = (bf16[1,4,7168]{2,1,0:T(4,128)(2,1)S(1)}, bf16[1,4,7168]{2,1,0:T(4,128)(2,1)}, u32[]{:S(2)}) copy-start(bf16[1,4,7168]{2,1,0:T(4,128)(2,1)} %param.13) | copy-start | bytes 172036
  0.6 9.2 %collective-permute-start = (bf16[4,7168]{1,0:T(4,128)(2,1)}, bf16[4,7168]{1,0:T(4,128)(2,1)S(1)}, u32[]{:S(2)}, u32[]{:S(2)}) collective-permute-start(bf16[4,7168]{1,0:T(4,128)(2,1)} %bitcast.11), channel_id=1, source_target_pairs={{0,12},{2,14},{4,8},{6,10},{8,4},{10,6},{12,0},{14,2},{1,13},{3,15... | collective-permute-start | bytes 172040 | tf_op jit(solution)/shard_map/ppermute | solution.py:52
  5.8 5.3 %collective-permute-start.1 = (bf16[4,7168]{1,0:T(4,128)(2,1)}, bf16[4,7168]{1,0:T(4,128)(2,1)S(1)}, u32[]{:S(2)}, u32[]{:S(2)}) collective-permute-start(bf16[4,7168]{1,0:T(4,128)(2,1)} %bitcast.12), channel_id=1, source_target_pairs={{0,8},{2,10},{4,12},{6,14},{8,0},{10,2},{12,4},{14,6},{1,9},{3,11}... | collective-permute-start | bytes 172040 | tf_op jit(solution)/shard_map/ppermute | solution.py:52
  5.8 5.3 %collective-permute-start.2 = (bf16[4,7168]{1,0:T(4,128)(2,1)}, bf16[4,7168]{1,0:T(4,128)(2,1)S(1)}, u32[]{:S(2)}, u32[]{:S(2)}) collective-permute-start(bf16[4,7168]{1,0:T(4,128)(2,1)} %bitcast.13), channel_id=1, source_target_pairs={{0,4},{2,6},{4,0},{6,2},{8,12},{10,14},{12,8},{14,10},{1,5},{3,7},... | collective-permute-start | bytes 172040 | tf_op jit(solution)/shard_map/ppermute | solution.py:52
  9.9 7.9 %copy-start.3 = (f32[7168]{0:T(1024)S(1)}, f32[7168]{0:T(1024)}, u32[]{:S(2)}) copy-start(f32[7168]{0:T(1024)} %param.14) | copy-start | bytes 86020
  11.2 5.0 %collective-permute-start.3 = (bf16[8,7168]{1,0:T(8,128)(2,1)S(1)}, bf16[8,7168]{1,0:T(8,128)(2,1)S(1)}, u32[]{:S(2)}, u32[]{:S(2)}) collective-permute-start(bf16[8,7168]{1,0:T(8,128)(2,1)S(1)} %get-tuple-element.14.refs_1_), channel_id=1, source_target_pairs={{0,2},{2,0},{4,6},{6,4},{8,10},{10,8},{12,14},{14,12},{1,3},{3,1},... | collective-permute-start | bytes 344072 | tf_op jit(solution)/shard_map/ppermute | solution.py:52
  16.3 1.4 %collective-permute-start.4 = (bf16[8,7168]{1,0:T(8,128)(2,1)S(1)}, bf16[8,7168]{1,0:T(8,128)(2,1)S(1)}, u32[]{:S(2)}, u32[]{:S(2)}) collective-permute-start(bf16[8,7168]{1,0:T(8,128)(2,1)S(1)} %add.21.refs_1_), channel_id=1, source_target_pairs={{0,1},{1,0},{2,3},{3,2},{4,5},{5,4},{6,7},{7,6},{8,9},{9,8},{10,11... | collective-permute-start | bytes 344072 | tf_op jit(solution)/shard_map/ppermute | solution.py:52
  17.7 12.3 %copy-start = (bf16[1,4,256,576]{2,3,1,0:T(8,128)(2,1)S(1)}, bf16[1,4,256,576]{2,3,1,0:T(8,128)(2,1)}, u32[]{:S(2)}) copy-start(bf16[1,4,256,576]{2,3,1,0:T(8,128)(2,1)} %param.10) | copy-start | bytes 3538948
  17.7 12.3 %copy-start.1 = (bf16[1,4,64,576]{3,2,1,0:T(8,128)(2,1)S(1)}, bf16[1,4,64,576]{3,2,1,0:T(8,128)(2,1)}, u32[]{:S(2)}) copy-start(bf16[1,4,64,576]{3,2,1,0:T(8,128)(2,1)} %param.9) | copy-start | bytes 884740
  17.7 12.3 %copy-start.4 = (s32[1,8]{1,0:T(1,128)S(1)}, s32[1,8]{1,0:T(1,128)}, u32[]{:S(2)}) copy-start(s32[1,8]{1,0:T(1,128)} %counts_ref.1) | copy-start | bytes 100
  17.7 12.3 %copy-start.5 = (s32[1,4]{1,0:T(1,128)S(1)}, s32[1,4]{1,0:T(1,128)}, u32[]{:S(2)}) copy-start(s32[1,4]{1,0:T(1,128)} %lengths_ref.1) | copy-start | bytes 52
  23.8 1.4 %collective-permute-start.5 = (bf16[8,7168]{1,0:T(8,128)(2,1)S(1)}, bf16[8,7168]{1,0:T(8,128)(2,1)S(1)}, u32[]{:S(2)}, u32[]{:S(2)}) collective-permute-start(bf16[8,7168]{1,0:T(8,128)(2,1)S(1)} %get-tuple-element.19._), channel_id=1, source_target_pairs={{0,1},{1,0},{2,3},{3,2},{4,5},{5,4},{6,7},{7,6},{8,9},{9,8},{10,11... | collective-permute-start | bytes 344072 | tf_op jit(solution)/shard_map/ppermute | solution.py:52
  25.3 6.3 %collective-permute-start.7 = (bf16[2,7168]{1,0:T(2,128)(2,1)S(1)}, bf16[2,7168]{1,0:T(2,128)(2,1)S(1)}, u32[]{:S(2)}, u32[]{:S(2)}) collective-permute-start(bf16[2,7168]{1,0:T(2,128)(2,1)S(1)} %get-tuple-element.24), channel_id=1, source_target_pairs={{0,6},{2,4},{4,2},{6,0},{8,14},{10,12},{12,10},{14,8},{1,15},{3,13... | collective-permute-start | bytes 86024 | tf_op jit(solution)/shard_map/ppermute | solution.py:60
  27.2 4.4 %collective-permute-start.8 = (bf16[2,7168]{1,0:T(2,128)(2,1)S(1)}, bf16[2,7168]{1,0:T(2,128)(2,1)S(1)}, u32[]{:S(2)}, u32[]{:S(2)}) collective-permute-start(bf16[2,7168]{1,0:T(2,128)(2,1)S(1)} %get-tuple-element.26), channel_id=1, source_target_pairs={{0,2},{2,0},{4,6},{6,4},{8,10},{10,8},{12,14},{14,12},{1,11},{3,9}... | collective-permute-start | bytes 86024 | tf_op jit(solution)/shard_map/ppermute | solution.py:60
  27.9 3.9 %collective-permute-start.9 = (bf16[2,7168]{1,0:T(2,128)(2,1)S(1)}, bf16[2,7168]{1,0:T(2,128)(2,1)S(1)}, u32[]{:S(2)}, u32[]{:S(2)}) collective-permute-start(bf16[2,7168]{1,0:T(2,128)(2,1)S(1)} %get-tuple-element.25), channel_id=1, source_target_pairs={{0,4},{2,6},{4,0},{6,2},{8,12},{10,14},{12,8},{14,10},{1,13},{3,15... | collective-permute-start | bytes 86024 | tf_op jit(solution)/shard_map/ppermute | solution.py:60
  28.9 4.0 %collective-permute-start.6 = (bf16[2,7168]{1,0:T(2,128)(2,1)S(1)}, bf16[2,7168]{1,0:T(2,128)(2,1)S(1)}, u32[]{:S(2)}, u32[]{:S(2)}) collective-permute-start(bf16[2,7168]{1,0:T(2,128)(2,1)S(1)} %slice.46), channel_id=1, source_target_pairs={{0,4},{2,6},{4,0},{6,2},{8,12},{10,14},{12,8},{14,10},{1,9},{3,11}... | collective-permute-start | bytes 86024 | tf_op jit(solution)/shard_map/ppermute | solution.py:60
  33.0 2.3 %collective-permute-start.10 = (f32[1,7168]{1,0:T(1,128)S(1)}, f32[1,7168]{1,0:T(1,128)S(1)}, u32[]{:S(2)}, u32[]{:S(2)}) collective-permute-start(f32[1,7168]{1,0:T(1,128)S(1)} %slice.29), channel_id=1, source_target_pairs={{0,1},{1,0},{2,3},{3,2},{4,5},{5,4},{6,7},{7,6},{8,9},{9,8},{10,11... | collective-permute-start | bytes 86024 | tf_op jit(solution)/shard_map/ppermute | solution.py:52

commit v10 on v9

--- a/solution.py
+++ b/solution.py
@@ -29,7 +29,9 @@
 
 
 def direct_offset(place, core):
-    return ((-place) & 3) | (core * 4)
+    near = -place & 3
+    far = place ^ (7 - (place >> 1))
+    return near + core * (far - near)
 
 
 def block_offset(position, stages):
@@ -53,10 +55,7 @@
 
 
 def direct_swap(x, place, size):
-    pairs = []
-    for core in range(2):
-        distance = direct_offset(place, core) or 2
-        pairs += [(2 * i + core, 2 * (i ^ distance) + core) for i in range(size)]
+    pairs = [(2 * i + core, 2 * (i ^ direct_offset(place, core)) + core) for i in range(size) for core in range(2)]
     return lax.ppermute(x, ("tp", "sub"), pairs)
 
 
@@ -223,11 +222,16 @@
     column = 512
     chunk = 192 if share % 192 == 0 else share
 
+    outs = [jax.ShapeDtypeStruct((requests, width), jnp.float32)]
+    if set_count == 2:
+        outs.append(jax.ShapeDtypeStruct((requests, width), jnp.bfloat16))
+        outs.append(jax.ShapeDtypeStruct((2, width), jnp.bfloat16))
+
     def body(*refs):
         gain_ref, refs = refs[0], refs[1:]
         set_refs, refs = refs[:set_count], refs[set_count:]
         gate_weight, up_weight, down_hbm, *refs = refs
-        out_refs, refs = refs[:set_count], refs[set_count:]
+        out_refs, refs = refs[: len(outs)], refs[len(outs) :]
         normed_ref, gate_ref, up_ref, hidden_ref, down_ref, down_sems = refs
 
         down_copy = (down_hbm, share_start(units, share), down_ref, down_sems)
@@ -248,8 +252,10 @@
         if set_count == 2:
             core = lax.axis_index("sub")
             other = place // requests
-            distance = direct_offset(place % requests // 2, core ^ other)
-            place = distance + ((place % 2) ^ other) * requests
+            holder = core ^ other
+            spot = place % requests // 2
+            flipped = jnp.where((spot == 0) & (holder == 1), 0, other)
+            place = direct_offset(spot, holder) + ((place % 2) ^ flipped) * requests
         order = (lax.broadcasted_iota(jnp.int32, (every, every), 1) == place).astype(jnp.bfloat16)
         hidden_ref[...] = lax.dot_general(
             order, hidden, (((1,), (1,)), ((), ())), preferred_element_type=jnp.float32
@@ -261,16 +267,14 @@
             out_refs[0][:, c : c + column] = out[:requests]
             if set_count == 2:
                 out_refs[1][:, c : c + column] = out[requests:].astype(jnp.bfloat16)
-
-    outs = [
-        jax.ShapeDtypeStruct((requests, width), jnp.float32),
-        jax.ShapeDtypeStruct((requests, width), jnp.bfloat16),
-    ][:set_count]
+                farthest = jnp.where(core == 1, out[:2], out[requests : requests + 2])
+                out_refs[2][:, c : c + column] = farthest.astype(jnp.bfloat16)
+
     return pl.pallas_call(
         body,
         out_shape=outs,
         in_specs=[VMEM] * (3 + set_count) + [ANY],
-        out_specs=[VMEM] * set_count,
+        out_specs=[VMEM] * len(outs),
         scratch_shapes=[
             pltpu.VMEM((every, width), jnp.bfloat16),
             pltpu.VMEM((share, every), jnp.float32),
@@ -319,13 +323,15 @@
         latent_ctx = attend(queries[0], cache, cache_lengths, live_counts, after)
         own_row = rows[:1].astype(jnp.float32)
         if split:
-            total = total + swap(other[0], "sub", 1, cores).astype(jnp.float32)
-            places = [total[2 * place : 2 * place + 2] for place in range(4)]
+            send, far = other
+            total = total + swap(send, "sub", 1, cores).astype(jnp.float32)
+            far = swap(far, "tp", direct_offset(0, 1), size).astype(jnp.float32)
             sums = [
-                direct_swap(places[place].astype(jnp.bfloat16), place, size).astype(jnp.float32)
-                for place in (1, 2, 3, 0)
+                direct_swap(total[2 * place : 2 * place + 2].astype(jnp.bfloat16), place, size).astype(jnp.float32)
+                for place in (1, 2, 3)
             ]
-            total = jnp.where(lax.axis_index("sub") == 0, places[0], sums[3]) + sums[0] + sums[2] + sums[1]
+            own = jnp.where(lax.axis_index("sub") == 0, total[:2], 0.0) + far
+            total = own + sums[0] + sums[2] + sums[1]
             total, latent_ctx = lax.optimization_barrier((total, latent_ctx))
             total = total[:1] + swap(total[1:], "sub", 1, cores)
         else:

time: 36 us -> 35.7 us (level)
  waiting for transfers between devices: 5.73 us -> 4.47 us
  starting transfers between devices: 13.7 us -> 14.6 us
    ppermute x7 -> x8, starting transfers between devices: 9.04 us -> 11.1 us  [swap(): return lax.ppermute(x, axis, [(i, i ^ distance) for i in range(size)])]
    ppermute x4 -> x3, starting transfers between devices: 4.67 us -> 3.55 us  [direct_swap(): return lax.ppermute(x, ('tp', 'sub'), pairs)]
    ppermute x7 -> x8, waiting for transfers between devices: 4.5 us -> 3.66 us  [swap(): return lax.ppermute(x, axis, [(i, i ^ distance) for i in range(size)])]
    ppermute x4 -> x3, waiting for transfers between devices: 1.23 us -> 0.81 us  [direct_swap(): return lax.ppermute(x, ('tp', 'sub'), pairs)]
  transfers between devices with their start and end apart: 11 -> 11, of which waited for: 6 -> 4; matrix products, arithmetic and copies ran while one was open for 0% -> 0% of each run, Pallas kernels for 24% -> 24%
where the time goes in v10:
time: 35.7 us; the launch traced here: 35.5 us
  Pallas kernels  14.7 us (41%)
  starting transfers between devices  14.6 us (41%)
  waiting for transfers between devices  4.47 us (13%)
  other arithmetic  0.78 us (2%)
  between operations  0.77 us (2%)
    ppermute x8, starting transfers between devices, swap(): return lax.ppermute(x, axis, [(i, i ^ distance) for i in range(size)])  11.1 us
    pallas_call x2, Pallas kernels, load_rows(): pl.pallas_call(body, out_shape=out_shape, in_specs=[ANY] * len(operands),...  6.91 us
    pallas_call x1, Pallas kernels, feed_forward(): pl.pallas_call(body, out_shape=outs, in_specs=[VMEM] * (3 + set_count) +...  6.04 us
    ppermute x8, waiting for transfers between devices, swap(): return lax.ppermute(x, axis, [(i, i ^ distance) for i in range(size)])  3.66 us
    ppermute x3, starting transfers between devices, direct_swap(): return lax.ppermute(x, ('tp', 'sub'), pairs)  3.55 us
    pallas_call x1, Pallas kernels, attend(): pl.pallas_call(body, out_shape=jax.ShapeDtypeStruct((slots, heads, KVL),...  1.6 us
    ppermute x3, waiting for transfers between devices, direct_swap(): return lax.ppermute(x, ('tp', 'sub'), pairs)  0.81 us
  transfers between devices with their start and end apart: 11, of which 4 were waited for; matrix products, arithmetic and copies ran while one was open for 0% of the time, Pallas kernels for 24%

profile of v10, /device:TPU:0, one launch (start us, length us, event | category | flops | bytes accessed | tf_op | source)
XLA Modules:
  0.0 35.5 jit_solution(10876669258152443489)
XLA Ops:
  0.6 0.0 copy-start.2
  0.6 5.1 %collective-permute-start = (bf16[4,7168]{1,0:T(4,128)(2,1)}, bf16[4,7168]{1,0:T(4,128)(2,1)S(1)}, u32[]{:S(2)}, u32[]{:S(2)}) collective-permute-start(bf16[4,7168]{1,0:T(4,128)(2,1)} %bitcast.11), channel_id=1, source_target_pairs={{0,12},{2,14},{4,8},{6,10},{8,4},{10,6},{12,0},{14,2},{1,13},{3,15... | collective-permute-start | bytes 172040 | tf_op jit(solution)/shard_map/ppermute | solution.py:54
  5.8 0.0 collective-permute-start.1
  5.8 0.6 %collective-permute-start.2 = (bf16[4,7168]{1,0:T(4,128)(2,1)}, bf16[4,7168]{1,0:T(4,128)(2,1)S(1)}, u32[]{:S(2)}, u32[]{:S(2)}) collective-permute-start(bf16[4,7168]{1,0:T(4,128)(2,1)} %bitcast.13), channel_id=1, source_target_pairs={{0,4},{2,6},{4,0},{6,2},{8,12},{10,14},{12,8},{14,10},{1,5},{3,7},... | collective-permute-start | bytes 172040 | tf_op jit(solution)/shard_map/ppermute | solution.py:54
  6.4 3.5 %load_rows.2 = (bf16[576,7168]{1,0:T(8,128)(2,1)S(1)}, bf16[16,16]{1,0:T(8,128)(2,1)S(1)}) custom-call(bf16[1152,7168]{1,0:T(8,128)(2,1)} %refs_0_.2, s32[1,8]{1,0:T(1,128)} %counts_ref.1), custom_call_target="tpu_custom_call" | custom-call | bytes 16515072 | tf_op jit(solution)/shard_map/load_rows/pallas_call | solution.py:177
  9.9 0.0 copy-start.3
  9.9 0.0 collective-permute-done.refs_2_
  9.9 1.1 %collective-permute-done.1.refs_3_ = bf16[4,7168]{1,0:T(4,128)(2,1)S(1)} collective-permute-done((bf16[4,7168]{1,0:T(4,128)(2,1)}, bf16[4,7168]{1,0:T(4,128)(2,1)S(1)}, u32[]{:S(2)}, u32[]{:S(2)}) %collective-permute-start.1) | collective-permute-done | bytes 57376 | tf_op jit(solution)/shard_map/ppermute | solution.py:54
  11.0 0.0 collective-permute-done.2.refs_4_
  11.0 0.0 copy-done.2
  11.0 0.2 compact.1
  11.2 1.6 %collective-permute-start.3 = (bf16[8,7168]{1,0:T(8,128)(2,1)S(1)}, bf16[8,7168]{1,0:T(8,128)(2,1)S(1)}, u32[]{:S(2)}, u32[]{:S(2)}) collective-permute-start(bf16[8,7168]{1,0:T(8,128)(2,1)S(1)} %get-tuple-element.15.refs_1_), channel_id=1, source_target_pairs={{0,2},{2,0},{4,6},{6,4},{8,10},{10,8},{12,14},{14,12},{1,3},{3,1},... | collective-permute-start | bytes 344072 | tf_op jit(solution)/shard_map/ppermute | solution.py:54
  12.8 3.4 %load_rows.3.refs_4_ = bf16[576,7168]{1,0:T(8,128)(2,1)S(1)} custom-call(bf16[1152,7168]{1,0:T(8,128)(2,1)} %refs_0_.3, bf16[8,7168]{1,0:T(8,128)(2,1)S(1)} %get-tuple-element.15.refs_1_), custom_call_target="tpu_custom_call" | custom-call | bytes 16515072 | tf_op jit(solution)/shard_map/load_rows/pallas_call | solution.py:177
  16.3 0.0 collective-permute-done.3
  16.3 0.1 collective-permute-start.4
  16.4 1.3 %collective-permute-done.4.refs_2_ = bf16[8,7168]{1,0:T(8,128)(2,1)S(1)} collective-permute-done((bf16[8,7168]{1,0:T(8,128)(2,1)S(1)}, bf16[8,7168]{1,0:T(8,128)(2,1)S(1)}, u32[]{:S(2)}, u32[]{:S(2)}) %collective-permute-start.4) | collective-permute-done | bytes 114720 | tf_op jit(solution)/shard_map/ppermute | solution.py:54
  17.7 0.0 copy-done.3
  17.7 0.0 copy-start
  17.7 0.0 copy-start.1
  17.7 0.0 copy-start.4
  17.7 0.0 copy-start.5
  17.7 6.0 %feed_forward.1 = (f32[8,7168]{1,0:T(8,128)S(1)}, bf16[8,7168]{1,0:T(8,128)(2,1)S(1)}, bf16[2,7168]{1,0:T(2,128)(2,1)S(1)}) custom-call(f32[1,7168]{1,0:T(1,128)S(1)} %bitcast.15, bf16[8,7168]{1,0:T(8,128)(2,1)S(1)} %add.24.refs_1_, bf16[8,7168]{1,0:T(8,128)(2,1)S(1)} %collective-permute-done.4.refs_2_, bf16[576,7168]{1,0:T(8,128)(2,1)S(1)} %get-tuple-element.17.refs_3_, ...), custom_call_target="tpu_custom_call" | custom-call | flops 396361728 | bytes 24772608 | tf_op jit(solution)/shard_map/feed_forward/pallas_call | solution.py:273
  23.8 0.2 collective-permute-start.5
  24.0 3.4 %collective-permute-start.6 = (bf16[2,7168]{1,0:T(2,128)(2,1)S(1)}, bf16[2,7168]{1,0:T(2,128)(2,1)S(1)}, u32[]{:S(2)}, u32[]{:S(2)}) collective-permute-start(bf16[2,7168]{1,0:T(2,128)(2,1)S(1)} %get-tuple-element.21), channel_id=1, source_target_pairs={{0,14},{2,12},{4,10},{6,8},{8,6},{10,4},{12,2},{14,0},{1,15},{3,13... | collective-permute-start | bytes 86024 | tf_op jit(solution)/shard_map/ppermute | solution.py:54
  27.4 0.0 collective-permute-done.5
  27.4 0.1 fusion.8
  27.5 0.2 collective-permute-start.7
  27.7 1.3 %collective-permute-start.8 = (bf16[2,7168]{1,0:T(2,128)(2,1)S(1)}, bf16[2,7168]{1,0:T(2,128)(2,1)S(1)}, u32[]{:S(2)}, u32[]{:S(2)}) collective-permute-start(bf16[2,7168]{1,0:T(2,128)(2,1)S(1)} %get-tuple-element.28), channel_id=1, source_target_pairs={{0,2},{1,11},{2,0},{3,9},{4,6},{5,15},{6,4},{7,13},{8,10},{9,3},{1... | collective-permute-start | bytes 86024 | tf_op jit(solution)/shard_map/ppermute | solution.py:59
  29.0 2.1 %collective-permute-start.9 = (bf16[2,7168]{1,0:T(2,128)(2,1)S(1)}, bf16[2,7168]{1,0:T(2,128)(2,1)S(1)}, u32[]{:S(2)}, u32[]{:S(2)}) collective-permute-start(bf16[2,7168]{1,0:T(2,128)(2,1)S(1)} %get-tuple-element.27), channel_id=1, source_target_pairs={{0,4},{1,9},{2,6},{3,11},{4,0},{5,13},{6,2},{7,15},{8,12},{9,1},{1... | collective-permute-start | bytes 86024 | tf_op jit(solution)/shard_map/ppermute | solution.py:59
  31.1 0.0 copy-done
  31.1 0.0 copy-done.1
  31.1 0.0 copy-done.4
  31.1 0.0 copy-done.5
  31.1 1.6 %attend.1 = bf16[4,64,512]{2,1,0:T(8,128)(2,1)} custom-call(s32[1,4]{1,0:T(1,128)S(1)} %copy-done.5, s32[1,8]{1,0:T(1,128)S(1)} %copy-done.4, bf16[4,64,576]{2,1,0:T(8,128)(2,1)S(1)} %bitcast.10, bf16[4,576,256]{2,1,0:T(8,128)(2,1)S(1)} %bitcast.9, bf16[8,7168]{1,0:T(8,128)(2,1)S(1)} %get-tuple-element.20._), custom_call_target="tpu_custom_call" | custom-call | flops 134217728 | bytes 1474560 | tf_op jit(solution)/shard_map/attend/pallas_call | solution.py:136
  32.7 0.0 collective-permute-done.6
  32.7 0.0 collective-permute-done.7
  32.7 0.0 collective-permute-done.8
  32.7 0.8 %collective-permute-done.9 = bf16[2,7168]{1,0:T(2,128)(2,1)S(1)} collective-permute-done((bf16[2,7168]{1,0:T(2,128)(2,1)S(1)}, bf16[2,7168]{1,0:T(2,128)(2,1)S(1)}, u32[]{:S(2)}, u32[]{:S(2)}) %collective-permute-start.9) | collective-permute-done | bytes 28704 | tf_op jit(solution)/shard_map/ppermute | solution.py:59
  33.5 0.1 fusion.3
  33.6 0.1 collective-permute-start.10
  33.7 1.2 %collective-permute-done.10 = f32[1,7168]{1,0:T(1,128)S(1)} collective-permute-done((f32[1,7168]{1,0:T(1,128)S(1)}, f32[1,7168]{1,0:T(1,128)S(1)}, u32[]{:S(2)}, u32[]{:S(2)}) %collective-permute-start.10) | collective-permute-done | bytes 28704 | tf_op jit(solution)/shard_map/ppermute | solution.py:54
  34.9 0.6 %fusion.6 = bf16[1,1,7168]{2,1,0:T(2,128)(2,1)} fusion(bf16[8,7168]{1,0:T(8,128)(2,1)S(1)} %add.24.refs_1_, f32[1,7168]{1,0:T(1,128)S(1)} %collective-permute-done.10, f32[2,7168]{1,0:T(2,128)S(1)} %fusion.3), kind=kLoop, calls=%fused_computation.9 | loop fusion | flops 28672 | bytes 86016 | tf_op jit(solution)/shard_map/broadcast_in_dim | solution.py:344
  (3 shorter events, 0.1 us)
Async XLA Ops:
  0.6 10.4 %copy-start.2 = (bf16[1,4,7168]{2,1,0:T(4,128)(2,1)S(1)}, bf16[1,4,7168]{2,1,0:T(4,128)(2,1)}, u32[]{:S(2)}) copy-start(bf16[1,4,7168]{2,1,0:T(4,128)(2,1)} %param.13) | copy-start | bytes 172036
  0.6 9.2 %collective-permute-start = (bf16[4,7168]{1,0:T(4,128)(2,1)}, bf16[4,7168]{1,0:T(4,128)(2,1)S(1)}, u32[]{:S(2)}, u32[]{:S(2)}) collective-permute-start(bf16[4,7168]{1,0:T(4,128)(2,1)} %bitcast.11), channel_id=1, source_target_pairs={{0,12},{2,14},{4,8},{6,10},{8,4},{10,6},{12,0},{14,2},{1,13},{3,15... | collective-permute-start | bytes 172040 | tf_op jit(solution)/shard_map/ppermute | solution.py:54
  5.8 5.3 %collective-permute-start.1 = (bf16[4,7168]{1,0:T(4,128)(2,1)}, bf16[4,7168]{1,0:T(4,128)(2,1)S(1)}, u32[]{:S(2)}, u32[]{:S(2)}) collective-permute-start(bf16[4,7168]{1,0:T(4,128)(2,1)} %bitcast.12), channel_id=1, source_target_pairs={{0,8},{2,10},{4,12},{6,14},{8,0},{10,2},{12,4},{14,6},{1,9},{3,11}... | collective-permute-start | bytes 172040 | tf_op jit(solution)/shard_map/ppermute | solution.py:54
  5.8 5.3 %collective-permute-start.2 = (bf16[4,7168]{1,0:T(4,128)(2,1)}, bf16[4,7168]{1,0:T(4,128)(2,1)S(1)}, u32[]{:S(2)}, u32[]{:S(2)}) collective-permute-start(bf16[4,7168]{1,0:T(4,128)(2,1)} %bitcast.13), channel_id=1, source_target_pairs={{0,4},{2,6},{4,0},{6,2},{8,12},{10,14},{12,8},{14,10},{1,5},{3,7},... | collective-permute-start | bytes 172040 | tf_op jit(solution)/shard_map/ppermute | solution.py:54
  9.9 7.9 %copy-start.3 = (f32[7168]{0:T(1024)S(1)}, f32[7168]{0:T(1024)}, u32[]{:S(2)}) copy-start(f32[7168]{0:T(1024)} %param.14) | copy-start | bytes 86020
  11.2 5.0 %collective-permute-start.3 = (bf16[8,7168]{1,0:T(8,128)(2,1)S(1)}, bf16[8,7168]{1,0:T(8,128)(2,1)S(1)}, u32[]{:S(2)}, u32[]{:S(2)}) collective-permute-start(bf16[8,7168]{1,0:T(8,128)(2,1)S(1)} %get-tuple-element.15.refs_1_), channel_id=1, source_target_pairs={{0,2},{2,0},{4,6},{6,4},{8,10},{10,8},{12,14},{14,12},{1,3},{3,1},... | collective-permute-start | bytes 344072 | tf_op jit(solution)/shard_map/ppermute | solution.py:54
  16.3 1.4 %collective-permute-start.4 = (bf16[8,7168]{1,0:T(8,128)(2,1)S(1)}, bf16[8,7168]{1,0:T(8,128)(2,1)S(1)}, u32[]{:S(2)}, u32[]{:S(2)}) collective-permute-start(bf16[8,7168]{1,0:T(8,128)(2,1)S(1)} %add.24.refs_1_), channel_id=1, source_target_pairs={{0,1},{1,0},{2,3},{3,2},{4,5},{5,4},{6,7},{7,6},{8,9},{9,8},{10,11... | collective-permute-start | bytes 344072 | tf_op jit(solution)/shard_map/ppermute | solution.py:54
  17.7 13.3 %copy-start = (bf16[1,4,256,576]{2,3,1,0:T(8,128)(2,1)S(1)}, bf16[1,4,256,576]{2,3,1,0:T(8,128)(2,1)}, u32[]{:S(2)}) copy-start(bf16[1,4,256,576]{2,3,1,0:T(8,128)(2,1)} %param.10) | copy-start | bytes 3538948
  17.7 13.3 %copy-start.1 = (bf16[1,4,64,576]{3,2,1,0:T(8,128)(2,1)S(1)}, bf16[1,4,64,576]{3,2,1,0:T(8,128)(2,1)}, u32[]{:S(2)}) copy-start(bf16[1,4,64,576]{3,2,1,0:T(8,128)(2,1)} %param.9) | copy-start | bytes 884740
  17.7 13.3 %copy-start.4 = (s32[1,8]{1,0:T(1,128)S(1)}, s32[1,8]{1,0:T(1,128)}, u32[]{:S(2)}) copy-start(s32[1,8]{1,0:T(1,128)} %counts_ref.1) | copy-start | bytes 100
  17.7 13.3 %copy-start.5 = (s32[1,4]{1,0:T(1,128)S(1)}, s32[1,4]{1,0:T(1,128)}, u32[]{:S(2)}) copy-start(s32[1,4]{1,0:T(1,128)} %lengths_ref.1) | copy-start | bytes 52
  23.8 3.6 %collective-permute-start.5 = (bf16[8,7168]{1,0:T(8,128)(2,1)S(1)}, bf16[8,7168]{1,0:T(8,128)(2,1)S(1)}, u32[]{:S(2)}, u32[]{:S(2)}) collective-permute-start(bf16[8,7168]{1,0:T(8,128)(2,1)S(1)} %get-tuple-element.20._), channel_id=1, source_target_pairs={{0,1},{1,0},{2,3},{3,2},{4,5},{5,4},{6,7},{7,6},{8,9},{9,8},{10,11... | collective-permute-start | bytes 344072 | tf_op jit(solution)/shard_map/ppermute | solution.py:54
  24.0 8.7 %collective-permute-start.6 = (bf16[2,7168]{1,0:T(2,128)(2,1)S(1)}, bf16[2,7168]{1,0:T(2,128)(2,1)S(1)}, u32[]{:S(2)}, u32[]{:S(2)}) collective-permute-start(bf16[2,7168]{1,0:T(2,128)(2,1)S(1)} %get-tuple-element.21), channel_id=1, source_target_pairs={{0,14},{2,12},{4,10},{6,8},{8,6},{10,4},{12,2},{14,0},{1,15},{3,13... | collective-permute-start | bytes 86024 | tf_op jit(solution)/shard_map/ppermute | solution.py:54
  27.5 5.2 %collective-permute-start.7 = (bf16[2,7168]{1,0:T(2,128)(2,1)S(1)}, bf16[2,7168]{1,0:T(2,128)(2,1)S(1)}, u32[]{:S(2)}, u32[]{:S(2)}) collective-permute-start(bf16[2,7168]{1,0:T(2,128)(2,1)S(1)} %get-tuple-element.26), channel_id=1, source_target_pairs={{0,6},{1,13},{2,4},{3,15},{4,2},{5,9},{6,0},{7,11},{8,14},{9,5},{1... | collective-permute-start | bytes 86024 | tf_op jit(solution)/shard_map/ppermute | solution.py:59
  27.7 5.0 %collective-permute-start.8 = (bf16[2,7168]{1,0:T(2,128)(2,1)S(1)}, bf16[2,7168]{1,0:T(2,128)(2,1)S(1)}, u32[]{:S(2)}, u32[]{:S(2)}) collective-permute-start(bf16[2,7168]{1,0:T(2,128)(2,1)S(1)} %get-tuple-element.28), channel_id=1, source_target_pairs={{0,2},{1,11},{2,0},{3,9},{4,6},{5,15},{6,4},{7,13},{8,10},{9,3},{1... | collective-permute-start | bytes 86024 | tf_op jit(solution)/shard_map/ppermute | solution.py:59
  29.0 4.5 %collective-permute-start.9 = (bf16[2,7168]{1,0:T(2,128)(2,1)S(1)}, bf16[2,7168]{1,0:T(2,128)(2,1)S(1)}, u32[]{:S(2)}, u32[]{:S(2)}) collective-permute-start(bf16[2,7168]{1,0:T(2,128)(2,1)S(1)} %get-tuple-element.27), channel_id=1, source_target_pairs={{0,4},{1,9},{2,6},{3,11},{4,0},{5,13},{6,2},{7,15},{8,12},{9,1},{1... | collective-permute-start | bytes 86024 | tf_op jit(solution)/shard_map/ppermute | solution.py:59
  33.6 1.3 %collective-permute-start.10 = (f32[1,7168]{1,0:T(1,128)S(1)}, f32[1,7168]{1,0:T(1,128)S(1)}, u32[]{:S(2)}, u32[]{:S(2)}) collective-permute-start(f32[1,7168]{1,0:T(1,128)S(1)} %slice.29), channel_id=1, source_target_pairs={{0,1},{1,0},{2,3},{3,2},{4,5},{5,4},{6,7},{7,6},{8,9},{9,8},{10,11... | collective-permute-start | bytes 86024 | tf_op jit(solution)/shard_map/ppermute | solution.py:54

commit v11 on v10

--- a/solution.py
+++ b/solution.py
@@ -30,7 +30,7 @@
 
 def direct_offset(place, core):
     near = -place & 3
-    far = place ^ (7 - (place >> 1))
+    far = place ^ 6
     return near + core * (far - near)
 
 
@@ -232,22 +232,22 @@
         set_refs, refs = refs[:set_count], refs[set_count:]
         gate_weight, up_weight, down_hbm, *refs = refs
         out_refs, refs = refs[: len(outs)], refs[len(outs) :]
-        normed_ref, gate_ref, up_ref, hidden_ref, down_ref, down_sems = refs
+        scaled_ref, gate_ref, up_ref, hidden_ref, down_ref, down_sems = refs
 
         down_copy = (down_hbm, share_start(units, share), down_ref, down_sems)
         start_pieces(down_copy)
 
         rows = [ref[...].astype(jnp.float32) for ref in set_refs]
         rows = rows[0] if set_count == 1 else jnp.concatenate(rows, axis=0)
-        inv_rms = lax.rsqrt(jnp.mean(rows * rows, axis=1, keepdims=True) + norm_eps)
-        normed_ref[...] = (rows * inv_rms * gain_ref[...]).astype(jnp.bfloat16)
+        scaled_ref[...] = (rows * gain_ref[...]).astype(jnp.bfloat16)
+        inv_rms = lax.rsqrt(jnp.mean(rows * rows, axis=1, keepdims=True) + norm_eps).T
 
         for weight_ref, out_ref in ((gate_weight, gate_ref), (up_weight, up_ref)):
             for j in range(0, share, chunk):
                 out_ref[j : j + chunk, :] = lax.dot_general(
-                    weight_ref[j : j + chunk, :], normed_ref[...], (((1,), (1,)), ((), ())), preferred_element_type=jnp.float32
+                    weight_ref[j : j + chunk, :], scaled_ref[...], (((1,), (1,)), ((), ())), preferred_element_type=jnp.float32
                 )
-        hidden = (jax.nn.silu(gate_ref[...]) * up_ref[...]).astype(jnp.bfloat16)
+        hidden = (jax.nn.silu(gate_ref[...] * inv_rms) * (up_ref[...] * inv_rms)).astype(jnp.bfloat16)
         place = lax.broadcasted_iota(jnp.int32, (every, every), 0)
         if set_count == 2:
             core = lax.axis_index("sub")
@@ -267,8 +267,8 @@
             out_refs[0][:, c : c + column] = out[:requests]
             if set_count == 2:
                 out_refs[1][:, c : c + column] = out[requests:].astype(jnp.bfloat16)
-                farthest = jnp.where(core == 1, out[:2], out[requests : requests + 2])
-                out_refs[2][:, c : c + column] = farthest.astype(jnp.bfloat16)
+                far = jnp.where(core == 1, out[:2], out[requests : requests + 2])
+                out_refs[2][:, c : c + column] = far.astype(jnp.bfloat16)
 
     return pl.pallas_call(
         body,

time: 35.7 us -> 34.8 us (0.975)
  waiting for transfers between devices: 4.47 us -> 3.88 us
  transfers between devices with their start and end apart: 11 -> 11, of which waited for: 4 -> 4; matrix products, arithmetic and copies ran while one was open for 0% -> 0% of each run, Pallas kernels for 24% -> 25%
where the time goes in v11:
time: 34.8 us; the launch traced here: 34.6 us
  Pallas kernels  14.6 us (42%)
  starting transfers between devices  14.5 us (42%)
  waiting for transfers between devices  3.88 us (11%)
  other arithmetic  0.78 us (2%)
  between operations  0.76 us (2%)
    ppermute x8, starting transfers between devices, swap(): return lax.ppermute(x, axis, [(i, i ^ distance) for i in range(size)])  11 us
    pallas_call x2, Pallas kernels, load_rows(): pl.pallas_call(body, out_shape=out_shape, in_specs=[ANY] * len(operands),...  6.91 us
    pallas_call x1, Pallas kernels, feed_forward(): pl.pallas_call(body, out_shape=outs, in_specs=[VMEM] * (3 + set_count) +...  5.87 us
    ppermute x3, starting transfers between devices, direct_swap(): return lax.ppermute(x, ('tp', 'sub'), pairs)  3.55 us
    ppermute x8, waiting for transfers between devices, swap(): return lax.ppermute(x, axis, [(i, i ^ distance) for i in range(size)])  3.33 us
    pallas_call x1, Pallas kernels, attend(): pl.pallas_call(body, out_shape=jax.ShapeDtypeStruct((slots, heads, KVL),...  1.6 us
  transfers between devices with their start and end apart: 11, of which 4 were waited for; matrix products, arithmetic and copies ran while one was open for 0% of the time, Pallas kernels for 25%

profile of v11, /device:TPU:0, one launch (start us, length us, event | category | flops | bytes accessed | tf_op | source)
XLA Modules:
  0.0 34.6 jit_solution(1406657967583616549)
XLA Ops:
  0.6 0.0 copy-start.2
  0.6 5.1 %collective-permute-start = (bf16[4,7168]{1,0:T(4,128)(2,1)}, bf16[4,7168]{1,0:T(4,128)(2,1)S(1)}, u32[]{:S(2)}, u32[]{:S(2)}) collective-permute-start(bf16[4,7168]{1,0:T(4,128)(2,1)} %bitcast.11), channel_id=1, source_target_pairs={{0,12},{2,14},{4,8},{6,10},{8,4},{10,6},{12,0},{14,2},{1,13},{3,15... | collective-permute-start | bytes 172040 | tf_op jit(solution)/shard_map/ppermute | solution.py:54
  5.8 0.0 collective-permute-start.1
  5.8 0.6 %collective-permute-start.2 = (bf16[4,7168]{1,0:T(4,128)(2,1)}, bf16[4,7168]{1,0:T(4,128)(2,1)S(1)}, u32[]{:S(2)}, u32[]{:S(2)}) collective-permute-start(bf16[4,7168]{1,0:T(4,128)(2,1)} %bitcast.13), channel_id=1, source_target_pairs={{0,4},{2,6},{4,0},{6,2},{8,12},{10,14},{12,8},{14,10},{1,5},{3,7},... | collective-permute-start | bytes 172040 | tf_op jit(solution)/shard_map/ppermute | solution.py:54
  6.4 3.5 %load_rows.2 = (bf16[576,7168]{1,0:T(8,128)(2,1)S(1)}, bf16[16,16]{1,0:T(8,128)(2,1)S(1)}) custom-call(bf16[1152,7168]{1,0:T(8,128)(2,1)} %refs_0_.2, s32[1,8]{1,0:T(1,128)} %counts_ref.1), custom_call_target="tpu_custom_call" | custom-call | bytes 16515072 | tf_op jit(solution)/shard_map/load_rows/pallas_call | solution.py:177
  9.9 0.0 copy-start.3
  9.9 0.0 collective-permute-done.refs_2_
  9.9 1.1 %collective-permute-done.1.refs_3_ = bf16[4,7168]{1,0:T(4,128)(2,1)S(1)} collective-permute-done((bf16[4,7168]{1,0:T(4,128)(2,1)}, bf16[4,7168]{1,0:T(4,128)(2,1)S(1)}, u32[]{:S(2)}, u32[]{:S(2)}) %collective-permute-start.1) | collective-permute-done | bytes 57376 | tf_op jit(solution)/shard_map/ppermute | solution.py:54
  11.0 0.0 collective-permute-done.2.refs_4_
  11.0 0.0 copy-done.2
  11.0 0.2 compact.1
  11.2 1.6 %collective-permute-start.3 = (bf16[8,7168]{1,0:T(8,128)(2,1)S(1)}, bf16[8,7168]{1,0:T(8,128)(2,1)S(1)}, u32[]{:S(2)}, u32[]{:S(2)}) collective-permute-start(bf16[8,7168]{1,0:T(8,128)(2,1)S(1)} %get-tuple-element.15.refs_1_), channel_id=1, source_target_pairs={{0,2},{2,0},{4,6},{6,4},{8,10},{10,8},{12,14},{14,12},{1,3},{3,1},... | collective-permute-start | bytes 344072 | tf_op jit(solution)/shard_map/ppermute | solution.py:54
  12.8 3.4 %load_rows.3.refs_4_ = bf16[576,7168]{1,0:T(8,128)(2,1)S(1)} custom-call(bf16[1152,7168]{1,0:T(8,128)(2,1)} %refs_0_.3, bf16[8,7168]{1,0:T(8,128)(2,1)S(1)} %get-tuple-element.15.refs_1_), custom_call_target="tpu_custom_call" | custom-call | bytes 16515072 | tf_op jit(solution)/shard_map/load_rows/pallas_call | solution.py:177
  16.3 0.0 collective-permute-done.3
  16.3 0.1 collective-permute-start.4
  16.4 1.3 %collective-permute-done.4.refs_2_ = bf16[8,7168]{1,0:T(8,128)(2,1)S(1)} collective-permute-done((bf16[8,7168]{1,0:T(8,128)(2,1)S(1)}, bf16[8,7168]{1,0:T(8,128)(2,1)S(1)}, u32[]{:S(2)}, u32[]{:S(2)}) %collective-permute-start.4) | collective-permute-done | bytes 114720 | tf_op jit(solution)/shard_map/ppermute | solution.py:54
  17.7 0.0 copy-done.3
  17.7 0.0 copy-start
  17.7 0.0 copy-start.1
  17.7 0.0 copy-start.4
  17.7 0.0 copy-start.5
  17.7 5.9 %feed_forward.1 = (f32[8,7168]{1,0:T(8,128)S(1)}, bf16[8,7168]{1,0:T(8,128)(2,1)S(1)}, bf16[2,7168]{1,0:T(2,128)(2,1)S(1)}) custom-call(f32[1,7168]{1,0:T(1,128)S(1)} %bitcast.15, bf16[8,7168]{1,0:T(8,128)(2,1)S(1)} %add.24.refs_1_, bf16[8,7168]{1,0:T(8,128)(2,1)S(1)} %collective-permute-done.4.refs_2_, bf16[576,7168]{1,0:T(8,128)(2,1)S(1)} %get-tuple-element.17.refs_3_, ...), custom_call_target="tpu_custom_call" | custom-call | flops 396361728 | bytes 24772608 | tf_op jit(solution)/shard_map/feed_forward/pallas_call | solution.py:273
  23.6 0.2 collective-permute-start.5
  23.8 2.6 %collective-permute-start.6 = (bf16[2,7168]{1,0:T(2,128)(2,1)S(1)}, bf16[2,7168]{1,0:T(2,128)(2,1)S(1)}, u32[]{:S(2)}, u32[]{:S(2)}) collective-permute-start(bf16[2,7168]{1,0:T(2,128)(2,1)S(1)} %get-tuple-element.21), channel_id=1, source_target_pairs={{0,12},{2,14},{4,8},{6,10},{8,4},{10,6},{12,0},{14,2},{1,13},{3,15... | collective-permute-start | bytes 86024 | tf_op jit(solution)/shard_map/ppermute | solution.py:54
  26.5 0.0 collective-permute-done.5
  26.5 0.1 fusion.8
  26.6 0.8 %collective-permute-start.7 = (bf16[2,7168]{1,0:T(2,128)(2,1)S(1)}, bf16[2,7168]{1,0:T(2,128)(2,1)S(1)}, u32[]{:S(2)}, u32[]{:S(2)}) collective-permute-start(bf16[2,7168]{1,0:T(2,128)(2,1)S(1)} %get-tuple-element.26), channel_id=1, source_target_pairs={{0,6},{1,15},{2,4},{3,13},{4,2},{5,11},{6,0},{7,9},{8,14},{9,7},{1... | collective-permute-start | bytes 86024 | tf_op jit(solution)/shard_map/ppermute | solution.py:59
  27.4 0.7 %collective-permute-start.8 = (bf16[2,7168]{1,0:T(2,128)(2,1)S(1)}, bf16[2,7168]{1,0:T(2,128)(2,1)S(1)}, u32[]{:S(2)}, u32[]{:S(2)}) collective-permute-start(bf16[2,7168]{1,0:T(2,128)(2,1)S(1)} %get-tuple-element.28), channel_id=1, source_target_pairs={{0,2},{1,11},{2,0},{3,9},{4,6},{5,15},{6,4},{7,13},{8,10},{9,3},{1... | collective-permute-start | bytes 86024 | tf_op jit(solution)/shard_map/ppermute | solution.py:59
  28.1 2.1 %collective-permute-start.9 = (bf16[2,7168]{1,0:T(2,128)(2,1)S(1)}, bf16[2,7168]{1,0:T(2,128)(2,1)S(1)}, u32[]{:S(2)}, u32[]{:S(2)}) collective-permute-start(bf16[2,7168]{1,0:T(2,128)(2,1)S(1)} %get-tuple-element.27), channel_id=1, source_target_pairs={{0,4},{1,9},{2,6},{3,11},{4,0},{5,13},{6,2},{7,15},{8,12},{9,1},{1... | collective-permute-start | bytes 86024 | tf_op jit(solution)/shard_map/ppermute | solution.py:59
  30.1 0.0 copy-done
  30.1 0.0 copy-done.1
  30.1 0.0 copy-done.4
  30.1 0.0 copy-done.5
  30.1 1.6 %attend.1 = bf16[4,64,512]{2,1,0:T(8,128)(2,1)} custom-call(s32[1,4]{1,0:T(1,128)S(1)} %copy-done.5, s32[1,8]{1,0:T(1,128)S(1)} %copy-done.4, bf16[4,64,576]{2,1,0:T(8,128)(2,1)S(1)} %bitcast.10, bf16[4,576,256]{2,1,0:T(8,128)(2,1)S(1)} %bitcast.9, bf16[8,7168]{1,0:T(8,128)(2,1)S(1)} %get-tuple-element.20._), custom_call_target="tpu_custom_call" | custom-call | flops 134217728 | bytes 1474560 | tf_op jit(solution)/shard_map/attend/pallas_call | solution.py:136
  31.8 0.0 collective-permute-done.6
  31.8 0.0 collective-permute-done.7
  31.8 0.0 collective-permute-done.8
  31.8 0.5 %collective-permute-done.9 = bf16[2,7168]{1,0:T(2,128)(2,1)S(1)} collective-permute-done((bf16[2,7168]{1,0:T(2,128)(2,1)S(1)}, bf16[2,7168]{1,0:T(2,128)(2,1)S(1)}, u32[]{:S(2)}, u32[]{:S(2)}) %collective-permute-start.9) | collective-permute-done | bytes 28704 | tf_op jit(solution)/shard_map/ppermute | solution.py:59
  32.3 0.1 fusion.3
  32.4 0.7 %collective-permute-start.10 = (f32[1,7168]{1,0:T(1,128)S(1)}, f32[1,7168]{1,0:T(1,128)S(1)}, u32[]{:S(2)}, u32[]{:S(2)}) collective-permute-start(f32[1,7168]{1,0:T(1,128)S(1)} %slice.29), channel_id=1, source_target_pairs={{0,1},{1,0},{2,3},{3,2},{4,5},{5,4},{6,7},{7,6},{8,9},{9,8},{10,11... | collective-permute-start | bytes 86024 | tf_op jit(solution)/shard_map/ppermute | solution.py:54
  33.1 0.9 %collective-permute-done.10 = f32[1,7168]{1,0:T(1,128)S(1)} collective-permute-done((f32[1,7168]{1,0:T(1,128)S(1)}, f32[1,7168]{1,0:T(1,128)S(1)}, u32[]{:S(2)}, u32[]{:S(2)}) %collective-permute-start.10) | collective-permute-done | bytes 28704 | tf_op jit(solution)/shard_map/ppermute | solution.py:54
  34.0 0.6 %fusion.6 = bf16[1,1,7168]{2,1,0:T(2,128)(2,1)} fusion(bf16[8,7168]{1,0:T(8,128)(2,1)S(1)} %add.24.refs_1_, f32[1,7168]{1,0:T(1,128)S(1)} %collective-permute-done.10, f32[2,7168]{1,0:T(2,128)S(1)} %fusion.3), kind=kLoop, calls=%fused_computation.9 | loop fusion | flops 28672 | bytes 86016 | tf_op jit(solution)/shard_map/broadcast_in_dim | solution.py:344
  (3 shorter events, 0.1 us)
Async XLA Ops:
  0.6 10.4 %copy-start.2 = (bf16[1,4,7168]{2,1,0:T(4,128)(2,1)S(1)}, bf16[1,4,7168]{2,1,0:T(4,128)(2,1)}, u32[]{:S(2)}) copy-start(bf16[1,4,7168]{2,1,0:T(4,128)(2,1)} %param.13) | copy-start | bytes 172036
  0.6 9.2 %collective-permute-start = (bf16[4,7168]{1,0:T(4,128)(2,1)}, bf16[4,7168]{1,0:T(4,128)(2,1)S(1)}, u32[]{:S(2)}, u32[]{:S(2)}) collective-permute-start(bf16[4,7168]{1,0:T(4,128)(2,1)} %bitcast.11), channel_id=1, source_target_pairs={{0,12},{2,14},{4,8},{6,10},{8,4},{10,6},{12,0},{14,2},{1,13},{3,15... | collective-permute-start | bytes 172040 | tf_op jit(solution)/shard_map/ppermute | solution.py:54
  5.8 5.3 %collective-permute-start.1 = (bf16[4,7168]{1,0:T(4,128)(2,1)}, bf16[4,7168]{1,0:T(4,128)(2,1)S(1)}, u32[]{:S(2)}, u32[]{:S(2)}) collective-permute-start(bf16[4,7168]{1,0:T(4,128)(2,1)} %bitcast.12), channel_id=1, source_target_pairs={{0,8},{2,10},{4,12},{6,14},{8,0},{10,2},{12,4},{14,6},{1,9},{3,11}... | collective-permute-start | bytes 172040 | tf_op jit(solution)/shard_map/ppermute | solution.py:54
  5.8 5.3 %collective-permute-start.2 = (bf16[4,7168]{1,0:T(4,128)(2,1)}, bf16[4,7168]{1,0:T(4,128)(2,1)S(1)}, u32[]{:S(2)}, u32[]{:S(2)}) collective-permute-start(bf16[4,7168]{1,0:T(4,128)(2,1)} %bitcast.13), channel_id=1, source_target_pairs={{0,4},{2,6},{4,0},{6,2},{8,12},{10,14},{12,8},{14,10},{1,5},{3,7},... | collective-permute-start | bytes 172040 | tf_op jit(solution)/shard_map/ppermute | solution.py:54
  9.9 7.9 %copy-start.3 = (f32[7168]{0:T(1024)S(1)}, f32[7168]{0:T(1024)}, u32[]{:S(2)}) copy-start(f32[7168]{0:T(1024)} %param.14) | copy-start | bytes 86020
  11.2 5.0 %collective-permute-start.3 = (bf16[8,7168]{1,0:T(8,128)(2,1)S(1)}, bf16[8,7168]{1,0:T(8,128)(2,1)S(1)}, u32[]{:S(2)}, u32[]{:S(2)}) collective-permute-start(bf16[8,7168]{1,0:T(8,128)(2,1)S(1)} %get-tuple-element.15.refs_1_), channel_id=1, source_target_pairs={{0,2},{2,0},{4,6},{6,4},{8,10},{10,8},{12,14},{14,12},{1,3},{3,1},... | collective-permute-start | bytes 344072 | tf_op jit(solution)/shard_map/ppermute | solution.py:54
  16.3 1.4 %collective-permute-start.4 = (bf16[8,7168]{1,0:T(8,128)(2,1)S(1)}, bf16[8,7168]{1,0:T(8,128)(2,1)S(1)}, u32[]{:S(2)}, u32[]{:S(2)}) collective-permute-start(bf16[8,7168]{1,0:T(8,128)(2,1)S(1)} %add.24.refs_1_), channel_id=1, source_target_pairs={{0,1},{1,0},{2,3},{3,2},{4,5},{5,4},{6,7},{7,6},{8,9},{9,8},{10,11... | collective-permute-start | bytes 344072 | tf_op jit(solution)/shard_map/ppermute | solution.py:54
  17.7 12.4 %copy-start = (bf16[1,4,256,576]{2,3,1,0:T(8,128)(2,1)S(1)}, bf16[1,4,256,576]{2,3,1,0:T(8,128)(2,1)}, u32[]{:S(2)}) copy-start(bf16[1,4,256,576]{2,3,1,0:T(8,128)(2,1)} %param.10) | copy-start | bytes 3538948
  17.7 12.4 %copy-start.1 = (bf16[1,4,64,576]{3,2,1,0:T(8,128)(2,1)S(1)}, bf16[1,4,64,576]{3,2,1,0:T(8,128)(2,1)}, u32[]{:S(2)}) copy-start(bf16[1,4,64,576]{3,2,1,0:T(8,128)(2,1)} %param.9) | copy-start | bytes 884740
  17.7 12.4 %copy-start.4 = (s32[1,8]{1,0:T(1,128)S(1)}, s32[1,8]{1,0:T(1,128)}, u32[]{:S(2)}) copy-start(s32[1,8]{1,0:T(1,128)} %counts_ref.1) | copy-start | bytes 100
  17.7 12.4 %copy-start.5 = (s32[1,4]{1,0:T(1,128)S(1)}, s32[1,4]{1,0:T(1,128)}, u32[]{:S(2)}) copy-start(s32[1,4]{1,0:T(1,128)} %lengths_ref.1) | copy-start | bytes 52
  23.6 2.8 %collective-permute-start.5 = (bf16[8,7168]{1,0:T(8,128)(2,1)S(1)}, bf16[8,7168]{1,0:T(8,128)(2,1)S(1)}, u32[]{:S(2)}, u32[]{:S(2)}) collective-permute-start(bf16[8,7168]{1,0:T(8,128)(2,1)S(1)} %get-tuple-element.20._), channel_id=1, source_target_pairs={{0,1},{1,0},{2,3},{3,2},{4,5},{5,4},{6,7},{7,6},{8,9},{9,8},{10,11... | collective-permute-start | bytes 344072 | tf_op jit(solution)/shard_map/ppermute | solution.py:54
  23.8 7.9 %collective-permute-start.6 = (bf16[2,7168]{1,0:T(2,128)(2,1)S(1)}, bf16[2,7168]{1,0:T(2,128)(2,1)S(1)}, u32[]{:S(2)}, u32[]{:S(2)}) collective-permute-start(bf16[2,7168]{1,0:T(2,128)(2,1)S(1)} %get-tuple-element.21), channel_id=1, source_target_pairs={{0,12},{2,14},{4,8},{6,10},{8,4},{10,6},{12,0},{14,2},{1,13},{3,15... | collective-permute-start | bytes 86024 | tf_op jit(solution)/shard_map/ppermute | solution.py:54
  26.6 5.2 %collective-permute-start.7 = (bf16[2,7168]{1,0:T(2,128)(2,1)S(1)}, bf16[2,7168]{1,0:T(2,128)(2,1)S(1)}, u32[]{:S(2)}, u32[]{:S(2)}) collective-permute-start(bf16[2,7168]{1,0:T(2,128)(2,1)S(1)} %get-tuple-element.26), channel_id=1, source_target_pairs={{0,6},{1,15},{2,4},{3,13},{4,2},{5,11},{6,0},{7,9},{8,14},{9,7},{1... | collective-permute-start | bytes 86024 | tf_op jit(solution)/shard_map/ppermute | solution.py:59
  27.4 4.4 %collective-permute-start.8 = (bf16[2,7168]{1,0:T(2,128)(2,1)S(1)}, bf16[2,7168]{1,0:T(2,128)(2,1)S(1)}, u32[]{:S(2)}, u32[]{:S(2)}) collective-permute-start(bf16[2,7168]{1,0:T(2,128)(2,1)S(1)} %get-tuple-element.28), channel_id=1, source_target_pairs={{0,2},{1,11},{2,0},{3,9},{4,6},{5,15},{6,4},{7,13},{8,10},{9,3},{1... | collective-permute-start | bytes 86024 | tf_op jit(solution)/shard_map/ppermute | solution.py:59
  28.1 4.2 %collective-permute-start.9 = (bf16[2,7168]{1,0:T(2,128)(2,1)S(1)}, bf16[2,7168]{1,0:T(2,128)(2,1)S(1)}, u32[]{:S(2)}, u32[]{:S(2)}) collective-permute-start(bf16[2,7168]{1,0:T(2,128)(2,1)S(1)} %get-tuple-element.27), channel_id=1, source_target_pairs={{0,4},{1,9},{2,6},{3,11},{4,0},{5,13},{6,2},{7,15},{8,12},{9,1},{1... | collective-permute-start | bytes 86024 | tf_op jit(solution)/shard_map/ppermute | solution.py:59
  32.4 1.6 %collective-permute-start.10 = (f32[1,7168]{1,0:T(1,128)S(1)}, f32[1,7168]{1,0:T(1,128)S(1)}, u32[]{:S(2)}, u32[]{:S(2)}) collective-permute-start(f32[1,7168]{1,0:T(1,128)S(1)} %slice.29), channel_id=1, source_target_pairs={{0,1},{1,0},{2,3},{3,2},{4,5},{5,4},{6,7},{7,6},{8,9},{9,8},{10,11... | collective-permute-start | bytes 86024 | tf_op jit(solution)/shard_map/ppermute | solution.py:54

commit v12 on v10

--- a/solution.py
+++ b/solution.py
@@ -30,7 +30,7 @@
 
 def direct_offset(place, core):
     near = -place & 3
-    far = place ^ (7 - (place >> 1))
+    far = place ^ 6
     return near + core * (far - near)
 
 
@@ -267,8 +267,8 @@
             out_refs[0][:, c : c + column] = out[:requests]
             if set_count == 2:
                 out_refs[1][:, c : c + column] = out[requests:].astype(jnp.bfloat16)
-                farthest = jnp.where(core == 1, out[:2], out[requests : requests + 2])
-                out_refs[2][:, c : c + column] = farthest.astype(jnp.bfloat16)
+                far = jnp.where(core == 1, out[:2], out[requests : requests + 2])
+                out_refs[2][:, c : c + column] = far.astype(jnp.bfloat16)
 
     return pl.pallas_call(
         body,

time: 35.7 us -> 35 us (0.980)
  waiting for transfers between devices: 4.47 us -> 3.88 us
where the time goes in v12:
time: 35 us; the launch traced here: 34.8 us
  Pallas kernels  14.8 us (42%)
  starting transfers between devices  14.5 us (41%)
  waiting for transfers between devices  3.88 us (11%)
  other arithmetic  0.78 us (2%)
  between operations  0.76 us (2%)
    ppermute x8, starting transfers between devices, swap(): return lax.ppermute(x, axis, [(i, i ^ distance) for i in range(size)])  10.9 us
    pallas_call x2, Pallas kernels, load_rows(): pl.pallas_call(body, out_shape=out_shape, in_specs=[ANY] * len(operands),...  6.91 us
    pallas_call x1, Pallas kernels, feed_forward(): pl.pallas_call(body, out_shape=outs, in_specs=[VMEM] * (3 + set_count) +...  6.04 us
    ppermute x3, starting transfers between devices, direct_swap(): return lax.ppermute(x, ('tp', 'sub'), pairs)  3.55 us
    ppermute x8, waiting for transfers between devices, swap(): return lax.ppermute(x, axis, [(i, i ^ distance) for i in range(size)])  3.33 us
    pallas_call x1, Pallas kernels, attend(): pl.pallas_call(body, out_shape=jax.ShapeDtypeStruct((slots, heads, KVL),...  1.6 us
  transfers between devices with their start and end apart: 11, of which 4 were waited for; matrix products, arithmetic and copies ran while one was open for 0% of the time, Pallas kernels for 24%

profile of v12, /device:TPU:0, one launch (start us, length us, event | category | flops | bytes accessed | tf_op | source)
XLA Modules:
  0.0 34.8 jit_solution(14453176568005697063)
XLA Ops:
  0.6 0.0 copy-start.2
  0.6 5.1 %collective-permute-start = (bf16[4,7168]{1,0:T(4,128)(2,1)}, bf16[4,7168]{1,0:T(4,128)(2,1)S(1)}, u32[]{:S(2)}, u32[]{:S(2)}) collective-permute-start(bf16[4,7168]{1,0:T(4,128)(2,1)} %bitcast.11), channel_id=1, source_target_pairs={{0,12},{2,14},{4,8},{6,10},{8,4},{10,6},{12,0},{14,2},{1,13},{3,15... | collective-permute-start | bytes 172040 | tf_op jit(solution)/shard_map/ppermute | solution.py:54
  5.8 0.0 collective-permute-start.1
  5.8 0.6 %collective-permute-start.2 = (bf16[4,7168]{1,0:T(4,128)(2,1)}, bf16[4,7168]{1,0:T(4,128)(2,1)S(1)}, u32[]{:S(2)}, u32[]{:S(2)}) collective-permute-start(bf16[4,7168]{1,0:T(4,128)(2,1)} %bitcast.13), channel_id=1, source_target_pairs={{0,4},{2,6},{4,0},{6,2},{8,12},{10,14},{12,8},{14,10},{1,5},{3,7},... | collective-permute-start | bytes 172040 | tf_op jit(solution)/shard_map/ppermute | solution.py:54
  6.4 3.5 %load_rows.2 = (bf16[576,7168]{1,0:T(8,128)(2,1)S(1)}, bf16[16,16]{1,0:T(8,128)(2,1)S(1)}) custom-call(bf16[1152,7168]{1,0:T(8,128)(2,1)} %refs_0_.2, s32[1,8]{1,0:T(1,128)} %counts_ref.1), custom_call_target="tpu_custom_call" | custom-call | bytes 16515072 | tf_op jit(solution)/shard_map/load_rows/pallas_call | solution.py:177
  9.9 0.0 copy-start.3
  9.9 0.0 collective-permute-done.refs_2_
  9.9 1.1 %collective-permute-done.1.refs_3_ = bf16[4,7168]{1,0:T(4,128)(2,1)S(1)} collective-permute-done((bf16[4,7168]{1,0:T(4,128)(2,1)}, bf16[4,7168]{1,0:T(4,128)(2,1)S(1)}, u32[]{:S(2)}, u32[]{:S(2)}) %collective-permute-start.1) | collective-permute-done | bytes 57376 | tf_op jit(solution)/shard_map/ppermute | solution.py:54
  11.0 0.0 collective-permute-done.2.refs_4_
  11.0 0.0 copy-done.2
  11.0 0.2 compact.1
  11.2 1.6 %collective-permute-start.3 = (bf16[8,7168]{1,0:T(8,128)(2,1)S(1)}, bf16[8,7168]{1,0:T(8,128)(2,1)S(1)}, u32[]{:S(2)}, u32[]{:S(2)}) collective-permute-start(bf16[8,7168]{1,0:T(8,128)(2,1)S(1)} %get-tuple-element.15.refs_1_), channel_id=1, source_target_pairs={{0,2},{2,0},{4,6},{6,4},{8,10},{10,8},{12,14},{14,12},{1,3},{3,1},... | collective-permute-start | bytes 344072 | tf_op jit(solution)/shard_map/ppermute | solution.py:54
  12.8 3.4 %load_rows.3.refs_4_ = bf16[576,7168]{1,0:T(8,128)(2,1)S(1)} custom-call(bf16[1152,7168]{1,0:T(8,128)(2,1)} %refs_0_.3, bf16[8,7168]{1,0:T(8,128)(2,1)S(1)} %get-tuple-element.15.refs_1_), custom_call_target="tpu_custom_call" | custom-call | bytes 16515072 | tf_op jit(solution)/shard_map/load_rows/pallas_call | solution.py:177
  16.3 0.0 collective-permute-done.3
  16.3 0.1 collective-permute-start.4
  16.4 1.3 %collective-permute-done.4.refs_2_ = bf16[8,7168]{1,0:T(8,128)(2,1)S(1)} collective-permute-done((bf16[8,7168]{1,0:T(8,128)(2,1)S(1)}, bf16[8,7168]{1,0:T(8,128)(2,1)S(1)}, u32[]{:S(2)}, u32[]{:S(2)}) %collective-permute-start.4) | collective-permute-done | bytes 114720 | tf_op jit(solution)/shard_map/ppermute | solution.py:54
  17.7 0.0 copy-done.3
  17.7 0.0 copy-start
  17.7 0.0 copy-start.1
  17.7 0.0 copy-start.4
  17.7 0.0 copy-start.5
  17.7 6.0 %feed_forward.1 = (f32[8,7168]{1,0:T(8,128)S(1)}, bf16[8,7168]{1,0:T(8,128)(2,1)S(1)}, bf16[2,7168]{1,0:T(2,128)(2,1)S(1)}) custom-call(f32[1,7168]{1,0:T(1,128)S(1)} %bitcast.15, bf16[8,7168]{1,0:T(8,128)(2,1)S(1)} %add.24.refs_1_, bf16[8,7168]{1,0:T(8,128)(2,1)S(1)} %collective-permute-done.4.refs_2_, bf16[576,7168]{1,0:T(8,128)(2,1)S(1)} %get-tuple-element.17.refs_3_, ...), custom_call_target="tpu_custom_call" | custom-call | flops 396361728 | bytes 24772608 | tf_op jit(solution)/shard_map/feed_forward/pallas_call | solution.py:273
  23.8 0.2 collective-permute-start.5
  24.0 2.6 %collective-permute-start.6 = (bf16[2,7168]{1,0:T(2,128)(2,1)S(1)}, bf16[2,7168]{1,0:T(2,128)(2,1)S(1)}, u32[]{:S(2)}, u32[]{:S(2)}) collective-permute-start(bf16[2,7168]{1,0:T(2,128)(2,1)S(1)} %get-tuple-element.21), channel_id=1, source_target_pairs={{0,12},{2,14},{4,8},{6,10},{8,4},{10,6},{12,0},{14,2},{1,13},{3,15... | collective-permute-start | bytes 86024 | tf_op jit(solution)/shard_map/ppermute | solution.py:54
  26.6 0.0 collective-permute-done.5
  26.7 0.1 fusion.8
  26.8 0.8 %collective-permute-start.7 = (bf16[2,7168]{1,0:T(2,128)(2,1)S(1)}, bf16[2,7168]{1,0:T(2,128)(2,1)S(1)}, u32[]{:S(2)}, u32[]{:S(2)}) collective-permute-start(bf16[2,7168]{1,0:T(2,128)(2,1)S(1)} %get-tuple-element.26), channel_id=1, source_target_pairs={{0,6},{1,15},{2,4},{3,13},{4,2},{5,11},{6,0},{7,9},{8,14},{9,7},{1... | collective-permute-start | bytes 86024 | tf_op jit(solution)/shard_map/ppermute | solution.py:59
  27.5 0.7 %collective-permute-start.8 = (bf16[2,7168]{1,0:T(2,128)(2,1)S(1)}, bf16[2,7168]{1,0:T(2,128)(2,1)S(1)}, u32[]{:S(2)}, u32[]{:S(2)}) collective-permute-start(bf16[2,7168]{1,0:T(2,128)(2,1)S(1)} %get-tuple-element.28), channel_id=1, source_target_pairs={{0,2},{1,11},{2,0},{3,9},{4,6},{5,15},{6,4},{7,13},{8,10},{9,3},{1... | collective-permute-start | bytes 86024 | tf_op jit(solution)/shard_map/ppermute | solution.py:59
  28.2 2.1 %collective-permute-start.9 = (bf16[2,7168]{1,0:T(2,128)(2,1)S(1)}, bf16[2,7168]{1,0:T(2,128)(2,1)S(1)}, u32[]{:S(2)}, u32[]{:S(2)}) collective-permute-start(bf16[2,7168]{1,0:T(2,128)(2,1)S(1)} %get-tuple-element.27), channel_id=1, source_target_pairs={{0,4},{1,9},{2,6},{3,11},{4,0},{5,13},{6,2},{7,15},{8,12},{9,1},{1... | collective-permute-start | bytes 86024 | tf_op jit(solution)/shard_map/ppermute | solution.py:59
  30.3 0.0 copy-done
  30.3 0.0 copy-done.1
  30.3 0.0 copy-done.4
  30.3 0.0 copy-done.5
  30.3 1.6 %attend.1 = bf16[4,64,512]{2,1,0:T(8,128)(2,1)} custom-call(s32[1,4]{1,0:T(1,128)S(1)} %copy-done.5, s32[1,8]{1,0:T(1,128)S(1)} %copy-done.4, bf16[4,64,576]{2,1,0:T(8,128)(2,1)S(1)} %bitcast.10, bf16[4,576,256]{2,1,0:T(8,128)(2,1)S(1)} %bitcast.9, bf16[8,7168]{1,0:T(8,128)(2,1)S(1)} %get-tuple-element.20._), custom_call_target="tpu_custom_call" | custom-call | flops 134217728 | bytes 1474560 | tf_op jit(solution)/shard_map/attend/pallas_call | solution.py:136
  31.9 0.0 collective-permute-done.6
  31.9 0.0 collective-permute-done.7
  31.9 0.0 collective-permute-done.8
  31.9 0.5 %collective-permute-done.9 = bf16[2,7168]{1,0:T(2,128)(2,1)S(1)} collective-permute-done((bf16[2,7168]{1,0:T(2,128)(2,1)S(1)}, bf16[2,7168]{1,0:T(2,128)(2,1)S(1)}, u32[]{:S(2)}, u32[]{:S(2)}) %collective-permute-start.9) | collective-permute-done | bytes 28704 | tf_op jit(solution)/shard_map/ppermute | solution.py:59
  32.5 0.1 fusion.3
  32.6 0.7 %collective-permute-start.10 = (f32[1,7168]{1,0:T(1,128)S(1)}, f32[1,7168]{1,0:T(1,128)S(1)}, u32[]{:S(2)}, u32[]{:S(2)}) collective-permute-start(f32[1,7168]{1,0:T(1,128)S(1)} %slice.29), channel_id=1, source_target_pairs={{0,1},{1,0},{2,3},{3,2},{4,5},{5,4},{6,7},{7,6},{8,9},{9,8},{10,11... | collective-permute-start | bytes 86024 | tf_op jit(solution)/shard_map/ppermute | solution.py:54
  33.3 0.9 %collective-permute-done.10 = f32[1,7168]{1,0:T(1,128)S(1)} collective-permute-done((f32[1,7168]{1,0:T(1,128)S(1)}, f32[1,7168]{1,0:T(1,128)S(1)}, u32[]{:S(2)}, u32[]{:S(2)}) %collective-permute-start.10) | collective-permute-done | bytes 28704 | tf_op jit(solution)/shard_map/ppermute | solution.py:54
  34.2 0.6 %fusion.6 = bf16[1,1,7168]{2,1,0:T(2,128)(2,1)} fusion(bf16[8,7168]{1,0:T(8,128)(2,1)S(1)} %add.24.refs_1_, f32[1,7168]{1,0:T(1,128)S(1)} %collective-permute-done.10, f32[2,7168]{1,0:T(2,128)S(1)} %fusion.3), kind=kLoop, calls=%fused_computation.9 | loop fusion | flops 28672 | bytes 86016 | tf_op jit(solution)/shard_map/broadcast_in_dim | solution.py:344
  (3 shorter events, 0.1 us)
Async XLA Ops:
  0.6 10.4 %copy-start.2 = (bf16[1,4,7168]{2,1,0:T(4,128)(2,1)S(1)}, bf16[1,4,7168]{2,1,0:T(4,128)(2,1)}, u32[]{:S(2)}) copy-start(bf16[1,4,7168]{2,1,0:T(4,128)(2,1)} %param.13) | copy-start | bytes 172036
  0.6 9.2 %collective-permute-start = (bf16[4,7168]{1,0:T(4,128)(2,1)}, bf16[4,7168]{1,0:T(4,128)(2,1)S(1)}, u32[]{:S(2)}, u32[]{:S(2)}) collective-permute-start(bf16[4,7168]{1,0:T(4,128)(2,1)} %bitcast.11), channel_id=1, source_target_pairs={{0,12},{2,14},{4,8},{6,10},{8,4},{10,6},{12,0},{14,2},{1,13},{3,15... | collective-permute-start | bytes 172040 | tf_op jit(solution)/shard_map/ppermute | solution.py:54
  5.8 5.3 %collective-permute-start.1 = (bf16[4,7168]{1,0:T(4,128)(2,1)}, bf16[4,7168]{1,0:T(4,128)(2,1)S(1)}, u32[]{:S(2)}, u32[]{:S(2)}) collective-permute-start(bf16[4,7168]{1,0:T(4,128)(2,1)} %bitcast.12), channel_id=1, source_target_pairs={{0,8},{2,10},{4,12},{6,14},{8,0},{10,2},{12,4},{14,6},{1,9},{3,11}... | collective-permute-start | bytes 172040 | tf_op jit(solution)/shard_map/ppermute | solution.py:54
  5.8 5.3 %collective-permute-start.2 = (bf16[4,7168]{1,0:T(4,128)(2,1)}, bf16[4,7168]{1,0:T(4,128)(2,1)S(1)}, u32[]{:S(2)}, u32[]{:S(2)}) collective-permute-start(bf16[4,7168]{1,0:T(4,128)(2,1)} %bitcast.13), channel_id=1, source_target_pairs={{0,4},{2,6},{4,0},{6,2},{8,12},{10,14},{12,8},{14,10},{1,5},{3,7},... | collective-permute-start | bytes 172040 | tf_op jit(solution)/shard_map/ppermute | solution.py:54
  9.9 7.9 %copy-start.3 = (f32[7168]{0:T(1024)S(1)}, f32[7168]{0:T(1024)}, u32[]{:S(2)}) copy-start(f32[7168]{0:T(1024)} %param.14) | copy-start | bytes 86020
  11.2 5.0 %collective-permute-start.3 = (bf16[8,7168]{1,0:T(8,128)(2,1)S(1)}, bf16[8,7168]{1,0:T(8,128)(2,1)S(1)}, u32[]{:S(2)}, u32[]{:S(2)}) collective-permute-start(bf16[8,7168]{1,0:T(8,128)(2,1)S(1)} %get-tuple-element.15.refs_1_), channel_id=1, source_target_pairs={{0,2},{2,0},{4,6},{6,4},{8,10},{10,8},{12,14},{14,12},{1,3},{3,1},... | collective-permute-start | bytes 344072 | tf_op jit(solution)/shard_map/ppermute | solution.py:54
  16.3 1.4 %collective-permute-start.4 = (bf16[8,7168]{1,0:T(8,128)(2,1)S(1)}, bf16[8,7168]{1,0:T(8,128)(2,1)S(1)}, u32[]{:S(2)}, u32[]{:S(2)}) collective-permute-start(bf16[8,7168]{1,0:T(8,128)(2,1)S(1)} %add.24.refs_1_), channel_id=1, source_target_pairs={{0,1},{1,0},{2,3},{3,2},{4,5},{5,4},{6,7},{7,6},{8,9},{9,8},{10,11... | collective-permute-start | bytes 344072 | tf_op jit(solution)/shard_map/ppermute | solution.py:54
  17.7 12.6 %copy-start = (bf16[1,4,256,576]{2,3,1,0:T(8,128)(2,1)S(1)}, bf16[1,4,256,576]{2,3,1,0:T(8,128)(2,1)}, u32[]{:S(2)}) copy-start(bf16[1,4,256,576]{2,3,1,0:T(8,128)(2,1)} %param.10) | copy-start | bytes 3538948
  17.7 12.6 %copy-start.1 = (bf16[1,4,64,576]{3,2,1,0:T(8,128)(2,1)S(1)}, bf16[1,4,64,576]{3,2,1,0:T(8,128)(2,1)}, u32[]{:S(2)}) copy-start(bf16[1,4,64,576]{3,2,1,0:T(8,128)(2,1)} %param.9) | copy-start | bytes 884740
  17.7 12.6 %copy-start.4 = (s32[1,8]{1,0:T(1,128)S(1)}, s32[1,8]{1,0:T(1,128)}, u32[]{:S(2)}) copy-start(s32[1,8]{1,0:T(1,128)} %counts_ref.1) | copy-start | bytes 100
  17.7 12.6 %copy-start.5 = (s32[1,4]{1,0:T(1,128)S(1)}, s32[1,4]{1,0:T(1,128)}, u32[]{:S(2)}) copy-start(s32[1,4]{1,0:T(1,128)} %lengths_ref.1) | copy-start | bytes 52
  23.8 2.8 %collective-permute-start.5 = (bf16[8,7168]{1,0:T(8,128)(2,1)S(1)}, bf16[8,7168]{1,0:T(8,128)(2,1)S(1)}, u32[]{:S(2)}, u32[]{:S(2)}) collective-permute-start(bf16[8,7168]{1,0:T(8,128)(2,1)S(1)} %get-tuple-element.20._), channel_id=1, source_target_pairs={{0,1},{1,0},{2,3},{3,2},{4,5},{5,4},{6,7},{7,6},{8,9},{9,8},{10,11... | collective-permute-start | bytes 344072 | tf_op jit(solution)/shard_map/ppermute | solution.py:54
  24.0 7.9 %collective-permute-start.6 = (bf16[2,7168]{1,0:T(2,128)(2,1)S(1)}, bf16[2,7168]{1,0:T(2,128)(2,1)S(1)}, u32[]{:S(2)}, u32[]{:S(2)}) collective-permute-start(bf16[2,7168]{1,0:T(2,128)(2,1)S(1)} %get-tuple-element.21), channel_id=1, source_target_pairs={{0,12},{2,14},{4,8},{6,10},{8,4},{10,6},{12,0},{14,2},{1,13},{3,15... | collective-permute-start | bytes 86024 | tf_op jit(solution)/shard_map/ppermute | solution.py:54
  26.8 5.2 %collective-permute-start.7 = (bf16[2,7168]{1,0:T(2,128)(2,1)S(1)}, bf16[2,7168]{1,0:T(2,128)(2,1)S(1)}, u32[]{:S(2)}, u32[]{:S(2)}) collective-permute-start(bf16[2,7168]{1,0:T(2,128)(2,1)S(1)} %get-tuple-element.26), channel_id=1, source_target_pairs={{0,6},{1,15},{2,4},{3,13},{4,2},{5,11},{6,0},{7,9},{8,14},{9,7},{1... | collective-permute-start | bytes 86024 | tf_op jit(solution)/shard_map/ppermute | solution.py:59
  27.5 4.4 %collective-permute-start.8 = (bf16[2,7168]{1,0:T(2,128)(2,1)S(1)}, bf16[2,7168]{1,0:T(2,128)(2,1)S(1)}, u32[]{:S(2)}, u32[]{:S(2)}) collective-permute-start(bf16[2,7168]{1,0:T(2,128)(2,1)S(1)} %get-tuple-element.28), channel_id=1, source_target_pairs={{0,2},{1,11},{2,0},{3,9},{4,6},{5,15},{6,4},{7,13},{8,10},{9,3},{1... | collective-permute-start | bytes 86024 | tf_op jit(solution)/shard_map/ppermute | solution.py:59
  28.2 4.2 %collective-permute-start.9 = (bf16[2,7168]{1,0:T(2,128)(2,1)S(1)}, bf16[2,7168]{1,0:T(2,128)(2,1)S(1)}, u32[]{:S(2)}, u32[]{:S(2)}) collective-permute-start(bf16[2,7168]{1,0:T(2,128)(2,1)S(1)} %get-tuple-element.27), channel_id=1, source_target_pairs={{0,4},{1,9},{2,6},{3,11},{4,0},{5,13},{6,2},{7,15},{8,12},{9,1},{1... | collective-permute-start | bytes 86024 | tf_op jit(solution)/shard_map/ppermute | solution.py:59
  32.6 1.6 %collective-permute-start.10 = (f32[1,7168]{1,0:T(1,128)S(1)}, f32[1,7168]{1,0:T(1,128)S(1)}, u32[]{:S(2)}, u32[]{:S(2)}) collective-permute-start(f32[1,7168]{1,0:T(1,128)S(1)} %slice.29), channel_id=1, source_target_pairs={{0,1},{1,0},{2,3},{3,2},{4,5},{5,4},{6,7},{7,6},{8,9},{9,8},{10,11... | collective-permute-start | bytes 86024 | tf_op jit(solution)/shard_map/ppermute | solution.py:54

commit v13 on v12

--- a/solution.py
+++ b/solution.py
@@ -213,6 +213,25 @@
     )(pick, *blocks)
 
 
+def normalize(rows, gain):
+    inv_rms = lax.rsqrt(jnp.mean(rows * rows, axis=1, keepdims=True) + norm_eps)
+    return (rows * inv_rms * gain).astype(jnp.bfloat16)
+
+
+def normalized(rows, gain):
+    def body(rows_ref, gain_ref, out_ref):
+        out_ref[...] = normalize(rows_ref[...].astype(jnp.float32), gain_ref[...])
+
+    return pl.pallas_call(
+        body,
+        out_shape=jax.ShapeDtypeStruct(rows.shape, jnp.bfloat16),
+        in_specs=[VMEM] * 2,
+        out_specs=VMEM,
+        compiler_params=pltpu.CompilerParams(vmem_limit_bytes=16 * MIB),
+        name="normalized",
+    )(rows, gain[None])
+
+
 def feed_forward(gain, row_sets, gate, up, w_down):
     requests, width = row_sets[0].shape
     units = w_down.shape[0]
@@ -237,10 +256,11 @@
         down_copy = (down_hbm, share_start(units, share), down_ref, down_sems)
         start_pieces(down_copy)
 
-        rows = [ref[...].astype(jnp.float32) for ref in set_refs]
+        rows = [set_refs[0][...].astype(jnp.float32)]
+        for ref in set_refs[1:]:
+            rows.append(normalize(ref[...].astype(jnp.float32), gain_ref[...]).astype(jnp.float32))
         rows = rows[0] if set_count == 1 else jnp.concatenate(rows, axis=0)
-        inv_rms = lax.rsqrt(jnp.mean(rows * rows, axis=1, keepdims=True) + norm_eps)
-        normed_ref[...] = (rows * inv_rms * gain_ref[...]).astype(jnp.bfloat16)
+        normed_ref[...] = rows.astype(jnp.bfloat16)
 
         for weight_ref, out_ref in ((gate_weight, gate_ref), (up_weight, up_ref)):
             for j in range(0, share, chunk):
@@ -315,7 +335,9 @@
         (up,) = load_rows(w_up, share, after=send)
         arrived, up = lax.optimization_barrier((arrived, up))
         rows = own + arrived
-        row_sets = [rows, swap(rows, "sub", 1, cores)] if split else [rows]
+        row_sets = [normalized(rows, norm_gain)]
+        if split:
+            row_sets.append(swap(rows, "sub", 1, cores))
         total, *other = feed_forward(norm_gain, row_sets, gate, up, w_down)
 
         cache = jnp.swapaxes(kv_cache[0], 1, 2)

time: 35 us -> 34.9 us (level)
  transfers between devices with their start and end apart: 11 -> 11, of which waited for: 4 -> 4; matrix products, arithmetic and copies ran while one was open for 0% -> 0% of each run, Pallas kernels for 24% -> 25%
where the time goes in v13:
time: 34.9 us; the launch traced here: 34.8 us
  Pallas kernels  14.9 us (43%)
  starting transfers between devices  14.5 us (42%)
  waiting for transfers between devices  3.69 us (11%)
  other arithmetic  0.78 us (2%)
  between operations  0.77 us (2%)
    ppermute x8, starting transfers between devices, swap(): return lax.ppermute(x, axis, [(i, i ^ distance) for i in range(size)])  11 us
    pallas_call x2, Pallas kernels, load_rows(): pl.pallas_call(body, out_shape=out_shape, in_specs=[ANY] * len(operands),...  6.91 us
    pallas_call x1, Pallas kernels, feed_forward(): pl.pallas_call(body, out_shape=outs, in_specs=[VMEM] * (3 + set_count) +...  6.02 us
    ppermute x3, starting transfers between devices, direct_swap(): return lax.ppermute(x, ('tp', 'sub'), pairs)  3.55 us
    ppermute x8, waiting for transfers between devices, swap(): return lax.ppermute(x, axis, [(i, i ^ distance) for i in range(size)])  3.14 us
    pallas_call x1, Pallas kernels, attend(): pl.pallas_call(body, out_shape=jax.ShapeDtypeStruct((slots, heads, KVL),...  1.6 us
  transfers between devices with their start and end apart: 11, of which 4 were waited for; matrix products, arithmetic and copies ran while one was open for 0% of the time, Pallas kernels for 25%

profile of v13, /device:TPU:0, one launch (start us, length us, event | category | flops | bytes accessed | tf_op | source)
XLA Modules:
  0.0 34.8 jit_solution(3710422371089573458)
XLA Ops:
  0.6 0.0 copy-start.3
  0.6 5.1 %collective-permute-start = (bf16[4,7168]{1,0:T(4,128)(2,1)}, bf16[4,7168]{1,0:T(4,128)(2,1)S(1)}, u32[]{:S(2)}, u32[]{:S(2)}) collective-permute-start(bf16[4,7168]{1,0:T(4,128)(2,1)} %bitcast.13), channel_id=1, source_target_pairs={{0,12},{2,14},{4,8},{6,10},{8,4},{10,6},{12,0},{14,2},{1,13},{3,15... | collective-permute-start | bytes 172040 | tf_op jit(solution)/shard_map/ppermute | solution.py:54
  5.8 0.0 collective-permute-start.1
  5.8 0.6 %collective-permute-start.2 = (bf16[4,7168]{1,0:T(4,128)(2,1)}, bf16[4,7168]{1,0:T(4,128)(2,1)S(1)}, u32[]{:S(2)}, u32[]{:S(2)}) collective-permute-start(bf16[4,7168]{1,0:T(4,128)(2,1)} %bitcast.15), channel_id=1, source_target_pairs={{0,4},{2,6},{4,0},{6,2},{8,12},{10,14},{12,8},{14,10},{1,5},{3,7},... | collective-permute-start | bytes 172040 | tf_op jit(solution)/shard_map/ppermute | solution.py:54
  6.4 3.5 %load_rows.2 = (bf16[576,7168]{1,0:T(8,128)(2,1)S(1)}, bf16[16,16]{1,0:T(8,128)(2,1)S(1)}) custom-call(bf16[1152,7168]{1,0:T(8,128)(2,1)} %refs_0_.2, s32[1,8]{1,0:T(1,128)} %counts_ref.1), custom_call_target="tpu_custom_call" | custom-call | bytes 16515072 | tf_op jit(solution)/shard_map/load_rows/pallas_call | solution.py:177
  9.9 0.0 copy-start.2
  9.9 0.0 collective-permute-done.refs_2_
  9.9 1.1 %collective-permute-done.1.refs_3_ = bf16[4,7168]{1,0:T(4,128)(2,1)S(1)} collective-permute-done((bf16[4,7168]{1,0:T(4,128)(2,1)}, bf16[4,7168]{1,0:T(4,128)(2,1)S(1)}, u32[]{:S(2)}, u32[]{:S(2)}) %collective-permute-start.1) | collective-permute-done | bytes 57376 | tf_op jit(solution)/shard_map/ppermute | solution.py:54
  11.0 0.0 collective-permute-done.2.refs_4_
  11.0 0.0 copy-done.3
  11.0 0.2 compact.1
  11.2 1.6 %collective-permute-start.3 = (bf16[8,7168]{1,0:T(8,128)(2,1)S(1)}, bf16[8,7168]{1,0:T(8,128)(2,1)S(1)}, u32[]{:S(2)}, u32[]{:S(2)}) collective-permute-start(bf16[8,7168]{1,0:T(8,128)(2,1)S(1)} %get-tuple-element.15.refs_1_), channel_id=1, source_target_pairs={{0,2},{2,0},{4,6},{6,4},{8,10},{10,8},{12,14},{14,12},{1,3},{3,1},... | collective-permute-start | bytes 344072 | tf_op jit(solution)/shard_map/ppermute | solution.py:54
  12.8 3.4 %load_rows.3.refs_4_ = bf16[576,7168]{1,0:T(8,128)(2,1)S(1)} custom-call(bf16[1152,7168]{1,0:T(8,128)(2,1)} %refs_0_.3, bf16[8,7168]{1,0:T(8,128)(2,1)S(1)} %get-tuple-element.15.refs_1_), custom_call_target="tpu_custom_call" | custom-call | bytes 16515072 | tf_op jit(solution)/shard_map/load_rows/pallas_call | solution.py:177
  16.3 0.0 collective-permute-done.3
  16.3 0.1 collective-permute-start.4
  16.4 0.0 copy-done.2
  16.4 0.2 normalized.1.refs_1_
  16.6 1.1 %collective-permute-done.4.refs_2_ = bf16[8,7168]{1,0:T(8,128)(2,1)S(1)} collective-permute-done((bf16[8,7168]{1,0:T(8,128)(2,1)S(1)}, bf16[8,7168]{1,0:T(8,128)(2,1)S(1)}, u32[]{:S(2)}, u32[]{:S(2)}) %collective-permute-start.4) | collective-permute-done | bytes 114720 | tf_op jit(solution)/shard_map/ppermute | solution.py:54
  17.7 0.0 copy-start
  17.7 0.0 copy-start.1
  17.7 0.0 copy-start.4
  17.7 0.0 copy-start.5
  17.7 6.0 %feed_forward.1 = (f32[8,7168]{1,0:T(8,128)S(1)}, bf16[8,7168]{1,0:T(8,128)(2,1)S(1)}, bf16[2,7168]{1,0:T(2,128)(2,1)S(1)}) custom-call(f32[1,7168]{1,0:T(1,128)S(1)} %bitcast.12, bf16[8,7168]{1,0:T(8,128)(2,1)S(1)} %normalized.1.refs_1_, bf16[8,7168]{1,0:T(8,128)(2,1)S(1)} %collective-permute-done.4.refs_2_, ...), custom_call_target="tpu_custom_call" | custom-call | flops 396361728 | bytes 24772608 | tf_op jit(solution)/shard_map/feed_forward/pallas_call | solution.py:293
  23.8 0.2 collective-permute-start.5
  24.0 2.6 %collective-permute-start.6 = (bf16[2,7168]{1,0:T(2,128)(2,1)S(1)}, bf16[2,7168]{1,0:T(2,128)(2,1)S(1)}, u32[]{:S(2)}, u32[]{:S(2)}) collective-permute-start(bf16[2,7168]{1,0:T(2,128)(2,1)S(1)} %get-tuple-element.21), channel_id=1, source_target_pairs={{0,12},{2,14},{4,8},{6,10},{8,4},{10,6},{12,0},{14,2},{1,13},{3,15... | collective-permute-start | bytes 86024 | tf_op jit(solution)/shard_map/ppermute | solution.py:54
  26.6 0.0 collective-permute-done.5
  26.6 0.1 fusion.8
  26.7 0.8 %collective-permute-start.7 = (bf16[2,7168]{1,0:T(2,128)(2,1)S(1)}, bf16[2,7168]{1,0:T(2,128)(2,1)S(1)}, u32[]{:S(2)}, u32[]{:S(2)}) collective-permute-start(bf16[2,7168]{1,0:T(2,128)(2,1)S(1)} %get-tuple-element.26), channel_id=1, source_target_pairs={{0,6},{1,15},{2,4},{3,13},{4,2},{5,11},{6,0},{7,9},{8,14},{9,7},{1... | collective-permute-start | bytes 86024 | tf_op jit(solution)/shard_map/ppermute | solution.py:59
  27.5 0.7 %collective-permute-start.8 = (bf16[2,7168]{1,0:T(2,128)(2,1)S(1)}, bf16[2,7168]{1,0:T(2,128)(2,1)S(1)}, u32[]{:S(2)}, u32[]{:S(2)}) collective-permute-start(bf16[2,7168]{1,0:T(2,128)(2,1)S(1)} %get-tuple-element.28), channel_id=1, source_target_pairs={{0,2},{1,11},{2,0},{3,9},{4,6},{5,15},{6,4},{7,13},{8,10},{9,3},{1... | collective-permute-start | bytes 86024 | tf_op jit(solution)/shard_map/ppermute | solution.py:59
  28.2 2.1 %collective-permute-start.9 = (bf16[2,7168]{1,0:T(2,128)(2,1)S(1)}, bf16[2,7168]{1,0:T(2,128)(2,1)S(1)}, u32[]{:S(2)}, u32[]{:S(2)}) collective-permute-start(bf16[2,7168]{1,0:T(2,128)(2,1)S(1)} %get-tuple-element.27), channel_id=1, source_target_pairs={{0,4},{1,9},{2,6},{3,11},{4,0},{5,13},{6,2},{7,15},{8,12},{9,1},{1... | collective-permute-start | bytes 86024 | tf_op jit(solution)/shard_map/ppermute | solution.py:59
  30.3 0.0 copy-done
  30.3 0.0 copy-done.1
  30.3 0.0 copy-done.4
  30.3 0.0 copy-done.5
  30.3 1.6 %attend.1 = bf16[4,64,512]{2,1,0:T(8,128)(2,1)} custom-call(s32[1,4]{1,0:T(1,128)S(1)} %copy-done.5, s32[1,8]{1,0:T(1,128)S(1)} %copy-done.4, bf16[4,64,576]{2,1,0:T(8,128)(2,1)S(1)} %bitcast.10, bf16[4,576,256]{2,1,0:T(8,128)(2,1)S(1)} %bitcast.9, bf16[8,7168]{1,0:T(8,128)(2,1)S(1)} %get-tuple-element.20._), custom_call_target="tpu_custom_call" | custom-call | flops 134217728 | bytes 1474560 | tf_op jit(solution)/shard_map/attend/pallas_call | solution.py:136
  31.9 0.0 collective-permute-done.6
  31.9 0.0 collective-permute-done.7
  31.9 0.0 collective-permute-done.8
  31.9 0.5 %collective-permute-done.9 = bf16[2,7168]{1,0:T(2,128)(2,1)S(1)} collective-permute-done((bf16[2,7168]{1,0:T(2,128)(2,1)S(1)}, bf16[2,7168]{1,0:T(2,128)(2,1)S(1)}, u32[]{:S(2)}, u32[]{:S(2)}) %collective-permute-start.9) | collective-permute-done | bytes 28704 | tf_op jit(solution)/shard_map/ppermute | solution.py:59
  32.4 0.1 fusion.3
  32.6 0.7 %collective-permute-start.10 = (f32[1,7168]{1,0:T(1,128)S(1)}, f32[1,7168]{1,0:T(1,128)S(1)}, u32[]{:S(2)}, u32[]{:S(2)}) collective-permute-start(f32[1,7168]{1,0:T(1,128)S(1)} %slice.29), channel_id=1, source_target_pairs={{0,1},{1,0},{2,3},{3,2},{4,5},{5,4},{6,7},{7,6},{8,9},{9,8},{10,11... | collective-permute-start | bytes 86024 | tf_op jit(solution)/shard_map/ppermute | solution.py:54
  33.3 0.9 %collective-permute-done.10 = f32[1,7168]{1,0:T(1,128)S(1)} collective-permute-done((f32[1,7168]{1,0:T(1,128)S(1)}, f32[1,7168]{1,0:T(1,128)S(1)}, u32[]{:S(2)}, u32[]{:S(2)}) %collective-permute-start.10) | collective-permute-done | bytes 28704 | tf_op jit(solution)/shard_map/ppermute | solution.py:54
  34.1 0.6 %fusion.6 = bf16[1,1,7168]{2,1,0:T(2,128)(2,1)} fusion(bf16[8,7168]{1,0:T(8,128)(2,1)S(1)} %add.24.rows_ref, f32[1,7168]{1,0:T(1,128)S(1)} %collective-permute-done.10, f32[2,7168]{1,0:T(2,128)S(1)} %fusion.3), kind=kLoop, calls=%fused_computation.9 | loop fusion | flops 28672 | bytes 86016 | tf_op jit(solution)/shard_map/broadcast_in_dim | solution.py:366
  (3 shorter events, 0.1 us)
Async XLA Ops:
  0.6 10.4 %copy-start.3 = (bf16[1,4,7168]{2,1,0:T(4,128)(2,1)S(1)}, bf16[1,4,7168]{2,1,0:T(4,128)(2,1)}, u32[]{:S(2)}) copy-start(bf16[1,4,7168]{2,1,0:T(4,128)(2,1)} %param.13) | copy-start | bytes 172036
  0.6 9.2 %collective-permute-start = (bf16[4,7168]{1,0:T(4,128)(2,1)}, bf16[4,7168]{1,0:T(4,128)(2,1)S(1)}, u32[]{:S(2)}, u32[]{:S(2)}) collective-permute-start(bf16[4,7168]{1,0:T(4,128)(2,1)} %bitcast.13), channel_id=1, source_target_pairs={{0,12},{2,14},{4,8},{6,10},{8,4},{10,6},{12,0},{14,2},{1,13},{3,15... | collective-permute-start | bytes 172040 | tf_op jit(solution)/shard_map/ppermute | solution.py:54
  5.8 5.3 %collective-permute-start.1 = (bf16[4,7168]{1,0:T(4,128)(2,1)}, bf16[4,7168]{1,0:T(4,128)(2,1)S(1)}, u32[]{:S(2)}, u32[]{:S(2)}) collective-permute-start(bf16[4,7168]{1,0:T(4,128)(2,1)} %bitcast.14), channel_id=1, source_target_pairs={{0,8},{2,10},{4,12},{6,14},{8,0},{10,2},{12,4},{14,6},{1,9},{3,11}... | collective-permute-start | bytes 172040 | tf_op jit(solution)/shard_map/ppermute | solution.py:54
  5.8 5.3 %collective-permute-start.2 = (bf16[4,7168]{1,0:T(4,128)(2,1)}, bf16[4,7168]{1,0:T(4,128)(2,1)S(1)}, u32[]{:S(2)}, u32[]{:S(2)}) collective-permute-start(bf16[4,7168]{1,0:T(4,128)(2,1)} %bitcast.15), channel_id=1, source_target_pairs={{0,4},{2,6},{4,0},{6,2},{8,12},{10,14},{12,8},{14,10},{1,5},{3,7},... | collective-permute-start | bytes 172040 | tf_op jit(solution)/shard_map/ppermute | solution.py:54
  9.9 6.5 %copy-start.2 = (f32[7168]{0:T(1024)S(1)}, f32[7168]{0:T(1024)}, u32[]{:S(2)}) copy-start(f32[7168]{0:T(1024)} %param.14) | copy-start | bytes 86020
  11.2 5.0 %collective-permute-start.3 = (bf16[8,7168]{1,0:T(8,128)(2,1)S(1)}, bf16[8,7168]{1,0:T(8,128)(2,1)S(1)}, u32[]{:S(2)}, u32[]{:S(2)}) collective-permute-start(bf16[8,7168]{1,0:T(8,128)(2,1)S(1)} %get-tuple-element.15.refs_1_), channel_id=1, source_target_pairs={{0,2},{2,0},{4,6},{6,4},{8,10},{10,8},{12,14},{14,12},{1,3},{3,1},... | collective-permute-start | bytes 344072 | tf_op jit(solution)/shard_map/ppermute | solution.py:54
  16.3 1.4 %collective-permute-start.4 = (bf16[8,7168]{1,0:T(8,128)(2,1)S(1)}, bf16[8,7168]{1,0:T(8,128)(2,1)S(1)}, u32[]{:S(2)}, u32[]{:S(2)}) collective-permute-start(bf16[8,7168]{1,0:T(8,128)(2,1)S(1)} %add.24.rows_ref), channel_id=1, source_target_pairs={{0,1},{1,0},{2,3},{3,2},{4,5},{5,4},{6,7},{7,6},{8,9},{9,8},{10,11... | collective-permute-start | bytes 344072 | tf_op jit(solution)/shard_map/ppermute | solution.py:54
  17.7 12.5 %copy-start = (bf16[1,4,256,576]{2,3,1,0:T(8,128)(2,1)S(1)}, bf16[1,4,256,576]{2,3,1,0:T(8,128)(2,1)}, u32[]{:S(2)}) copy-start(bf16[1,4,256,576]{2,3,1,0:T(8,128)(2,1)} %param.10) | copy-start | bytes 3538948
  17.7 12.5 %copy-start.1 = (bf16[1,4,64,576]{3,2,1,0:T(8,128)(2,1)S(1)}, bf16[1,4,64,576]{3,2,1,0:T(8,128)(2,1)}, u32[]{:S(2)}) copy-start(bf16[1,4,64,576]{3,2,1,0:T(8,128)(2,1)} %param.9) | copy-start | bytes 884740
  17.7 12.5 %copy-start.4 = (s32[1,8]{1,0:T(1,128)S(1)}, s32[1,8]{1,0:T(1,128)}, u32[]{:S(2)}) copy-start(s32[1,8]{1,0:T(1,128)} %counts_ref.1) | copy-start | bytes 100
  17.7 12.5 %copy-start.5 = (s32[1,4]{1,0:T(1,128)S(1)}, s32[1,4]{1,0:T(1,128)}, u32[]{:S(2)}) copy-start(s32[1,4]{1,0:T(1,128)} %lengths_ref.1) | copy-start | bytes 52
  23.8 2.8 %collective-permute-start.5 = (bf16[8,7168]{1,0:T(8,128)(2,1)S(1)}, bf16[8,7168]{1,0:T(8,128)(2,1)S(1)}, u32[]{:S(2)}, u32[]{:S(2)}) collective-permute-start(bf16[8,7168]{1,0:T(8,128)(2,1)S(1)} %get-tuple-element.20._), channel_id=1, source_target_pairs={{0,1},{1,0},{2,3},{3,2},{4,5},{5,4},{6,7},{7,6},{8,9},{9,8},{10,11... | collective-permute-start | bytes 344072 | tf_op jit(solution)/shard_map/ppermute | solution.py:54
  24.0 7.9 %collective-permute-start.6 = (bf16[2,7168]{1,0:T(2,128)(2,1)S(1)}, bf16[2,7168]{1,0:T(2,128)(2,1)S(1)}, u32[]{:S(2)}, u32[]{:S(2)}) collective-permute-start(bf16[2,7168]{1,0:T(2,128)(2,1)S(1)} %get-tuple-element.21), channel_id=1, source_target_pairs={{0,12},{2,14},{4,8},{6,10},{8,4},{10,6},{12,0},{14,2},{1,13},{3,15... | collective-permute-start | bytes 86024 | tf_op jit(solution)/shard_map/ppermute | solution.py:54
  26.7 5.2 %collective-permute-start.7 = (bf16[2,7168]{1,0:T(2,128)(2,1)S(1)}, bf16[2,7168]{1,0:T(2,128)(2,1)S(1)}, u32[]{:S(2)}, u32[]{:S(2)}) collective-permute-start(bf16[2,7168]{1,0:T(2,128)(2,1)S(1)} %get-tuple-element.26), channel_id=1, source_target_pairs={{0,6},{1,15},{2,4},{3,13},{4,2},{5,11},{6,0},{7,9},{8,14},{9,7},{1... | collective-permute-start | bytes 86024 | tf_op jit(solution)/shard_map/ppermute | solution.py:59
  27.5 4.4 %collective-permute-start.8 = (bf16[2,7168]{1,0:T(2,128)(2,1)S(1)}, bf16[2,7168]{1,0:T(2,128)(2,1)S(1)}, u32[]{:S(2)}, u32[]{:S(2)}) collective-permute-start(bf16[2,7168]{1,0:T(2,128)(2,1)S(1)} %get-tuple-element.28), channel_id=1, source_target_pairs={{0,2},{1,11},{2,0},{3,9},{4,6},{5,15},{6,4},{7,13},{8,10},{9,3},{1... | collective-permute-start | bytes 86024 | tf_op jit(solution)/shard_map/ppermute | solution.py:59
  28.2 4.2 %collective-permute-start.9 = (bf16[2,7168]{1,0:T(2,128)(2,1)S(1)}, bf16[2,7168]{1,0:T(2,128)(2,1)S(1)}, u32[]{:S(2)}, u32[]{:S(2)}) collective-permute-start(bf16[2,7168]{1,0:T(2,128)(2,1)S(1)} %get-tuple-element.27), channel_id=1, source_target_pairs={{0,4},{1,9},{2,6},{3,11},{4,0},{5,13},{6,2},{7,15},{8,12},{9,1},{1... | collective-permute-start | bytes 86024 | tf_op jit(solution)/shard_map/ppermute | solution.py:59
  32.6 1.6 %collective-permute-start.10 = (f32[1,7168]{1,0:T(1,128)S(1)}, f32[1,7168]{1,0:T(1,128)S(1)}, u32[]{:S(2)}, u32[]{:S(2)}) collective-permute-start(f32[1,7168]{1,0:T(1,128)S(1)} %slice.29), channel_id=1, source_target_pairs={{0,1},{1,0},{2,3},{3,2},{4,5},{5,4},{6,7},{7,6},{8,9},{9,8},{10,11... | collective-permute-start | bytes 86024 | tf_op jit(solution)/shard_map/ppermute | solution.py:54

commit v14 on v13

--- a/solution.py
+++ b/solution.py
@@ -267,6 +267,8 @@
                 out_ref[j : j + chunk, :] = lax.dot_general(
                     weight_ref[j : j + chunk, :], normed_ref[...], (((1,), (1,)), ((), ())), preferred_element_type=jnp.float32
                 )
+        wait_pieces(down_copy)
+
         hidden = (jax.nn.silu(gate_ref[...]) * up_ref[...]).astype(jnp.bfloat16)
         place = lax.broadcasted_iota(jnp.int32, (every, every), 0)
         if set_count == 2:
@@ -280,8 +282,6 @@
         hidden_ref[...] = lax.dot_general(
             order, hidden, (((1,), (1,)), ((), ())), preferred_element_type=jnp.float32
         ).astype(jnp.bfloat16)
-
-        wait_pieces(down_copy)
         for c in range(0, width, column):
             out = jnp.dot(hidden_ref[...], down_ref[:, c : c + column], preferred_element_type=jnp.float32)
             out_refs[0][:, c : c + column] = out[:requests]

time: 34.9 us -> 34.9 us (level)
  no operation moved by 1% of the time
where the time goes in v14:
time: 34.9 us; the launch traced here: 34.8 us
  Pallas kernels  14.9 us (43%)
  starting transfers between devices  14.5 us (42%)
  waiting for transfers between devices  3.69 us (11%)
  other arithmetic  0.78 us (2%)
  between operations  0.77 us (2%)
    ppermute x8, starting transfers between devices, swap(): return lax.ppermute(x, axis, [(i, i ^ distance) for i in range(size)])  11 us
    pallas_call x2, Pallas kernels, load_rows(): pl.pallas_call(body, out_shape=out_shape, in_specs=[ANY] * len(operands),...  6.91 us
    pallas_call x1, Pallas kernels, feed_forward(): pl.pallas_call(body, out_shape=outs, in_specs=[VMEM] * (3 + set_count) +...  5.99 us
    ppermute x3, starting transfers between devices, direct_swap(): return lax.ppermute(x, ('tp', 'sub'), pairs)  3.55 us
    ppermute x8, waiting for transfers between devices, swap(): return lax.ppermute(x, axis, [(i, i ^ distance) for i in range(size)])  3.14 us
    pallas_call x1, Pallas kernels, attend(): pl.pallas_call(body, out_shape=jax.ShapeDtypeStruct((slots, heads, KVL),...  1.6 us
  transfers between devices with their start and end apart: 11, of which 4 were waited for; matrix products, arithmetic and copies ran while one was open for 0% of the time, Pallas kernels for 25%

profile of v14, /device:TPU:0, one launch (start us, length us, event | category | flops | bytes accessed | tf_op | source)
XLA Modules:
  0.0 34.8 jit_solution(5258948652462991512)
XLA Ops:
  0.6 0.0 copy-start.3
  0.6 5.1 %collective-permute-start = (bf16[4,7168]{1,0:T(4,128)(2,1)}, bf16[4,7168]{1,0:T(4,128)(2,1)S(1)}, u32[]{:S(2)}, u32[]{:S(2)}) collective-permute-start(bf16[4,7168]{1,0:T(4,128)(2,1)} %bitcast.13), channel_id=1, source_target_pairs={{0,12},{2,14},{4,8},{6,10},{8,4},{10,6},{12,0},{14,2},{1,13},{3,15... | collective-permute-start | bytes 172040 | tf_op jit(solution)/shard_map/ppermute | solution.py:54
  5.8 0.0 collective-permute-start.1
  5.8 0.6 %collective-permute-start.2 = (bf16[4,7168]{1,0:T(4,128)(2,1)}, bf16[4,7168]{1,0:T(4,128)(2,1)S(1)}, u32[]{:S(2)}, u32[]{:S(2)}) collective-permute-start(bf16[4,7168]{1,0:T(4,128)(2,1)} %bitcast.15), channel_id=1, source_target_pairs={{0,4},{2,6},{4,0},{6,2},{8,12},{10,14},{12,8},{14,10},{1,5},{3,7},... | collective-permute-start | bytes 172040 | tf_op jit(solution)/shard_map/ppermute | solution.py:54
  6.4 3.5 %load_rows.2 = (bf16[576,7168]{1,0:T(8,128)(2,1)S(1)}, bf16[16,16]{1,0:T(8,128)(2,1)S(1)}) custom-call(bf16[1152,7168]{1,0:T(8,128)(2,1)} %refs_0_.2, s32[1,8]{1,0:T(1,128)} %counts_ref.1), custom_call_target="tpu_custom_call" | custom-call | bytes 16515072 | tf_op jit(solution)/shard_map/load_rows/pallas_call | solution.py:177
  9.9 0.0 copy-start.2
  9.9 0.0 collective-permute-done.refs_2_
  9.9 1.1 %collective-permute-done.1.refs_3_ = bf16[4,7168]{1,0:T(4,128)(2,1)S(1)} collective-permute-done((bf16[4,7168]{1,0:T(4,128)(2,1)}, bf16[4,7168]{1,0:T(4,128)(2,1)S(1)}, u32[]{:S(2)}, u32[]{:S(2)}) %collective-permute-start.1) | collective-permute-done | bytes 57376 | tf_op jit(solution)/shard_map/ppermute | solution.py:54
  11.0 0.0 collective-permute-done.2.refs_4_
  11.0 0.0 copy-done.3
  11.0 0.2 compact.1
  11.2 1.6 %collective-permute-start.3 = (bf16[8,7168]{1,0:T(8,128)(2,1)S(1)}, bf16[8,7168]{1,0:T(8,128)(2,1)S(1)}, u32[]{:S(2)}, u32[]{:S(2)}) collective-permute-start(bf16[8,7168]{1,0:T(8,128)(2,1)S(1)} %get-tuple-element.15.refs_1_), channel_id=1, source_target_pairs={{0,2},{2,0},{4,6},{6,4},{8,10},{10,8},{12,14},{14,12},{1,3},{3,1},... | collective-permute-start | bytes 344072 | tf_op jit(solution)/shard_map/ppermute | solution.py:54
  12.8 3.4 %load_rows.3.refs_4_ = bf16[576,7168]{1,0:T(8,128)(2,1)S(1)} custom-call(bf16[1152,7168]{1,0:T(8,128)(2,1)} %refs_0_.3, bf16[8,7168]{1,0:T(8,128)(2,1)S(1)} %get-tuple-element.15.refs_1_), custom_call_target="tpu_custom_call" | custom-call | bytes 16515072 | tf_op jit(solution)/shard_map/load_rows/pallas_call | solution.py:177
  16.3 0.0 collective-permute-done.3
  16.3 0.1 collective-permute-start.4
  16.4 0.0 copy-done.2
  16.4 0.2 normalized.1.refs_1_
  16.6 1.1 %collective-permute-done.4.refs_2_ = bf16[8,7168]{1,0:T(8,128)(2,1)S(1)} collective-permute-done((bf16[8,7168]{1,0:T(8,128)(2,1)S(1)}, bf16[8,7168]{1,0:T(8,128)(2,1)S(1)}, u32[]{:S(2)}, u32[]{:S(2)}) %collective-permute-start.4) | collective-permute-done | bytes 114720 | tf_op jit(solution)/shard_map/ppermute | solution.py:54
  17.7 0.0 copy-start
  17.7 0.0 copy-start.1
  17.7 0.0 copy-start.4
  17.7 0.0 copy-start.5
  17.7 6.0 %feed_forward.1 = (f32[8,7168]{1,0:T(8,128)S(1)}, bf16[8,7168]{1,0:T(8,128)(2,1)S(1)}, bf16[2,7168]{1,0:T(2,128)(2,1)S(1)}) custom-call(f32[1,7168]{1,0:T(1,128)S(1)} %bitcast.12, bf16[8,7168]{1,0:T(8,128)(2,1)S(1)} %normalized.1.refs_1_, bf16[8,7168]{1,0:T(8,128)(2,1)S(1)} %collective-permute-done.4.refs_2_, ...), custom_call_target="tpu_custom_call" | custom-call | flops 396361728 | bytes 24772608 | tf_op jit(solution)/shard_map/feed_forward/pallas_call | solution.py:293
  23.7 0.2 collective-permute-start.5
  23.9 2.6 %collective-permute-start.6 = (bf16[2,7168]{1,0:T(2,128)(2,1)S(1)}, bf16[2,7168]{1,0:T(2,128)(2,1)S(1)}, u32[]{:S(2)}, u32[]{:S(2)}) collective-permute-start(bf16[2,7168]{1,0:T(2,128)(2,1)S(1)} %get-tuple-element.21), channel_id=1, source_target_pairs={{0,12},{2,14},{4,8},{6,10},{8,4},{10,6},{12,0},{14,2},{1,13},{3,15... | collective-permute-start | bytes 86024 | tf_op jit(solution)/shard_map/ppermute | solution.py:54
  26.6 0.0 collective-permute-done.5
  26.6 0.1 fusion.8
  26.7 0.8 %collective-permute-start.7 = (bf16[2,7168]{1,0:T(2,128)(2,1)S(1)}, bf16[2,7168]{1,0:T(2,128)(2,1)S(1)}, u32[]{:S(2)}, u32[]{:S(2)}) collective-permute-start(bf16[2,7168]{1,0:T(2,128)(2,1)S(1)} %get-tuple-element.26), channel_id=1, source_target_pairs={{0,6},{1,15},{2,4},{3,13},{4,2},{5,11},{6,0},{7,9},{8,14},{9,7},{1... | collective-permute-start | bytes 86024 | tf_op jit(solution)/shard_map/ppermute | solution.py:59
  27.5 0.7 %collective-permute-start.8 = (bf16[2,7168]{1,0:T(2,128)(2,1)S(1)}, bf16[2,7168]{1,0:T(2,128)(2,1)S(1)}, u32[]{:S(2)}, u32[]{:S(2)}) collective-permute-start(bf16[2,7168]{1,0:T(2,128)(2,1)S(1)} %get-tuple-element.28), channel_id=1, source_target_pairs={{0,2},{1,11},{2,0},{3,9},{4,6},{5,15},{6,4},{7,13},{8,10},{9,3},{1... | collective-permute-start | bytes 86024 | tf_op jit(solution)/shard_map/ppermute | solution.py:59
  28.2 2.1 %collective-permute-start.9 = (bf16[2,7168]{1,0:T(2,128)(2,1)S(1)}, bf16[2,7168]{1,0:T(2,128)(2,1)S(1)}, u32[]{:S(2)}, u32[]{:S(2)}) collective-permute-start(bf16[2,7168]{1,0:T(2,128)(2,1)S(1)} %get-tuple-element.27), channel_id=1, source_target_pairs={{0,4},{1,9},{2,6},{3,11},{4,0},{5,13},{6,2},{7,15},{8,12},{9,1},{1... | collective-permute-start | bytes 86024 | tf_op jit(solution)/shard_map/ppermute | solution.py:59
  30.2 0.0 copy-done
  30.2 0.0 copy-done.1
  30.2 0.0 copy-done.4
  30.2 0.0 copy-done.5
  30.2 1.6 %attend.1 = bf16[4,64,512]{2,1,0:T(8,128)(2,1)} custom-call(s32[1,4]{1,0:T(1,128)S(1)} %copy-done.5, s32[1,8]{1,0:T(1,128)S(1)} %copy-done.4, bf16[4,64,576]{2,1,0:T(8,128)(2,1)S(1)} %bitcast.10, bf16[4,576,256]{2,1,0:T(8,128)(2,1)S(1)} %bitcast.9, bf16[8,7168]{1,0:T(8,128)(2,1)S(1)} %get-tuple-element.20._), custom_call_target="tpu_custom_call" | custom-call | flops 134217728 | bytes 1474560 | tf_op jit(solution)/shard_map/attend/pallas_call | solution.py:136
  31.9 0.0 collective-permute-done.6
  31.9 0.0 collective-permute-done.7
  31.9 0.0 collective-permute-done.8
  31.9 0.5 %collective-permute-done.9 = bf16[2,7168]{1,0:T(2,128)(2,1)S(1)} collective-permute-done((bf16[2,7168]{1,0:T(2,128)(2,1)S(1)}, bf16[2,7168]{1,0:T(2,128)(2,1)S(1)}, u32[]{:S(2)}, u32[]{:S(2)}) %collective-permute-start.9) | collective-permute-done | bytes 28704 | tf_op jit(solution)/shard_map/ppermute | solution.py:59
  32.4 0.1 fusion.3
  32.5 0.7 %collective-permute-start.10 = (f32[1,7168]{1,0:T(1,128)S(1)}, f32[1,7168]{1,0:T(1,128)S(1)}, u32[]{:S(2)}, u32[]{:S(2)}) collective-permute-start(f32[1,7168]{1,0:T(1,128)S(1)} %slice.29), channel_id=1, source_target_pairs={{0,1},{1,0},{2,3},{3,2},{4,5},{5,4},{6,7},{7,6},{8,9},{9,8},{10,11... | collective-permute-start | bytes 86024 | tf_op jit(solution)/shard_map/ppermute | solution.py:54
  33.2 0.9 %collective-permute-done.10 = f32[1,7168]{1,0:T(1,128)S(1)} collective-permute-done((f32[1,7168]{1,0:T(1,128)S(1)}, f32[1,7168]{1,0:T(1,128)S(1)}, u32[]{:S(2)}, u32[]{:S(2)}) %collective-permute-start.10) | collective-permute-done | bytes 28704 | tf_op jit(solution)/shard_map/ppermute | solution.py:54
  34.1 0.6 %fusion.6 = bf16[1,1,7168]{2,1,0:T(2,128)(2,1)} fusion(bf16[8,7168]{1,0:T(8,128)(2,1)S(1)} %add.24.rows_ref, f32[1,7168]{1,0:T(1,128)S(1)} %collective-permute-done.10, f32[2,7168]{1,0:T(2,128)S(1)} %fusion.3), kind=kLoop, calls=%fused_computation.9 | loop fusion | flops 28672 | bytes 86016 | tf_op jit(solution)/shard_map/broadcast_in_dim | solution.py:366
  (3 shorter events, 0.1 us)
Async XLA Ops:
  0.6 10.4 %copy-start.3 = (bf16[1,4,7168]{2,1,0:T(4,128)(2,1)S(1)}, bf16[1,4,7168]{2,1,0:T(4,128)(2,1)}, u32[]{:S(2)}) copy-start(bf16[1,4,7168]{2,1,0:T(4,128)(2,1)} %param.13) | copy-start | bytes 172036
  0.6 9.2 %collective-permute-start = (bf16[4,7168]{1,0:T(4,128)(2,1)}, bf16[4,7168]{1,0:T(4,128)(2,1)S(1)}, u32[]{:S(2)}, u32[]{:S(2)}) collective-permute-start(bf16[4,7168]{1,0:T(4,128)(2,1)} %bitcast.13), channel_id=1, source_target_pairs={{0,12},{2,14},{4,8},{6,10},{8,4},{10,6},{12,0},{14,2},{1,13},{3,15... | collective-permute-start | bytes 172040 | tf_op jit(solution)/shard_map/ppermute | solution.py:54
  5.8 5.3 %collective-permute-start.1 = (bf16[4,7168]{1,0:T(4,128)(2,1)}, bf16[4,7168]{1,0:T(4,128)(2,1)S(1)}, u32[]{:S(2)}, u32[]{:S(2)}) collective-permute-start(bf16[4,7168]{1,0:T(4,128)(2,1)} %bitcast.14), channel_id=1, source_target_pairs={{0,8},{2,10},{4,12},{6,14},{8,0},{10,2},{12,4},{14,6},{1,9},{3,11}... | collective-permute-start | bytes 172040 | tf_op jit(solution)/shard_map/ppermute | solution.py:54
  5.8 5.3 %collective-permute-start.2 = (bf16[4,7168]{1,0:T(4,128)(2,1)}, bf16[4,7168]{1,0:T(4,128)(2,1)S(1)}, u32[]{:S(2)}, u32[]{:S(2)}) collective-permute-start(bf16[4,7168]{1,0:T(4,128)(2,1)} %bitcast.15), channel_id=1, source_target_pairs={{0,4},{2,6},{4,0},{6,2},{8,12},{10,14},{12,8},{14,10},{1,5},{3,7},... | collective-permute-start | bytes 172040 | tf_op jit(solution)/shard_map/ppermute | solution.py:54
  9.9 6.5 %copy-start.2 = (f32[7168]{0:T(1024)S(1)}, f32[7168]{0:T(1024)}, u32[]{:S(2)}) copy-start(f32[7168]{0:T(1024)} %param.14) | copy-start | bytes 86020
  11.2 5.0 %collective-permute-start.3 = (bf16[8,7168]{1,0:T(8,128)(2,1)S(1)}, bf16[8,7168]{1,0:T(8,128)(2,1)S(1)}, u32[]{:S(2)}, u32[]{:S(2)}) collective-permute-start(bf16[8,7168]{1,0:T(8,128)(2,1)S(1)} %get-tuple-element.15.refs_1_), channel_id=1, source_target_pairs={{0,2},{2,0},{4,6},{6,4},{8,10},{10,8},{12,14},{14,12},{1,3},{3,1},... | collective-permute-start | bytes 344072 | tf_op jit(solution)/shard_map/ppermute | solution.py:54
  16.3 1.4 %collective-permute-start.4 = (bf16[8,7168]{1,0:T(8,128)(2,1)S(1)}, bf16[8,7168]{1,0:T(8,128)(2,1)S(1)}, u32[]{:S(2)}, u32[]{:S(2)}) collective-permute-start(bf16[8,7168]{1,0:T(8,128)(2,1)S(1)} %add.24.rows_ref), channel_id=1, source_target_pairs={{0,1},{1,0},{2,3},{3,2},{4,5},{5,4},{6,7},{7,6},{8,9},{9,8},{10,11... | collective-permute-start | bytes 344072 | tf_op jit(solution)/shard_map/ppermute | solution.py:54
  17.7 12.5 %copy-start = (bf16[1,4,256,576]{2,3,1,0:T(8,128)(2,1)S(1)}, bf16[1,4,256,576]{2,3,1,0:T(8,128)(2,1)}, u32[]{:S(2)}) copy-start(bf16[1,4,256,576]{2,3,1,0:T(8,128)(2,1)} %param.10) | copy-start | bytes 3538948
  17.7 12.5 %copy-start.1 = (bf16[1,4,64,576]{3,2,1,0:T(8,128)(2,1)S(1)}, bf16[1,4,64,576]{3,2,1,0:T(8,128)(2,1)}, u32[]{:S(2)}) copy-start(bf16[1,4,64,576]{3,2,1,0:T(8,128)(2,1)} %param.9) | copy-start | bytes 884740
  17.7 12.5 %copy-start.4 = (s32[1,8]{1,0:T(1,128)S(1)}, s32[1,8]{1,0:T(1,128)}, u32[]{:S(2)}) copy-start(s32[1,8]{1,0:T(1,128)} %counts_ref.1) | copy-start | bytes 100
  17.7 12.5 %copy-start.5 = (s32[1,4]{1,0:T(1,128)S(1)}, s32[1,4]{1,0:T(1,128)}, u32[]{:S(2)}) copy-start(s32[1,4]{1,0:T(1,128)} %lengths_ref.1) | copy-start | bytes 52
  23.7 2.8 %collective-permute-start.5 = (bf16[8,7168]{1,0:T(8,128)(2,1)S(1)}, bf16[8,7168]{1,0:T(8,128)(2,1)S(1)}, u32[]{:S(2)}, u32[]{:S(2)}) collective-permute-start(bf16[8,7168]{1,0:T(8,128)(2,1)S(1)} %get-tuple-element.20._), channel_id=1, source_target_pairs={{0,1},{1,0},{2,3},{3,2},{4,5},{5,4},{6,7},{7,6},{8,9},{9,8},{10,11... | collective-permute-start | bytes 344072 | tf_op jit(solution)/shard_map/ppermute | solution.py:54
  23.9 7.9 %collective-permute-start.6 = (bf16[2,7168]{1,0:T(2,128)(2,1)S(1)}, bf16[2,7168]{1,0:T(2,128)(2,1)S(1)}, u32[]{:S(2)}, u32[]{:S(2)}) collective-permute-start(bf16[2,7168]{1,0:T(2,128)(2,1)S(1)} %get-tuple-element.21), channel_id=1, source_target_pairs={{0,12},{2,14},{4,8},{6,10},{8,4},{10,6},{12,0},{14,2},{1,13},{3,15... | collective-permute-start | bytes 86024 | tf_op jit(solution)/shard_map/ppermute | solution.py:54
  26.7 5.2 %collective-permute-start.7 = (bf16[2,7168]{1,0:T(2,128)(2,1)S(1)}, bf16[2,7168]{1,0:T(2,128)(2,1)S(1)}, u32[]{:S(2)}, u32[]{:S(2)}) collective-permute-start(bf16[2,7168]{1,0:T(2,128)(2,1)S(1)} %get-tuple-element.26), channel_id=1, source_target_pairs={{0,6},{1,15},{2,4},{3,13},{4,2},{5,11},{6,0},{7,9},{8,14},{9,7},{1... | collective-permute-start | bytes 86024 | tf_op jit(solution)/shard_map/ppermute | solution.py:59
  27.5 4.4 %collective-permute-start.8 = (bf16[2,7168]{1,0:T(2,128)(2,1)S(1)}, bf16[2,7168]{1,0:T(2,128)(2,1)S(1)}, u32[]{:S(2)}, u32[]{:S(2)}) collective-permute-start(bf16[2,7168]{1,0:T(2,128)(2,1)S(1)} %get-tuple-element.28), channel_id=1, source_target_pairs={{0,2},{1,11},{2,0},{3,9},{4,6},{5,15},{6,4},{7,13},{8,10},{9,3},{1... | collective-permute-start | bytes 86024 | tf_op jit(solution)/shard_map/ppermute | solution.py:59
  28.2 4.2 %collective-permute-start.9 = (bf16[2,7168]{1,0:T(2,128)(2,1)S(1)}, bf16[2,7168]{1,0:T(2,128)(2,1)S(1)}, u32[]{:S(2)}, u32[]{:S(2)}) collective-permute-start(bf16[2,7168]{1,0:T(2,128)(2,1)S(1)} %get-tuple-element.27), channel_id=1, source_target_pairs={{0,4},{1,9},{2,6},{3,11},{4,0},{5,13},{6,2},{7,15},{8,12},{9,1},{1... | collective-permute-start | bytes 86024 | tf_op jit(solution)/shard_map/ppermute | solution.py:59
  32.5 1.6 %collective-permute-start.10 = (f32[1,7168]{1,0:T(1,128)S(1)}, f32[1,7168]{1,0:T(1,128)S(1)}, u32[]{:S(2)}, u32[]{:S(2)}) collective-permute-start(f32[1,7168]{1,0:T(1,128)S(1)} %slice.29), channel_id=1, source_target_pairs={{0,1},{1,0},{2,3},{3,2},{4,5},{5,4},{6,7},{7,6},{8,9},{9,8},{10,11... | collective-permute-start | bytes 86024 | tf_op jit(solution)/shard_map/ppermute | solution.py:54
